TPU v7x, 32 devices: a whole 2x2x4 slice. The times are simulated.
32 devices in a mesh: member: 4 (over z), tile: 4 (over x, core), batch: 2 (over y).
Axes of the slice: x: 2, y: 2, z: 4, core: 2. Of those that a mesh axis runs over, the one named last changes fastest.
Arguments:
- latent: bfloat16 [4, 2, 4096, 1024], P('member', 'batch', 'tile'), may hold values from -6 to 6
- w_in: bfloat16 [1024, 1024], replicated, may hold values from -0.1875 to 0.1875
- w_out: bfloat16 [1024, 112], replicated, may hold values from -0.1875 to 0.1875
- observed: bfloat16 [2, 512, 1792], P('batch', 'tile'), may hold values from -5 to 5
- patch_index: int32 [2, 256], P('batch', 'tile'), may hold values from 0 to 127
- counts: int32 [2, 256], P('batch', 'tile'), may hold values from 1 to 8
Outputs:
- grad_w1: float32 [1024, 1024], P(('member', 'tile', 'batch'))
- grad_w2: float32 [1024, 112], P(('member', 'tile', 'batch'))
Inputs may be any that keep to these rules, and one draw needn't show every extreme that they name: `patch_index`: a candidate of the same tile and lead time.
All inputs are finite; a program needn't handle non-finite values.
Results may differ from a plain program's by a relative error of at most 0.0017.
Values sent between devices are 32-bit elements; how exact they have to be, the bound alone decides.
No kernel may reach another device: no remote copies, remote signals or barrier semaphores. Data moves between devices by JAX's collectives and lax.ppermute only.
A program may use at most 64 MiB of HBM per device.

v0:
```python
import jax
import jax.numpy as jnp
from jax import lax
from jax.sharding import PartitionSpec as P

PATCH = 16


def smooth_grad(deltas):
    return deltas / jnp.sqrt(jnp.sum(deltas * deltas, axis=-1, keepdims=True) + 1.0)


def shards(latent, w_in, w_out, observed, patch_index, counts):
    rows_in = latent[0, 0]
    nrows = rows_in.shape[0]
    channels = w_out.shape[1]
    width = w_in.shape[1]
    members = lax.axis_size("member")
    preact = jnp.dot(rows_in, w_in, preferred_element_type=jnp.float32)
    hidden = jax.nn.silu(preact).astype(jnp.bfloat16)
    decoded = jnp.dot(hidden, w_out, preferred_element_type=jnp.float32)
    npatch = nrows // PATCH
    patches = decoded.reshape(npatch, PATCH * channels)
    blocks = patches.reshape(members, 1, npatch // members, PATCH * channels)
    grouped = lax.all_to_all(blocks, "member", split_axis=0, concat_axis=1, tiled=True)
    deltas = grouped[:, :, None] - grouped[:, None, :]
    summed = jnp.sum(smooth_grad(deltas), axis=2)
    returned = lax.all_to_all(summed, "member", split_axis=1, concat_axis=0, tiled=True)
    pair = returned.reshape(npatch, PATCH * channels)
    pool = observed[0]
    picked = patch_index[0]
    choose = (picked[:, None] == jnp.arange(pool.shape[0], dtype=jnp.int32)[None, :]).astype(
        jnp.bfloat16
    )
    target = jnp.dot(choose, pool, preferred_element_type=jnp.float32)
    own = smooth_grad(patches - target)
    weight = counts[0].astype(jnp.float32)[:, None]
    grad_patch = weight * (own / members - pair / (members * members))
    grad_out = grad_patch.reshape(nrows, channels).astype(jnp.bfloat16)
    grad_hidden = lax.dot_general(
        grad_out, w_out, (((1,), (1,)), ((), ())), preferred_element_type=jnp.float32
    )
    sigma = jax.nn.sigmoid(preact)
    grad_preact = (grad_hidden * sigma * (1.0 + preact * (1.0 - sigma))).astype(jnp.bfloat16)
    first = lax.dot_general(
        rows_in, grad_preact, (((0,), (0,)), ((), ())), preferred_element_type=jnp.float32
    )
    second = lax.dot_general(
        hidden, grad_out, (((0,), (0,)), ((), ())), preferred_element_type=jnp.float32
    )
    totals = lax.psum_scatter(
        jnp.concatenate([first, second], axis=1),
        ("member", "tile", "batch"),
        scatter_dimension=0,
        tiled=True,
    )
    return (totals[:, :width], totals[:, width:])


def solution(mesh):
    in_specs = (
        P("member", "batch", "tile", None),
        P(),
        P(),
        P("batch", "tile", None),
        P("batch", "tile"),
        P("batch", "tile"),
    )
    out_specs = (P(("member", "tile", "batch"), None), P(("member", "tile", "batch"), None))
    return jax.shard_map(shards, mesh=mesh, in_specs=in_specs, out_specs=out_specs, check_vma=False)
```

profile of v0, /device:TPU:0, one launch (start us, length us, event | category | flops | bytes accessed | tf_op | source)
XLA Modules:
  0.0 192.5 jit_solution(8611842942700841871)
XLA Ops:
  7.2 0.0 copy-start
  7.2 0.0 copy-start.2
  7.2 1.6 copy-done
  8.8 6.2 %multiply_convert_fusion.1 = (bf16[1024,1024]{1,0:T(8,128)(2,1)S(1)}, f32[1024,1024]{1,0:T(8,128)}) fusion(bf16[1024,1024]{1,0:T(8,128)(2,1)} %param.7, bf16[1,1,1024,1024]{3,2,1,0:T(8,128)(2,1)S(1)} %copy-done), kind=kOutput, calls=%fused_computation.2 | convolution fusion | flops 2152726528 | bytes 10485760 | tf_op jit(solution)/shard_map/dot_general | solution.py:19
  14.9 0.0 copy-start.1
  14.9 1.3 copy-done.1
  16.2 0.0 copy-done.2
  16.3 0.7 fusion.10
  17.0 1.0 reshape_reshape.3
  18.0 6.3 %all-to-all-start = ((f32[4,1,16,1792]{3,2,1,0:T(8,128)}), f32[4,1,16,1792]{3,2,1,0:T(8,128)S(1)}, u32[]{:S(2)}, u32[]{:S(2)}) async-start(f32[4,1,16,1792]{3,2,1,0:T(8,128)} %bitcast.4), calls=%async_computation | async-start | bytes 917504 | tf_op jit(solution)/shard_map/all_to_all | solution.py:25
  24.3 0.2 reshape.65
  24.6 12.8 %all-to-all-done = f32[4,1,16,1792]{3,2,1,0:T(8,128)S(1)} async-done(((f32[4,1,16,1792]{3,2,1,0:T(8,128)}), f32[4,1,16,1792]{3,2,1,0:T(8,128)S(1)}, u32[]{:S(2)}, u32[]{:S(2)}) %all-to-all-start) | async-done | bytes 458784 | tf_op jit(solution)/shard_map/all_to_all | solution.py:25
  37.4 0.3 fusion.4
  37.7 1.1 fusion.3
  38.7 3.5 %all-to-all-start.1 = ((f32[1,4,16,1792]{3,2,0,1:T(8,128)}), f32[1,4,16,1792]{3,2,0,1:T(8,128)S(1)}, u32[]{:S(2)}, u32[]{:S(2)}) async-start(f32[1,4,16,1792]{3,2,0,1:T(8,128)} %bitcast.38), calls=%async_computation.1 | async-start | bytes 917504 | tf_op jit(solution)/shard_map/all_to_all | solution.py:28
  42.2 0.0 reduce-scatter.4.cloned.1.call-start
  42.3 0.0 copy-done.5
  42.3 0.0 copy-done.4
  42.3 1.4 multiply_reduce_fusion
  43.7 11.1 %all-to-all-done.1 = f32[1,4,16,1792]{3,2,0,1:T(8,128)S(1)} async-done(((f32[1,4,16,1792]{3,2,0,1:T(8,128)}), f32[1,4,16,1792]{3,2,0,1:T(8,128)S(1)}, u32[]{:S(2)}, u32[]{:S(2)}) %all-to-all-start.1) | async-done | bytes 458784 | tf_op jit(solution)/shard_map/all_to_all | solution.py:28
  54.8 0.1 fusion.6
  55.0 0.4 convert_element_type.27
  55.3 0.0 copy-start.3
  55.3 2.1 %fusion.11 = f32[1024,112]{0,1:T(8,128)S(1)} fusion(bf16[1024,1024]{1,0:T(8,128)(2,1)} %copy-done.1, bf16[1024,112]{1,0:T(8,128)(2,1)S(1)} %convert_element_type.27), kind=kOutput, calls=%fused_computation.26 | convolution fusion | flops 234881024 | bytes 2785280 | tf_op jit(solution)/shard_map/dot_general | solution.py:48
  57.5 0.0 copy-done.3
  57.5 7.9 %convolution_bitcast_fusion = f32[1024,1024]{0,1:T(8,128)} fusion(bf16[1,1,1024,1024]{3,2,1,0:T(8,128)(2,1)S(1)} %copy-done, f32[1024,1024]{1,0:T(8,128)} %get-tuple-element.11, bf16[1024,112]{1,0:T(8,128)(2,1)S(1)} %convert_element_type.27, bf16[1024,112]{0,1:T(8,128)(2,1)S(1)} %copy-done.3), kind=kOutput, calls=%fused_computation.7 | convolution fusion | flops 2391801856 | bytes 10944512 | tf_op jit(solution)/shard_map/dot_general | solution.py:45
  65.4 5.0 %pad_maximum_fusion = f32[1024,1136]{0,1:T(8,128)} fusion(f32[1024,112]{0,1:T(8,128)S(1)} %fusion.11, f32[1024,1024]{0,1:T(8,128)} %convolution_bitcast_fusion), kind=kLoop, calls=%fused_computation | loop fusion | flops 1163264 | bytes 9306112 | tf_op jit(solution)/shard_map/concatenate | solution.py:52
  70.4 6.1 %copy.26 = f32[1024,1136]{1,0:T(8,128)} copy(f32[1024,1136]{0,1:T(8,128)} %pad_maximum_fusion) | data formatting | bytes 9306112
  76.5 0.0 reduce-scatter.4.cloned.1.call-update
  76.5 106.3 %reduce-scatter.4.cloned.1.call-done = f32[32,1136]{1,0:T(8,128)} async-done(((f32[1024,1136]{1,0:T(8,128)}), f32[32,1136]{1,0:T(8,128)}) %reduce-scatter.4.cloned.1.call-update) | async-done | bytes 145424
  182.8 1.3 slice.9
  184.1 1.6 slice.8
  (6 shorter events, 0.1 us)
Async XLA Ops:
  7.2 1.6 copy-start
  7.2 9.1 %copy-start.2 = (bf16[1024,112]{0,1:T(8,128)(2,1)S(1)}, bf16[1024,112]{0,1:T(8,128)(2,1)}, u32[]{:S(2)}) copy-start(bf16[1024,112]{0,1:T(8,128)(2,1)} %param.8) | copy-start | bytes 688132
  14.9 1.3 copy-start.1
  18.0 19.4 %all-to-all-start = ((f32[4,1,16,1792]{3,2,1,0:T(8,128)}), f32[4,1,16,1792]{3,2,1,0:T(8,128)S(1)}, u32[]{:S(2)}, u32[]{:S(2)}) async-start(f32[4,1,16,1792]{3,2,1,0:T(8,128)} %bitcast.4), calls=%async_computation | async-start | bytes 917504 | tf_op jit(solution)/shard_map/all_to_all | solution.py:25
  24.3 18.0 %copy-start.5 = (s32[1,64]{1,0:T(1,128)S(1)}, s32[1,64]{1,0:T(1,128)}, u32[]{:S(2)}) copy-start(s32[1,64]{1,0:T(1,128)} %param.11) | copy-start | bytes 772
  24.3 18.0 %copy-start.4 = (s32[1,64]{1,0:T(1,128)S(1)}, s32[1,64]{1,0:T(1,128)}, u32[]{:S(2)}) copy-start(s32[1,64]{1,0:T(1,128)} %param.10) | copy-start | bytes 772
  38.7 16.0 %all-to-all-start.1 = ((f32[1,4,16,1792]{3,2,0,1:T(8,128)}), f32[1,4,16,1792]{3,2,0,1:T(8,128)S(1)}, u32[]{:S(2)}, u32[]{:S(2)}) async-start(f32[1,4,16,1792]{3,2,0,1:T(8,128)} %bitcast.38), calls=%async_computation.1 | async-start | bytes 917504 | tf_op jit(solution)/shard_map/all_to_all | solution.py:28
  42.2 140.6 %reduce-scatter.4.cloned.1.call-start = ((), (), s32[]{:S(2)}) async-start(), calls=%async_computation.3 | async-start | bytes 4866048
  55.3 2.1 %copy-start.3 = (bf16[1024,112]{0,1:T(8,128)(2,1)S(1)}, bf16[1024,112]{0,1:T(8,128)(2,1)}, u32[]{:S(2)}) copy-start(bf16[1024,112]{0,1:T(8,128)(2,1)} %param.8) | copy-start | bytes 688132
Sparse Core Ops, SparseCore 0:
  76.6 106.0 reduce-scatter.3
where the time goes:
time: 193 us
  waiting for transfers between devices  130 us (67%)
  matrix products  18.3 us (9%)
  between operations  14.2 us (7%)
  local copies, waits for them, and re-layouts  13.5 us (7%)
  starting transfers between devices  9.83 us (5%)
  other arithmetic  6.56 us (3%)
    unnamed x2, waiting for transfers between devices  106 us
    all_to_all x1, waiting for transfers between devices, shards(): lax.all_to_all(blocks, 'member', split_axis=0, concat_axis=1, tiled=True)  12.8 us
    all_to_all x1, waiting for transfers between devices, shards(): lax.all_to_all(summed, 'member', split_axis=1, concat_axis=0, tiled=True)  11.1 us
    unnamed x13, local copies, waits for them, and re-layouts  8.97 us
    dot_general x1, matrix products, shards(): lax.dot_general(rows_in, grad_preact, (((0,), (0,)), ((), ())), preferred...  7.91 us
    all_to_all x1, starting transfers between devices, shards(): lax.all_to_all(blocks, 'member', split_axis=0, concat_axis=1, tiled=True)  6.32 us
    dot_general x1, matrix products, shards(): preact = jnp.dot(rows_in, w_in, preferred_element_type=jnp.float32)  6.18 us
    concatenate x1, other arithmetic, shards(): jnp.concatenate([first, second], axis=1)  5.03 us
  transfers between devices with their start and end apart: 3, of which 3 were waited for; matrix products, arithmetic and copies ran while one was open for 1% of the time, Pallas kernels for 0%

commit v1 on v0

v1 whole, which is shorter than its diff:
```python
import functools

import jax
import jax.numpy as jnp
import numpy as np
from jax import lax
from jax.experimental import pallas as pl
from jax.experimental.pallas import tpu as pltpu
from jax.sharding import PartitionSpec as P

PATCH = 16
CORES = 2
MIB = 1 << 20
NT = (((1,), (1,)), ((), ()))
WHOLE = pl.BlockSpec(memory_space=pltpu.VMEM)


def chunk_of(extent, target):
    return target if extent % target == 0 else extent


def forward_body(latent_ref, w_in_ref, w_out_t_ref, hidden_ref, slope_ref, decoded_ref):
    preact = jnp.dot(latent_ref[...], w_in_ref[...], preferred_element_type=jnp.float32)
    sigma = 1.0 / (1.0 + jnp.exp(-preact))
    hidden = (preact * sigma).astype(jnp.bfloat16)
    hidden_ref[...] = hidden
    slope_ref[...] = sigma * (1.0 + preact * (1.0 - sigma))
    decoded_ref[...] = lax.dot_general(hidden, w_out_t_ref[...], NT, preferred_element_type=jnp.float32)


def forward(rows_in, w_in, w_out_t):
    nrows, depth = rows_in.shape
    width = w_in.shape[1]
    channels = w_out_t.shape[0]
    block = chunk_of(nrows, 256)
    return pl.pallas_call(
        forward_body,
        grid=(nrows // block,),
        in_specs=[
            pl.BlockSpec((block, depth), lambda i: (i, 0)),
            pl.BlockSpec((depth, width), lambda i: (0, 0)),
            pl.BlockSpec((channels, width), lambda i: (0, 0)),
        ],
        out_specs=[
            pl.BlockSpec((block, width), lambda i: (i, 0)),
            pl.BlockSpec((block, width), lambda i: (i, 0)),
            pl.BlockSpec((block, channels), lambda i: (i, 0)),
        ],
        out_shape=[
            jax.ShapeDtypeStruct((nrows, width), jnp.bfloat16),
            jax.ShapeDtypeStruct((nrows, width), jnp.float32),
            jax.ShapeDtypeStruct((nrows, channels), jnp.float32),
        ],
        compiler_params=pltpu.CompilerParams(vmem_limit_bytes=24 * MIB),
        cost_estimate=pl.CostEstimate(
            flops=2 * nrows * width * (depth + channels), bytes_accessed=10 * MIB, transcendentals=nrows * width
        ),
        name="forward",
    )(rows_in, w_in, w_out_t)


def score_body(x_ref, pool_ref, index_ref, count_ref, out_ref):
    members, npatch, _ = x_ref.shape
    npool = pool_ref.shape[0]
    choose = index_ref[...] == lax.broadcasted_iota(jnp.int32, (npatch, npool), 1)
    target = jnp.dot(choose.astype(jnp.bfloat16), pool_ref[...], preferred_element_type=jnp.float32)
    weight = count_ref[...].astype(jnp.float32)

    def direction(delta):
        return delta / jnp.sqrt(jnp.sum(delta * delta, axis=-1, keepdims=True) + 1.0)

    xs = [x_ref[m] for m in range(members)]
    pair = [jnp.zeros_like(xs[0]) for _ in range(members)]
    for m in range(members):
        for k in range(m + 1, members):
            term = direction(xs[m] - xs[k])
            pair[m] = pair[m] + term
            pair[k] = pair[k] - term
    for m in range(members):
        own = direction(xs[m] - target)
        out_ref[m] = weight * (own / members - pair[m] / (members * members))


def score(grouped, pool, index, count):
    return pl.pallas_call(
        score_body,
        in_specs=[WHOLE] * 4,
        out_specs=WHOLE,
        out_shape=jax.ShapeDtypeStruct(grouped.shape, jnp.float32),
        compiler_params=pltpu.CompilerParams(vmem_limit_bytes=24 * MIB),
        cost_estimate=pl.CostEstimate(flops=30 * grouped.size, bytes_accessed=8 * grouped.size, transcendentals=0),
        name="score",
    )(grouped, pool, index, count)


def first_body(step, g_ref, slope_ref, w_out_t_ref, latent_t_ref, hidden_t_ref, out_ref, gp_ref, g16_ref):
    j = pl.program_id(0)
    width = out_ref.shape[1] - g_ref.shape[1]
    g16 = g_ref[...].astype(jnp.bfloat16)
    gh = jnp.dot(g16, w_out_t_ref[...], preferred_element_type=jnp.float32)
    gp = (gh * slope_ref[...]).astype(jnp.bfloat16)
    gp_ref[...] = gp
    columns = pl.ds(pl.multiple_of(j * step, step), step)
    out_ref[:, columns] = jnp.dot(latent_t_ref[...], gp, preferred_element_type=jnp.float32)

    @pl.when(j == 0)
    def _():
        g16_ref[...] = g16
        out_ref[:, width:] = jnp.dot(hidden_t_ref[...], g16, preferred_element_type=jnp.float32)


def first_products(g, slope, w_out_t, latent_t, hidden_t):
    nrows, channels = g.shape
    width = slope.shape[1]
    picked = latent_t.shape[0]
    step = chunk_of(width, 256)
    return pl.pallas_call(
        functools.partial(first_body, step),
        grid=(width // step,),
        in_specs=[
            pl.BlockSpec((nrows, channels), lambda j: (0, 0)),
            pl.BlockSpec((nrows, step), lambda j: (0, j)),
            pl.BlockSpec((channels, step), lambda j: (0, j)),
            pl.BlockSpec((picked, nrows), lambda j: (0, 0)),
            pl.BlockSpec((picked, nrows), lambda j: (0, 0)),
        ],
        out_specs=[
            pl.BlockSpec((picked, width + channels), lambda j: (0, 0)),
            pl.BlockSpec((nrows, step), lambda j: (0, j)),
            pl.BlockSpec((nrows, channels), lambda j: (0, 0)),
        ],
        out_shape=[
            jax.ShapeDtypeStruct((picked, width + channels), jnp.float32),
            jax.ShapeDtypeStruct((nrows, width), jnp.bfloat16),
            jax.ShapeDtypeStruct((nrows, channels), jnp.bfloat16),
        ],
        compiler_params=pltpu.CompilerParams(vmem_limit_bytes=24 * MIB),
        cost_estimate=pl.CostEstimate(
            flops=2 * nrows * (width * (channels + picked)), bytes_accessed=8 * MIB, transcendentals=0
        ),
        name="first_products",
    )(g, slope, w_out_t, latent_t, hidden_t)


def more_body(step, cuts, gp_ref, g16_ref, latent_t_ref, hidden_t_ref, *out_refs):
    j = pl.program_id(0)
    width = out_refs[0].shape[1] - g16_ref.shape[1]
    columns = pl.ds(pl.multiple_of(j * step, step), step)
    product = jnp.dot(latent_t_ref[...], gp_ref[...], preferred_element_type=jnp.float32)
    for out_ref, low, high in zip(out_refs, cuts[:-1], cuts[1:]):
        out_ref[:, columns] = product[low:high]

    @pl.when(j == 0)
    def _():
        second = jnp.dot(hidden_t_ref[...], g16_ref[...], preferred_element_type=jnp.float32)
        for out_ref, low, high in zip(out_refs, cuts[:-1], cuts[1:]):
            out_ref[:, width:] = second[low:high]


def more_products(gp, g16, latent_t, hidden_t, sizes):
    nrows, channels = g16.shape
    width = gp.shape[1]
    picked = latent_t.shape[0]
    step = chunk_of(width, 256)
    cuts = tuple(int(c) for c in np.cumsum([0, *sizes]))
    return pl.pallas_call(
        functools.partial(more_body, step, cuts),
        grid=(width // step,),
        in_specs=[
            pl.BlockSpec((nrows, step), lambda j: (0, j)),
            pl.BlockSpec((nrows, channels), lambda j: (0, 0)),
            pl.BlockSpec((picked, nrows), lambda j: (0, 0)),
            pl.BlockSpec((picked, nrows), lambda j: (0, 0)),
        ],
        out_specs=[pl.BlockSpec((size, width + channels), lambda j: (0, 0)) for size in sizes],
        out_shape=[jax.ShapeDtypeStruct((size, width + channels), jnp.float32) for size in sizes],
        compiler_params=pltpu.CompilerParams(vmem_limit_bytes=24 * MIB),
        cost_estimate=pl.CostEstimate(
            flops=2 * nrows * picked * (width + channels), bytes_accessed=6 * MIB, transcendentals=0
        ),
        name="more_products",
    )(gp, g16, latent_t, hidden_t)


def piece_orders(nz, nx, nc, ny, ra, rb, rc):
    def grid(xs, ys, zs, rows, order):
        cells = {"x": list(xs), "y": list(ys), "z": list(zs), "r": list(rows)}
        mesh = np.meshgrid(*[cells[k] for k in order], indexing="ij")
        by = {k: v.reshape(-1) for k, v in zip(order, mesh)}
        return np.stack([by["z"], by["x"], by["y"], by["r"]], axis=1)

    a_rows, b_rows, c_rows = range(ra), range(ra, ra + rb), range(ra + rb, ra + rb + rc)
    z, x, y = range(nz), range(nx), range(ny)
    a_send = grid(x[1:], y, z, a_rows, "xyzr")
    b_send = grid(x, y[1:], z, b_rows, "yxzr")
    c_all = grid(x, y, z, c_rows, "zxyr")
    a_keep = grid(x[:1], y, z, a_rows, "xyzr")
    b_keep = grid(x, y[:1], z, b_rows, "yxzr")

    def at(core, parts):
        rows = np.concatenate(parts, axis=0)
        return np.concatenate([np.full((len(rows), 1), core), rows], axis=1)

    other = [at(core, [a_send, b_send]) for core in range(1, nc)]
    rest = [at(core, [c_all, a_keep, b_keep]) for core in range(1, nc)]
    return {
        "sizes": (len(a_send), len(b_send), len(c_all), len(a_keep), len(b_keep)),
        "first": np.concatenate(other, axis=0),
        "second": np.concatenate(rest + [at(0, [a_send, b_send])], axis=0),
        "third": at(0, [c_all, a_keep, b_keep]),
    }


def shards(latent, w_in, w_out, observed, patch_index, counts):
    rows_in = latent[0, 0]
    nrows, depth = rows_in.shape
    width, channels = w_out.shape
    nz, nt, ny = (lax.axis_size(name) for name in ("member", "tile", "batch"))
    nc, nx = CORES, nt // CORES
    me_z, me_t, me_y = (lax.axis_index(name) for name in ("member", "tile", "batch"))
    me_x, me_c = me_t // nc, me_t % nc
    w_out_t = w_out.T

    hidden, slope, decoded = forward(rows_in, w_in, w_out_t)
    npatch = nrows // PATCH
    share = npatch // nz
    blocks = decoded.reshape(nz, share, PATCH * channels)
    grouped = lax.all_to_all(blocks, "member", split_axis=0, concat_axis=0, tiled=True)

    height = depth // (nz * nt * ny)
    rc = max(height // 4, 1)
    ra = (height - rc) // 2
    rb = height - rc - ra
    orders = piece_orders(nz, nx, nc, ny, ra, rb, rc)

    def pick(order, matrix):
        core, z, x, y, row = (jnp.asarray(order[:, k], jnp.int32) for k in range(5))
        tile = (x + me_x) % nx * nc + (core + me_c) % nc
        source = ((z * nt + tile) * ny + (y + me_y) % ny) * height + row
        choose = (source[:, None] == jnp.arange(matrix.shape[1], dtype=jnp.int32)[None, :]).astype(jnp.bfloat16)
        return lax.dot_general(choose, matrix, NT, preferred_element_type=jnp.float32).astype(jnp.bfloat16)

    latent_t = {name: pick(orders[name], rows_in) for name in ("first", "second", "third")}
    hidden_t = {name: pick(orders[name], hidden) for name in ("first", "second", "third")}

    index = lax.dynamic_slice_in_dim(patch_index[0], me_z * share, share, 0)[:, None]
    count = lax.dynamic_slice_in_dim(counts[0], me_z * share, share, 0)[:, None]
    scored = score(grouped, observed[0], index, count)
    returned = lax.all_to_all(scored, "member", split_axis=0, concat_axis=0, tiled=True)
    g = returned.reshape(nrows, channels)

    def shift_core(value, j):
        return lax.ppermute(value, "tile", [(t, t // nc * nc + (t % nc + j) % nc) for t in range(nt)])

    def shift_x(value, j):
        return lax.ppermute(value, "tile", [(t, (t // nc + j) % nx * nc + t % nc) for t in range(nt)])

    def shift_y(value, j):
        return lax.ppermute(value, "batch", [(t, (t + j) % ny) for t in range(ny)])

    na_send, nb_send, n_c, na_keep, nb_keep = orders["sizes"]
    n_rest = n_c + na_keep + nb_keep

    first, gp, g16 = first_products(g, slope, w_out_t, latent_t["first"], hidden_t["first"])
    from_core_send = shift_core(first, 1)
    rest, a_send, b_send = more_products(
        gp, g16, latent_t["second"], hidden_t["second"], (n_rest, na_send, nb_send)
    )
    from_core_rest = shift_core(rest, 1)
    a_send = a_send + from_core_send[:na_send]
    b_send = b_send + from_core_send[na_send:]

    def pieces(value, count):
        return value.reshape(count, value.shape[0] // count, value.shape[1])

    def send_all(value, count, shift):
        stacked = pieces(value, count)
        return [shift(stacked[j], j + 1) for j in range(count)]

    a_got = send_all(a_send, nx - 1, shift_x)
    b_got = send_all(b_send, ny - 1, shift_y)
    c_own, a_keep, b_keep = more_products(gp, g16, latent_t["third"], hidden_t["third"], (n_c, na_keep, nb_keep))
    c_own = c_own + from_core_rest[:n_c]
    c_got = lax.all_to_all(pieces(c_own, nz), "member", split_axis=0, concat_axis=0, tiled=True)
    a_keep = sum(a_got, a_keep + from_core_rest[n_c:n_c + na_keep])
    b_keep = sum(b_got, b_keep + from_core_rest[n_c + na_keep:])

    a_keep, b_keep = pieces(a_keep, ny), pieces(b_keep, nx)
    a_got = [shift_y(a_keep[j], j) for j in range(1, ny)]
    b_got = [shift_x(b_keep[j], j) for j in range(1, nx)]
    a_here = pieces(sum(a_got, a_keep[0]), nz)
    b_here = pieces(sum(b_got, b_keep[0]), nz)
    ab_got = lax.all_to_all(
        jnp.concatenate([a_here, b_here], axis=1), "member", split_axis=0, concat_axis=0, tiled=True
    )

    c_here = pieces(jnp.sum(c_got, axis=0), nx)
    c_here = sum([shift_x(c_here[j], j) for j in range(1, nx)], c_here[0])
    c_here = pieces(c_here, ny)
    c_here = sum([shift_y(c_here[j], j) for j in range(1, ny)], c_here[0])
    total = jnp.concatenate([jnp.sum(ab_got, axis=0), c_here], axis=0)
    return (total[:, :width], total[:, width:])


def solution(mesh):
    in_specs = (
        P("member", "batch", "tile", None),
        P(),
        P(),
        P("batch", "tile", None),
        P("batch", "tile"),
        P("batch", "tile"),
    )
    out_specs = (P(("member", "tile", "batch"), None), P(("member", "tile", "batch"), None))
    return jax.shard_map(shards, mesh=mesh, in_specs=in_specs, out_specs=out_specs, check_vma=False)
```

time: 193 us -> 123 us (0.64)
  waiting for transfers between devices: 130 us -> 52.4 us
  Pallas kernels: 0 us -> 15.5 us
  starting transfers between devices: 9.83 us -> 24.2 us
  between operations: 14.2 us -> 1.05 us
  matrix products: 18.3 us -> 8.47 us
    unnamed x2 -> x0, waiting for transfers between devices: 106 us -> none
    ppermute x0 -> x8, waiting for transfers between devices: none -> 16.1 us  [the longest x3 14.8 us: shift_x(): lax.ppermute(value, 'tile', [(t, (t // nc + j) % nx * nc + t % nc) for t...]
    pallas_call x0 -> x5, Pallas kernels: none -> 15.5 us  [the longest x2 5.63 us: more_products(): pl.pallas_call(functools.partial(more_body, step, cuts), grid=(width // s...]
    all_to_all x2 -> x4, waiting for transfers between devices: 23.9 us -> 36.4 us  [the longest x1 12.8 us: shards(): lax.all_to_all(blocks, 'member', split_axis=0, concat_axis=0, tiled=True)]
    dot_general x5 -> x6, matrix products: 18.3 us -> 8.47 us  [pick(): lax.dot_general(choose, matrix, NT, preferred_element_type=jnp.float32)]
    all_to_all x2 -> x4, starting transfers between devices: 9.79 us -> 17.5 us  [the longest x1 6.3 us: shards(): lax.all_to_all(blocks, 'member', split_axis=0, concat_axis=0, tiled=True)]
    ppermute x0 -> x8, starting transfers between devices: none -> 6.76 us  [the longest x3 3.66 us: shift_y(): return lax.ppermute(value, 'batch', [(t, (t + j) % ny) for t in range(ny)])]
    add x0 -> x10, other arithmetic: none -> 4.73 us  [the longest x1 1.95 us: shards(): c_own = c_own + from_core_rest[:n_c]]
  transfers between devices with their start and end apart: 3 -> 12, of which waited for: 3 -> 8; matrix products, arithmetic and copies ran while one was open for 1% -> 11% of each run, Pallas kernels for 0% -> 5%
where the time goes in v1:
time: 123 us; the launch traced here: 122 us
  waiting for transfers between devices  52.4 us (43%)
  starting transfers between devices  24.2 us (20%)
  Pallas kernels  15.5 us (13%)
  local copies, waits for them, and re-layouts  13.7 us (11%)
  matrix products  8.47 us (7%)
  other arithmetic  6.86 us (6%)
    ppermute x3, waiting for transfers between devices, shift_x(): lax.ppermute(value, 'tile', [(t, (t // nc + j) % nx * nc + t % nc) for t...  14.8 us
    all_to_all x1, waiting for transfers between devices, shards(): lax.all_to_all(blocks, 'member', split_axis=0, concat_axis=0, tiled=True)  12.8 us
    unnamed x58, local copies, waits for them, and re-layouts  11 us
    all_to_all x1, waiting for transfers between devices, shards(): lax.all_to_all(scored, 'member', split_axis=0, concat_axis=0, tiled=True)  8.49 us
    dot_general x6, matrix products, pick(): lax.dot_general(choose, matrix, NT, preferred_element_type=jnp.float32)  8.47 us
    all_to_all x1, waiting for transfers between devices, shards(): lax.all_to_all(pieces(c_own, nz), 'member', split_axis=0, concat_axis=0,...  8.02 us
    all_to_all x1, waiting for transfers between devices, shards(): lax.all_to_all(jnp.concatenate([a_here, b_here], axis=1), 'member', split...  7.11 us
    all_to_all x1, starting transfers between devices, shards(): lax.all_to_all(blocks, 'member', split_axis=0, concat_axis=0, tiled=True)  6.3 us
  transfers between devices with their start and end apart: 12, of which 8 were waited for; matrix products, arithmetic and copies ran while one was open for 11% of the time, Pallas kernels for 5%

profile of v1, /device:TPU:0, one launch (start us, length us, event | category | flops | bytes accessed | tf_op | source)
XLA Modules:
  0.0 122.2 jit_solution(14550264393260354507)
XLA Ops:
  1.6 1.6 %copy-done.6 = bf16[1024,1024]{1,0:T(8,128)(2,1)S(1)} copy-done((bf16[1024,1024]{1,0:T(8,128)(2,1)S(1)}, bf16[1024,1024]{1,0:T(8,128)(2,1)}, u32[]{:S(2)}) %copy-start.6) | copy-done | bytes 2097176
  3.2 1.6 %copy-done.7 = bf16[1,1,1024,1024]{3,2,1,0:T(8,128)(2,1)S(1)} copy-done((bf16[1,1,1024,1024]{3,2,1,0:T(8,128)(2,1)S(1)}, bf16[1,1,1024,1024]{3,2,1,0:T(8,128)(2,1)}, u32[]{:S(2)}) %copy-start.7) | copy-done | bytes 2097176
  4.8 4.6 %forward.1 = (bf16[1024,1024]{1,0:T(8,128)(2,1)S(1)}, f32[1024,1024]{1,0:T(8,128)S(1)}, f32[1024,112]{1,0:T(8,128)S(1)}) custom-call(bf16[1024,1024]{1,0:T(8,128)(2,1)S(1)} %bitcast.20, bf16[1024,1024]{1,0:T(8,128)(2,1)S(1)} %copy-done.6, bf16[112,1024]{1,0:T(8,128)(2,1)S(1)} %bitcast.18), custom_call_target="tpu_custom_call" | custom-call | flops 2382364672 | bytes 10485760 | tf_op jit(solution)/shard_map/forward/pallas_call | solution.py:36
  9.4 1.9 %copy-done = f32[1024,1024]{1,0:T(8,128)} copy-done((f32[1024,1024]{1,0:T(8,128)}, f32[1024,1024]{1,0:T(8,128)S(1)}, u32[]{:S(2)}) %copy-start) | copy-done | bytes 4194328
  11.4 1.4 %copy-done.10 = bf16[1024,1024]{1,0:T(8,128)(2,1)} copy-done((bf16[1024,1024]{1,0:T(8,128)(2,1)}, bf16[1024,1024]{1,0:T(8,128)(2,1)S(1)}, u32[]{:S(2)}) %copy-start.10) | copy-done | bytes 2097176
  13.8 6.3 %all-to-all-start = ((f32[4,16,1792]{2,1,0:T(8,128)}), f32[4,16,1792]{2,1,0:T(8,128)S(1)}, u32[]{:S(2)}, u32[]{:S(2)}) async-start(f32[4,16,1792]{2,1,0:T(8,128)} %reshape.49), calls=%async_computation | async-start | bytes 917504 | tf_op jit(solution)/shard_map/all_to_all | solution.py:228
  20.4 12.8 %all-to-all-done.x_ref = f32[4,16,1792]{2,1,0:T(8,128)S(1)} async-done(((f32[4,16,1792]{2,1,0:T(8,128)}), f32[4,16,1792]{2,1,0:T(8,128)S(1)}, u32[]{:S(2)}, u32[]{:S(2)}) %all-to-all-start) | async-done | bytes 458784 | tf_op jit(solution)/shard_map/all_to_all | solution.py:228
  34.4 4.2 %all-to-all-start.1 = ((f32[4,16,1792]{2,1,0:T(8,128)}), f32[4,16,1792]{2,1,0:T(8,128)}, u32[]{:S(2)}, u32[]{:S(2)}) async-start(f32[4,16,1792]{2,1,0:T(8,128)} %score.1), calls=%async_computation.1 | async-start | bytes 917504 | tf_op jit(solution)/shard_map/all_to_all | solution.py:249
  38.7 2.4 %convolution_convert_fusion.3.latent_t_ref = bf16[192,1024]{1,0:T(8,128)(2,1)S(1)} fusion(s32[192]{0:T(256)S(1)} %fusion.39, bf16[1,1,1024,1024]{3,2,1,0:T(8,128)(2,1)} %param.36), kind=kOutput, calls=%fused_computation.9 | convolution fusion | flops 403046400 | bytes 2491136 | tf_op jit(solution)/shard_map/dot_general | solution.py:241
  41.2 1.6 %convolution_convert_fusion.2.hidden_t_ref = bf16[192,1024]{1,0:T(8,128)(2,1)} fusion(bf16[1024,1024]{1,0:T(8,128)(2,1)S(1)} %copy-done.11, s32[192]{0:T(256)S(1)} %fusion.39), kind=kOutput, calls=%fused_computation.8 | convolution fusion | flops 403046400 | bytes 2491136 | tf_op jit(solution)/shard_map/dot_general | solution.py:241
  42.8 8.5 %all-to-all-done.1 = f32[4,16,1792]{2,1,0:T(8,128)} async-done(((f32[4,16,1792]{2,1,0:T(8,128)}), f32[4,16,1792]{2,1,0:T(8,128)}, u32[]{:S(2)}, u32[]{:S(2)}) %all-to-all-start.1) | async-done | bytes 458784 | tf_op jit(solution)/shard_map/all_to_all | solution.py:249
  51.3 1.3 %reshape.50.g_ref = f32[1024,112]{1,0:T(8,128)S(1)} reshape(f32[4,16,1792]{2,1,0:T(8,128)} %all-to-all-done.1) | data formatting | bytes 917504 | tf_op jit(solution)/shard_map/reshape | solution.py:250
  52.6 2.2 %copy-done.1 = f32[1024,1024]{1,0:T(8,128)S(1)} copy-done((f32[1024,1024]{1,0:T(8,128)S(1)}, f32[1024,1024]{1,0:T(8,128)}, u32[]{:S(2)}) %copy-start.1) | copy-done | bytes 4194328
  55.8 4.0 %first_products.1 = (f32[192,1136]{1,0:T(8,128)}, bf16[1024,1024]{1,0:T(8,128)(2,1)S(1)}, bf16[1024,112]{1,0:T(8,128)(2,1)S(1)}) custom-call(f32[1024,112]{1,0:T(8,128)S(1)} %reshape.50.g_ref, f32[1024,1024]{1,0:T(8,128)S(1)} %copy-done.1, bf16[112,1024]{1,0:T(8,128)(2,1)S(1)} %bitcast.19, bf16[192,1024]{1,0:T(8,128)(2,1)S(1)} %convolution_convert_fusion.3.latent_t_ref, ...), custom_call_target="tpu_custom_call" | custom-call | flops 637534208 | bytes 8388608 | tf_op jit(solution)/shard_map/first_products/pallas_call | solution.py:117
  59.8 1.3 %fusion.3.hidden_t_ref = bf16[512,1024]{1,0:T(8,128)(2,1)S(1)} fusion(bf16[1024,1024]{1,0:T(8,128)(2,1)S(1)} %copy-done.12, s32[512]{0:T(512)S(1)} %fusion.26), kind=kOutput, calls=%fused_computation.4 | convolution fusion | flops 1074790400 | bytes 3147776 | tf_op jit(solution)/shard_map/dot_general | solution.py:241
  61.4 1.3 %fusion.2.latent_t_ref = bf16[512,1024]{1,0:T(8,128)(2,1)S(1)} fusion(s32[512]{0:T(512)S(1)} %fusion.26, bf16[1,1,1024,1024]{3,2,1,0:T(8,128)(2,1)S(1)} %copy-done.8), kind=kOutput, calls=%fused_computation.3 | convolution fusion | flops 1074790400 | bytes 3147776 | tf_op jit(solution)/shard_map/dot_general | solution.py:241
  62.8 3.6 %more_products.3 = (f32[320,1136]{1,0:T(8,128)}, f32[96,1136]{1,0:T(8,128)S(1)}, f32[96,1136]{1,0:T(8,128)S(1)}) custom-call(bf16[1024,1024]{1,0:T(8,128)(2,1)S(1)} %get-tuple-element.17.gp_ref, bf16[1024,112]{1,0:T(8,128)(2,1)S(1)} %get-tuple-element.18.g16_ref, bf16[512,1024]{1,0:T(8,128)(2,1)S(1)} %fusion.2.latent_t_ref, ...), custom_call_target="tpu_custom_call" | custom-call | flops 1191182336 | bytes 6291456 | tf_op jit(solution)/shard_map/more_products/pallas_call | solution.py:166
  66.7 1.4 %slice_add_fusion.3 = (f32[96,1136]{1,0:T(8,128)S(1)}, f32[96,1136]{1,0:T(8,128)S(1)}) fusion(f32[96,1136]{1,0:T(8,128)S(1)} %get-tuple-element.21, f32[192,1136]{1,0:T(8,128)} %collective-permute-done.1, f32[96,1136]{1,0:T(8,128)S(1)} %get-tuple-element.24), kind=kLoop, calls=%fused_computation.19 | loop fusion | flops 218112 | bytes 2617344 | tf_op jit(solution)/shard_map/add | solution.py:270
  68.1 1.6 %collective-permute-start.2 = (f32[96,1136]{1,0:T(8,128)S(1)}, f32[96,1136]{1,0:T(8,128)S(1)}, u32[]{:S(2)}, u32[]{:S(2)}) collective-permute-start(f32[96,1136]{1,0:T(8,128)S(1)} %get-tuple-element.28), channel_id=1, source_target_pairs={{0,4},{2,6},{4,0},{6,2},{1,5},{3,7},{5,1},{7,3},{8,12},{10,14},{12... | collective-permute-start | bytes 1308680 | tf_op jit(solution)/shard_map/ppermute | solution.py:256
  69.7 1.5 %collective-permute-start.4 = (f32[96,1136]{1,0:T(8,128)S(1)}, f32[96,1136]{1,0:T(8,128)S(1)}, u32[]{:S(2)}, u32[]{:S(2)}) collective-permute-start(f32[96,1136]{1,0:T(8,128)S(1)} %get-tuple-element.29), channel_id=1, source_target_pairs={{0,1},{1,0},{2,3},{3,2},{4,5},{5,4},{6,7},{7,6},{8,9},{9,8},{10,11... | collective-permute-start | bytes 1308680 | tf_op jit(solution)/shard_map/ppermute | solution.py:259
  73.0 2.0 %more_products.2 = (f32[128,1136]{1,0:T(8,128)S(1)}, f32[96,1136]{1,0:T(8,128)S(1)}, f32[96,1136]{1,0:T(8,128)S(1)}) custom-call(bf16[1024,1024]{1,0:T(8,128)(2,1)S(1)} %get-tuple-element.17.gp_ref, bf16[1024,112]{1,0:T(8,128)(2,1)S(1)} %get-tuple-element.18.g16_ref, bf16[320,1024]{1,0:T(8,128)(2,1)S(1)} %convolution_convert_fusion.1.latent_t_ref, ...), custom_call_target="tpu_custom_call" | custom-call | flops 744488960 | bytes 6291456 | tf_op jit(solution)/shard_map/more_products/pallas_call | solution.py:166
  75.0 5.5 %collective-permute-done.2 = f32[96,1136]{1,0:T(8,128)S(1)} collective-permute-done((f32[96,1136]{1,0:T(8,128)S(1)}, f32[96,1136]{1,0:T(8,128)S(1)}, u32[]{:S(2)}, u32[]{:S(2)}) %collective-permute-start.2) | collective-permute-done | bytes 436256 | tf_op jit(solution)/shard_map/ppermute | solution.py:256
  80.5 1.2 %collective-permute-done.4 = f32[96,1136]{1,0:T(8,128)S(1)} collective-permute-done((f32[96,1136]{1,0:T(8,128)S(1)}, f32[96,1136]{1,0:T(8,128)S(1)}, u32[]{:S(2)}, u32[]{:S(2)}) %collective-permute-start.4) | collective-permute-done | bytes 436256 | tf_op jit(solution)/shard_map/ppermute | solution.py:259
  81.8 1.3 %fusion.9 = (f32[96,1136]{1,0:T(8,128)S(1)}, f32[96,1136]{1,0:T(8,128)S(1)}) fusion(f32[96,1136]{1,0:T(8,128)S(1)} %collective-permute-done.2, f32[96,1136]{1,0:T(8,128)S(1)} %get-tuple-element.19, f32[320,1136]{1,0:T(8,128)} %collective-permute-done, f32[96,1136]{1,0:T(8,128)S(1)} %collective-permute-done.4, f32[96,1136]{1,0:T(8,128)S(1)} %get-tuple-element.23), kind=kLoop, calls=%fused_computation.21 | loop fusion | flops 436224 | bytes 3489792 | tf_op jit(solution)/shard_map/add | solution.py:285
  83.0 1.6 %collective-permute-start.3 = (f32[48,1136]{1,0:T(8,128)S(1)}, f32[48,1136]{1,0:T(8,128)S(1)}, u32[]{:S(2)}, u32[]{:S(2)}) collective-permute-start(f32[48,1136]{1,0:T(8,128)S(1)} %slice.71), channel_id=1, source_target_pairs={{0,1},{1,0},{2,3},{3,2},{4,5},{5,4},{6,7},{7,6},{8,9},{9,8},{10,11... | collective-permute-start | bytes 654344 | tf_op jit(solution)/shard_map/ppermute | solution.py:259
  84.6 1.9 %slice_add_fusion = f32[128,1136]{1,0:T(8,128)} fusion(f32[128,1136]{1,0:T(8,128)S(1)} %get-tuple-element.25, f32[320,1136]{1,0:T(8,128)} %collective-permute-done), kind=kLoop, calls=%fused_computation.15 | loop fusion | flops 145408 | bytes 1744896 | tf_op jit(solution)/shard_map/add | solution.py:283
  86.6 3.5 %all-to-all-start.3 = ((f32[4,32,1136]{2,1,0:T(8,128)}), f32[4,32,1136]{2,1,0:T(8,128)S(1)}, u32[]{:S(2)}, u32[]{:S(2)}) async-start(f32[4,32,1136]{2,1,0:T(8,128)} %bitcast.5), calls=%async_computation.3 | async-start | bytes 1179648 | tf_op jit(solution)/shard_map/all_to_all | solution.py:284
  90.8 5.6 %collective-permute-done.5 = f32[48,1136]{1,0:T(8,128)S(1)} collective-permute-done((f32[48,1136]{1,0:T(8,128)S(1)}, f32[48,1136]{1,0:T(8,128)S(1)}, u32[]{:S(2)}, u32[]{:S(2)}) %collective-permute-start.5) | collective-permute-done | bytes 218144 | tf_op jit(solution)/shard_map/ppermute | solution.py:256
  97.2 8.0 %all-to-all-done.3 = f32[4,32,1136]{2,1,0:T(8,128)S(1)} async-done(((f32[4,32,1136]{2,1,0:T(8,128)}), f32[4,32,1136]{2,1,0:T(8,128)S(1)}, u32[]{:S(2)}, u32[]{:S(2)}) %all-to-all-start.3) | async-done | bytes 581664 | tf_op jit(solution)/shard_map/all_to_all | solution.py:284
  105.2 3.5 %all-to-all-start.2 = ((f32[4,24,1136]{2,1,0:T(8,128)}), f32[4,24,1136]{2,1,0:T(8,128)S(1)}, u32[]{:S(2)}, u32[]{:S(2)}) async-start(f32[4,24,1136]{2,1,0:T(8,128)} %pad_maximum_fusion), calls=%async_computation.2 | async-start | bytes 884736 | tf_op jit(solution)/shard_map/all_to_all | solution.py:293
  109.4 3.8 %collective-permute-done.6 = f32[16,1136]{1,0:T(8,128)S(1)} collective-permute-done((f32[16,1136]{1,0:T(8,128)S(1)}, f32[16,1136]{1,0:T(8,128)S(1)}, u32[]{:S(2)}, u32[]{:S(2)}) %collective-permute-start.6) | collective-permute-done | bytes 72736 | tf_op jit(solution)/shard_map/ppermute | solution.py:256
  113.8 7.1 %all-to-all-done.2 = f32[4,24,1136]{2,1,0:T(8,128)S(1)} async-done(((f32[4,24,1136]{2,1,0:T(8,128)}), f32[4,24,1136]{2,1,0:T(8,128)S(1)}, u32[]{:S(2)}, u32[]{:S(2)}) %all-to-all-start.2) | async-done | bytes 436256 | tf_op jit(solution)/shard_map/all_to_all | solution.py:293
  (87 shorter events, 11.1 us)
Async XLA Ops:
  4.8 15.4 %copy-start.27 = (s32[1,64]{1,0:T(1,128)S(1)}, s32[1,64]{1,0:T(1,128)}, u32[]{:S(2)}) copy-start(s32[1,64]{1,0:T(1,128)} %param.41) | copy-start | bytes 772
  4.8 15.4 %copy-start.28 = (s32[1,64]{1,0:T(1,128)S(1)}, s32[1,64]{1,0:T(1,128)}, u32[]{:S(2)}) copy-start(s32[1,64]{1,0:T(1,128)} %param.40) | copy-start | bytes 772
  4.8 15.6 %copy-start.14 = (s32[512]{0:T(512)S(1)}, s32[512]{0:T(512)}, u32[]{:S(2)}) copy-start(s32[512]{0:T(512)} %constant.189.clone) | copy-start | bytes 6148
  4.8 15.6 %copy-start.15 = (s32[512]{0:T(512)S(1)}, s32[512]{0:T(512)}, u32[]{:S(2)}) copy-start(s32[512]{0:T(512)} %constant.191.clone) | copy-start | bytes 6148
  4.8 15.6 %copy-start.16 = (s32[512]{0:T(512)S(1)}, s32[512]{0:T(512)}, u32[]{:S(2)}) copy-start(s32[512]{0:T(512)} %constant.192.clone) | copy-start | bytes 6148
  4.8 15.6 %copy-start.17 = (s32[512]{0:T(512)S(1)}, s32[512]{0:T(512)}, u32[]{:S(2)}) copy-start(s32[512]{0:T(512)} %constant.193.clone) | copy-start | bytes 6148
  4.8 15.6 %copy-start.18 = (s32[512]{0:T(512)S(1)}, s32[512]{0:T(512)}, u32[]{:S(2)}) copy-start(s32[512]{0:T(512)} %constant.205) | copy-start | bytes 6148
  12.8 20.4 %copy-start.2 = (bf16[1,128,1792]{2,1,0:T(8,128)(2,1)S(1)}, bf16[1,128,1792]{2,1,0:T(8,128)(2,1)}, u32[]{:S(2)}) copy-start(bf16[1,128,1792]{2,1,0:T(8,128)(2,1)} %param.39) | copy-start | bytes 1376260
  12.8 25.9 %copy-start.23 = (s32[192]{0:T(256)S(1)}, s32[192]{0:T(256)}, u32[]{:S(2)}) copy-start(s32[192]{0:T(256)} %constant.186.clone) | copy-start | bytes 2308
  12.8 25.9 %copy-start.24 = (s32[192]{0:T(256)S(1)}, s32[192]{0:T(256)}, u32[]{:S(2)}) copy-start(s32[192]{0:T(256)} %constant.187.clone) | copy-start | bytes 2308
  12.8 25.9 %copy-start.25 = (s32[192]{0:T(256)S(1)}, s32[192]{0:T(256)}, u32[]{:S(2)}) copy-start(s32[192]{0:T(256)} %constant.188.clone) | copy-start | bytes 2308
  12.8 25.9 %copy-start.26 = (s32[192]{0:T(256)S(1)}, s32[192]{0:T(256)}, u32[]{:S(2)}) copy-start(s32[192]{0:T(256)} %constant.203) | copy-start | bytes 2308
  13.8 19.4 %all-to-all-start = ((f32[4,16,1792]{2,1,0:T(8,128)}), f32[4,16,1792]{2,1,0:T(8,128)S(1)}, u32[]{:S(2)}, u32[]{:S(2)}) async-start(f32[4,16,1792]{2,1,0:T(8,128)} %reshape.49), calls=%async_computation | async-start | bytes 917504 | tf_op jit(solution)/shard_map/all_to_all | solution.py:228
  34.4 6.8 %copy-start.11 = (bf16[1024,1024]{1,0:T(8,128)(2,1)S(1)}, bf16[1024,1024]{1,0:T(8,128)(2,1)}, u32[]{:S(2)}) copy-start(bf16[1024,1024]{1,0:T(8,128)(2,1)} %copy-done.10) | copy-start | bytes 6291460
  34.4 16.9 %all-to-all-start.1 = ((f32[4,16,1792]{2,1,0:T(8,128)}), f32[4,16,1792]{2,1,0:T(8,128)}, u32[]{:S(2)}, u32[]{:S(2)}) async-start(f32[4,16,1792]{2,1,0:T(8,128)} %score.1), calls=%async_computation.1 | async-start | bytes 917504 | tf_op jit(solution)/shard_map/all_to_all | solution.py:249
  41.2 11.5 %copy-start.5 = (bf16[1024,112]{0,1:T(8,128)(2,1)S(1)}, bf16[1024,112]{0,1:T(8,128)(2,1)}, u32[]{:S(2)}) copy-start(bf16[1024,112]{0,1:T(8,128)(2,1)} %param.38) | copy-start | bytes 688132
  55.8 4.0 %copy-start.12 = (bf16[1024,1024]{1,0:T(8,128)(2,1)S(1)}, bf16[1024,1024]{1,0:T(8,128)(2,1)}, u32[]{:S(2)}) copy-start(bf16[1024,1024]{1,0:T(8,128)(2,1)} %copy-done.10) | copy-start | bytes 6291460
  59.8 6.9 %collective-permute-start.1 = (f32[192,1136]{1,0:T(8,128)}, f32[192,1136]{1,0:T(8,128)}, u32[]{:S(2)}, u32[]{:S(2)}) collective-permute-start(f32[192,1136]{1,0:T(8,128)} %get-tuple-element.22), channel_id=1, source_target_pairs={{0,2},{2,0},{4,6},{6,4},{1,3},{3,1},{5,7},{7,5},{8,10},{10,8},{12,... | collective-permute-start | bytes 2617352 | tf_op jit(solution)/shard_map/ppermute | solution.py:253
  62.7 3.9 %copy-start.19 = (s32[320]{0:T(512)S(1)}, s32[320]{0:T(512)}, u32[]{:S(2)}) copy-start(s32[320]{0:T(512)} %constant.196.clone) | copy-start | bytes 3844
  62.8 3.9 %copy-start.20 = (s32[320]{0:T(512)S(1)}, s32[320]{0:T(512)}, u32[]{:S(2)}) copy-start(s32[320]{0:T(512)} %constant.197.clone) | copy-start | bytes 3844
  62.8 3.9 %copy-start.21 = (s32[320]{0:T(512)S(1)}, s32[320]{0:T(512)}, u32[]{:S(2)}) copy-start(s32[320]{0:T(512)} %constant.198.clone) | copy-start | bytes 3844
  62.8 3.9 %copy-start.22 = (s32[320]{0:T(512)S(1)}, s32[320]{0:T(512)}, u32[]{:S(2)}) copy-start(s32[320]{0:T(512)} %constant.204) | copy-start | bytes 3844
  66.4 15.3 %collective-permute-start = (f32[320,1136]{1,0:T(8,128)}, f32[320,1136]{1,0:T(8,128)}, u32[]{:S(2)}, u32[]{:S(2)}) collective-permute-start(f32[320,1136]{1,0:T(8,128)} %get-tuple-element.20), channel_id=1, source_target_pairs={{0,2},{2,0},{4,6},{6,4},{1,3},{3,1},{5,7},{7,5},{8,10},{10,8},{12,... | collective-permute-start | bytes 4362248 | tf_op jit(solution)/shard_map/ppermute | solution.py:253
  66.7 4.5 %copy-start.13 = (bf16[1024,1024]{1,0:T(8,128)(2,1)S(1)}, bf16[1024,1024]{1,0:T(8,128)(2,1)}, u32[]{:S(2)}) copy-start(bf16[1024,1024]{1,0:T(8,128)(2,1)} %copy-done.10) | copy-start | bytes 6291460
  68.1 12.4 %collective-permute-start.2 = (f32[96,1136]{1,0:T(8,128)S(1)}, f32[96,1136]{1,0:T(8,128)S(1)}, u32[]{:S(2)}, u32[]{:S(2)}) collective-permute-start(f32[96,1136]{1,0:T(8,128)S(1)} %get-tuple-element.28), channel_id=1, source_target_pairs={{0,4},{2,6},{4,0},{6,2},{1,5},{3,7},{5,1},{7,3},{8,12},{10,14},{12... | collective-permute-start | bytes 1308680 | tf_op jit(solution)/shard_map/ppermute | solution.py:256
  69.7 12.1 %collective-permute-start.4 = (f32[96,1136]{1,0:T(8,128)S(1)}, f32[96,1136]{1,0:T(8,128)S(1)}, u32[]{:S(2)}, u32[]{:S(2)}) collective-permute-start(f32[96,1136]{1,0:T(8,128)S(1)} %get-tuple-element.29), channel_id=1, source_target_pairs={{0,1},{1,0},{2,3},{3,2},{4,5},{5,4},{6,7},{7,6},{8,9},{9,8},{10,11... | collective-permute-start | bytes 1308680 | tf_op jit(solution)/shard_map/ppermute | solution.py:259
  83.0 7.6 %collective-permute-start.3 = (f32[48,1136]{1,0:T(8,128)S(1)}, f32[48,1136]{1,0:T(8,128)S(1)}, u32[]{:S(2)}, u32[]{:S(2)}) collective-permute-start(f32[48,1136]{1,0:T(8,128)S(1)} %slice.71), channel_id=1, source_target_pairs={{0,1},{1,0},{2,3},{3,2},{4,5},{5,4},{6,7},{7,6},{8,9},{9,8},{10,11... | collective-permute-start | bytes 654344 | tf_op jit(solution)/shard_map/ppermute | solution.py:259
  86.6 18.7 %all-to-all-start.3 = ((f32[4,32,1136]{2,1,0:T(8,128)}), f32[4,32,1136]{2,1,0:T(8,128)S(1)}, u32[]{:S(2)}, u32[]{:S(2)}) async-start(f32[4,32,1136]{2,1,0:T(8,128)} %bitcast.5), calls=%async_computation.3 | async-start | bytes 1179648 | tf_op jit(solution)/shard_map/all_to_all | solution.py:284
  90.1 6.3 %collective-permute-start.5 = (f32[48,1136]{1,0:T(8,128)S(1)}, f32[48,1136]{1,0:T(8,128)S(1)}, u32[]{:S(2)}, u32[]{:S(2)}) collective-permute-start(f32[48,1136]{1,0:T(8,128)S(1)} %slice.75), channel_id=1, source_target_pairs={{0,4},{2,6},{4,0},{6,2},{1,5},{3,7},{5,1},{7,3},{8,12},{10,14},{12... | collective-permute-start | bytes 654344 | tf_op jit(solution)/shard_map/ppermute | solution.py:256
  105.2 15.7 %all-to-all-start.2 = ((f32[4,24,1136]{2,1,0:T(8,128)}), f32[4,24,1136]{2,1,0:T(8,128)S(1)}, u32[]{:S(2)}, u32[]{:S(2)}) async-start(f32[4,24,1136]{2,1,0:T(8,128)} %pad_maximum_fusion), calls=%async_computation.2 | async-start | bytes 884736 | tf_op jit(solution)/shard_map/all_to_all | solution.py:293
  108.7 4.4 %collective-permute-start.6 = (f32[16,1136]{1,0:T(8,128)S(1)}, f32[16,1136]{1,0:T(8,128)S(1)}, u32[]{:S(2)}, u32[]{:S(2)}) collective-permute-start(f32[16,1136]{1,0:T(8,128)S(1)} %slice.78), channel_id=1, source_target_pairs={{0,4},{2,6},{4,0},{6,2},{1,5},{3,7},{5,1},{7,3},{8,12},{10,14},{12... | collective-permute-start | bytes 218120 | tf_op jit(solution)/shard_map/ppermute | solution.py:256
  113.2 7.7 %collective-permute-start.7 = (f32[8,1136]{1,0:T(8,128)S(1)}, f32[8,1136]{1,0:T(8,128)S(1)}, u32[]{:S(2)}, u32[]{:S(2)}) collective-permute-start(f32[8,1136]{1,0:T(8,128)S(1)} %slice.80), channel_id=1, source_target_pairs={{0,1},{1,0},{2,3},{3,2},{4,5},{5,4},{6,7},{7,6},{8,9},{9,8},{10,11... | collective-permute-start | bytes 109064 | tf_op jit(solution)/shard_map/ppermute | solution.py:259
  (9 other events, 14.6 us)

commit v2 on v0

v2 whole, which is shorter than its diff:
```python
import functools

import jax
import jax.numpy as jnp
import numpy as np
from jax import lax
from jax.experimental import pallas as pl
from jax.experimental.pallas import tpu as pltpu
from jax.sharding import PartitionSpec as P

PATCH = 16
CORES = 2
LANES = 128
MIB = 1 << 20
NT = (((1,), (1,)), ((), ()))
WHOLE = pl.BlockSpec(memory_space=pltpu.VMEM)


def params(mib=24):
    return pltpu.CompilerParams(vmem_limit_bytes=mib * MIB)


def cost(flops, moved):
    return pl.CostEstimate(flops=int(flops), bytes_accessed=int(moved), transcendentals=0)


def packing(channels):
    spare = LANES - channels
    carriers = PATCH * channels // LANES
    per_cell = channels // spare
    assert carriers * LANES == PATCH * channels and per_cell * spare == channels
    return spare, carriers, per_cell


def pack(cell, channels):
    spare, carriers, per_cell = packing(channels)
    extra = [cell(j) for j in range(carriers, PATCH)]
    lane = lax.broadcasted_iota(jnp.int32, extra[0].shape, 1)
    rows = []
    for j in range(carriers):
        piece = extra[j // per_cell]
        moved = pltpu.roll(piece, channels - j % per_cell * spare, 1)
        rows.append(jnp.where(lane < channels, cell(j), moved))
    return rows


def unpack(rows, channels):
    spare, carriers, per_cell = packing(channels)
    lane = lax.broadcasted_iota(jnp.int32, rows[0].shape, 1)
    cells = list(rows)
    for first in range(0, carriers, per_cell):
        value = jnp.zeros_like(rows[0])
        for i in range(per_cell):
            moved = pltpu.roll(rows[first + i], (i * spare - channels) % LANES, 1)
            value = jnp.where((lane >= i * spare) & (lane < (i + 1) * spare), moved, value)
        cells.append(value)
    return cells


def decode_body(latent_ref, w_in_ref, w_out_t_ref, packed_ref, cells):
    channels = w_out_t_ref.shape[0]
    share = packed_ref.shape[2]
    preact = jnp.dot(latent_ref[...], w_in_ref[...], preferred_element_type=jnp.float32)
    hidden = (preact / (1.0 + jnp.exp(-preact))).astype(jnp.bfloat16)
    cells[:, :channels] = lax.dot_general(hidden, w_out_t_ref[...], NT, preferred_element_type=jnp.float32)
    for j, row in enumerate(pack(lambda j: cells[pl.ds(j, share, stride=PATCH), :], channels)):
        packed_ref[0, j] = row


def decode(rows_in, w_in, w_out_t, parts):
    nrows, depth = rows_in.shape
    width = w_in.shape[1]
    channels = w_out_t.shape[0]
    block = nrows // parts
    share = block // PATCH
    carriers = packing(channels)[1]
    return pl.pallas_call(
        decode_body,
        grid=(parts,),
        in_specs=[
            pl.BlockSpec((block, depth), lambda i: (i, 0)),
            pl.BlockSpec((depth, width), lambda i: (0, 0)),
            pl.BlockSpec((channels, width), lambda i: (0, 0)),
        ],
        out_specs=pl.BlockSpec((1, carriers, share, LANES), lambda i: (i, 0, 0, 0)),
        out_shape=jax.ShapeDtypeStruct((parts, carriers, share, LANES), jnp.float32),
        scratch_shapes=[pltpu.VMEM((block, LANES), jnp.float32)],
        compiler_params=params(56),
        cost_estimate=cost(2 * nrows * width * (depth + channels), 5 * MIB),
        name="decode",
    )(rows_in, w_in, w_out_t)


def fill_choice(source_ref, choice):
    picked, extent = choice.shape
    for low in range(0, picked, LANES):
        high = min(low + LANES, picked)
        across = jnp.broadcast_to(source_ref[:, low:high], (LANES, high - low))
        down = jnp.transpose(across)
        for left in range(0, extent, LANES):
            here = lax.broadcasted_iota(jnp.int32, down.shape, 1) + left
            choice[low:high, left:left + LANES] = jnp.where(down == here, 1.0, 0.0).astype(jnp.bfloat16)


def slope_body(source_ref, latent_ref, w_in_ref, slope_ref, hidden_t_ref, choice):
    @pl.when(pl.program_id(0) == 0)
    def _():
        fill_choice(source_ref, choice)

    preact = jnp.dot(latent_ref[...], w_in_ref[...], preferred_element_type=jnp.float32)
    scale = 1.0 + jnp.exp(-preact)
    sigma = 1.0 / scale
    slope_ref[...] = sigma * (1.0 + preact * (1.0 - sigma))
    hidden = (preact / scale).astype(jnp.bfloat16)
    ordered = lax.dot_general(choice[...], hidden, NT, preferred_element_type=jnp.float32)
    hidden_t_ref[...] = ordered.astype(jnp.bfloat16)


def slopes(source, rows_in, w_in):
    nrows, depth = rows_in.shape
    width = w_in.shape[1]
    picked = source.shape[1]
    block = 256 if nrows % 256 == 0 else nrows
    return pl.pallas_call(
        slope_body,
        grid=(nrows // block,),
        in_specs=[
            pl.BlockSpec((1, picked), lambda i: (0, 0)),
            pl.BlockSpec((block, depth), lambda i: (i, 0)),
            pl.BlockSpec((depth, width), lambda i: (0, 0)),
        ],
        out_specs=[
            pl.BlockSpec((block, width), lambda i: (i, 0)),
            pl.BlockSpec((picked, block), lambda i: (0, i)),
        ],
        out_shape=[
            jax.ShapeDtypeStruct((nrows, width), jnp.float32),
            jax.ShapeDtypeStruct((picked, nrows), jnp.bfloat16),
        ],
        scratch_shapes=[pltpu.VMEM((picked, width), jnp.bfloat16)],
        compiler_params=params(),
        cost_estimate=cost(2 * nrows * width * depth, 4 * MIB),
        name="slopes",
    )(source, rows_in, w_in)


def order_body(source_ref, matrix_ref, out_ref, choice):
    @pl.when(pl.program_id(0) == 0)
    def _():
        fill_choice(source_ref, choice)

    ordered = lax.dot_general(choice[...], matrix_ref[...], NT, preferred_element_type=jnp.float32)
    out_ref[...] = ordered.astype(jnp.bfloat16)


def ordered_transpose(source, matrix):
    nrows, extent = matrix.shape
    picked = source.shape[1]
    block = 256 if nrows % 256 == 0 else nrows
    return pl.pallas_call(
        order_body,
        grid=(nrows // block,),
        in_specs=[
            pl.BlockSpec((1, picked), lambda i: (0, 0)),
            pl.BlockSpec((block, extent), lambda i: (i, 0)),
        ],
        out_specs=pl.BlockSpec((picked, block), lambda i: (0, i)),
        out_shape=jax.ShapeDtypeStruct((picked, nrows), jnp.bfloat16),
        scratch_shapes=[pltpu.VMEM((picked, extent), jnp.bfloat16)],
        compiler_params=params(),
        cost_estimate=cost(nrows * extent * picked, 4 * MIB),
        name="ordered_transpose",
    )(source, matrix)


def score_body(channels, x_ref, pool_ref, index_ref, count_ref, out_ref):
    members, carriers, share, _ = x_ref.shape
    npool, total = pool_ref.shape
    choose = index_ref[...] == lax.broadcasted_iota(jnp.int32, (share, npool), 1)
    flat = jnp.dot(
        jnp.where(choose, 1.0, 0.0).astype(jnp.bfloat16), pool_ref[...], preferred_element_type=jnp.float32
    )
    weight = count_ref[...].astype(jnp.float32)

    def cell(j):
        start = j * channels
        low = start // LANES * LANES
        part = flat[:, low:min(low + 2 * LANES, total)]
        return pltpu.roll(part, (low - start) % part.shape[1], 1)[:, :LANES]

    target = pack(cell, channels)

    def inverse_norm(delta):
        squares = sum(d * d for d in delta)
        return 1.0 / jnp.sqrt(jnp.sum(squares, axis=-1, keepdims=True) + 1.0)

    xs = [[x_ref[m, j] for j in range(carriers)] for m in range(members)]
    pair = [[jnp.zeros_like(xs[0][0])] * carriers for _ in range(members)]
    for m in range(members):
        for k in range(m + 1, members):
            delta = [p - q for p, q in zip(xs[m], xs[k])]
            inverse = inverse_norm(delta)
            pair[m] = [p + d * inverse for p, d in zip(pair[m], delta)]
            pair[k] = [p - d * inverse for p, d in zip(pair[k], delta)]
    for m in range(members):
        delta = [p - q for p, q in zip(xs[m], target)]
        inverse = inverse_norm(delta)
        for j in range(carriers):
            out_ref[m, j] = weight * (delta[j] * inverse / members - pair[m][j] / (members * members))


def score(grouped, pool, index, count, channels):
    return pl.pallas_call(
        functools.partial(score_body, channels),
        in_specs=[WHOLE] * 4,
        out_specs=WHOLE,
        out_shape=jax.ShapeDtypeStruct(grouped.shape, jnp.float32),
        compiler_params=params(),
        cost_estimate=cost(30 * grouped.size, 8 * grouped.size),
        name="score",
    )(grouped, pool, index, count)


def column_steps(width):
    step = 256 if width % 256 == 0 else width
    return [slice(low, low + step) for low in range(0, width, step)]


def first_body(low, high, scored_ref, slope_ref, w_out_t_ref, latent_t_ref, hidden_t_ref, out_ref, gp_ref, g16_ref, cells):
    parts, carriers, share, _ = scored_ref.shape
    channels, width = w_out_t_ref.shape
    for q in range(parts):
        rows = [scored_ref[q, j] for j in range(carriers)]
        for j, value in enumerate(unpack(rows, channels)):
            cells[pl.ds(q * share * PATCH + j, share, stride=PATCH), :] = value
    g16 = cells[:, :channels].astype(jnp.bfloat16)
    g16_ref[...] = g16
    for columns in column_steps(width):
        gh = jnp.dot(g16, w_out_t_ref[:, columns], preferred_element_type=jnp.float32)
        gp = (gh * slope_ref[:, columns]).astype(jnp.bfloat16)
        gp_ref[:, columns] = gp
        out_ref[:, columns] = jnp.dot(latent_t_ref[low:high], gp, preferred_element_type=jnp.float32)
    out_ref[:, width:] = jnp.dot(hidden_t_ref[low:high], g16, preferred_element_type=jnp.float32)


def first_products(scored, slope, w_out_t, latent_t, hidden_t, low, high):
    nrows, width = slope.shape
    channels = w_out_t.shape[0]
    return pl.pallas_call(
        functools.partial(first_body, low, high),
        in_specs=[WHOLE] * 5,
        out_specs=[WHOLE] * 3,
        out_shape=[
            jax.ShapeDtypeStruct((high - low, width + channels), jnp.float32),
            jax.ShapeDtypeStruct((nrows, width), jnp.bfloat16),
            jax.ShapeDtypeStruct((nrows, channels), jnp.bfloat16),
        ],
        scratch_shapes=[pltpu.VMEM((nrows, LANES), jnp.float32)],
        compiler_params=params(),
        cost_estimate=cost(2 * nrows * width * (channels + high - low), 8 * MIB),
        name="first_products",
    )(scored, slope, w_out_t, latent_t, hidden_t)


def more_body(cuts, gp_ref, g16_ref, latent_t_ref, hidden_t_ref, *out_refs):
    width = gp_ref.shape[1]
    low, high = cuts[0][0], cuts[-1][1]

    def put(columns, product):
        for out_ref, (start, end) in zip(out_refs, cuts):
            out_ref[:, columns] = product[start - low:end - low]

    for columns in column_steps(width):
        put(columns, jnp.dot(latent_t_ref[low:high], gp_ref[:, columns], preferred_element_type=jnp.float32))
    put(slice(width, None), jnp.dot(hidden_t_ref[low:high], g16_ref[...], preferred_element_type=jnp.float32))


def more_products(gp, g16, latent_t, hidden_t, cuts):
    nrows, channels = g16.shape
    width = gp.shape[1]
    picked = cuts[-1][1] - cuts[0][0]
    return pl.pallas_call(
        functools.partial(more_body, tuple(cuts)),
        in_specs=[WHOLE] * 4,
        out_specs=[WHOLE] * len(cuts),
        out_shape=[jax.ShapeDtypeStruct((end - start, width + channels), jnp.float32) for start, end in cuts],
        compiler_params=params(),
        cost_estimate=cost(2 * nrows * picked * (width + channels), 6 * MIB),
        name="more_products",
    )(gp, g16, latent_t, hidden_t)


def add_body(plans, count, *refs):
    inputs, outputs = refs[:count], refs[count:]
    for out_ref, plan in zip(outputs, plans):
        for at, rows, sources in plan:
            total = None
            for which, low in sources:
                value = inputs[which][low:low + rows]
                total = value if total is None else total + value
            out_ref[at:at + rows] = total


def add_rows(inputs, plans):
    columns = inputs[0].shape[1]
    sizes = [sum(rows for _, rows, _ in plan) for plan in plans]
    return pl.pallas_call(
        functools.partial(add_body, plans, len(inputs)),
        in_specs=[WHOLE] * len(inputs),
        out_specs=[WHOLE] * len(plans),
        out_shape=[jax.ShapeDtypeStruct((size, columns), jnp.float32) for size in sizes],
        compiler_params=params(),
        cost_estimate=cost(3 * sum(sizes) * columns, 12 * sum(sizes) * columns),
        name="add_rows",
    )(*inputs)


def finish_body(across_ref, *refs):
    *rest_refs, first_ref, second_ref = refs
    width = first_ref.shape[1]
    rows = across_ref.shape[1]
    total = across_ref[0]
    for z in range(1, across_ref.shape[0]):
        total = total + across_ref[z]
    last = rest_refs[0][...]
    for ref in rest_refs[1:]:
        last = last + ref[...]
    for low, high, value in ((0, rows, total), (rows, first_ref.shape[0], last)):
        first_ref[low:high] = value[:, :width]
        second_ref[low:high] = value[:, width:]


def finish(across, rest, width):
    height = across.shape[1] + rest[0].shape[0]
    columns = across.shape[2]
    return pl.pallas_call(
        finish_body,
        in_specs=[WHOLE] * (1 + len(rest)),
        out_specs=[WHOLE] * 2,
        out_shape=[
            jax.ShapeDtypeStruct((height, width), jnp.float32),
            jax.ShapeDtypeStruct((height, columns - width), jnp.float32),
        ],
        compiler_params=params(),
        cost_estimate=cost(across.size, 4 * across.size),
        name="finish",
    )(across, *rest)


def row_order(nz, nx, nc, ny, height):
    near = 2 if nz % 2 == 0 else 1
    far = nz // near
    rc = max(height // 4, 1)
    more = -(-(height - rc) * 2 // 3)
    a_rows = [range(0, more if z % 2 == 0 else height - rc - more) for z in range(nz)]
    b_rows = [range(a_rows[z].stop, height - rc) for z in range(nz)]
    c_rows = range(height - rc, height)
    x_last, y_last, far_last = [[*range(1, n), 0] for n in (nx, ny, far)]

    def part_a(xs):
        return [(x, y, 0, z // near, z % near, r) for x in xs for y in y_last for z in range(nz) for r in a_rows[z]]

    def part_b(ys):
        return [(x, y, 0, z // near, z % near, r) for y in ys for x in x_last for z in range(nz) for r in b_rows[z]]

    def part_c(nears):
        return [(x, y, 1, f, n, r) for n in nears for f in far_last for x in x_last for y in y_last for r in c_rows]

    pieces = [
        part_a(range(1, nx)), part_b(range(1, ny)), part_c(range(1, near)),
        part_c([0]), part_a([0]), part_b([0]),
    ]
    sizes = [len(piece) for piece in pieces]
    half = [row for piece in pieces for row in piece]
    table = np.array([(core, *row) for core in [*range(1, nc), 0] for row in half], np.int32).T
    return table, sizes, near, far, a_rows, b_rows, rc


def shards(latent, w_in, w_out, observed, patch_index, counts):
    rows_in = latent[0, 0]
    nrows, depth = rows_in.shape
    width, channels = w_out.shape
    nz, nt, ny = (lax.axis_size(name) for name in ("member", "tile", "batch"))
    nc, nx = CORES, nt // CORES
    me_z, me_t, me_y = (lax.axis_index(name) for name in ("member", "tile", "batch"))
    me_x, me_c = me_t // nc, me_t % nc
    w_out_t = w_out.T
    height = depth // (nz * nt * ny)
    table, sizes, near, far, a_rows, b_rows, rc = row_order(nz, nx, nc, ny, height)

    share = nrows // PATCH // nz
    packed = decode(rows_in, w_in, w_out_t, nz)
    grouped = lax.all_to_all(packed, "member", split_axis=0, concat_axis=0, tiled=True)

    core, x, y, relative, f, n, row = (jnp.asarray(table[k:k + 1]) for k in range(7))
    z = (f + relative * (me_z // near)) % far * near + (n + relative * (me_z % near)) % near
    tile = (x + me_x) % nx * nc + (core + me_c) % nc
    source = ((z * nt + tile) * ny + (y + me_y) % ny) * height + row
    slope, hidden_t = slopes(source, rows_in, w_in)
    index = lax.dynamic_slice_in_dim(patch_index[0], me_z * share, share, 0)[:, None]
    count = lax.dynamic_slice_in_dim(counts[0], me_z * share, share, 0)[:, None]
    grouped, slope, hidden_t, index, count = lax.optimization_barrier((grouped, slope, hidden_t, index, count))

    scored = score(grouped, observed[0], index, count, channels)
    returned = lax.all_to_all(scored, "member", split_axis=0, concat_axis=0, tiled=True)
    latent_t = ordered_transpose(source, rows_in)
    returned, latent_t = lax.optimization_barrier((returned, latent_t))

    def shift_core(value, j):
        return lax.ppermute(value, "tile", [(t, t // nc * nc + (t % nc + j) % nc) for t in range(nt)])

    def shift_x(value, j):
        return lax.ppermute(value, "tile", [(t, (t // nc + j) % nx * nc + t % nc) for t in range(nt)])

    def shift_y(value, j):
        return lax.ppermute(value, "batch", [(t, (t + j) % ny) for t in range(ny)])

    def shift_near(value, j):
        return lax.ppermute(value, "member", [(t, t // near * near + (t % near + j) % near) for t in range(nz)])

    def shift_far(value, j):
        return lax.ppermute(value, "member", [(t, (t // near + j) % far * near + t % near) for t in range(nz)])

    def send_all(value, others, shift):
        if others == 1:
            return [shift(value, 1)]
        return [shift(v, j + 1) for j, v in enumerate(jnp.split(value, others, axis=0))] if others else []

    na, nb, nc_send, nc_keep, na_keep, nb_keep = sizes
    n_send, n_keep = na + nb + nc_send, nc_keep + na_keep + nb_keep
    half = n_send + n_keep

    first, gp, g16 = first_products(returned, slope, w_out_t, latent_t, hidden_t, 0, n_send)
    from_core = shift_core(first, 1)
    (own_send,) = more_products(gp, g16, latent_t, hidden_t, [(half, half + n_send)])
    a_send, b_send, c_send = add_rows(
        [own_send, from_core],
        [
            [(0, na, [(0, 0), (1, 0)])],
            [(0, nb, [(0, na), (1, na)])],
            [(0, nc_send, [(0, na + nb), (1, na + nb)])],
        ],
    )
    a_got = send_all(a_send, nx - 1, shift_x)
    b_got = send_all(b_send, ny - 1, shift_y)
    c_got = send_all(c_send, near - 1, shift_near)
    other_keep, own_keep = more_products(
        gp, g16, latent_t, hidden_t, [(n_send, half)]
    ) + more_products(gp, g16, latent_t, hidden_t, [(half + n_send, 2 * half)])
    core_keep = shift_core(other_keep, 1)

    inputs = [own_keep, core_keep, *a_got, *b_got, *c_got]
    a_in = range(2, 2 + len(a_got))
    b_in = range(a_in.stop, a_in.stop + len(b_got))
    c_in = range(b_in.stop, b_in.stop + len(c_got))

    def summed(base, got, low, rows):
        return [(0, rows, [(0, base + low), (1, base + low), *[(k, low) for k in got]])]

    a_base, b_base = nc_keep, nc_keep + na_keep
    a_cut, b_cut, c_cut = na_keep // ny * (ny - 1), nb_keep // nx * (nx - 1), nc_keep // far * (far - 1)
    c_send, a_send, b_send = add_rows(
        inputs,
        [
            summed(0, c_in, 0, c_cut),
            summed(a_base, a_in, 0, a_cut),
            summed(b_base, b_in, 0, b_cut),
        ],
    )
    c_got = send_all(c_send, far - 1, shift_far)
    a_got = send_all(a_send, ny - 1, shift_y)
    b_got = send_all(b_send, nx - 1, shift_x)
    c_keep, a_keep, b_keep = add_rows(
        inputs,
        [
            summed(0, c_in, c_cut, nc_keep - c_cut),
            summed(a_base, a_in, a_cut, na_keep - a_cut),
            summed(b_base, b_in, b_cut, nb_keep - b_cut),
        ],
    )

    inputs = [a_keep, *a_got, b_keep, *b_got]
    plan, a_low, b_low, at = [], 0, 0, 0
    for k in range(nz):
        plan.append((at, len(a_rows[k]), [(i, a_low) for i in range(1 + len(a_got))]))
        a_low, at = a_low + len(a_rows[k]), at + len(a_rows[k])
        plan.append((at, len(b_rows[k]), [(1 + len(a_got) + i, b_low) for i in range(1 + len(b_got))]))
        b_low, at = b_low + len(b_rows[k]), at + len(b_rows[k])
    (joined,) = add_rows(inputs, [plan])
    across = lax.all_to_all(
        joined.reshape(nz, height - rc, joined.shape[1]), "member", split_axis=0, concat_axis=0, tiled=True
    )
    c_rows = c_keep.shape[0]
    cut = c_rows // nx * (nx - 1)
    (c_send, c_keep) = add_rows(
        [c_keep, *c_got],
        [
            [(0, cut, [(i, 0) for i in range(1 + len(c_got))])],
            [(0, c_rows - cut, [(i, cut) for i in range(1 + len(c_got))])],
        ],
    )
    c_got = send_all(c_send, nx - 1, shift_x)
    c_rows = c_keep.shape[0]
    cut = c_rows // ny * (ny - 1)
    (c_send, c_keep) = add_rows(
        [c_keep, *c_got],
        [
            [(0, cut, [(i, 0) for i in range(1 + len(c_got))])],
            [(0, c_rows - cut, [(i, cut) for i in range(1 + len(c_got))])],
        ],
    )
    c_got = send_all(c_send, ny - 1, shift_y)
    return tuple(finish(across, [c_keep, *c_got], width))


def solution(mesh):
    in_specs = (
        P("member", "batch", "tile", None),
        P(),
        P(),
        P("batch", "tile", None),
        P("batch", "tile"),
        P("batch", "tile"),
    )
    out_specs = (P(("member", "tile", "batch"), None), P(("member", "tile", "batch"), None))
    return jax.shard_map(shards, mesh=mesh, in_specs=in_specs, out_specs=out_specs, check_vma=False)
```

time: 193 us -> 126 us (0.65)
  waiting for transfers between devices: 130 us -> 39.5 us
  Pallas kernels: 0 us -> 28.7 us
  local copies, waits for them, and re-layouts: 13.5 us -> 31.9 us
  matrix products: 18.3 us -> 0 us
  starting transfers between devices: 9.83 us -> 23.7 us
  between operations: 14.2 us -> 0.94 us
  other arithmetic: 6.56 us -> 0.09 us
    unnamed x2 -> x0, waiting for transfers between devices: 106 us -> none
    ppermute x0 -> x10, waiting for transfers between devices: none -> 31.4 us  [the longest x1 14.3 us: shift_far(): lax.ppermute(value, 'member', [(t, (t // near + j) % far * near + t % nea...]
    pallas_call x0 -> x15, Pallas kernels: none -> 28.7 us  [the longest x1 7.05 us: decode(): pl.pallas_call(decode_body, grid=(parts,), in_specs=[pl.BlockSpec((block,...]
    dot_general x5 -> x0, matrix products: 18.3 us -> none  [the longest x1 7.91 us: shards(): lax.dot_general(rows_in, grad_preact, (((0,), (0,)), ((), ())), preferred...]
    all_to_all x2 -> x3, waiting for transfers between devices: 23.9 us -> 8.13 us  [the longest x1 7.24 us: shards(): lax.all_to_all(scored, 'member', split_axis=0, concat_axis=0, tiled=True)]
    unnamed x13 -> x64, local copies, waits for them, and re-layouts: 8.97 us -> 24.4 us
    ppermute x0 -> x10, starting transfers between devices: none -> 9.7 us  [the longest x3 3.61 us: shift_y(): return lax.ppermute(value, 'batch', [(t, (t + j) % ny) for t in range(ny)])]
    concatenate x1 -> x0, other arithmetic: 5.03 us -> none  [shards(): jnp.concatenate([first, second], axis=1)]
  transfers between devices with their start and end apart: 3 -> 13, of which waited for: 3 -> 10; matrix products, arithmetic and copies ran while one was open for 1% -> 4% of each run, Pallas kernels for 0% -> 13%
where the time goes in v2:
time: 126 us; the launch traced here: 125 us
  waiting for transfers between devices  39.5 us (31%)
  local copies, waits for them, and re-layouts  31.9 us (25%)
  Pallas kernels  28.7 us (23%)
  starting transfers between devices  23.7 us (19%)
    unnamed x64, local copies, waits for them, and re-layouts  24.4 us
    ppermute x1, waiting for transfers between devices, shift_far(): lax.ppermute(value, 'member', [(t, (t // near + j) % far * near + t % nea...  14.3 us
    all_to_all x1, waiting for transfers between devices, shards(): lax.all_to_all(scored, 'member', split_axis=0, concat_axis=0, tiled=True)  7.24 us
    pallas_call x1, Pallas kernels, decode(): pl.pallas_call(decode_body, grid=(parts,), in_specs=[pl.BlockSpec((block,...  7.05 us
    pallas_call x1, Pallas kernels, slopes(): pl.pallas_call(slope_body, grid=(nrows // block,), in_specs=[pl.BlockSpec...  6.98 us
    ppermute x3, waiting for transfers between devices, shift_y(): return lax.ppermute(value, 'batch', [(t, (t + j) % ny) for t in range(ny)])  6.78 us
    all_to_all x1, starting transfers between devices, shards(): lax.all_to_all(packed, 'member', split_axis=0, concat_axis=0, tiled=True)  6.33 us
    ppermute x3, waiting for transfers between devices, shift_x(): lax.ppermute(value, 'tile', [(t, (t // nc + j) % nx * nc + t % nc) for t...  5.75 us
  transfers between devices with their start and end apart: 13, of which 10 were waited for; matrix products, arithmetic and copies ran while one was open for 4% of the time, Pallas kernels for 13%

profile of v2, /device:TPU:0, one launch (start us, length us, event | category | flops | bytes accessed | tf_op | source)
XLA Modules:
  0.0 124.9 jit_solution(9681383440084400663)
XLA Ops:
  0.8 7.0 %decode.1 = f32[4,14,16,128]{3,2,1,0:T(8,128)} custom-call(bf16[1024,1024]{1,0:T(8,128)(2,1)} %bitcast.8, bf16[1024,1024]{1,0:T(8,128)(2,1)} %w_in_ref.3, bf16[112,1024]{1,0:T(8,128)(2,1)} %bitcast.12), custom_call_target="tpu_custom_call" | custom-call | flops 2382364672 | bytes 5242880 | tf_op jit(solution)/shard_map/decode/pallas_call | solution.py:77
  7.8 6.3 %all-to-all-start = ((f32[4,14,16,128]{3,2,1,0:T(8,128)}), f32[4,14,16,128]{3,2,1,0:T(8,128)S(1)}, u32[]{:S(2)}, u32[]{:S(2)}) async-start(f32[4,14,16,128]{3,2,1,0:T(8,128)} %decode.1), calls=%async_computation | async-start | bytes 917504 | tf_op jit(solution)/shard_map/all_to_all | solution.py:393
  14.4 1.6 %copy-done.20 = bf16[1024,1024]{1,0:T(8,128)(2,1)S(1)} copy-done((bf16[1024,1024]{1,0:T(8,128)(2,1)S(1)}, bf16[1024,1024]{1,0:T(8,128)(2,1)}, u32[]{:S(2)}) %copy-start.20) | copy-done | bytes 2097176
  16.0 7.0 %slopes.1 = (f32[1024,1024]{1,0:T(8,128)S(1)}, bf16[1024,1024]{1,0:T(8,128)(2,1)S(1)}) custom-call(s32[1,1024]{1,0:T(1,128)S(1)} %fusion.10.source_ref, bf16[1024,1024]{1,0:T(8,128)(2,1)S(1)} %bitcast.9, bf16[1024,1024]{1,0:T(8,128)(2,1)S(1)} %copy-done.20), custom_call_target="tpu_custom_call" | custom-call | flops 2147483648 | bytes 4194304 | tf_op jit(solution)/shard_map/slopes/pallas_call | solution.py:124
  24.3 2.0 %copy-done.11 = f32[1024,1024]{1,0:T(8,128)} copy-done((f32[1024,1024]{1,0:T(8,128)}, f32[1024,1024]{1,0:T(8,128)S(1)}, u32[]{:S(2)}) %copy-start.11) | copy-done | bytes 4194328
  27.4 1.4 %score.1 = f32[4,14,16,128]{3,2,1,0:T(8,128)} custom-call(f32[4,14,16,128]{3,2,1,0:T(8,128)S(1)} %all-to-all-done.x_ref, bf16[128,1792]{1,0:T(8,128)(2,1)S(1)} %bitcast.11, s32[16,1]{1,0:T(8,128)S(1)} %copy.17.index_ref, s32[16,1]{1,0:T(8,128)S(1)} %copy.18.count_ref), custom_call_target="tpu_custom_call" | custom-call | flops 3440640 | bytes 917504 | tf_op jit(solution)/shard_map/score/pallas_call | solution.py:213
  28.8 4.2 %all-to-all-start.1 = ((f32[4,14,16,128]{3,2,1,0:T(8,128)}), f32[4,14,16,128]{3,2,1,0:T(8,128)S(1)}, u32[]{:S(2)}, u32[]{:S(2)}) async-start(f32[4,14,16,128]{3,2,1,0:T(8,128)} %score.1), calls=%async_computation.1 | async-start | bytes 917504 | tf_op jit(solution)/shard_map/all_to_all | solution.py:405
  33.0 1.6 %copy-done.14 = bf16[1,1,1024,1024]{3,2,1,0:T(8,128)(2,1)S(1)} copy-done((bf16[1,1,1024,1024]{3,2,1,0:T(8,128)(2,1)S(1)}, bf16[1,1,1024,1024]{3,2,1,0:T(8,128)(2,1)}, u32[]{:S(2)}) %copy-start.14) | copy-done | bytes 2097176
  34.6 3.7 %ordered_transpose.1.latent_t_ref = bf16[1024,1024]{1,0:T(8,128)(2,1)S(1)} custom-call(s32[1,1024]{1,0:T(1,128)S(1)} %fusion.10.source_ref, bf16[1024,1024]{1,0:T(8,128)(2,1)S(1)} %bitcast.10), custom_call_target="tpu_custom_call" | custom-call | flops 1073741824 | bytes 4194304 | tf_op jit(solution)/shard_map/ordered_transpose/pallas_call | solution.py:160
  38.3 7.2 %all-to-all-done.1.scored_ref = f32[4,14,16,128]{3,2,1,0:T(8,128)S(1)} async-done(((f32[4,14,16,128]{3,2,1,0:T(8,128)}), f32[4,14,16,128]{3,2,1,0:T(8,128)S(1)}, u32[]{:S(2)}, u32[]{:S(2)}) %all-to-all-start.1) | async-done | bytes 458784 | tf_op jit(solution)/shard_map/all_to_all | solution.py:405
  45.5 1.6 %copy-done.1 = bf16[1024,1024]{1,0:T(8,128)(2,1)S(1)} copy-done((bf16[1024,1024]{1,0:T(8,128)(2,1)S(1)}, bf16[1024,1024]{1,0:T(8,128)(2,1)}, u32[]{:S(2)}) %copy-start.1) | copy-done | bytes 2097176
  47.1 2.2 %copy-done.12 = f32[1024,1024]{1,0:T(8,128)S(1)} copy-done((f32[1024,1024]{1,0:T(8,128)S(1)}, f32[1024,1024]{1,0:T(8,128)}, u32[]{:S(2)}) %copy-start.12) | copy-done | bytes 4194328
  49.3 1.6 %first_products.1 = (f32[256,1136]{1,0:T(8,128)S(1)}, bf16[1024,1024]{1,0:T(8,128)(2,1)S(1)}, bf16[1024,112]{1,0:T(8,128)(2,1)S(1)}) custom-call(f32[4,14,16,128]{3,2,1,0:T(8,128)S(1)} %all-to-all-done.1.scored_ref, f32[1024,1024]{1,0:T(8,128)S(1)} %copy-done.12, bf16[112,1024]{1,0:T(8,128)(2,1)S(1)} %bitcast.13, ...), custom_call_target="tpu_custom_call" | custom-call | flops 771751936 | bytes 8388608 | tf_op jit(solution)/shard_map/first_products/pallas_call | solution.py:249
  53.4 2.7 %copy.20 = f32[256,1136]{0,1:T(8,128)} copy(f32[256,1136]{1,0:T(8,128)} %copy-done.15) | data formatting | bytes 2326528 | tf_op jit(solution)/shard_map/first_products/pallas_call | solution.py:249
  56.1 1.6 %copy-done.2 = bf16[1024,1024]{1,0:T(8,128)(2,1)S(1)} copy-done((bf16[1024,1024]{1,0:T(8,128)(2,1)S(1)}, bf16[1024,1024]{1,0:T(8,128)(2,1)}, u32[]{:S(2)}) %copy-start.2) | copy-done | bytes 2097176
  57.7 1.6 %copy-done.6 = bf16[1024,1024]{1,0:T(8,128)(2,1)S(1)} copy-done((bf16[1024,1024]{1,0:T(8,128)(2,1)S(1)}, bf16[1024,1024]{1,0:T(8,128)(2,1)}, u32[]{:S(2)}) %copy-start.6) | copy-done | bytes 2097176
  60.1 1.4 %copy.19 = f32[256,1136]{0,1:T(8,128)} copy(f32[256,1136]{1,0:T(8,128)S(1)} %more_products.4) | data formatting | bytes 2326528 | tf_op jit(solution)/shard_map/more_products/pallas_call | solution.py:282
  62.0 1.6 %copy-done.3 = bf16[1024,1024]{1,0:T(8,128)(2,1)S(1)} copy-done((bf16[1024,1024]{1,0:T(8,128)(2,1)S(1)}, bf16[1024,1024]{1,0:T(8,128)(2,1)}, u32[]{:S(2)}) %copy-start.3) | copy-done | bytes 2097176
  63.6 1.6 %copy-done.7 = bf16[1024,1024]{1,0:T(8,128)(2,1)S(1)} copy-done((bf16[1024,1024]{1,0:T(8,128)(2,1)S(1)}, bf16[1024,1024]{1,0:T(8,128)(2,1)}, u32[]{:S(2)}) %copy-start.7) | copy-done | bytes 2097176
  67.1 1.6 %copy.21.refs_1_ = f32[256,1136]{1,0:T(8,128)S(1)} copy(f32[256,1136]{0,1:T(8,128)} %collective-permute-done.1) | data formatting | bytes 2326528 | tf_op jit(solution)/shard_map/ppermute | solution.py:410
  71.2 1.5 %collective-permute-start.2 = (f32[96,1136]{1,0:T(8,128)}, f32[96,1136]{1,0:T(8,128)}, u32[]{:S(2)}, u32[]{:S(2)}) collective-permute-start(f32[96,1136]{1,0:T(8,128)} %get-tuple-element.39), channel_id=1, source_target_pairs={{0,4},{2,6},{4,0},{6,2},{1,5},{3,7},{5,1},{7,3},{8,12},{10,14},{12... | collective-permute-start | bytes 1308680 | tf_op jit(solution)/shard_map/ppermute | solution.py:413
  72.7 1.5 %collective-permute-start.3 = (f32[96,1136]{1,0:T(8,128)}, f32[96,1136]{1,0:T(8,128)}, u32[]{:S(2)}, u32[]{:S(2)}) collective-permute-start(f32[96,1136]{1,0:T(8,128)} %get-tuple-element.40), channel_id=1, source_target_pairs={{0,1},{1,0},{2,3},{3,2},{4,5},{5,4},{6,7},{7,6},{8,9},{9,8},{10,11... | collective-permute-start | bytes 1308680 | tf_op jit(solution)/shard_map/ppermute | solution.py:416
  74.2 1.6 %copy-done.8 = bf16[1024,1024]{1,0:T(8,128)(2,1)S(1)} copy-done((bf16[1024,1024]{1,0:T(8,128)(2,1)S(1)}, bf16[1024,1024]{1,0:T(8,128)(2,1)}, u32[]{:S(2)}) %copy-start.8) | copy-done | bytes 2097176
  76.7 1.6 %copy.22.refs_1_ = f32[256,1136]{1,0:T(8,128)S(1)} copy(f32[256,1136]{0,1:T(8,128)} %collective-permute-done) | data formatting | bytes 2326528 | tf_op jit(solution)/shard_map/ppermute | solution.py:410
  78.3 4.6 %collective-permute-done.4.refs_4_ = f32[64,1136]{1,0:T(8,128)} collective-permute-done((f32[64,1136]{1,0:T(8,128)}, f32[64,1136]{1,0:T(8,128)}, u32[]{:S(2)}, u32[]{:S(2)}) %collective-permute-start.4) | collective-permute-done | bytes 290848 | tf_op jit(solution)/shard_map/ppermute | solution.py:419
  86.8 1.5 %collective-permute-start.5 = (f32[48,1136]{1,0:T(8,128)S(1)}, f32[48,1136]{1,0:T(8,128)S(1)}, u32[]{:S(2)}, u32[]{:S(2)}) collective-permute-start(f32[48,1136]{1,0:T(8,128)S(1)} %get-tuple-element.43), channel_id=1, source_target_pairs={{0,1},{1,0},{2,3},{3,2},{4,5},{5,4},{6,7},{7,6},{8,9},{9,8},{10,11... | collective-permute-start | bytes 654344 | tf_op jit(solution)/shard_map/ppermute | solution.py:416
  90.8 2.1 %collective-permute-done.5.refs_1_ = f32[48,1136]{1,0:T(8,128)S(1)} collective-permute-done((f32[48,1136]{1,0:T(8,128)S(1)}, f32[48,1136]{1,0:T(8,128)S(1)}, u32[]{:S(2)}, u32[]{:S(2)}) %collective-permute-start.5) | collective-permute-done | bytes 218144 | tf_op jit(solution)/shard_map/ppermute | solution.py:416
  95.1 3.5 %all-to-all-start.2 = ((f32[4,24,1136]{2,1,0:T(8,128)}), f32[4,24,1136]{2,1,0:T(8,128)S(1)}, u32[]{:S(2)}, u32[]{:S(2)}) async-start(f32[4,24,1136]{2,1,0:T(8,128)} %bitcast.5), calls=%async_computation.2 | async-start | bytes 884736 | tf_op jit(solution)/shard_map/all_to_all | solution.py:490
  98.5 2.9 %collective-permute-start.7 = (f32[32,1136]{1,0:T(8,128)S(1)}, f32[32,1136]{1,0:T(8,128)S(1)}, u32[]{:S(2)}, u32[]{:S(2)}) collective-permute-start(f32[32,1136]{1,0:T(8,128)S(1)} %copy-done.22), channel_id=1, source_target_pairs={{0,16},{8,24},{16,0},{24,8},{1,17},{9,25},{17,1},{25,9},{2,18},{10... | collective-permute-start | bytes 436232 | tf_op jit(solution)/shard_map/ppermute | solution.py:422
  101.4 14.3 %collective-permute-done.7.refs_1_ = f32[32,1136]{1,0:T(8,128)S(1)} collective-permute-done((f32[32,1136]{1,0:T(8,128)S(1)}, f32[32,1136]{1,0:T(8,128)S(1)}, u32[]{:S(2)}, u32[]{:S(2)}) %collective-permute-start.7) | collective-permute-done | bytes 145440 | tf_op jit(solution)/shard_map/ppermute | solution.py:422
  116.4 3.8 %collective-permute-done.8.refs_1_ = f32[16,1136]{1,0:T(8,128)S(1)} collective-permute-done((f32[16,1136]{1,0:T(8,128)S(1)}, f32[16,1136]{1,0:T(8,128)S(1)}, u32[]{:S(2)}, u32[]{:S(2)}) %collective-permute-start.8) | collective-permute-done | bytes 72736 | tf_op jit(solution)/shard_map/ppermute | solution.py:413
  120.7 3.4 %collective-permute-done.9.refs_1_ = f32[8,1136]{1,0:T(8,128)S(1)} collective-permute-done((f32[8,1136]{1,0:T(8,128)S(1)}, f32[8,1136]{1,0:T(8,128)S(1)}, u32[]{:S(2)}, u32[]{:S(2)}) %collective-permute-start.9) | collective-permute-done | bytes 36384 | tf_op jit(solution)/shard_map/ppermute | solution.py:416
  (81 shorter events, 22.0 us)
Async XLA Ops:
  0.6 13.5 %copy-start.30 = (s32[1,64]{1,0:T(1,128)S(1)}, s32[1,64]{1,0:T(1,128)}, u32[]{:S(2)}) copy-start(s32[1,64]{1,0:T(1,128)} %param.18) | copy-start | bytes 772
  0.6 13.5 %copy-start.31 = (s32[1,64]{1,0:T(1,128)S(1)}, s32[1,64]{1,0:T(1,128)}, u32[]{:S(2)}) copy-start(s32[1,64]{1,0:T(1,128)} %param.17) | copy-start | bytes 772
  0.6 13.6 %copy-start.23 = (s32[1,1024]{1,0:T(1,128)S(1)}, s32[1,1024]{1,0:T(1,128)}, u32[]{:S(2)}) copy-start(s32[1,1024]{1,0:T(1,128)} %constant.106.clone) | copy-start | bytes 12292
  0.7 13.5 %copy-start.24 = (s32[1,1024]{1,0:T(1,128)S(1)}, s32[1,1024]{1,0:T(1,128)}, u32[]{:S(2)}) copy-start(s32[1,1024]{1,0:T(1,128)} %constant.105.clone) | copy-start | bytes 12292
  0.7 13.5 %copy-start.25 = (s32[1,1024]{1,0:T(1,128)S(1)}, s32[1,1024]{1,0:T(1,128)}, u32[]{:S(2)}) copy-start(s32[1,1024]{1,0:T(1,128)} %constant.104.clone) | copy-start | bytes 12292
  0.7 13.5 %copy-start.26 = (s32[1,1024]{1,0:T(1,128)S(1)}, s32[1,1024]{1,0:T(1,128)}, u32[]{:S(2)}) copy-start(s32[1,1024]{1,0:T(1,128)} %constant.103.clone) | copy-start | bytes 12292
  0.7 13.5 %copy-start.27 = (s32[1,1024]{1,0:T(1,128)S(1)}, s32[1,1024]{1,0:T(1,128)}, u32[]{:S(2)}) copy-start(s32[1,1024]{1,0:T(1,128)} %constant.102.clone) | copy-start | bytes 12292
  0.7 13.5 %copy-start.28 = (s32[1,1024]{1,0:T(1,128)S(1)}, s32[1,1024]{1,0:T(1,128)}, u32[]{:S(2)}) copy-start(s32[1,1024]{1,0:T(1,128)} %constant.101.clone) | copy-start | bytes 12292
  0.7 13.5 %copy-start.29 = (s32[1,1024]{1,0:T(1,128)S(1)}, s32[1,1024]{1,0:T(1,128)}, u32[]{:S(2)}) copy-start(s32[1,1024]{1,0:T(1,128)} %constant.100.clone) | copy-start | bytes 12292
  0.7 13.6 %copy-start.13 = (bf16[1,1,1024,1024]{3,2,1,0:T(8,128)(2,1)S(1)}, bf16[1,1,1024,1024]{3,2,1,0:T(8,128)(2,1)}, u32[]{:S(2)}) copy-start(bf16[1,1,1024,1024]{3,2,1,0:T(8,128)(2,1)} %param.13) | copy-start | bytes 6291460
  7.8 19.4 %all-to-all-start = ((f32[4,14,16,128]{3,2,1,0:T(8,128)}), f32[4,14,16,128]{3,2,1,0:T(8,128)S(1)}, u32[]{:S(2)}, u32[]{:S(2)}) async-start(f32[4,14,16,128]{3,2,1,0:T(8,128)} %decode.1), calls=%async_computation | async-start | bytes 917504 | tf_op jit(solution)/shard_map/all_to_all | solution.py:393
  14.4 1.6 %copy-start.20 = (bf16[1024,1024]{1,0:T(8,128)(2,1)S(1)}, bf16[1024,1024]{1,0:T(8,128)(2,1)}, u32[]{:S(2)}) copy-start(bf16[1024,1024]{1,0:T(8,128)(2,1)} %w_in_ref.3) | copy-start | bytes 6291460
  16.0 11.4 %copy-start.16 = (bf16[1,128,1792]{2,1,0:T(8,128)(2,1)S(1)}, bf16[1,128,1792]{2,1,0:T(8,128)(2,1)}, u32[]{:S(2)}) copy-start(bf16[1,128,1792]{2,1,0:T(8,128)(2,1)} %param.16) | copy-start | bytes 1376260
  24.3 2.0 %copy-start.11 = (f32[1024,1024]{1,0:T(8,128)}, f32[1024,1024]{1,0:T(8,128)S(1)}, u32[]{:S(2)}) copy-start(f32[1024,1024]{1,0:T(8,128)S(1)} %get-tuple-element.33.slope_ref) | copy-start | bytes 12582916
  28.8 16.7 %all-to-all-start.1 = ((f32[4,14,16,128]{3,2,1,0:T(8,128)}), f32[4,14,16,128]{3,2,1,0:T(8,128)S(1)}, u32[]{:S(2)}, u32[]{:S(2)}) async-start(f32[4,14,16,128]{3,2,1,0:T(8,128)} %score.1), calls=%async_computation.1 | async-start | bytes 917504 | tf_op jit(solution)/shard_map/all_to_all | solution.py:405
  34.6 10.9 %copy-start.17 = (bf16[1024,112]{0,1:T(8,128)(2,1)S(1)}, bf16[1024,112]{0,1:T(8,128)(2,1)}, u32[]{:S(2)}) copy-start(bf16[1024,112]{0,1:T(8,128)(2,1)} %param.15) | copy-start | bytes 688132
  45.5 1.6 %copy-start.1 = (bf16[1024,1024]{1,0:T(8,128)(2,1)S(1)}, bf16[1024,1024]{1,0:T(8,128)(2,1)}, u32[]{:S(2)}) copy-start(bf16[1024,1024]{1,0:T(8,128)(2,1)} %copy-done) | copy-start | bytes 6291460
  47.1 2.2 %copy-start.12 = (f32[1024,1024]{1,0:T(8,128)S(1)}, f32[1024,1024]{1,0:T(8,128)}, u32[]{:S(2)}) copy-start(f32[1024,1024]{1,0:T(8,128)} %copy-done.11) | copy-start | bytes 12582916
  56.1 11.0 %collective-permute-start.1 = (f32[256,1136]{0,1:T(8,128)}, f32[256,1136]{0,1:T(8,128)}, u32[]{:S(2)}, u32[]{:S(2)}) collective-permute-start(f32[256,1136]{0,1:T(8,128)} %copy.20), channel_id=1, source_target_pairs={{0,2},{2,0},{4,6},{6,4},{1,3},{3,1},{5,7},{7,5},{8,10},{10,8},{12,... | collective-permute-start | bytes 3489800 | tf_op jit(solution)/shard_map/ppermute | solution.py:410
  61.5 15.1 %collective-permute-start = (f32[256,1136]{0,1:T(8,128)}, f32[256,1136]{0,1:T(8,128)}, u32[]{:S(2)}, u32[]{:S(2)}) collective-permute-start(f32[256,1136]{0,1:T(8,128)} %copy.19), channel_id=1, source_target_pairs={{0,2},{2,0},{4,6},{6,4},{1,3},{3,1},{5,7},{7,5},{8,10},{10,8},{12,... | collective-permute-start | bytes 3489800 | tf_op jit(solution)/shard_map/ppermute | solution.py:410
  70.0 4.2 %copy-start.4 = (bf16[1024,1024]{1,0:T(8,128)(2,1)S(1)}, bf16[1024,1024]{1,0:T(8,128)(2,1)}, u32[]{:S(2)}) copy-start(bf16[1024,1024]{1,0:T(8,128)(2,1)} %copy-done) | copy-start | bytes 6291460
  71.2 12.4 %collective-permute-start.2 = (f32[96,1136]{1,0:T(8,128)}, f32[96,1136]{1,0:T(8,128)}, u32[]{:S(2)}, u32[]{:S(2)}) collective-permute-start(f32[96,1136]{1,0:T(8,128)} %get-tuple-element.39), channel_id=1, source_target_pairs={{0,4},{2,6},{4,0},{6,2},{1,5},{3,7},{5,1},{7,3},{8,12},{10,14},{12... | collective-permute-start | bytes 1308680 | tf_op jit(solution)/shard_map/ppermute | solution.py:413
  72.7 12.1 %collective-permute-start.3 = (f32[96,1136]{1,0:T(8,128)}, f32[96,1136]{1,0:T(8,128)}, u32[]{:S(2)}, u32[]{:S(2)}) collective-permute-start(f32[96,1136]{1,0:T(8,128)} %get-tuple-element.40), channel_id=1, source_target_pairs={{0,1},{1,0},{2,3},{3,2},{4,5},{5,4},{6,7},{7,6},{8,9},{9,8},{10,11... | collective-permute-start | bytes 1308680 | tf_op jit(solution)/shard_map/ppermute | solution.py:416
  74.2 8.7 %collective-permute-start.4 = (f32[64,1136]{1,0:T(8,128)}, f32[64,1136]{1,0:T(8,128)}, u32[]{:S(2)}, u32[]{:S(2)}) collective-permute-start(f32[64,1136]{1,0:T(8,128)} %get-tuple-element.41), channel_id=1, source_target_pairs={{0,8},{8,0},{16,24},{24,16},{1,9},{9,1},{17,25},{25,17},{2,10},{10... | collective-permute-start | bytes 872456 | tf_op jit(solution)/shard_map/ppermute | solution.py:419
  86.8 6.2 %collective-permute-start.5 = (f32[48,1136]{1,0:T(8,128)S(1)}, f32[48,1136]{1,0:T(8,128)S(1)}, u32[]{:S(2)}, u32[]{:S(2)}) collective-permute-start(f32[48,1136]{1,0:T(8,128)S(1)} %get-tuple-element.43), channel_id=1, source_target_pairs={{0,1},{1,0},{2,3},{3,2},{4,5},{5,4},{6,7},{7,6},{8,9},{9,8},{10,11... | collective-permute-start | bytes 654344 | tf_op jit(solution)/shard_map/ppermute | solution.py:416
  88.3 5.9 %collective-permute-start.6 = (f32[48,1136]{1,0:T(8,128)S(1)}, f32[48,1136]{1,0:T(8,128)S(1)}, u32[]{:S(2)}, u32[]{:S(2)}) collective-permute-start(f32[48,1136]{1,0:T(8,128)S(1)} %get-tuple-element.45), channel_id=1, source_target_pairs={{0,4},{2,6},{4,0},{6,2},{1,5},{3,7},{5,1},{7,3},{8,12},{10,14},{12... | collective-permute-start | bytes 654344 | tf_op jit(solution)/shard_map/ppermute | solution.py:413
  90.8 7.7 %copy-start.22 = (f32[32,1136]{1,0:T(8,128)S(1)}, f32[32,1136]{1,0:T(8,128)}, u32[]{:S(2)}) copy-start(f32[32,1136]{1,0:T(8,128)} %copy-done.21) | copy-start | bytes 436228
  93.0 22.7 %copy-start.19 = (f32[32,1136]{1,0:T(8,128)S(1)}, f32[32,1136]{1,0:T(8,128)}, u32[]{:S(2)}) copy-start(f32[32,1136]{1,0:T(8,128)} %copy-done.18) | copy-start | bytes 436228
  95.1 29.1 %all-to-all-start.2 = ((f32[4,24,1136]{2,1,0:T(8,128)}), f32[4,24,1136]{2,1,0:T(8,128)S(1)}, u32[]{:S(2)}, u32[]{:S(2)}) async-start(f32[4,24,1136]{2,1,0:T(8,128)} %bitcast.5), calls=%async_computation.2 | async-start | bytes 884736 | tf_op jit(solution)/shard_map/all_to_all | solution.py:490
  98.5 17.2 %collective-permute-start.7 = (f32[32,1136]{1,0:T(8,128)S(1)}, f32[32,1136]{1,0:T(8,128)S(1)}, u32[]{:S(2)}, u32[]{:S(2)}) collective-permute-start(f32[32,1136]{1,0:T(8,128)S(1)} %copy-done.22), channel_id=1, source_target_pairs={{0,16},{8,24},{16,0},{24,8},{1,17},{9,25},{17,1},{25,9},{2,18},{10... | collective-permute-start | bytes 436232 | tf_op jit(solution)/shard_map/ppermute | solution.py:422
  115.7 4.4 %collective-permute-start.8 = (f32[16,1136]{1,0:T(8,128)S(1)}, f32[16,1136]{1,0:T(8,128)S(1)}, u32[]{:S(2)}, u32[]{:S(2)}) collective-permute-start(f32[16,1136]{1,0:T(8,128)S(1)} %get-tuple-element.49), channel_id=1, source_target_pairs={{0,4},{2,6},{4,0},{6,2},{1,5},{3,7},{5,1},{7,3},{8,12},{10,14},{12... | collective-permute-start | bytes 218120 | tf_op jit(solution)/shard_map/ppermute | solution.py:413
  120.2 4.0 %collective-permute-start.9 = (f32[8,1136]{1,0:T(8,128)S(1)}, f32[8,1136]{1,0:T(8,128)S(1)}, u32[]{:S(2)}, u32[]{:S(2)}) collective-permute-start(f32[8,1136]{1,0:T(8,128)S(1)} %get-tuple-element.51), channel_id=1, source_target_pairs={{0,1},{1,0},{2,3},{3,2},{4,5},{5,4},{6,7},{7,6},{8,9},{9,8},{10,11... | collective-permute-start | bytes 109064 | tf_op jit(solution)/shard_map/ppermute | solution.py:416
  (13 other events, 16.9 us)

commit v3 on v2

--- a/solution.py
+++ b/solution.py
@@ -13,7 +13,9 @@
 LANES = 128
 MIB = 1 << 20
 NT = (((1,), (1,)), ((), ()))
-WHOLE = pl.BlockSpec(memory_space=pltpu.VMEM)
+WHOLE = pl.BlockSpec()
+ANY = pl.BlockSpec(memory_space=pl.ANY)
+MOST = 56
 
 
 def params(mib=24):
@@ -57,14 +59,52 @@
     return cells
 
 
-def decode_body(latent_ref, w_in_ref, w_out_t_ref, packed_ref, cells):
-    channels = w_out_t_ref.shape[0]
-    share = packed_ref.shape[2]
-    preact = jnp.dot(latent_ref[...], w_in_ref[...], preferred_element_type=jnp.float32)
-    hidden = (preact / (1.0 + jnp.exp(-preact))).astype(jnp.bfloat16)
-    cells[:, :channels] = lax.dot_general(hidden, w_out_t_ref[...], NT, preferred_element_type=jnp.float32)
-    for j, row in enumerate(pack(lambda j: cells[pl.ds(j, share, stride=PATCH), :], channels)):
-        packed_ref[0, j] = row
+def column_steps(width):
+    step = 256 if width % 256 == 0 else width
+    return [slice(low, low + step) for low in range(0, width, step)]
+
+
+def decode_body(latent_ref, w_in_ref, w_out_t_ref, packed_ref, rows, w_in, w_out_t, hidden, cells, packed, row_sems, w_sems, sems):
+    parts, block, _ = rows.shape
+    channels, width = w_out_t.shape
+    share = packed.shape[2]
+    column = column_steps(width)
+    row_copies = [
+        pltpu.make_async_copy(latent_ref.at[pl.ds(q * block, block)], rows.at[q], row_sems.at[q]) for q in range(parts)
+    ]
+    w_copies = [
+        pltpu.make_async_copy(w_in_ref.at[:, pl.ds(c.start, c.stop - c.start)], w_in.at[:, c], w_sems.at[k])
+        for k, c in enumerate(column)
+    ]
+    last_copy = pltpu.make_async_copy(w_out_t_ref, w_out_t, sems.at[parts])
+    row_copies[0].start()
+    for copy in w_copies:
+        copy.start()
+    last_copy.start()
+    for copy in row_copies[1:]:
+        copy.start()
+
+    def silu(preact):
+        return (preact / (1.0 + jnp.exp(-preact))).astype(jnp.bfloat16)
+
+    results = []
+    for q in range(parts):
+        row_copies[q].wait()
+        if q == 0:
+            for copy, c in zip(w_copies, column):
+                copy.wait()
+                hidden[:, c] = silu(jnp.dot(rows[q], w_in[:, c], preferred_element_type=jnp.float32))
+            last_copy.wait()
+            value = hidden[...]
+        else:
+            value = silu(jnp.dot(rows[q], w_in[...], preferred_element_type=jnp.float32))
+        cells[:, :channels] = lax.dot_general(value, w_out_t[...], NT, preferred_element_type=jnp.float32)
+        for j, row in enumerate(pack(lambda j: cells[pl.ds(j, share, stride=PATCH), :], channels)):
+            packed[q, j] = row
+        results.append(pltpu.make_async_copy(packed.at[q], packed_ref.at[q], sems.at[q]))
+        results[-1].start()
+    for copy in results:
+        copy.wait()
 
 
 def decode(rows_in, w_in, w_out_t, parts):
@@ -74,18 +114,24 @@
     block = nrows // parts
     share = block // PATCH
     carriers = packing(channels)[1]
+    out = (parts, carriers, share, LANES)
     return pl.pallas_call(
         decode_body,
-        grid=(parts,),
-        in_specs=[
-            pl.BlockSpec((block, depth), lambda i: (i, 0)),
-            pl.BlockSpec((depth, width), lambda i: (0, 0)),
-            pl.BlockSpec((channels, width), lambda i: (0, 0)),
-        ],
-        out_specs=pl.BlockSpec((1, carriers, share, LANES), lambda i: (i, 0, 0, 0)),
-        out_shape=jax.ShapeDtypeStruct((parts, carriers, share, LANES), jnp.float32),
-        scratch_shapes=[pltpu.VMEM((block, LANES), jnp.float32)],
-        compiler_params=params(56),
+        in_specs=[ANY] * 3,
+        out_specs=ANY,
+        out_shape=jax.ShapeDtypeStruct(out, jnp.float32),
+        scratch_shapes=[
+            pltpu.VMEM((parts, block, depth), jnp.bfloat16),
+            pltpu.VMEM((depth, width), jnp.bfloat16),
+            pltpu.VMEM((channels, width), jnp.bfloat16),
+            pltpu.VMEM((block, width), jnp.bfloat16),
+            pltpu.VMEM((block, LANES), jnp.float32),
+            pltpu.VMEM(out, jnp.float32),
+            pltpu.SemaphoreType.DMA((parts,)),
+            pltpu.SemaphoreType.DMA((len(column_steps(width)),)),
+            pltpu.SemaphoreType.DMA((parts + 1,)),
+        ],
+        compiler_params=params(MOST),
         cost_estimate=cost(2 * nrows * width * (depth + channels), 5 * MIB),
         name="decode",
     )(rows_in, w_in, w_out_t)
@@ -138,7 +184,7 @@
             jax.ShapeDtypeStruct((picked, nrows), jnp.bfloat16),
         ],
         scratch_shapes=[pltpu.VMEM((picked, width), jnp.bfloat16)],
-        compiler_params=params(),
+        compiler_params=params(MOST),
         cost_estimate=cost(2 * nrows * width * depth, 4 * MIB),
         name="slopes",
     )(source, rows_in, w_in)
@@ -167,7 +213,7 @@
         out_specs=pl.BlockSpec((picked, block), lambda i: (0, i)),
         out_shape=jax.ShapeDtypeStruct((picked, nrows), jnp.bfloat16),
         scratch_shapes=[pltpu.VMEM((picked, extent), jnp.bfloat16)],
-        compiler_params=params(),
+        compiler_params=params(MOST),
         cost_estimate=cost(nrows * extent * picked, 4 * MIB),
         name="ordered_transpose",
     )(source, matrix)
@@ -221,73 +267,93 @@
     )(grouped, pool, index, count)
 
 
-def column_steps(width):
-    step = 256 if width % 256 == 0 else width
-    return [slice(low, low + step) for low in range(0, width, step)]
-
-
-def first_body(low, high, scored_ref, slope_ref, w_out_t_ref, latent_t_ref, hidden_t_ref, out_ref, gp_ref, g16_ref, cells):
-    parts, carriers, share, _ = scored_ref.shape
-    channels, width = w_out_t_ref.shape
+def products_body(
+    cuts, scored_ref, slope_ref, w_out_t_ref, latent_t_ref, hidden_t_ref, *refs
+):
+    out_refs, scratch = refs[:len(cuts)], refs[len(cuts):]
+    scored, slope, w_out_t, latent_t, hidden_t, cells, result, in_sems, slope_sems, out_sems = scratch
+    parts, carriers, share, _ = scored.shape
+    channels, width = w_out_t.shape
+    column = column_steps(width)
+    scored_copy, w_copy, latent_copy, hidden_copy = (
+        pltpu.make_async_copy(source, target, in_sems.at[k])
+        for k, (source, target) in enumerate(
+            [(scored_ref, scored), (w_out_t_ref, w_out_t), (latent_t_ref, latent_t), (hidden_t_ref, hidden_t)]
+        )
+    )
+    slope_copies = [
+        pltpu.make_async_copy(slope_ref.at[:, pl.ds(c.start, c.stop - c.start)], slope.at[:, c], slope_sems.at[k])
+        for k, c in enumerate(column)
+    ]
+    scored_copy.start()
+    w_copy.start()
+    slope_copies[0].start()
+    latent_copy.start()
+    for copy in slope_copies[1:]:
+        copy.start()
+    hidden_copy.start()
+
+    scored_copy.wait()
     for q in range(parts):
-        rows = [scored_ref[q, j] for j in range(carriers)]
+        rows = [scored[q, j] for j in range(carriers)]
         for j, value in enumerate(unpack(rows, channels)):
             cells[pl.ds(q * share * PATCH + j, share, stride=PATCH), :] = value
-    g16 = cells[:, :channels].astype(jnp.bfloat16)
-    g16_ref[...] = g16
-    for columns in column_steps(width):
-        gh = jnp.dot(g16, w_out_t_ref[:, columns], preferred_element_type=jnp.float32)
-        gp = (gh * slope_ref[:, columns]).astype(jnp.bfloat16)
-        gp_ref[:, columns] = gp
-        out_ref[:, columns] = jnp.dot(latent_t_ref[low:high], gp, preferred_element_type=jnp.float32)
-    out_ref[:, width:] = jnp.dot(hidden_t_ref[low:high], g16, preferred_element_type=jnp.float32)
-
-
-def first_products(scored, slope, w_out_t, latent_t, hidden_t, low, high):
+    lane = lax.broadcasted_iota(jnp.int32, cells.shape, 1)
+    g = jnp.where(lane < channels, cells[...], 0.0).astype(jnp.bfloat16)
+
+    results = []
+
+    def put(k, c, product):
+        result[:, c] = product
+        for i, (out_ref, (start, end)) in enumerate(zip(out_refs, cuts)):
+            copy = pltpu.make_async_copy(
+                result.at[pl.ds(start, end - start), c],
+                out_ref.at[:, pl.ds(c.start, c.stop - c.start)],
+                out_sems.at[k, i],
+            )
+            copy.start()
+            results.append(copy)
+
+    w_copy.wait()
+    for k, c in enumerate(column):
+        gh = jnp.dot(g[:, :channels], w_out_t[:, c], preferred_element_type=jnp.float32)
+        slope_copies[k].wait()
+        gp = (gh * slope[:, c]).astype(jnp.bfloat16)
+        if k == 0:
+            latent_copy.wait()
+        put(k, c, jnp.dot(latent_t[...], gp, preferred_element_type=jnp.float32))
+    hidden_copy.wait()
+    put(len(column), slice(width, width + LANES), jnp.dot(hidden_t[...], g, preferred_element_type=jnp.float32))
+    for copy in results:
+        copy.wait()
+
+
+def products(scored, slope, w_out_t, latent_t, hidden_t, cuts):
     nrows, width = slope.shape
     channels = w_out_t.shape[0]
-    return pl.pallas_call(
-        functools.partial(first_body, low, high),
-        in_specs=[WHOLE] * 5,
-        out_specs=[WHOLE] * 3,
-        out_shape=[
-            jax.ShapeDtypeStruct((high - low, width + channels), jnp.float32),
-            jax.ShapeDtypeStruct((nrows, width), jnp.bfloat16),
-            jax.ShapeDtypeStruct((nrows, channels), jnp.bfloat16),
-        ],
-        scratch_shapes=[pltpu.VMEM((nrows, LANES), jnp.float32)],
-        compiler_params=params(),
-        cost_estimate=cost(2 * nrows * width * (channels + high - low), 8 * MIB),
-        name="first_products",
+    picked = latent_t.shape[0]
+    steps = len(column_steps(width))
+    return pl.pallas_call(
+        functools.partial(products_body, tuple(cuts)),
+        in_specs=[ANY] * 5,
+        out_specs=[ANY] * len(cuts),
+        out_shape=[jax.ShapeDtypeStruct((end - start, width + LANES), jnp.float32) for start, end in cuts],
+        scratch_shapes=[
+            pltpu.VMEM(scored.shape, jnp.float32),
+            pltpu.VMEM(slope.shape, jnp.float32),
+            pltpu.VMEM(w_out_t.shape, jnp.bfloat16),
+            pltpu.VMEM(latent_t.shape, jnp.bfloat16),
+            pltpu.VMEM(hidden_t.shape, jnp.bfloat16),
+            pltpu.VMEM((nrows, LANES), jnp.float32),
+            pltpu.VMEM((picked, width + LANES), jnp.float32),
+            pltpu.SemaphoreType.DMA((4,)),
+            pltpu.SemaphoreType.DMA((steps,)),
+            pltpu.SemaphoreType.DMA((steps + 1, len(cuts))),
+        ],
+        compiler_params=params(MOST),
+        cost_estimate=cost(2 * nrows * width * (channels + picked), 12 * MIB),
+        name="products",
     )(scored, slope, w_out_t, latent_t, hidden_t)
-
-
-def more_body(cuts, gp_ref, g16_ref, latent_t_ref, hidden_t_ref, *out_refs):
-    width = gp_ref.shape[1]
-    low, high = cuts[0][0], cuts[-1][1]
-
-    def put(columns, product):
-        for out_ref, (start, end) in zip(out_refs, cuts):
-            out_ref[:, columns] = product[start - low:end - low]
-
-    for columns in column_steps(width):
-        put(columns, jnp.dot(latent_t_ref[low:high], gp_ref[:, columns], preferred_element_type=jnp.float32))
-    put(slice(width, None), jnp.dot(hidden_t_ref[low:high], g16_ref[...], preferred_element_type=jnp.float32))
-
-
-def more_products(gp, g16, latent_t, hidden_t, cuts):
-    nrows, channels = g16.shape
-    width = gp.shape[1]
-    picked = cuts[-1][1] - cuts[0][0]
-    return pl.pallas_call(
-        functools.partial(more_body, tuple(cuts)),
-        in_specs=[WHOLE] * 4,
-        out_specs=[WHOLE] * len(cuts),
-        out_shape=[jax.ShapeDtypeStruct((end - start, width + channels), jnp.float32) for start, end in cuts],
-        compiler_params=params(),
-        cost_estimate=cost(2 * nrows * picked * (width + channels), 6 * MIB),
-        name="more_products",
-    )(gp, g16, latent_t, hidden_t)
 
 
 def add_body(plans, count, *refs):
@@ -327,19 +393,18 @@
         last = last + ref[...]
     for low, high, value in ((0, rows, total), (rows, first_ref.shape[0], last)):
         first_ref[low:high] = value[:, :width]
-        second_ref[low:high] = value[:, width:]
-
-
-def finish(across, rest, width):
+        second_ref[low:high] = value[:, width:width + second_ref.shape[1]]
+
+
+def finish(across, rest, width, channels):
     height = across.shape[1] + rest[0].shape[0]
-    columns = across.shape[2]
     return pl.pallas_call(
         finish_body,
         in_specs=[WHOLE] * (1 + len(rest)),
         out_specs=[WHOLE] * 2,
         out_shape=[
             jax.ShapeDtypeStruct((height, width), jnp.float32),
-            jax.ShapeDtypeStruct((height, columns - width), jnp.float32),
+            jax.ShapeDtypeStruct((height, channels), jnp.float32),
         ],
         compiler_params=params(),
         cost_estimate=cost(across.size, 4 * across.size),
@@ -430,25 +495,18 @@
     n_send, n_keep = na + nb + nc_send, nc_keep + na_keep + nb_keep
     half = n_send + n_keep
 
-    first, gp, g16 = first_products(returned, slope, w_out_t, latent_t, hidden_t, 0, n_send)
-    from_core = shift_core(first, 1)
-    (own_send,) = more_products(gp, g16, latent_t, hidden_t, [(half, half + n_send)])
-    a_send, b_send, c_send = add_rows(
-        [own_send, from_core],
-        [
-            [(0, na, [(0, 0), (1, 0)])],
-            [(0, nb, [(0, na), (1, na)])],
-            [(0, nc_send, [(0, na + nb), (1, na + nb)])],
-        ],
-    )
+    other_send, other_keep, own_send, own_keep = products(
+        returned, slope, w_out_t, latent_t, hidden_t,
+        [(0, n_send), (n_send, half), (half, half + n_send), (half + n_send, 2 * half)],
+    )
+    core_send = shift_core(other_send, 1)
+    core_keep = shift_core(other_keep, 1)
+    a_send = own_send[:na] + core_send[:na]
+    b_send = own_send[na:na + nb] + core_send[na:na + nb]
+    c_send = own_send[na + nb:] + core_send[na + nb:]
     a_got = send_all(a_send, nx - 1, shift_x)
     b_got = send_all(b_send, ny - 1, shift_y)
     c_got = send_all(c_send, near - 1, shift_near)
-    other_keep, own_keep = more_products(
-        gp, g16, latent_t, hidden_t, [(n_send, half)]
-    ) + more_products(gp, g16, latent_t, hidden_t, [(half + n_send, 2 * half)])
-    core_keep = shift_core(other_keep, 1)
-
     inputs = [own_keep, core_keep, *a_got, *b_got, *c_got]
     a_in = range(2, 2 + len(a_got))
     b_in = range(a_in.stop, a_in.stop + len(b_got))
@@ -479,6 +537,7 @@
         ],
     )
 
+    a_got, b_got, c_got = lax.optimization_barrier((a_got, b_got, c_got))
     inputs = [a_keep, *a_got, b_keep, *b_got]
     plan, a_low, b_low, at = [], 0, 0, 0
     for k in range(nz):
@@ -510,7 +569,7 @@
         ],
     )
     c_got = send_all(c_send, ny - 1, shift_y)
-    return tuple(finish(across, [c_keep, *c_got], width))
+    return tuple(finish(across, [c_keep, *c_got], width, channels))
 
 
 def solution(mesh):

time: 126 us -> 101 us (0.80)
  local copies, waits for them, and re-layouts: 31.9 us -> 1.05 us
  Pallas kernels: 28.7 us -> 35.7 us
  other arithmetic: 0.09 us -> 3.01 us
  starting transfers between devices: 23.7 us -> 21.5 us
    unnamed x64 -> x24, local copies, waits for them, and re-layouts: 24.4 us -> 0.82 us
    ppermute x1, waiting for transfers between devices: 14.3 us -> 7.06 us  [shift_far(): lax.ppermute(value, 'member', [(t, (t // near + j) % far * near + t % nea...]
    pallas_call x5 -> x2, Pallas kernels: 11.2 us -> 17.1 us  [the longest x1 9.5 us: products(): pl.pallas_call(functools.partial(products_body, tuple(cuts)), in_specs=[A...]
    ppermute x3, waiting for transfers between devices: 6.78 us -> 2.54 us  [shift_y(): return lax.ppermute(value, 'batch', [(t, (t + j) % ny) for t in range(ny)])]
    pallas_call x2 -> x0, local copies, waits for them, and re-layouts: 4.09 us -> none  [the longest x1 2.69 us: first_products(): pl.pallas_call(functools.partial(first_body, low, high), in_specs=[WHOLE]...]
    ppermute x1, waiting for transfers between devices: 4.58 us -> 8.47 us  [shift_near(): lax.ppermute(value, 'member', [(t, t // near * near + (t % near + j) % ne...]
    all_to_all x1, waiting for transfers between devices: 0.01 us -> 3.79 us  [shards(): lax.all_to_all(joined.reshape(nz, height - rc, joined.shape[1]), 'member'...]
    pallas_call x6 -> x5, Pallas kernels: 4.69 us -> 1.03 us  [add_rows(): pl.pallas_call(functools.partial(add_body, plans, len(inputs)), in_specs=...]
  transfers between devices with their start and end apart: 13 -> 13, of which waited for: 10 -> 9; matrix products, arithmetic and copies ran while one was open for 4% -> 3% of each run, Pallas kernels for 13% -> 16%
where the time goes in v3:
time: 101 us; the launch traced here: 100 us
  waiting for transfers between devices  38.3 us (38%)
  Pallas kernels  35.7 us (35%)
  starting transfers between devices  21.5 us (21%)
  other arithmetic  3.01 us (3%)
  local copies, waits for them, and re-layouts  1.05 us (1%)
    pallas_call x1, Pallas kernels, slopes(): pl.pallas_call(slope_body, grid=(nrows // block,), in_specs=[pl.BlockSpec...  9.56 us
    pallas_call x1, Pallas kernels, products(): pl.pallas_call(functools.partial(products_body, tuple(cuts)), in_specs=[A...  9.5 us
    ppermute x1, waiting for transfers between devices, shift_near(): lax.ppermute(value, 'member', [(t, t // near * near + (t % near + j) % ne...  8.47 us
    pallas_call x1, Pallas kernels, decode(): pl.pallas_call(decode_body, in_specs=[ANY] * 3, out_specs=ANY, out_shape=...  7.58 us
    ppermute x1, waiting for transfers between devices, shift_far(): lax.ppermute(value, 'member', [(t, (t // near + j) % far * near + t % nea...  7.06 us
    all_to_all x1, waiting for transfers between devices, shards(): lax.all_to_all(scored, 'member', split_axis=0, concat_axis=0, tiled=True)  6.47 us
    all_to_all x1, starting transfers between devices, shards(): lax.all_to_all(packed, 'member', split_axis=0, concat_axis=0, tiled=True)  6.33 us
    pallas_call x1, Pallas kernels, ordered_transpose(): pl.pallas_call(order_body, grid=(nrows // block,), in_specs=[pl.BlockSpec...  5.91 us
  transfers between devices with their start and end apart: 13, of which 9 were waited for; matrix products, arithmetic and copies ran while one was open for 3% of the time, Pallas kernels for 16%

profile of v3, /device:TPU:0, one launch (start us, length us, event | category | flops | bytes accessed | tf_op | source)
XLA Modules:
  0.0 100.4 jit_solution(9874653406795136376)
XLA Ops:
  0.7 7.6 %decode.1 = f32[4,14,16,128]{3,2,1,0:T(8,128)} custom-call(bf16[1024,1024]{1,0:T(8,128)(2,1)} %bitcast.9, bf16[1024,1024]{1,0:T(8,128)(2,1)} %w_in_ref.3, bf16[112,1024]{1,0:T(8,128)(2,1)} %bitcast.12), custom_call_target="tpu_custom_call" | custom-call | flops 2382364672 | bytes 5242880 | tf_op jit(solution)/shard_map/decode/pallas_call | solution.py:118
  8.3 6.3 %all-to-all-start = ((f32[4,14,16,128]{3,2,1,0:T(8,128)}), f32[4,14,16,128]{3,2,1,0:T(8,128)S(1)}, u32[]{:S(2)}, u32[]{:S(2)}) async-start(f32[4,14,16,128]{3,2,1,0:T(8,128)} %decode.1), calls=%async_computation | async-start | bytes 917504 | tf_op jit(solution)/shard_map/all_to_all | solution.py:458
  14.8 0.7 fusion.10.source_ref
  15.5 9.6 %slopes.1 = (f32[1024,1024]{1,0:T(8,128)}, bf16[1024,1024]{1,0:T(8,128)(2,1)}) custom-call(s32[1,1024]{1,0:T(1,128)} %fusion.10.source_ref, bf16[1024,1024]{1,0:T(8,128)(2,1)} %bitcast.10, bf16[1024,1024]{1,0:T(8,128)(2,1)} %w_in_ref.3), custom_call_target="tpu_custom_call" | custom-call | flops 2147483648 | bytes 4194304 | tf_op jit(solution)/shard_map/slopes/pallas_call | solution.py:170
  25.0 2.7 %all-to-all-done.x_ref = f32[4,14,16,128]{3,2,1,0:T(8,128)S(1)} async-done(((f32[4,14,16,128]{3,2,1,0:T(8,128)}), f32[4,14,16,128]{3,2,1,0:T(8,128)S(1)}, u32[]{:S(2)}, u32[]{:S(2)}) %all-to-all-start) | async-done | bytes 458784 | tf_op jit(solution)/shard_map/all_to_all | solution.py:458
  27.9 1.5 %score.1 = f32[4,14,16,128]{3,2,1,0:T(8,128)} custom-call(f32[4,14,16,128]{3,2,1,0:T(8,128)S(1)} %all-to-all-done.x_ref, bf16[128,1792]{1,0:T(8,128)(2,1)S(1)} %bitcast.8, s32[16,1]{1,0:T(8,128)S(1)} %copy.15.index_ref, s32[16,1]{1,0:T(8,128)S(1)} %copy.16.count_ref), custom_call_target="tpu_custom_call" | custom-call | flops 3440640 | bytes 917504 | tf_op jit(solution)/shard_map/score/pallas_call | solution.py:259
  29.4 3.6 %all-to-all-start.1 = ((f32[4,14,16,128]{3,2,1,0:T(8,128)}), f32[4,14,16,128]{3,2,1,0:T(8,128)S(1)}, u32[]{:S(2)}, u32[]{:S(2)}) async-start(f32[4,14,16,128]{3,2,1,0:T(8,128)} %score.1), calls=%async_computation.1 | async-start | bytes 917504 | tf_op jit(solution)/shard_map/all_to_all | solution.py:470
  33.0 5.9 %ordered_transpose.1.latent_t_ref = bf16[1024,1024]{1,0:T(8,128)(2,1)} custom-call(s32[1,1024]{1,0:T(1,128)} %fusion.10.source_ref, bf16[1024,1024]{1,0:T(8,128)(2,1)} %bitcast.11), custom_call_target="tpu_custom_call" | custom-call | flops 1073741824 | bytes 4194304 | tf_op jit(solution)/shard_map/ordered_transpose/pallas_call | solution.py:206
  38.9 6.5 %all-to-all-done.1.scored_ref = f32[4,14,16,128]{3,2,1,0:T(8,128)S(1)} async-done(((f32[4,14,16,128]{3,2,1,0:T(8,128)}), f32[4,14,16,128]{3,2,1,0:T(8,128)S(1)}, u32[]{:S(2)}, u32[]{:S(2)}) %all-to-all-start.1) | async-done | bytes 458784 | tf_op jit(solution)/shard_map/all_to_all | solution.py:470
  45.4 0.8 copy-done.2
  46.2 9.5 %products.1 = (f32[256,1152]{1,0:T(8,128)}, f32[256,1152]{1,0:T(8,128)}, f32[256,1152]{1,0:T(8,128)}, f32[256,1152]{1,0:T(8,128)}) custom-call(f32[4,14,16,128]{3,2,1,0:T(8,128)} %copy-done.2, f32[1024,1024]{1,0:T(8,128)} %get-tuple-element.34.slope_ref, bf16[112,1024]{1,0:T(8,128)(2,1)} %bitcast.13, bf16[1024,1024]{1,0:T(8,128)(2,1)} %ordered_transpose.1.latent_t_ref, ...), custom_call_target="tpu_custom_call" | custom-call | flops 2382364672 | bytes 12582912 | tf_op jit(solution)/shard_map/products/pallas_call | solution.py:336
  55.8 0.5 collective-permute-start
  56.3 2.5 %collective-permute-done.1 = f32[256,1152]{1,0:T(8,128)S(1)} collective-permute-done((f32[256,1152]{1,0:T(8,128)}, f32[256,1152]{1,0:T(8,128)S(1)}, u32[]{:S(2)}, u32[]{:S(2)}) %collective-permute-start.1) | collective-permute-done | bytes 1179680 | tf_op jit(solution)/shard_map/ppermute | solution.py:475
  58.8 1.3 %slice_add_fusion = (f32[96,1152]{1,0:T(8,128)S(1)}, f32[96,1152]{1,0:T(8,128)S(1)}) fusion(f32[256,1152]{1,0:T(8,128)S(1)} %collective-permute-done.1, f32[256,1152]{1,0:T(8,128)} %get-tuple-element.39), kind=kLoop, calls=%fused_computation | loop fusion | flops 221184 | bytes 2654208 | tf_op jit(solution)/shard_map/add | solution.py:505
  60.1 1.6 %collective-permute-start.3 = (f32[96,1152]{1,0:T(8,128)S(1)}, f32[96,1152]{1,0:T(8,128)S(1)}, u32[]{:S(2)}, u32[]{:S(2)}) collective-permute-start(f32[96,1152]{1,0:T(8,128)S(1)} %get-tuple-element.54), channel_id=1, source_target_pairs={{0,1},{1,0},{2,3},{3,2},{4,5},{5,4},{6,7},{7,6},{8,9},{9,8},{10,11... | collective-permute-start | bytes 1327112 | tf_op jit(solution)/shard_map/ppermute | solution.py:481
  61.7 1.5 %collective-permute-start.2 = (f32[96,1152]{1,0:T(8,128)S(1)}, f32[96,1152]{1,0:T(8,128)S(1)}, u32[]{:S(2)}, u32[]{:S(2)}) collective-permute-start(f32[96,1152]{1,0:T(8,128)S(1)} %get-tuple-element.55), channel_id=1, source_target_pairs={{0,4},{2,6},{4,0},{6,2},{1,5},{3,7},{5,1},{7,3},{8,12},{10,14},{12... | collective-permute-start | bytes 1327112 | tf_op jit(solution)/shard_map/ppermute | solution.py:478
  63.2 1.0 slice_add_fusion.2
  64.3 8.5 %collective-permute-done.4.refs_4_ = f32[64,1152]{1,0:T(8,128)S(1)} collective-permute-done((f32[64,1152]{1,0:T(8,128)S(1)}, f32[64,1152]{1,0:T(8,128)S(1)}, u32[]{:S(2)}, u32[]{:S(2)}) %collective-permute-start.4) | collective-permute-done | bytes 294944 | tf_op jit(solution)/shard_map/ppermute | solution.py:484
  72.8 0.9 collective-permute-done.2.refs_2_
  73.7 0.1 add_rows.6
  73.8 0.6 collective-permute-start.5
  74.3 1.5 %collective-permute-start.6 = (f32[48,1152]{1,0:T(8,128)S(1)}, f32[48,1152]{1,0:T(8,128)S(1)}, u32[]{:S(2)}, u32[]{:S(2)}) collective-permute-start(f32[48,1152]{1,0:T(8,128)S(1)} %get-tuple-element.43), channel_id=1, source_target_pairs={{0,4},{2,6},{4,0},{6,2},{1,5},{3,7},{5,1},{7,3},{8,12},{10,14},{12... | collective-permute-start | bytes 663560 | tf_op jit(solution)/shard_map/ppermute | solution.py:478
  75.8 0.1 add_rows.5
  75.9 7.1 %collective-permute-done.7.refs_1_ = f32[32,1152]{1,0:T(8,128)S(1)} collective-permute-done((f32[32,1152]{1,0:T(8,128)S(1)}, f32[32,1152]{1,0:T(8,128)S(1)}, u32[]{:S(2)}, u32[]{:S(2)}) %collective-permute-start.7) | collective-permute-done | bytes 147488 | tf_op jit(solution)/shard_map/ppermute | solution.py:487
  83.0 0.8 add_rows.7
  83.8 3.6 %all-to-all-start.2 = ((f32[4,24,1152]{2,1,0:T(8,128)}), f32[4,24,1152]{2,1,0:T(8,128)S(1)}, u32[]{:S(2)}, u32[]{:S(2)}) async-start(f32[4,24,1152]{2,1,0:T(8,128)} %bitcast.5), calls=%async_computation.2 | async-start | bytes 884736 | tf_op jit(solution)/shard_map/all_to_all | solution.py:549
  87.5 0.6 collective-permute-start.8
  88.1 3.8 %collective-permute-done.8.refs_1_ = f32[16,1152]{1,0:T(8,128)S(1)} collective-permute-done((f32[16,1152]{1,0:T(8,128)S(1)}, f32[16,1152]{1,0:T(8,128)S(1)}, u32[]{:S(2)}, u32[]{:S(2)}) %collective-permute-start.8) | collective-permute-done | bytes 73760 | tf_op jit(solution)/shard_map/ppermute | solution.py:478
  91.9 1.5 %collective-permute-start.9 = (f32[8,1152]{1,0:T(8,128)S(1)}, f32[8,1152]{1,0:T(8,128)S(1)}, u32[]{:S(2)}, u32[]{:S(2)}) collective-permute-start(f32[8,1152]{1,0:T(8,128)S(1)} %get-tuple-element.53), channel_id=1, source_target_pairs={{0,1},{1,0},{2,3},{3,2},{4,5},{5,4},{6,7},{7,6},{8,9},{9,8},{10,11... | collective-permute-start | bytes 110600 | tf_op jit(solution)/shard_map/ppermute | solution.py:481
  93.4 2.5 %collective-permute-done.9.refs_1_ = f32[8,1152]{1,0:T(8,128)S(1)} collective-permute-done((f32[8,1152]{1,0:T(8,128)S(1)}, f32[8,1152]{1,0:T(8,128)S(1)}, u32[]{:S(2)}, u32[]{:S(2)}) %collective-permute-start.9) | collective-permute-done | bytes 36896 | tf_op jit(solution)/shard_map/ppermute | solution.py:481
  95.9 3.8 %all-to-all-done.2.across_ref = f32[4,24,1152]{2,1,0:T(8,128)S(1)} async-done(((f32[4,24,1152]{2,1,0:T(8,128)}), f32[4,24,1152]{2,1,0:T(8,128)S(1)}, u32[]{:S(2)}, u32[]{:S(2)}) %all-to-all-start.2) | async-done | bytes 442400 | tf_op jit(solution)/shard_map/all_to_all | solution.py:549
  99.7 0.7 finish.1
  (35 shorter events, 0.5 us)
Async XLA Ops:
  0.6 14.0 %copy-start.10 = (s32[1,64]{1,0:T(1,128)S(1)}, s32[1,64]{1,0:T(1,128)}, u32[]{:S(2)}) copy-start(s32[1,64]{1,0:T(1,128)} %param.18) | copy-start | bytes 772
  0.6 14.0 %copy-start.11 = (s32[1,64]{1,0:T(1,128)S(1)}, s32[1,64]{1,0:T(1,128)}, u32[]{:S(2)}) copy-start(s32[1,64]{1,0:T(1,128)} %param.17) | copy-start | bytes 772
  0.6 14.1 %copy-start.3 = (s32[1,1024]{1,0:T(1,128)S(1)}, s32[1,1024]{1,0:T(1,128)}, u32[]{:S(2)}) copy-start(s32[1,1024]{1,0:T(1,128)} %constant.106.clone) | copy-start | bytes 12292
  0.7 14.1 %copy-start.4 = (s32[1,1024]{1,0:T(1,128)S(1)}, s32[1,1024]{1,0:T(1,128)}, u32[]{:S(2)}) copy-start(s32[1,1024]{1,0:T(1,128)} %constant.105.clone) | copy-start | bytes 12292
  0.7 14.1 %copy-start.5 = (s32[1,1024]{1,0:T(1,128)S(1)}, s32[1,1024]{1,0:T(1,128)}, u32[]{:S(2)}) copy-start(s32[1,1024]{1,0:T(1,128)} %constant.104.clone) | copy-start | bytes 12292
  0.7 14.1 %copy-start.6 = (s32[1,1024]{1,0:T(1,128)S(1)}, s32[1,1024]{1,0:T(1,128)}, u32[]{:S(2)}) copy-start(s32[1,1024]{1,0:T(1,128)} %constant.103.clone) | copy-start | bytes 12292
  0.7 14.1 %copy-start.7 = (s32[1,1024]{1,0:T(1,128)S(1)}, s32[1,1024]{1,0:T(1,128)}, u32[]{:S(2)}) copy-start(s32[1,1024]{1,0:T(1,128)} %constant.102.clone) | copy-start | bytes 12292
  0.7 14.1 %copy-start.8 = (s32[1,1024]{1,0:T(1,128)S(1)}, s32[1,1024]{1,0:T(1,128)}, u32[]{:S(2)}) copy-start(s32[1,1024]{1,0:T(1,128)} %constant.101.clone) | copy-start | bytes 12292
  0.7 14.1 %copy-start.9 = (s32[1,1024]{1,0:T(1,128)S(1)}, s32[1,1024]{1,0:T(1,128)}, u32[]{:S(2)}) copy-start(s32[1,1024]{1,0:T(1,128)} %constant.100.clone) | copy-start | bytes 12292
  8.3 19.4 %all-to-all-start = ((f32[4,14,16,128]{3,2,1,0:T(8,128)}), f32[4,14,16,128]{3,2,1,0:T(8,128)S(1)}, u32[]{:S(2)}, u32[]{:S(2)}) async-start(f32[4,14,16,128]{3,2,1,0:T(8,128)} %decode.1), calls=%async_computation | async-start | bytes 917504 | tf_op jit(solution)/shard_map/all_to_all | solution.py:458
  15.5 12.4 %copy-start.1 = (bf16[1,128,1792]{2,1,0:T(8,128)(2,1)S(1)}, bf16[1,128,1792]{2,1,0:T(8,128)(2,1)}, u32[]{:S(2)}) copy-start(bf16[1,128,1792]{2,1,0:T(8,128)(2,1)} %param.16) | copy-start | bytes 1376260
  29.4 16.0 %all-to-all-start.1 = ((f32[4,14,16,128]{3,2,1,0:T(8,128)}), f32[4,14,16,128]{3,2,1,0:T(8,128)S(1)}, u32[]{:S(2)}, u32[]{:S(2)}) async-start(f32[4,14,16,128]{3,2,1,0:T(8,128)} %score.1), calls=%async_computation.1 | async-start | bytes 917504 | tf_op jit(solution)/shard_map/all_to_all | solution.py:470
  45.4 0.8 copy-start.2
  55.7 3.1 %collective-permute-start.1 = (f32[256,1152]{1,0:T(8,128)}, f32[256,1152]{1,0:T(8,128)S(1)}, u32[]{:S(2)}, u32[]{:S(2)}) collective-permute-start(f32[256,1152]{1,0:T(8,128)} %get-tuple-element.40), channel_id=1, source_target_pairs={{0,2},{2,0},{4,6},{6,4},{1,3},{3,1},{5,7},{7,5},{8,10},{10,8},{12,... | collective-permute-start | bytes 3538952 | tf_op jit(solution)/shard_map/ppermute | solution.py:475
  55.8 8.5 %collective-permute-start = (f32[256,1152]{1,0:T(8,128)}, f32[256,1152]{1,0:T(8,128)S(1)}, u32[]{:S(2)}, u32[]{:S(2)}) collective-permute-start(f32[256,1152]{1,0:T(8,128)} %get-tuple-element.38), channel_id=1, source_target_pairs={{0,2},{2,0},{4,6},{6,4},{1,3},{3,1},{5,7},{7,5},{8,10},{10,8},{12,... | collective-permute-start | bytes 3538952 | tf_op jit(solution)/shard_map/ppermute | solution.py:475
  58.8 14.9 %copy-start = (f32[256,1152]{1,0:T(8,128)S(1)}, f32[256,1152]{1,0:T(8,128)}, u32[]{:S(2)}) copy-start(f32[256,1152]{1,0:T(8,128)} %get-tuple-element.37.refs_0_) | copy-start | bytes 3538948
  60.1 12.6 %collective-permute-start.3 = (f32[96,1152]{1,0:T(8,128)S(1)}, f32[96,1152]{1,0:T(8,128)S(1)}, u32[]{:S(2)}, u32[]{:S(2)}) collective-permute-start(f32[96,1152]{1,0:T(8,128)S(1)} %get-tuple-element.54), channel_id=1, source_target_pairs={{0,1},{1,0},{2,3},{3,2},{4,5},{5,4},{6,7},{7,6},{8,9},{9,8},{10,11... | collective-permute-start | bytes 1327112 | tf_op jit(solution)/shard_map/ppermute | solution.py:481
  61.7 11.9 %collective-permute-start.2 = (f32[96,1152]{1,0:T(8,128)S(1)}, f32[96,1152]{1,0:T(8,128)S(1)}, u32[]{:S(2)}, u32[]{:S(2)}) collective-permute-start(f32[96,1152]{1,0:T(8,128)S(1)} %get-tuple-element.55), channel_id=1, source_target_pairs={{0,4},{2,6},{4,0},{6,2},{1,5},{3,7},{5,1},{7,3},{8,12},{10,14},{12... | collective-permute-start | bytes 1327112 | tf_op jit(solution)/shard_map/ppermute | solution.py:478
  64.2 8.6 %collective-permute-start.4 = (f32[64,1152]{1,0:T(8,128)S(1)}, f32[64,1152]{1,0:T(8,128)S(1)}, u32[]{:S(2)}, u32[]{:S(2)}) collective-permute-start(f32[64,1152]{1,0:T(8,128)S(1)} %slice_add_fusion.2), channel_id=1, source_target_pairs={{0,8},{8,0},{16,24},{24,16},{1,9},{9,1},{17,25},{25,17},{2,10},{10... | collective-permute-start | bytes 884744 | tf_op jit(solution)/shard_map/ppermute | solution.py:484
  73.8 9.2 %collective-permute-start.5 = (f32[48,1152]{1,0:T(8,128)S(1)}, f32[48,1152]{1,0:T(8,128)S(1)}, u32[]{:S(2)}, u32[]{:S(2)}) collective-permute-start(f32[48,1152]{1,0:T(8,128)S(1)} %get-tuple-element.42), channel_id=1, source_target_pairs={{0,1},{1,0},{2,3},{3,2},{4,5},{5,4},{6,7},{7,6},{8,9},{9,8},{10,11... | collective-permute-start | bytes 663560 | tf_op jit(solution)/shard_map/ppermute | solution.py:481
  74.3 8.7 %collective-permute-start.6 = (f32[48,1152]{1,0:T(8,128)S(1)}, f32[48,1152]{1,0:T(8,128)S(1)}, u32[]{:S(2)}, u32[]{:S(2)}) collective-permute-start(f32[48,1152]{1,0:T(8,128)S(1)} %get-tuple-element.43), channel_id=1, source_target_pairs={{0,4},{2,6},{4,0},{6,2},{1,5},{3,7},{5,1},{7,3},{8,12},{10,14},{12... | collective-permute-start | bytes 663560 | tf_op jit(solution)/shard_map/ppermute | solution.py:478
  75.8 7.2 %collective-permute-start.7 = (f32[32,1152]{1,0:T(8,128)S(1)}, f32[32,1152]{1,0:T(8,128)S(1)}, u32[]{:S(2)}, u32[]{:S(2)}) collective-permute-start(f32[32,1152]{1,0:T(8,128)S(1)} %get-tuple-element.44), channel_id=1, source_target_pairs={{0,16},{8,24},{16,0},{24,8},{1,17},{9,25},{17,1},{25,9},{2,18},{10... | collective-permute-start | bytes 442376 | tf_op jit(solution)/shard_map/ppermute | solution.py:487
  83.8 15.9 %all-to-all-start.2 = ((f32[4,24,1152]{2,1,0:T(8,128)}), f32[4,24,1152]{2,1,0:T(8,128)S(1)}, u32[]{:S(2)}, u32[]{:S(2)}) async-start(f32[4,24,1152]{2,1,0:T(8,128)} %bitcast.5), calls=%async_computation.2 | async-start | bytes 884736 | tf_op jit(solution)/shard_map/all_to_all | solution.py:549
  87.5 4.4 %collective-permute-start.8 = (f32[16,1152]{1,0:T(8,128)S(1)}, f32[16,1152]{1,0:T(8,128)S(1)}, u32[]{:S(2)}, u32[]{:S(2)}) collective-permute-start(f32[16,1152]{1,0:T(8,128)S(1)} %get-tuple-element.51), channel_id=1, source_target_pairs={{0,4},{2,6},{4,0},{6,2},{1,5},{3,7},{5,1},{7,3},{8,12},{10,14},{12... | collective-permute-start | bytes 221192 | tf_op jit(solution)/shard_map/ppermute | solution.py:478
  91.9 4.0 %collective-permute-start.9 = (f32[8,1152]{1,0:T(8,128)S(1)}, f32[8,1152]{1,0:T(8,128)S(1)}, u32[]{:S(2)}, u32[]{:S(2)}) collective-permute-start(f32[8,1152]{1,0:T(8,128)S(1)} %get-tuple-element.53), channel_id=1, source_target_pairs={{0,1},{1,0},{2,3},{3,2},{4,5},{5,4},{6,7},{7,6},{8,9},{9,8},{10,11... | collective-permute-start | bytes 110600 | tf_op jit(solution)/shard_map/ppermute | solution.py:481

commit v4 on v3

--- a/solution.py
+++ b/solution.py
@@ -15,11 +15,13 @@
 NT = (((1,), (1,)), ((), ()))
 WHOLE = pl.BlockSpec()
 ANY = pl.BlockSpec(memory_space=pl.ANY)
+FEW = 24
+TIGHT = 60.3
 MOST = 56
 
 
 def params(mib=24):
-    return pltpu.CompilerParams(vmem_limit_bytes=mib * MIB)
+    return pltpu.CompilerParams(vmem_limit_bytes=int(mib * MIB))
 
 
 def cost(flops, moved):
@@ -64,7 +66,7 @@
     return [slice(low, low + step) for low in range(0, width, step)]
 
 
-def decode_body(latent_ref, w_in_ref, w_out_t_ref, packed_ref, rows, w_in, w_out_t, hidden, cells, packed, row_sems, w_sems, sems):
+def decode_body(latent_ref, w_in_ref, w_out_t_ref, packed_ref, rows, w_in, w_out_t, cells, packed, row_sems, w_sems, sems):
     parts, block, _ = rows.shape
     channels, width = w_out_t.shape
     share = packed.shape[2]
@@ -77,29 +79,20 @@
         for k, c in enumerate(column)
     ]
     last_copy = pltpu.make_async_copy(w_out_t_ref, w_out_t, sems.at[parts])
-    row_copies[0].start()
-    for copy in w_copies:
+    for copy in [*w_copies, *row_copies[:parts // 2], last_copy, *row_copies[parts // 2:]]:
         copy.start()
-    last_copy.start()
-    for copy in row_copies[1:]:
-        copy.start()
-
-    def silu(preact):
-        return (preact / (1.0 + jnp.exp(-preact))).astype(jnp.bfloat16)
 
     results = []
+    for copy in [*w_copies, *row_copies[:parts // 2], last_copy]:
+        copy.wait()
     for q in range(parts):
-        row_copies[q].wait()
-        if q == 0:
-            for copy, c in zip(w_copies, column):
+        if q == parts // 2:
+            for copy in row_copies[q:]:
                 copy.wait()
-                hidden[:, c] = silu(jnp.dot(rows[q], w_in[:, c], preferred_element_type=jnp.float32))
-            last_copy.wait()
-            value = hidden[...]
-        else:
-            value = silu(jnp.dot(rows[q], w_in[...], preferred_element_type=jnp.float32))
-        cells[:, :channels] = lax.dot_general(value, w_out_t[...], NT, preferred_element_type=jnp.float32)
-        for j, row in enumerate(pack(lambda j: cells[pl.ds(j, share, stride=PATCH), :], channels)):
+        preact = jnp.dot(rows[q], w_in[...], preferred_element_type=jnp.float32)
+        hidden = (preact / (1.0 + jnp.exp(-preact))).astype(jnp.bfloat16)
+        cells[q, :, :channels] = lax.dot_general(hidden, w_out_t[...], NT, preferred_element_type=jnp.float32)
+        for j, row in enumerate(pack(lambda j: cells[q, pl.ds(j, share, stride=PATCH), :], channels)):
             packed[q, j] = row
         results.append(pltpu.make_async_copy(packed.at[q], packed_ref.at[q], sems.at[q]))
         results[-1].start()
@@ -124,8 +117,7 @@
             pltpu.VMEM((parts, block, depth), jnp.bfloat16),
             pltpu.VMEM((depth, width), jnp.bfloat16),
             pltpu.VMEM((channels, width), jnp.bfloat16),
-            pltpu.VMEM((block, width), jnp.bfloat16),
-            pltpu.VMEM((block, LANES), jnp.float32),
+            pltpu.VMEM((parts, block, LANES), jnp.float32),
             pltpu.VMEM(out, jnp.float32),
             pltpu.SemaphoreType.DMA((parts,)),
             pltpu.SemaphoreType.DMA((len(column_steps(width)),)),
@@ -148,59 +140,45 @@
             choice[low:high, left:left + LANES] = jnp.where(down == here, 1.0, 0.0).astype(jnp.bfloat16)
 
 
-def slope_body(source_ref, latent_ref, w_in_ref, slope_ref, hidden_t_ref, choice):
-    @pl.when(pl.program_id(0) == 0)
-    def _():
-        fill_choice(source_ref, choice)
-
+def slope_body(latent_ref, w_in_ref, slope_ref, hidden_ref):
     preact = jnp.dot(latent_ref[...], w_in_ref[...], preferred_element_type=jnp.float32)
     scale = 1.0 + jnp.exp(-preact)
     sigma = 1.0 / scale
     slope_ref[...] = sigma * (1.0 + preact * (1.0 - sigma))
-    hidden = (preact / scale).astype(jnp.bfloat16)
-    ordered = lax.dot_general(choice[...], hidden, NT, preferred_element_type=jnp.float32)
-    hidden_t_ref[...] = ordered.astype(jnp.bfloat16)
-
-
-def slopes(source, rows_in, w_in):
+    hidden_ref[...] = (preact / scale).astype(jnp.bfloat16)
+
+
+def slopes(rows_in, w_in):
     nrows, depth = rows_in.shape
     width = w_in.shape[1]
-    picked = source.shape[1]
     block = 256 if nrows % 256 == 0 else nrows
     return pl.pallas_call(
         slope_body,
         grid=(nrows // block,),
-        in_specs=[
-            pl.BlockSpec((1, picked), lambda i: (0, 0)),
-            pl.BlockSpec((block, depth), lambda i: (i, 0)),
-            pl.BlockSpec((depth, width), lambda i: (0, 0)),
-        ],
-        out_specs=[
-            pl.BlockSpec((block, width), lambda i: (i, 0)),
-            pl.BlockSpec((picked, block), lambda i: (0, i)),
-        ],
+        in_specs=[pl.BlockSpec((block, depth), lambda i: (i, 0)), pl.BlockSpec((depth, width), lambda i: (0, 0))],
+        out_specs=[pl.BlockSpec((block, width), lambda i: (i, 0)), pl.BlockSpec((block, width), lambda i: (i, 0))],
         out_shape=[
             jax.ShapeDtypeStruct((nrows, width), jnp.float32),
-            jax.ShapeDtypeStruct((picked, nrows), jnp.bfloat16),
-        ],
-        scratch_shapes=[pltpu.VMEM((picked, width), jnp.bfloat16)],
+            jax.ShapeDtypeStruct((nrows, width), jnp.bfloat16),
+        ],
         compiler_params=params(MOST),
         cost_estimate=cost(2 * nrows * width * depth, 4 * MIB),
         name="slopes",
-    )(source, rows_in, w_in)
-
-
-def order_body(source_ref, matrix_ref, out_ref, choice):
+    )(rows_in, w_in)
+
+
+def order_body(source_ref, latent_ref, hidden_ref, out_ref, choice):
     @pl.when(pl.program_id(0) == 0)
     def _():
         fill_choice(source_ref, choice)
 
-    ordered = lax.dot_general(choice[...], matrix_ref[...], NT, preferred_element_type=jnp.float32)
-    out_ref[...] = ordered.astype(jnp.bfloat16)
-
-
-def ordered_transpose(source, matrix):
-    nrows, extent = matrix.shape
+    for k, matrix_ref in enumerate((latent_ref, hidden_ref)):
+        ordered = lax.dot_general(choice[...], matrix_ref[...], NT, preferred_element_type=jnp.float32)
+        out_ref[k] = ordered.astype(jnp.bfloat16)
+
+
+def ordered_transposes(source, latent, hidden):
+    nrows, extent = latent.shape
     picked = source.shape[1]
     block = 256 if nrows % 256 == 0 else nrows
     return pl.pallas_call(
@@ -209,14 +187,15 @@
         in_specs=[
             pl.BlockSpec((1, picked), lambda i: (0, 0)),
             pl.BlockSpec((block, extent), lambda i: (i, 0)),
-        ],
-        out_specs=pl.BlockSpec((picked, block), lambda i: (0, i)),
-        out_shape=jax.ShapeDtypeStruct((picked, nrows), jnp.bfloat16),
+            pl.BlockSpec((block, extent), lambda i: (i, 0)),
+        ],
+        out_specs=pl.BlockSpec((2, picked, block), lambda i: (0, 0, i)),
+        out_shape=jax.ShapeDtypeStruct((2, picked, nrows), jnp.bfloat16),
         scratch_shapes=[pltpu.VMEM((picked, extent), jnp.bfloat16)],
         compiler_params=params(MOST),
         cost_estimate=cost(nrows * extent * picked, 4 * MIB),
-        name="ordered_transpose",
-    )(source, matrix)
+        name="ordered_transposes",
+    )(source, latent, hidden)
 
 
 def score_body(channels, x_ref, pool_ref, index_ref, count_ref, out_ref):
@@ -267,31 +246,29 @@
     )(grouped, pool, index, count)
 
 
-def products_body(
-    cuts, scored_ref, slope_ref, w_out_t_ref, latent_t_ref, hidden_t_ref, *refs
+def first_body(
+    scored_ref, slope_ref, w_out_t_ref, ordered_ref, out_ref, gp_ref, g_ref,
+    scored, slope, w_out_t, latent_t, hidden_t, cells, gp, g, result, in_sems, slope_sems, gp_sems, out_sems,
 ):
-    out_refs, scratch = refs[:len(cuts)], refs[len(cuts):]
-    scored, slope, w_out_t, latent_t, hidden_t, cells, result, in_sems, slope_sems, out_sems = scratch
     parts, carriers, share, _ = scored.shape
     channels, width = w_out_t.shape
+    picked = result.shape[0]
     column = column_steps(width)
-    scored_copy, w_copy, latent_copy, hidden_copy = (
+    scored_copy, w_copy, hidden_copy, latent_copy = copies = [
         pltpu.make_async_copy(source, target, in_sems.at[k])
-        for k, (source, target) in enumerate(
-            [(scored_ref, scored), (w_out_t_ref, w_out_t), (latent_t_ref, latent_t), (hidden_t_ref, hidden_t)]
-        )
-    )
+        for k, (source, target) in enumerate([
+            (scored_ref, scored),
+            (w_out_t_ref, w_out_t),
+            (ordered_ref.at[1, pl.ds(0, picked)], hidden_t),
+            (ordered_ref.at[0, pl.ds(0, picked)], latent_t),
+        ])
+    ]
     slope_copies = [
         pltpu.make_async_copy(slope_ref.at[:, pl.ds(c.start, c.stop - c.start)], slope.at[:, c], slope_sems.at[k])
         for k, c in enumerate(column)
     ]
-    scored_copy.start()
-    w_copy.start()
-    slope_copies[0].start()
-    latent_copy.start()
-    for copy in slope_copies[1:]:
+    for copy in [*copies, *slope_copies]:
         copy.start()
-    hidden_copy.start()
 
     scored_copy.wait()
     for q in range(parts):
@@ -299,61 +276,125 @@
         for j, value in enumerate(unpack(rows, channels)):
             cells[pl.ds(q * share * PATCH + j, share, stride=PATCH), :] = value
     lane = lax.broadcasted_iota(jnp.int32, cells.shape, 1)
-    g = jnp.where(lane < channels, cells[...], 0.0).astype(jnp.bfloat16)
-
-    results = []
+    g[...] = jnp.where(lane < channels, cells[...], 0.0).astype(jnp.bfloat16)
+    results = [pltpu.make_async_copy(g, g_ref, gp_sems.at[len(column)])]
+    results[0].start()
 
     def put(k, c, product):
         result[:, c] = product
-        for i, (out_ref, (start, end)) in enumerate(zip(out_refs, cuts)):
-            copy = pltpu.make_async_copy(
-                result.at[pl.ds(start, end - start), c],
-                out_ref.at[:, pl.ds(c.start, c.stop - c.start)],
-                out_sems.at[k, i],
-            )
-            copy.start()
-            results.append(copy)
+        target = out_ref.at[:, pl.ds(c.start, c.stop - c.start)]
+        results.append(pltpu.make_async_copy(result.at[:, c], target, out_sems.at[k]))
+        results[-1].start()
 
     w_copy.wait()
+    backward = [
+        jnp.dot(g[:, :channels], w_out_t[:, c], preferred_element_type=jnp.float32) for c in column
+    ]
+    hidden_copy.wait()
+    last = slice(width, width + LANES)
+    put(len(column), last, jnp.dot(hidden_t[...], g[...], preferred_element_type=jnp.float32))
+    latent_copy.wait()
     for k, c in enumerate(column):
-        gh = jnp.dot(g[:, :channels], w_out_t[:, c], preferred_element_type=jnp.float32)
         slope_copies[k].wait()
-        gp = (gh * slope[:, c]).astype(jnp.bfloat16)
-        if k == 0:
-            latent_copy.wait()
-        put(k, c, jnp.dot(latent_t[...], gp, preferred_element_type=jnp.float32))
-    hidden_copy.wait()
-    put(len(column), slice(width, width + LANES), jnp.dot(hidden_t[...], g, preferred_element_type=jnp.float32))
+        gp[:, c] = (backward[k] * slope[:, c]).astype(jnp.bfloat16)
+        results.append(pltpu.make_async_copy(gp.at[:, c], gp_ref.at[:, pl.ds(c.start, c.stop - c.start)], gp_sems.at[k]))
+        results[-1].start()
+        put(k, c, jnp.dot(latent_t[...], gp[:, c], preferred_element_type=jnp.float32))
     for copy in results:
         copy.wait()
 
 
-def products(scored, slope, w_out_t, latent_t, hidden_t, cuts):
+def first_products(scored, slope, w_out_t, ordered, picked):
     nrows, width = slope.shape
     channels = w_out_t.shape[0]
-    picked = latent_t.shape[0]
     steps = len(column_steps(width))
     return pl.pallas_call(
-        functools.partial(products_body, tuple(cuts)),
-        in_specs=[ANY] * 5,
-        out_specs=[ANY] * len(cuts),
-        out_shape=[jax.ShapeDtypeStruct((end - start, width + LANES), jnp.float32) for start, end in cuts],
+        first_body,
+        in_specs=[ANY] * 4,
+        out_specs=[ANY] * 3,
+        out_shape=[
+            jax.ShapeDtypeStruct((picked, width + LANES), jnp.float32),
+            jax.ShapeDtypeStruct((nrows, width), jnp.bfloat16),
+            jax.ShapeDtypeStruct((nrows, LANES), jnp.bfloat16),
+        ],
         scratch_shapes=[
             pltpu.VMEM(scored.shape, jnp.float32),
             pltpu.VMEM(slope.shape, jnp.float32),
             pltpu.VMEM(w_out_t.shape, jnp.bfloat16),
-            pltpu.VMEM(latent_t.shape, jnp.bfloat16),
-            pltpu.VMEM(hidden_t.shape, jnp.bfloat16),
+            pltpu.VMEM((picked, nrows), jnp.bfloat16),
+            pltpu.VMEM((picked, nrows), jnp.bfloat16),
             pltpu.VMEM((nrows, LANES), jnp.float32),
+            pltpu.VMEM((nrows, width), jnp.bfloat16),
+            pltpu.VMEM((nrows, LANES), jnp.bfloat16),
             pltpu.VMEM((picked, width + LANES), jnp.float32),
             pltpu.SemaphoreType.DMA((4,)),
             pltpu.SemaphoreType.DMA((steps,)),
-            pltpu.SemaphoreType.DMA((steps + 1, len(cuts))),
-        ],
-        compiler_params=params(MOST),
-        cost_estimate=cost(2 * nrows * width * (channels + picked), 12 * MIB),
-        name="products",
-    )(scored, slope, w_out_t, latent_t, hidden_t)
+            pltpu.SemaphoreType.DMA((steps + 1,)),
+            pltpu.SemaphoreType.DMA((steps + 1,)),
+        ],
+        compiler_params=params(TIGHT),
+        cost_estimate=cost(2 * nrows * width * (channels + picked), 10 * MIB),
+        name="first_products",
+    )(scored, slope, w_out_t, ordered)
+
+
+def more_body(cuts, gp_ref, g_ref, ordered_ref, *refs):
+    out_refs, (gp, g, latent_t, hidden_t, result, in_sems, out_sems) = refs[:len(cuts)], refs[len(cuts):]
+    low, picked = cuts[0][0], result.shape[0]
+    width = gp.shape[1]
+    copies = [
+        pltpu.make_async_copy(source, target, in_sems.at[k])
+        for k, (source, target) in enumerate([
+            (ordered_ref.at[1, pl.ds(low, picked)], hidden_t),
+            (g_ref, g),
+            (ordered_ref.at[0, pl.ds(low, picked)], latent_t),
+            (gp_ref, gp),
+        ])
+    ]
+    for copy in copies:
+        copy.start()
+    for copy in copies[:2]:
+        copy.wait()
+    results = []
+
+    def put(k, c, product):
+        result[:, c] = product
+        for i, (out_ref, (start, end)) in enumerate(zip(out_refs, cuts)):
+            source = result.at[pl.ds(start - low, end - start), c]
+            target = out_ref.at[:, pl.ds(c.start, c.stop - c.start)]
+            results.append(pltpu.make_async_copy(source, target, out_sems.at[k, i]))
+            results[-1].start()
+
+    put(0, slice(width, width + LANES), jnp.dot(hidden_t[...], g[...], preferred_element_type=jnp.float32))
+    for copy in copies[2:]:
+        copy.wait()
+    for k, c in enumerate(column_steps(width)):
+        put(k + 1, c, jnp.dot(latent_t[...], gp[:, c], preferred_element_type=jnp.float32))
+    for copy in results:
+        copy.wait()
+
+
+def more_products(gp, g, ordered, cuts, beside=False):
+    nrows, width = gp.shape
+    picked = cuts[-1][1] - cuts[0][0]
+    return pl.pallas_call(
+        functools.partial(more_body, tuple(cuts)),
+        in_specs=[ANY] * 3,
+        out_specs=[ANY] * len(cuts),
+        out_shape=[jax.ShapeDtypeStruct((end - start, width + LANES), jnp.float32) for start, end in cuts],
+        scratch_shapes=[
+            pltpu.VMEM((nrows, width), jnp.bfloat16),
+            pltpu.VMEM((nrows, LANES), jnp.bfloat16),
+            pltpu.VMEM((picked, nrows), jnp.bfloat16),
+            pltpu.VMEM((picked, nrows), jnp.bfloat16),
+            pltpu.VMEM((picked, width + LANES), jnp.float32),
+            pltpu.SemaphoreType.DMA((4,)),
+            pltpu.SemaphoreType.DMA((len(column_steps(width)) + 1, len(cuts))),
+        ],
+        compiler_params=params(FEW if beside else TIGHT),
+        cost_estimate=cost(0, 0) if beside else cost(2 * nrows * picked * width, 6 * MIB),
+        name="more_products",
+    )(gp, g, ordered)
 
 
 def add_body(plans, count, *refs):
@@ -436,8 +477,9 @@
         part_c([0]), part_a([0]), part_b([0]),
     ]
     sizes = [len(piece) for piece in pieces]
-    half = [row for piece in pieces for row in piece]
-    table = np.array([(core, *row) for core in [*range(1, nc), 0] for row in half], np.int32).T
+    cores = [*range(1, nc), 0]
+    halves = [[row for piece in part for row in piece] for part in (pieces[:3], pieces[3:])]
+    table = np.array([(core, *row) for half in halves for core in cores for row in half], np.int32).T
     return table, sizes, near, far, a_rows, b_rows, rc
 
 
@@ -461,15 +503,17 @@
     z = (f + relative * (me_z // near)) % far * near + (n + relative * (me_z % near)) % near
     tile = (x + me_x) % nx * nc + (core + me_c) % nc
     source = ((z * nt + tile) * ny + (y + me_y) % ny) * height + row
-    slope, hidden_t = slopes(source, rows_in, w_in)
+    slope, hidden = slopes(rows_in, w_in)
     index = lax.dynamic_slice_in_dim(patch_index[0], me_z * share, share, 0)[:, None]
     count = lax.dynamic_slice_in_dim(counts[0], me_z * share, share, 0)[:, None]
-    grouped, slope, hidden_t, index, count = lax.optimization_barrier((grouped, slope, hidden_t, index, count))
+    grouped, slope, hidden, source, index, count = lax.optimization_barrier(
+        (grouped, slope, hidden, source, index, count)
+    )
 
     scored = score(grouped, observed[0], index, count, channels)
     returned = lax.all_to_all(scored, "member", split_axis=0, concat_axis=0, tiled=True)
-    latent_t = ordered_transpose(source, rows_in)
-    returned, latent_t = lax.optimization_barrier((returned, latent_t))
+    ordered = ordered_transposes(source, rows_in, hidden)
+    returned, ordered = lax.optimization_barrier((returned, ordered))
 
     def shift_core(value, j):
         return lax.ppermute(value, "tile", [(t, t // nc * nc + (t % nc + j) % nc) for t in range(nt)])
@@ -493,49 +537,58 @@
 
     na, nb, nc_send, nc_keep, na_keep, nb_keep = sizes
     n_send, n_keep = na + nb + nc_send, nc_keep + na_keep + nb_keep
-    half = n_send + n_keep
-
-    other_send, other_keep, own_send, own_keep = products(
-        returned, slope, w_out_t, latent_t, hidden_t,
-        [(0, n_send), (n_send, half), (half, half + n_send), (half + n_send, 2 * half)],
-    )
+    middle = 2 * n_send
+
+    other_send, gp, g = first_products(returned, slope, w_out_t, ordered, n_send)
     core_send = shift_core(other_send, 1)
-    core_keep = shift_core(other_keep, 1)
-    a_send = own_send[:na] + core_send[:na]
-    b_send = own_send[na:na + nb] + core_send[na:na + nb]
-    c_send = own_send[na + nb:] + core_send[na + nb:]
+    (own_send,) = more_products(gp, g, ordered, [(n_send, middle)])
+    a_send, b_send, c_send = add_rows(
+        [own_send, core_send],
+        [
+            [(0, na, [(0, 0), (1, 0)])],
+            [(0, nb, [(0, na), (1, na)])],
+            [(0, nc_send, [(0, na + nb), (1, na + nb)])],
+        ],
+    )
+    a_send, b_send, c_send, gp = lax.optimization_barrier((a_send, b_send, c_send, gp))
     a_got = send_all(a_send, nx - 1, shift_x)
     b_got = send_all(b_send, ny - 1, shift_y)
     c_got = send_all(c_send, near - 1, shift_near)
-    inputs = [own_keep, core_keep, *a_got, *b_got, *c_got]
-    a_in = range(2, 2 + len(a_got))
-    b_in = range(a_in.stop, a_in.stop + len(b_got))
-    c_in = range(b_in.stop, b_in.stop + len(c_got))
-
-    def summed(base, got, low, rows):
-        return [(0, rows, [(0, base + low), (1, base + low), *[(k, low) for k in got]])]
-
-    a_base, b_base = nc_keep, nc_keep + na_keep
     a_cut, b_cut, c_cut = na_keep // ny * (ny - 1), nb_keep // nx * (nx - 1), nc_keep // far * (far - 1)
-    c_send, a_send, b_send = add_rows(
-        inputs,
-        [
-            summed(0, c_in, 0, c_cut),
-            summed(a_base, a_in, 0, a_cut),
-            summed(b_base, b_in, 0, b_cut),
-        ],
-    )
+    keeps = [c_cut, nc_keep - c_cut, a_cut, na_keep - a_cut, b_cut, nb_keep - b_cut]
+    offsets = [int(low) for low in np.cumsum([0, *keeps])]
+    third = -(-n_keep // 24) * 8
+    parts = [0, min(third, n_keep), min(2 * third, n_keep), n_keep]
+    ends = [middle + low for low in parts]
+    *other_keep, own_keep = more_products(
+        gp, g, ordered, [*zip(ends[:-1], ends[1:]), (ends[-1], ends[-1] + n_keep)], True
+    )
+    core_keep = [shift_core(value, 1) for value in other_keep]
+
+    def summed(k, got, low):
+        plan = []
+        for i, (start, end) in enumerate(zip(parts[:-1], parts[1:])):
+            start, end = max(start, offsets[k]), min(end, offsets[k + 1])
+            if start < end:
+                at = start - offsets[k]
+                terms = [(0, start), (1 + i, start - parts[i])]
+                terms += [(1 + len(core_keep) + n, low + at) for n in range(len(got))]
+                plan.append((at, end - start, terms))
+        return [own_keep, *core_keep, *got], plan
+
+    def sums(*parts):
+        inputs, plans = [], []
+        for sources, plan in parts:
+            plans.append([(at, rows, [(len(inputs) + i, low) for i, low in terms]) for at, rows, terms in plan])
+            inputs.extend(sources)
+        return add_rows(inputs, plans)
+
+    c_send, a_send, b_send = sums(summed(0, c_got, 0), summed(2, a_got, 0), summed(4, b_got, 0))
+    keep_sums = [summed(1, c_got, c_cut), summed(3, a_got, a_cut), summed(5, b_got, b_cut)]
     c_got = send_all(c_send, far - 1, shift_far)
     a_got = send_all(a_send, ny - 1, shift_y)
     b_got = send_all(b_send, nx - 1, shift_x)
-    c_keep, a_keep, b_keep = add_rows(
-        inputs,
-        [
-            summed(0, c_in, c_cut, nc_keep - c_cut),
-            summed(a_base, a_in, a_cut, na_keep - a_cut),
-            summed(b_base, b_in, b_cut, nb_keep - b_cut),
-        ],
-    )
+    c_keep, a_keep, b_keep = sums(*keep_sums)
 
     a_got, b_got, c_got = lax.optimization_barrier((a_got, b_got, c_got))
     inputs = [a_keep, *a_got, b_keep, *b_got]

time: 101 us -> 98.1 us (0.971)
  waiting for transfers between devices: 38.3 us -> 29.7 us
  local copies, waits for them, and re-layouts: 1.05 us -> 4.67 us
  Pallas kernels: 35.7 us -> 38.5 us
  other arithmetic: 3.01 us -> 0.68 us
  starting transfers between devices: 21.5 us -> 23.1 us
    ppermute x1, waiting for transfers between devices: 8.47 us -> 0.01 us  [shift_near(): lax.ppermute(value, 'member', [(t, t // near * near + (t % near + j) % ne...]
    pallas_call x2 -> x4, Pallas kernels: 15.4 us -> 21 us  [the longest x1 8.24 us: ordered_transposes(): pl.pallas_call(order_body, grid=(nrows // block,), in_specs=[pl.BlockSpec...]
    unnamed x24 -> x30, local copies, waits for them, and re-layouts: 0.82 us -> 4.43 us
    all_to_all x1, waiting for transfers between devices: 6.47 us -> 4.14 us  [shards(): lax.all_to_all(scored, 'member', split_axis=0, concat_axis=0, tiled=True)]
    add x2 -> x0, other arithmetic: 2.33 us -> none  [the longest x1 1.33 us: shards(): b_send = own_send[na:na + nb] + core_send[na:na + nb]]
    ppermute x3, waiting for transfers between devices: 2.54 us -> 4.67 us  [shift_y(): return lax.ppermute(value, 'batch', [(t, (t + j) % ny) for t in range(ny)])]
    pallas_call x1, Pallas kernels: 9.56 us -> 7.72 us  [slopes(): pl.pallas_call(slope_body, grid=(nrows // block,), in_specs=[pl.BlockSpec...]
    all_to_all x1, waiting for transfers between devices: 2.71 us -> 4.48 us  [shards(): lax.all_to_all(packed, 'member', split_axis=0, concat_axis=0, tiled=True)]
  transfers between devices with their start and end apart: 13 -> 15, of which waited for: 9 -> 9; matrix products, arithmetic and copies ran while one was open for 3% -> 1% of each run, Pallas kernels for 16% -> 24%
where the time goes in v4:
time: 98.1 us; the launch traced here: 97.6 us
  Pallas kernels  38.5 us (39%)
  waiting for transfers between devices  29.7 us (30%)
  starting transfers between devices  23.1 us (24%)
  local copies, waits for them, and re-layouts  4.67 us (5%)
    pallas_call x1, Pallas kernels, ordered_transposes(): pl.pallas_call(order_body, grid=(nrows // block,), in_specs=[pl.BlockSpec...  8.24 us
    pallas_call x1, Pallas kernels, slopes(): pl.pallas_call(slope_body, grid=(nrows // block,), in_specs=[pl.BlockSpec...  7.72 us
    pallas_call x2, Pallas kernels, more_products(): pl.pallas_call(functools.partial(more_body, tuple(cuts)), in_specs=[ANY]...  7.58 us
    ppermute x1, waiting for transfers between devices, shift_far(): lax.ppermute(value, 'member', [(t, (t // near + j) % far * near + t % nea...  6.92 us
    pallas_call x1, Pallas kernels, decode(): pl.pallas_call(decode_body, in_specs=[ANY] * 3, out_specs=ANY, out_shape=...  6.47 us
    all_to_all x1, starting transfers between devices, shards(): lax.all_to_all(packed, 'member', split_axis=0, concat_axis=0, tiled=True)  6.33 us
    pallas_call x1, Pallas kernels, first_products(): pl.pallas_call(first_body, in_specs=[ANY] * 4, out_specs=[ANY] * 3, out_s...  5.17 us
    ppermute x3, waiting for transfers between devices, shift_y(): return lax.ppermute(value, 'batch', [(t, (t + j) % ny) for t in range(ny)])  4.67 us
  transfers between devices with their start and end apart: 15, of which 9 were waited for; matrix products, arithmetic and copies ran while one was open for 1% of the time, Pallas kernels for 24%

profile of v4, /device:TPU:0, one launch (start us, length us, event | category | flops | bytes accessed | tf_op | source)
XLA Modules:
  0.0 97.6 jit_solution(8294542480662275695)
XLA Ops:
  0.6 6.5 %decode.1 = f32[4,14,16,128]{3,2,1,0:T(8,128)} custom-call(bf16[1024,1024]{1,0:T(8,128)(2,1)} %bitcast.9, bf16[1024,1024]{1,0:T(8,128)(2,1)} %w_in_ref.3, bf16[112,1024]{1,0:T(8,128)(2,1)} %bitcast.12), custom_call_target="tpu_custom_call" | custom-call | flops 2382364672 | bytes 5242880 | tf_op jit(solution)/shard_map/decode/pallas_call | solution.py:111
  7.1 6.3 %all-to-all-start = ((f32[4,14,16,128]{3,2,1,0:T(8,128)}), f32[4,14,16,128]{3,2,1,0:T(8,128)S(1)}, u32[]{:S(2)}, u32[]{:S(2)}) async-start(f32[4,14,16,128]{3,2,1,0:T(8,128)} %decode.1), calls=%async_computation | async-start | bytes 917504 | tf_op jit(solution)/shard_map/all_to_all | solution.py:500
  13.6 7.7 %slopes.1 = (f32[1024,1024]{1,0:T(8,128)}, bf16[1024,1024]{1,0:T(8,128)(2,1)}) custom-call(bf16[1024,1024]{1,0:T(8,128)(2,1)} %bitcast.10, bf16[1024,1024]{1,0:T(8,128)(2,1)} %w_in_ref.3), custom_call_target="tpu_custom_call" | custom-call | flops 2147483648 | bytes 4194304 | tf_op jit(solution)/shard_map/slopes/pallas_call | solution.py:155
  21.4 0.7 fusion.10.source_ref
  22.1 4.5 %all-to-all-done.x_ref = f32[4,14,16,128]{3,2,1,0:T(8,128)S(1)} async-done(((f32[4,14,16,128]{3,2,1,0:T(8,128)}), f32[4,14,16,128]{3,2,1,0:T(8,128)S(1)}, u32[]{:S(2)}, u32[]{:S(2)}) %all-to-all-start) | async-done | bytes 458784 | tf_op jit(solution)/shard_map/all_to_all | solution.py:500
  26.7 1.4 %score.1 = f32[4,14,16,128]{3,2,1,0:T(8,128)} custom-call(f32[4,14,16,128]{3,2,1,0:T(8,128)S(1)} %all-to-all-done.x_ref, bf16[128,1792]{1,0:T(8,128)(2,1)S(1)} %bitcast.8, s32[16,1]{1,0:T(8,128)S(1)} %copy.15.index_ref, s32[16,1]{1,0:T(8,128)S(1)} %copy.16.count_ref), custom_call_target="tpu_custom_call" | custom-call | flops 3440640 | bytes 917504 | tf_op jit(solution)/shard_map/score/pallas_call | solution.py:238
  28.1 3.6 %all-to-all-start.1 = ((f32[4,14,16,128]{3,2,1,0:T(8,128)}), f32[4,14,16,128]{3,2,1,0:T(8,128)S(1)}, u32[]{:S(2)}, u32[]{:S(2)}) async-start(f32[4,14,16,128]{3,2,1,0:T(8,128)} %score.1), calls=%async_computation.1 | async-start | bytes 917504 | tf_op jit(solution)/shard_map/all_to_all | solution.py:514
  31.8 8.2 %ordered_transposes.1.ordered_ref = bf16[2,1024,1024]{2,1,0:T(8,128)(2,1)} custom-call(s32[1,1024]{1,0:T(1,128)} %fusion.10.source_ref, bf16[1024,1024]{1,0:T(8,128)(2,1)} %bitcast.11, bf16[1024,1024]{1,0:T(8,128)(2,1)} %get-tuple-element.45.hidden_ref), custom_call_target="tpu_custom_call" | custom-call | flops 1073741824 | bytes 4194304 | tf_op jit(solution)/shard_map/ordered_transposes/pallas_call | solution.py:184
  40.0 4.1 %all-to-all-done.1.scored_ref = f32[4,14,16,128]{3,2,1,0:T(8,128)S(1)} async-done(((f32[4,14,16,128]{3,2,1,0:T(8,128)}), f32[4,14,16,128]{3,2,1,0:T(8,128)S(1)}, u32[]{:S(2)}, u32[]{:S(2)}) %all-to-all-start.1) | async-done | bytes 458784 | tf_op jit(solution)/shard_map/all_to_all | solution.py:514
  44.2 0.8 copy-done.5
  44.9 5.2 %first_products.1 = (f32[256,1152]{1,0:T(8,128)}, bf16[1024,1024]{1,0:T(8,128)(2,1)}, bf16[1024,128]{1,0:T(8,128)(2,1)}) custom-call(f32[4,14,16,128]{3,2,1,0:T(8,128)} %copy-done.5, f32[1024,1024]{1,0:T(8,128)} %get-tuple-element.47.slope_ref, bf16[112,1024]{1,0:T(8,128)(2,1)} %bitcast.13, bf16[2,1024,1024]{2,1,0:T(8,128)(2,1)} %ordered_transposes.1.ordered_ref), custom_call_target="tpu_custom_call" | custom-call | flops 771751936 | bytes 10485760 | tf_op jit(solution)/shard_map/first_products/pallas_call | solution.py:311
  50.2 3.6 %more_products.2.refs_0_ = f32[256,1152]{1,0:T(8,128)} custom-call(bf16[1024,1024]{1,0:T(8,128)(2,1)} %get-tuple-element.55.gp_ref, bf16[1024,128]{1,0:T(8,128)(2,1)} %get-tuple-element.50.g_ref, bf16[2,1024,1024]{2,1,0:T(8,128)(2,1)} %ordered_transposes.1.ordered_ref), custom_call_target="tpu_custom_call" | custom-call | flops 536870912 | bytes 6291456 | tf_op jit(solution)/shard_map/more_products/pallas_call | solution.py:380
  53.9 1.4 %copy-done.2 = f32[256,1152]{1,0:T(8,128)S(1)} copy-done((f32[256,1152]{1,0:T(8,128)S(1)}, f32[256,1152]{1,0:T(8,128)}, u32[]{:S(2)}) %copy-start.2) | copy-done | bytes 1179672
  55.5 1.6 %collective-permute-start.5 = (f32[96,1152]{1,0:T(8,128)S(1)}, f32[96,1152]{1,0:T(8,128)S(1)}, u32[]{:S(2)}, u32[]{:S(2)}) collective-permute-start(f32[96,1152]{1,0:T(8,128)S(1)} %get-tuple-element.61), channel_id=1, source_target_pairs={{0,4},{2,6},{4,0},{6,2},{1,5},{3,7},{5,1},{7,3},{8,12},{10,14},{12... | collective-permute-start | bytes 1327112 | tf_op jit(solution)/shard_map/ppermute | solution.py:522
  57.1 1.5 %collective-permute-start.6 = (f32[96,1152]{1,0:T(8,128)S(1)}, f32[96,1152]{1,0:T(8,128)S(1)}, u32[]{:S(2)}, u32[]{:S(2)}) collective-permute-start(f32[96,1152]{1,0:T(8,128)S(1)} %get-tuple-element.62), channel_id=1, source_target_pairs={{0,1},{1,0},{2,3},{3,2},{4,5},{5,4},{6,7},{7,6},{8,9},{9,8},{10,11... | collective-permute-start | bytes 1327112 | tf_op jit(solution)/shard_map/ppermute | solution.py:525
  58.6 2.2 %copy-done = bf16[2,1024,1024]{2,1,0:T(8,128)(2,1)S(1)} copy-done((bf16[2,1024,1024]{2,1,0:T(8,128)(2,1)S(1)}, bf16[2,1024,1024]{2,1,0:T(8,128)(2,1)}, u32[]{:S(2)}) %copy-start) | copy-done | bytes 4194328
  60.8 3.9 %more_products.3 = (f32[88,1152]{1,0:T(8,128)S(1)}, f32[88,1152]{1,0:T(8,128)S(1)}, f32[80,1152]{1,0:T(8,128)S(1)}, f32[256,1152]{1,0:T(8,128)S(1)}) custom-call(bf16[1024,1024]{1,0:T(8,128)(2,1)S(1)} %copy-done.1, bf16[1024,128]{1,0:T(8,128)(2,1)S(1)} %copy-done.3, bf16[2,1024,1024]{2,1,0:T(8,128)(2,1)S(1)} %copy-done), custom_call_target="tpu_custom_call" | custom-call | tf_op jit(solution)/shard_map/more_products/pallas_call | solution.py:380
  64.8 0.5 collective-permute-start.2
  65.4 2.3 %collective-permute-done.3.refs_3_.refs_8_.refs_13_ = f32[80,1152]{1,0:T(8,128)S(1)} collective-permute-done((f32[80,1152]{1,0:T(8,128)S(1)}, f32[80,1152]{1,0:T(8,128)S(1)}, u32[]{:S(2)}, u32[]{:S(2)}) %collective-permute-start.3) | collective-permute-done | bytes 368672 | tf_op jit(solution)/shard_map/ppermute | solution.py:519
  68.2 1.2 %collective-permute-done.6.refs_14_ = f32[96,1152]{1,0:T(8,128)S(1)} collective-permute-done((f32[96,1152]{1,0:T(8,128)S(1)}, f32[96,1152]{1,0:T(8,128)S(1)}, u32[]{:S(2)}, u32[]{:S(2)}) %collective-permute-start.6) | collective-permute-done | bytes 442400 | tf_op jit(solution)/shard_map/ppermute | solution.py:525
  69.5 1.6 %collective-permute-start.7 = (f32[48,1152]{1,0:T(8,128)S(1)}, f32[48,1152]{1,0:T(8,128)S(1)}, u32[]{:S(2)}, u32[]{:S(2)}) collective-permute-start(f32[48,1152]{1,0:T(8,128)S(1)} %get-tuple-element.64), channel_id=1, source_target_pairs={{0,1},{1,0},{2,3},{3,2},{4,5},{5,4},{6,7},{7,6},{8,9},{9,8},{10,11... | collective-permute-start | bytes 663560 | tf_op jit(solution)/shard_map/ppermute | solution.py:525
  71.1 0.5 collective-permute-start.8
  71.6 1.7 %collective-permute-start.9 = (f32[32,1152]{1,0:T(8,128)S(1)}, f32[32,1152]{1,0:T(8,128)S(1)}, u32[]{:S(2)}, u32[]{:S(2)}) collective-permute-start(f32[32,1152]{1,0:T(8,128)S(1)} %get-tuple-element.66), channel_id=1, source_target_pairs={{0,16},{8,24},{16,0},{24,8},{1,17},{9,25},{17,1},{25,9},{2,18},{10... | collective-permute-start | bytes 442376 | tf_op jit(solution)/shard_map/ppermute | solution.py:531
  73.4 6.9 %collective-permute-done.9.refs_1_ = f32[32,1152]{1,0:T(8,128)S(1)} collective-permute-done((f32[32,1152]{1,0:T(8,128)S(1)}, f32[32,1152]{1,0:T(8,128)S(1)}, u32[]{:S(2)}, u32[]{:S(2)}) %collective-permute-start.9) | collective-permute-done | bytes 147488 | tf_op jit(solution)/shard_map/ppermute | solution.py:531
  80.3 0.8 add_rows.9
  81.1 3.5 %all-to-all-start.2 = ((f32[4,24,1152]{2,1,0:T(8,128)}), f32[4,24,1152]{2,1,0:T(8,128)S(1)}, u32[]{:S(2)}, u32[]{:S(2)}) async-start(f32[4,24,1152]{2,1,0:T(8,128)} %bitcast.5), calls=%async_computation.2 | async-start | bytes 884736 | tf_op jit(solution)/shard_map/all_to_all | solution.py:602
  84.6 1.5 %collective-permute-start.10 = (f32[16,1152]{1,0:T(8,128)S(1)}, f32[16,1152]{1,0:T(8,128)S(1)}, u32[]{:S(2)}, u32[]{:S(2)}) collective-permute-start(f32[16,1152]{1,0:T(8,128)S(1)} %get-tuple-element.73), channel_id=1, source_target_pairs={{0,4},{2,6},{4,0},{6,2},{1,5},{3,7},{5,1},{7,3},{8,12},{10,14},{12... | collective-permute-start | bytes 221192 | tf_op jit(solution)/shard_map/ppermute | solution.py:522
  86.1 2.9 %collective-permute-done.10.refs_1_ = f32[16,1152]{1,0:T(8,128)S(1)} collective-permute-done((f32[16,1152]{1,0:T(8,128)S(1)}, f32[16,1152]{1,0:T(8,128)S(1)}, u32[]{:S(2)}, u32[]{:S(2)}) %collective-permute-start.10) | collective-permute-done | bytes 73760 | tf_op jit(solution)/shard_map/ppermute | solution.py:522
  89.1 0.6 collective-permute-start.11
  89.6 3.5 %collective-permute-done.11.refs_1_ = f32[8,1152]{1,0:T(8,128)S(1)} collective-permute-done((f32[8,1152]{1,0:T(8,128)S(1)}, f32[8,1152]{1,0:T(8,128)S(1)}, u32[]{:S(2)}, u32[]{:S(2)}) %collective-permute-start.11) | collective-permute-done | bytes 36896 | tf_op jit(solution)/shard_map/ppermute | solution.py:525
  93.1 3.8 %all-to-all-done.2.across_ref = f32[4,24,1152]{2,1,0:T(8,128)S(1)} async-done(((f32[4,24,1152]{2,1,0:T(8,128)}), f32[4,24,1152]{2,1,0:T(8,128)S(1)}, u32[]{:S(2)}, u32[]{:S(2)}) %all-to-all-start.2) | async-done | bytes 442400 | tf_op jit(solution)/shard_map/all_to_all | solution.py:602
  96.9 0.7 finish.1
  (46 shorter events, 1.5 us)
Async XLA Ops:
  0.6 12.8 %copy-start.13 = (s32[1,64]{1,0:T(1,128)S(1)}, s32[1,64]{1,0:T(1,128)}, u32[]{:S(2)}) copy-start(s32[1,64]{1,0:T(1,128)} %param.18) | copy-start | bytes 772
  0.6 12.8 %copy-start.14 = (s32[1,64]{1,0:T(1,128)S(1)}, s32[1,64]{1,0:T(1,128)}, u32[]{:S(2)}) copy-start(s32[1,64]{1,0:T(1,128)} %param.17) | copy-start | bytes 772
  7.1 19.4 %all-to-all-start = ((f32[4,14,16,128]{3,2,1,0:T(8,128)}), f32[4,14,16,128]{3,2,1,0:T(8,128)S(1)}, u32[]{:S(2)}, u32[]{:S(2)}) async-start(f32[4,14,16,128]{3,2,1,0:T(8,128)} %decode.1), calls=%async_computation | async-start | bytes 917504 | tf_op jit(solution)/shard_map/all_to_all | solution.py:500
  13.5 7.8 %copy-start.6 = (s32[1,1024]{1,0:T(1,128)S(1)}, s32[1,1024]{1,0:T(1,128)}, u32[]{:S(2)}) copy-start(s32[1,1024]{1,0:T(1,128)} %constant.106.clone) | copy-start | bytes 12292
  13.5 7.8 %copy-start.7 = (s32[1,1024]{1,0:T(1,128)S(1)}, s32[1,1024]{1,0:T(1,128)}, u32[]{:S(2)}) copy-start(s32[1,1024]{1,0:T(1,128)} %constant.105.clone) | copy-start | bytes 12292
  13.5 7.8 %copy-start.8 = (s32[1,1024]{1,0:T(1,128)S(1)}, s32[1,1024]{1,0:T(1,128)}, u32[]{:S(2)}) copy-start(s32[1,1024]{1,0:T(1,128)} %constant.104.clone) | copy-start | bytes 12292
  13.5 7.8 %copy-start.9 = (s32[1,1024]{1,0:T(1,128)S(1)}, s32[1,1024]{1,0:T(1,128)}, u32[]{:S(2)}) copy-start(s32[1,1024]{1,0:T(1,128)} %constant.103.clone) | copy-start | bytes 12292
  13.5 7.8 %copy-start.10 = (s32[1,1024]{1,0:T(1,128)S(1)}, s32[1,1024]{1,0:T(1,128)}, u32[]{:S(2)}) copy-start(s32[1,1024]{1,0:T(1,128)} %constant.102.clone) | copy-start | bytes 12292
  13.6 7.8 %copy-start.11 = (s32[1,1024]{1,0:T(1,128)S(1)}, s32[1,1024]{1,0:T(1,128)}, u32[]{:S(2)}) copy-start(s32[1,1024]{1,0:T(1,128)} %constant.101.clone) | copy-start | bytes 12292
  13.6 7.8 %copy-start.12 = (s32[1,1024]{1,0:T(1,128)S(1)}, s32[1,1024]{1,0:T(1,128)}, u32[]{:S(2)}) copy-start(s32[1,1024]{1,0:T(1,128)} %constant.100.clone) | copy-start | bytes 12292
  13.6 13.1 %copy-start.4 = (bf16[1,128,1792]{2,1,0:T(8,128)(2,1)S(1)}, bf16[1,128,1792]{2,1,0:T(8,128)(2,1)}, u32[]{:S(2)}) copy-start(bf16[1,128,1792]{2,1,0:T(8,128)(2,1)} %param.16) | copy-start | bytes 1376260
  28.1 16.0 %all-to-all-start.1 = ((f32[4,14,16,128]{3,2,1,0:T(8,128)}), f32[4,14,16,128]{3,2,1,0:T(8,128)S(1)}, u32[]{:S(2)}, u32[]{:S(2)}) async-start(f32[4,14,16,128]{3,2,1,0:T(8,128)} %score.1), calls=%async_computation.1 | async-start | bytes 917504 | tf_op jit(solution)/shard_map/all_to_all | solution.py:514
  44.2 0.8 copy-start.5
  50.1 3.7 %collective-permute-start = (f32[256,1152]{1,0:T(8,128)}, f32[256,1152]{1,0:T(8,128)S(1)}, u32[]{:S(2)}, u32[]{:S(2)}) collective-permute-start(f32[256,1152]{1,0:T(8,128)} %get-tuple-element.51), channel_id=1, source_target_pairs={{0,2},{2,0},{4,6},{6,4},{1,3},{3,1},{5,7},{7,5},{8,10},{10,8},{12,... | collective-permute-start | bytes 3538952 | tf_op jit(solution)/shard_map/ppermute | solution.py:519
  53.8 4.8 %copy-start.1 = (bf16[1024,1024]{1,0:T(8,128)(2,1)S(1)}, bf16[1024,1024]{1,0:T(8,128)(2,1)}, u32[]{:S(2)}) copy-start(bf16[1024,1024]{1,0:T(8,128)(2,1)} %get-tuple-element.55.gp_ref) | copy-start | bytes 6291460
  53.9 1.4 %copy-start.2 = (f32[256,1152]{1,0:T(8,128)S(1)}, f32[256,1152]{1,0:T(8,128)}, u32[]{:S(2)}) copy-start(f32[256,1152]{1,0:T(8,128)} %more_products.2.refs_0_) | copy-start | bytes 3538948
  55.3 3.3 %copy-start.3 = (bf16[1024,128]{1,0:T(8,128)(2,1)S(1)}, bf16[1024,128]{1,0:T(8,128)(2,1)}, u32[]{:S(2)}) copy-start(bf16[1024,128]{1,0:T(8,128)(2,1)} %get-tuple-element.50.g_ref) | copy-start | bytes 786436
  55.4 9.9 %collective-permute-start.4 = (f32[64,1152]{1,0:T(8,128)S(1)}, f32[64,1152]{1,0:T(8,128)S(1)}, u32[]{:S(2)}, u32[]{:S(2)}) collective-permute-start(f32[64,1152]{1,0:T(8,128)S(1)} %get-tuple-element.60), channel_id=1, source_target_pairs={{0,8},{8,0},{16,24},{24,16},{1,9},{9,1},{17,25},{25,17},{2,10},{10... | collective-permute-start | bytes 884744 | tf_op jit(solution)/shard_map/ppermute | solution.py:528
  55.5 12.6 %collective-permute-start.5 = (f32[96,1152]{1,0:T(8,128)S(1)}, f32[96,1152]{1,0:T(8,128)S(1)}, u32[]{:S(2)}, u32[]{:S(2)}) collective-permute-start(f32[96,1152]{1,0:T(8,128)S(1)} %get-tuple-element.61), channel_id=1, source_target_pairs={{0,4},{2,6},{4,0},{6,2},{1,5},{3,7},{5,1},{7,3},{8,12},{10,14},{12... | collective-permute-start | bytes 1327112 | tf_op jit(solution)/shard_map/ppermute | solution.py:522
  57.1 12.3 %collective-permute-start.6 = (f32[96,1152]{1,0:T(8,128)S(1)}, f32[96,1152]{1,0:T(8,128)S(1)}, u32[]{:S(2)}, u32[]{:S(2)}) collective-permute-start(f32[96,1152]{1,0:T(8,128)S(1)} %get-tuple-element.62), channel_id=1, source_target_pairs={{0,1},{1,0},{2,3},{3,2},{4,5},{5,4},{6,7},{7,6},{8,9},{9,8},{10,11... | collective-permute-start | bytes 1327112 | tf_op jit(solution)/shard_map/ppermute | solution.py:525
  58.6 2.2 %copy-start = (bf16[2,1024,1024]{2,1,0:T(8,128)(2,1)S(1)}, bf16[2,1024,1024]{2,1,0:T(8,128)(2,1)}, u32[]{:S(2)}) copy-start(bf16[2,1024,1024]{2,1,0:T(8,128)(2,1)} %ordered_transposes.1.ordered_ref) | copy-start | bytes 12582916
  64.7 2.9 %collective-permute-start.1 = (f32[88,1152]{1,0:T(8,128)S(1)}, f32[88,1152]{1,0:T(8,128)S(1)}, u32[]{:S(2)}, u32[]{:S(2)}) collective-permute-start(f32[88,1152]{1,0:T(8,128)S(1)} %get-tuple-element.57), channel_id=1, source_target_pairs={{0,2},{2,0},{4,6},{6,4},{1,3},{3,1},{5,7},{7,5},{8,10},{10,8},{12,... | collective-permute-start | bytes 1216520 | tf_op jit(solution)/shard_map/ppermute | solution.py:519
  64.8 2.8 %collective-permute-start.2 = (f32[88,1152]{1,0:T(8,128)S(1)}, f32[88,1152]{1,0:T(8,128)S(1)}, u32[]{:S(2)}, u32[]{:S(2)}) collective-permute-start(f32[88,1152]{1,0:T(8,128)S(1)} %get-tuple-element.58), channel_id=1, source_target_pairs={{0,2},{2,0},{4,6},{6,4},{1,3},{3,1},{5,7},{7,5},{8,10},{10,8},{12,... | collective-permute-start | bytes 1216520 | tf_op jit(solution)/shard_map/ppermute | solution.py:519
  65.3 2.3 %collective-permute-start.3 = (f32[80,1152]{1,0:T(8,128)S(1)}, f32[80,1152]{1,0:T(8,128)S(1)}, u32[]{:S(2)}, u32[]{:S(2)}) collective-permute-start(f32[80,1152]{1,0:T(8,128)S(1)} %get-tuple-element.59), channel_id=1, source_target_pairs={{0,2},{2,0},{4,6},{6,4},{1,3},{3,1},{5,7},{7,5},{8,10},{10,8},{12,... | collective-permute-start | bytes 1105928 | tf_op jit(solution)/shard_map/ppermute | solution.py:519
  69.5 10.8 %collective-permute-start.7 = (f32[48,1152]{1,0:T(8,128)S(1)}, f32[48,1152]{1,0:T(8,128)S(1)}, u32[]{:S(2)}, u32[]{:S(2)}) collective-permute-start(f32[48,1152]{1,0:T(8,128)S(1)} %get-tuple-element.64), channel_id=1, source_target_pairs={{0,1},{1,0},{2,3},{3,2},{4,5},{5,4},{6,7},{7,6},{8,9},{9,8},{10,11... | collective-permute-start | bytes 663560 | tf_op jit(solution)/shard_map/ppermute | solution.py:525
  71.1 9.3 %collective-permute-start.8 = (f32[48,1152]{1,0:T(8,128)S(1)}, f32[48,1152]{1,0:T(8,128)S(1)}, u32[]{:S(2)}, u32[]{:S(2)}) collective-permute-start(f32[48,1152]{1,0:T(8,128)S(1)} %get-tuple-element.65), channel_id=1, source_target_pairs={{0,4},{2,6},{4,0},{6,2},{1,5},{3,7},{5,1},{7,3},{8,12},{10,14},{12... | collective-permute-start | bytes 663560 | tf_op jit(solution)/shard_map/ppermute | solution.py:522
  71.6 8.7 %collective-permute-start.9 = (f32[32,1152]{1,0:T(8,128)S(1)}, f32[32,1152]{1,0:T(8,128)S(1)}, u32[]{:S(2)}, u32[]{:S(2)}) collective-permute-start(f32[32,1152]{1,0:T(8,128)S(1)} %get-tuple-element.66), channel_id=1, source_target_pairs={{0,16},{8,24},{16,0},{24,8},{1,17},{9,25},{17,1},{25,9},{2,18},{10... | collective-permute-start | bytes 442376 | tf_op jit(solution)/shard_map/ppermute | solution.py:531
  81.1 15.8 %all-to-all-start.2 = ((f32[4,24,1152]{2,1,0:T(8,128)}), f32[4,24,1152]{2,1,0:T(8,128)S(1)}, u32[]{:S(2)}, u32[]{:S(2)}) async-start(f32[4,24,1152]{2,1,0:T(8,128)} %bitcast.5), calls=%async_computation.2 | async-start | bytes 884736 | tf_op jit(solution)/shard_map/all_to_all | solution.py:602
  84.6 4.4 %collective-permute-start.10 = (f32[16,1152]{1,0:T(8,128)S(1)}, f32[16,1152]{1,0:T(8,128)S(1)}, u32[]{:S(2)}, u32[]{:S(2)}) collective-permute-start(f32[16,1152]{1,0:T(8,128)S(1)} %get-tuple-element.73), channel_id=1, source_target_pairs={{0,4},{2,6},{4,0},{6,2},{1,5},{3,7},{5,1},{7,3},{8,12},{10,14},{12... | collective-permute-start | bytes 221192 | tf_op jit(solution)/shard_map/ppermute | solution.py:522
  89.1 4.0 %collective-permute-start.11 = (f32[8,1152]{1,0:T(8,128)S(1)}, f32[8,1152]{1,0:T(8,128)S(1)}, u32[]{:S(2)}, u32[]{:S(2)}) collective-permute-start(f32[8,1152]{1,0:T(8,128)S(1)} %get-tuple-element.75), channel_id=1, source_target_pairs={{0,1},{1,0},{2,3},{3,2},{4,5},{5,4},{6,7},{7,6},{8,9},{9,8},{10,11... | collective-permute-start | bytes 110600 | tf_op jit(solution)/shard_map/ppermute | solution.py:525

commit v5 on v4

--- a/solution.py
+++ b/solution.py
@@ -16,7 +16,6 @@
 WHOLE = pl.BlockSpec()
 ANY = pl.BlockSpec(memory_space=pl.ANY)
 FEW = 24
-TIGHT = 60.3
 MOST = 56
 
 
@@ -59,6 +58,10 @@
             value = jnp.where((lane >= i * spare) & (lane < (i + 1) * spare), moved, value)
         cells.append(value)
     return cells
+
+
+def in_hbm(value):
+    return pltpu.with_memory_space_constraint(value, pltpu.HBM)
 
 
 def column_steps(width):
@@ -247,17 +250,16 @@
 
 
 def first_body(
-    scored_ref, slope_ref, w_out_t_ref, ordered_ref, out_ref, gp_ref, g_ref,
-    scored, slope, w_out_t, latent_t, hidden_t, cells, gp, g, result, in_sems, slope_sems, gp_sems, out_sems,
+    scored, slope_ref, w_out_t_ref, ordered_ref, result, gp, g,
+    slope, w_out_t, latent_t, hidden_t, cells, in_sems, slope_sems,
 ):
     parts, carriers, share, _ = scored.shape
     channels, width = w_out_t.shape
     picked = result.shape[0]
     column = column_steps(width)
-    scored_copy, w_copy, hidden_copy, latent_copy = copies = [
+    w_copy, hidden_copy, latent_copy = copies = [
         pltpu.make_async_copy(source, target, in_sems.at[k])
         for k, (source, target) in enumerate([
-            (scored_ref, scored),
             (w_out_t_ref, w_out_t),
             (ordered_ref.at[1, pl.ds(0, picked)], hidden_t),
             (ordered_ref.at[0, pl.ds(0, picked)], latent_t),
@@ -270,38 +272,23 @@
     for copy in [*copies, *slope_copies]:
         copy.start()
 
-    scored_copy.wait()
     for q in range(parts):
         rows = [scored[q, j] for j in range(carriers)]
         for j, value in enumerate(unpack(rows, channels)):
             cells[pl.ds(q * share * PATCH + j, share, stride=PATCH), :] = value
     lane = lax.broadcasted_iota(jnp.int32, cells.shape, 1)
     g[...] = jnp.where(lane < channels, cells[...], 0.0).astype(jnp.bfloat16)
-    results = [pltpu.make_async_copy(g, g_ref, gp_sems.at[len(column)])]
-    results[0].start()
-
-    def put(k, c, product):
-        result[:, c] = product
-        target = out_ref.at[:, pl.ds(c.start, c.stop - c.start)]
-        results.append(pltpu.make_async_copy(result.at[:, c], target, out_sems.at[k]))
-        results[-1].start()
-
     w_copy.wait()
     backward = [
         jnp.dot(g[:, :channels], w_out_t[:, c], preferred_element_type=jnp.float32) for c in column
     ]
     hidden_copy.wait()
-    last = slice(width, width + LANES)
-    put(len(column), last, jnp.dot(hidden_t[...], g[...], preferred_element_type=jnp.float32))
+    result[:, width:] = jnp.dot(hidden_t[...], g[...], preferred_element_type=jnp.float32)
     latent_copy.wait()
     for k, c in enumerate(column):
         slope_copies[k].wait()
         gp[:, c] = (backward[k] * slope[:, c]).astype(jnp.bfloat16)
-        results.append(pltpu.make_async_copy(gp.at[:, c], gp_ref.at[:, pl.ds(c.start, c.stop - c.start)], gp_sems.at[k]))
-        results[-1].start()
-        put(k, c, jnp.dot(latent_t[...], gp[:, c], preferred_element_type=jnp.float32))
-    for copy in results:
-        copy.wait()
+        result[:, c] = jnp.dot(latent_t[...], gp[:, c], preferred_element_type=jnp.float32)
 
 
 def first_products(scored, slope, w_out_t, ordered, picked):
@@ -310,91 +297,67 @@
     steps = len(column_steps(width))
     return pl.pallas_call(
         first_body,
-        in_specs=[ANY] * 4,
-        out_specs=[ANY] * 3,
+        in_specs=[WHOLE, ANY, ANY, ANY],
+        out_specs=[WHOLE] * 3,
         out_shape=[
             jax.ShapeDtypeStruct((picked, width + LANES), jnp.float32),
             jax.ShapeDtypeStruct((nrows, width), jnp.bfloat16),
             jax.ShapeDtypeStruct((nrows, LANES), jnp.bfloat16),
         ],
         scratch_shapes=[
-            pltpu.VMEM(scored.shape, jnp.float32),
             pltpu.VMEM(slope.shape, jnp.float32),
             pltpu.VMEM(w_out_t.shape, jnp.bfloat16),
             pltpu.VMEM((picked, nrows), jnp.bfloat16),
             pltpu.VMEM((picked, nrows), jnp.bfloat16),
             pltpu.VMEM((nrows, LANES), jnp.float32),
-            pltpu.VMEM((nrows, width), jnp.bfloat16),
-            pltpu.VMEM((nrows, LANES), jnp.bfloat16),
-            pltpu.VMEM((picked, width + LANES), jnp.float32),
-            pltpu.SemaphoreType.DMA((4,)),
+            pltpu.SemaphoreType.DMA((3,)),
             pltpu.SemaphoreType.DMA((steps,)),
-            pltpu.SemaphoreType.DMA((steps + 1,)),
-            pltpu.SemaphoreType.DMA((steps + 1,)),
-        ],
-        compiler_params=params(TIGHT),
+        ],
+        compiler_params=params(FEW),
         cost_estimate=cost(2 * nrows * width * (channels + picked), 10 * MIB),
         name="first_products",
-    )(scored, slope, w_out_t, ordered)
-
-
-def more_body(cuts, gp_ref, g_ref, ordered_ref, *refs):
-    out_refs, (gp, g, latent_t, hidden_t, result, in_sems, out_sems) = refs[:len(cuts)], refs[len(cuts):]
-    low, picked = cuts[0][0], result.shape[0]
+    )(scored, in_hbm(slope), in_hbm(w_out_t), in_hbm(ordered))
+
+
+def more_body(cuts, gp, g, ordered_ref, *refs):
+    out_refs, (latent_t, hidden_t, in_sems) = refs[:len(cuts)], refs[len(cuts):]
+    low, (picked, _) = cuts[0][0], latent_t.shape
     width = gp.shape[1]
     copies = [
-        pltpu.make_async_copy(source, target, in_sems.at[k])
-        for k, (source, target) in enumerate([
-            (ordered_ref.at[1, pl.ds(low, picked)], hidden_t),
-            (g_ref, g),
-            (ordered_ref.at[0, pl.ds(low, picked)], latent_t),
-            (gp_ref, gp),
-        ])
+        pltpu.make_async_copy(ordered_ref.at[k, pl.ds(low, picked)], target, in_sems.at[k])
+        for k, target in enumerate((latent_t, hidden_t))
     ]
     for copy in copies:
         copy.start()
-    for copy in copies[:2]:
+
+    def put(columns, product):
+        for out_ref, (start, end) in zip(out_refs, cuts):
+            out_ref[:, columns] = product[start - low:end - low]
+
+    for copy in copies:
         copy.wait()
-    results = []
-
-    def put(k, c, product):
-        result[:, c] = product
-        for i, (out_ref, (start, end)) in enumerate(zip(out_refs, cuts)):
-            source = result.at[pl.ds(start - low, end - start), c]
-            target = out_ref.at[:, pl.ds(c.start, c.stop - c.start)]
-            results.append(pltpu.make_async_copy(source, target, out_sems.at[k, i]))
-            results[-1].start()
-
-    put(0, slice(width, width + LANES), jnp.dot(hidden_t[...], g[...], preferred_element_type=jnp.float32))
-    for copy in copies[2:]:
-        copy.wait()
-    for k, c in enumerate(column_steps(width)):
-        put(k + 1, c, jnp.dot(latent_t[...], gp[:, c], preferred_element_type=jnp.float32))
-    for copy in results:
-        copy.wait()
-
-
-def more_products(gp, g, ordered, cuts, beside=False):
+    for columns in column_steps(width):
+        put(columns, jnp.dot(latent_t[...], gp[:, columns], preferred_element_type=jnp.float32))
+    put(slice(width, None), jnp.dot(hidden_t[...], g[...], preferred_element_type=jnp.float32))
+
+
+def more_products(gp, g, ordered, cuts):
     nrows, width = gp.shape
     picked = cuts[-1][1] - cuts[0][0]
     return pl.pallas_call(
         functools.partial(more_body, tuple(cuts)),
-        in_specs=[ANY] * 3,
-        out_specs=[ANY] * len(cuts),
+        in_specs=[WHOLE, WHOLE, ANY],
+        out_specs=[WHOLE] * len(cuts),
         out_shape=[jax.ShapeDtypeStruct((end - start, width + LANES), jnp.float32) for start, end in cuts],
         scratch_shapes=[
-            pltpu.VMEM((nrows, width), jnp.bfloat16),
-            pltpu.VMEM((nrows, LANES), jnp.bfloat16),
             pltpu.VMEM((picked, nrows), jnp.bfloat16),
             pltpu.VMEM((picked, nrows), jnp.bfloat16),
-            pltpu.VMEM((picked, width + LANES), jnp.float32),
-            pltpu.SemaphoreType.DMA((4,)),
-            pltpu.SemaphoreType.DMA((len(column_steps(width)) + 1, len(cuts))),
-        ],
-        compiler_params=params(FEW if beside else TIGHT),
-        cost_estimate=cost(0, 0) if beside else cost(2 * nrows * picked * width, 6 * MIB),
+            pltpu.SemaphoreType.DMA((2,)),
+        ],
+        compiler_params=params(FEW),
+        cost_estimate=cost(2 * nrows * picked * width, 6 * MIB),
         name="more_products",
-    )(gp, g, ordered)
+    )(gp, g, in_hbm(ordered))
 
 
 def add_body(plans, count, *refs):
@@ -457,30 +420,21 @@
     near = 2 if nz % 2 == 0 else 1
     far = nz // near
     rc = max(height // 4, 1)
-    more = -(-(height - rc) * 2 // 3)
-    a_rows = [range(0, more if z % 2 == 0 else height - rc - more) for z in range(nz)]
-    b_rows = [range(a_rows[z].stop, height - rc) for z in range(nz)]
-    c_rows = range(height - rc, height)
-    x_last, y_last, far_last = [[*range(1, n), 0] for n in (nx, ny, far)]
-
-    def part_a(xs):
-        return [(x, y, 0, z // near, z % near, r) for x in xs for y in y_last for z in range(nz) for r in a_rows[z]]
-
-    def part_b(ys):
-        return [(x, y, 0, z // near, z % near, r) for y in ys for x in x_last for z in range(nz) for r in b_rows[z]]
+    main_rows, c_rows = range(height - rc), range(height - rc, height)
+    first_last, second_last, far_last = [[*range(1, n), 0] for n in (nx, ny, far)]
+
+    def main(firsts):
+        return [(f, s, 0, z // near, z % near, r) for f in firsts for s in second_last for z in range(nz) for r in main_rows]
 
     def part_c(nears):
-        return [(x, y, 1, f, n, r) for n in nears for f in far_last for x in x_last for y in y_last for r in c_rows]
-
-    pieces = [
-        part_a(range(1, nx)), part_b(range(1, ny)), part_c(range(1, near)),
-        part_c([0]), part_a([0]), part_b([0]),
-    ]
+        return [(f, s, 1, o, n, r) for n in nears for o in far_last for f in first_last for s in second_last for r in c_rows]
+
+    pieces = [main(range(1, nx)), part_c(range(1, near)), part_c([0]), main([0])]
     sizes = [len(piece) for piece in pieces]
     cores = [*range(1, nc), 0]
-    halves = [[row for piece in part for row in piece] for part in (pieces[:3], pieces[3:])]
+    halves = [[row for piece in part for row in piece] for part in (pieces[:2], pieces[2:])]
     table = np.array([(core, *row) for half in halves for core in cores for row in half], np.int32).T
-    return table, sizes, near, far, a_rows, b_rows, rc
+    return table, sizes, near, far, rc
 
 
 def shards(latent, w_in, w_out, observed, patch_index, counts):
@@ -493,15 +447,19 @@
     me_x, me_c = me_t // nc, me_t % nc
     w_out_t = w_out.T
     height = depth // (nz * nt * ny)
-    table, sizes, near, far, a_rows, b_rows, rc = row_order(nz, nx, nc, ny, height)
+    table, sizes, near, far, rc = row_order(nz, nx, nc, ny, height)
+    turned = 1 if nx == ny else 0
 
     share = nrows // PATCH // nz
     packed = decode(rows_in, w_in, w_out_t, nz)
     grouped = lax.all_to_all(packed, "member", split_axis=0, concat_axis=0, tiled=True)
 
-    core, x, y, relative, f, n, row = (jnp.asarray(table[k:k + 1]) for k in range(7))
+    core, first, second, relative, f, n, row = (jnp.asarray(table[k:k + 1]) for k in range(7))
     z = (f + relative * (me_z // near)) % far * near + (n + relative * (me_z % near)) % near
-    tile = (x + me_x) % nx * nc + (core + me_c) % nc
+    core = (core + me_c) % nc
+    turn = core * turned
+    x, y = first + turn * (second - first), second + turn * (first - second)
+    tile = (x + me_x) % nx * nc + core
     source = ((z * nt + tile) * ny + (y + me_y) % ny) * height + row
     slope, hidden = slopes(rows_in, w_in)
     index = lax.dynamic_slice_in_dim(patch_index[0], me_z * share, share, 0)[:, None]
@@ -515,113 +473,97 @@
     ordered = ordered_transposes(source, rows_in, hidden)
     returned, ordered = lax.optimization_barrier((returned, ordered))
 
+    everywhere = [(z, x, c, y) for z in range(nz) for x in range(nx) for c in range(nc) for y in range(ny)]
+
+    def shift(value, target):
+        def number(z, x, c, y):
+            return (z * nt + x * nc + c) * ny + y
+
+        return lax.ppermute(
+            value, ("member", "tile", "batch"), [(number(*place), number(*target(*place))) for place in everywhere]
+        )
+
     def shift_core(value, j):
-        return lax.ppermute(value, "tile", [(t, t // nc * nc + (t % nc + j) % nc) for t in range(nt)])
-
-    def shift_x(value, j):
-        return lax.ppermute(value, "tile", [(t, (t // nc + j) % nx * nc + t % nc) for t in range(nt)])
-
-    def shift_y(value, j):
-        return lax.ppermute(value, "batch", [(t, (t + j) % ny) for t in range(ny)])
+        return shift(value, lambda z, x, c, y: (z, x, (c + j) % nc, y))
+
+    def along(of_core):
+        def shift_one(value, j):
+            def target(z, x, c, y):
+                return (z, (x + j) % nx, c, y) if of_core(c) == 0 else (z, x, c, (y + j) % ny)
+
+            return shift(value, target)
+
+        return shift_one
+
+    shift_first, shift_second = along(lambda c: c * turned), along(lambda c: 1 - c * turned)
 
     def shift_near(value, j):
-        return lax.ppermute(value, "member", [(t, t // near * near + (t % near + j) % near) for t in range(nz)])
+        return shift(value, lambda z, x, c, y: (z // near * near + (z + j) % near, x, c, y))
 
     def shift_far(value, j):
-        return lax.ppermute(value, "member", [(t, (t // near + j) % far * near + t % near) for t in range(nz)])
-
-    def send_all(value, others, shift):
+        return shift(value, lambda z, x, c, y: ((z // near + j) % far * near + z % near, x, c, y))
+
+    def send_all(value, others, shift_one):
         if others == 1:
-            return [shift(value, 1)]
-        return [shift(v, j + 1) for j, v in enumerate(jnp.split(value, others, axis=0))] if others else []
-
-    na, nb, nc_send, nc_keep, na_keep, nb_keep = sizes
-    n_send, n_keep = na + nb + nc_send, nc_keep + na_keep + nb_keep
+            return [shift_one(value, 1)]
+        return [shift_one(v, j + 1) for j, v in enumerate(jnp.split(value, others, axis=0))] if others else []
+
+    n_main, nc_send, nc_keep, main_keep = sizes
+    n_send, n_keep = n_main + nc_send, nc_keep + main_keep
     middle = 2 * n_send
 
     other_send, gp, g = first_products(returned, slope, w_out_t, ordered, n_send)
     core_send = shift_core(other_send, 1)
-    (own_send,) = more_products(gp, g, ordered, [(n_send, middle)])
-    a_send, b_send, c_send = add_rows(
+    own_send, other_keep = more_products(gp, g, ordered, [(n_send, middle), (middle, middle + n_keep)])
+    core_keep = shift_core(other_keep, 1)
+    main_send, c_send = add_rows(
         [own_send, core_send],
-        [
-            [(0, na, [(0, 0), (1, 0)])],
-            [(0, nb, [(0, na), (1, na)])],
-            [(0, nc_send, [(0, na + nb), (1, na + nb)])],
-        ],
+        [[(0, n_main, [(0, 0), (1, 0)])], [(0, nc_send, [(0, n_main), (1, n_main)])]],
     )
-    a_send, b_send, c_send, gp = lax.optimization_barrier((a_send, b_send, c_send, gp))
-    a_got = send_all(a_send, nx - 1, shift_x)
-    b_got = send_all(b_send, ny - 1, shift_y)
+    main_send, c_send, gp = lax.optimization_barrier((main_send, c_send, gp))
+    main_got = send_all(main_send, nx - 1, shift_first)
     c_got = send_all(c_send, near - 1, shift_near)
-    a_cut, b_cut, c_cut = na_keep // ny * (ny - 1), nb_keep // nx * (nx - 1), nc_keep // far * (far - 1)
-    keeps = [c_cut, nc_keep - c_cut, a_cut, na_keep - a_cut, b_cut, nb_keep - b_cut]
+    c_cut, main_cut = nc_keep // far * (far - 1), main_keep // ny * (ny - 1)
+    keeps = [c_cut, nc_keep - c_cut, main_cut, main_keep - main_cut]
     offsets = [int(low) for low in np.cumsum([0, *keeps])]
-    third = -(-n_keep // 24) * 8
-    parts = [0, min(third, n_keep), min(2 * third, n_keep), n_keep]
-    ends = [middle + low for low in parts]
-    *other_keep, own_keep = more_products(
-        gp, g, ordered, [*zip(ends[:-1], ends[1:]), (ends[-1], ends[-1] + n_keep)], True
-    )
-    core_keep = [shift_core(value, 1) for value in other_keep]
+    (own_keep,) = more_products(gp, g, ordered, [(middle + n_keep, middle + 2 * n_keep)])
 
     def summed(k, got, low):
-        plan = []
-        for i, (start, end) in enumerate(zip(parts[:-1], parts[1:])):
-            start, end = max(start, offsets[k]), min(end, offsets[k + 1])
-            if start < end:
-                at = start - offsets[k]
-                terms = [(0, start), (1 + i, start - parts[i])]
-                terms += [(1 + len(core_keep) + n, low + at) for n in range(len(got))]
-                plan.append((at, end - start, terms))
-        return [own_keep, *core_keep, *got], plan
-
-    def sums(*parts):
+        terms = [(0, offsets[k]), (1, offsets[k]), *[(2 + i, low) for i in range(len(got))]]
+        return [own_keep, core_keep, *got], [(0, keeps[k], terms)]
+
+    def sums(*wanted):
         inputs, plans = [], []
-        for sources, plan in parts:
+        for sources, plan in wanted:
             plans.append([(at, rows, [(len(inputs) + i, low) for i, low in terms]) for at, rows, terms in plan])
             inputs.extend(sources)
         return add_rows(inputs, plans)
 
-    c_send, a_send, b_send = sums(summed(0, c_got, 0), summed(2, a_got, 0), summed(4, b_got, 0))
-    keep_sums = [summed(1, c_got, c_cut), summed(3, a_got, a_cut), summed(5, b_got, b_cut)]
+    c_send, main_send = sums(summed(0, c_got, 0), summed(2, main_got, 0))
+    kept = [summed(1, c_got, c_cut), summed(3, main_got, main_cut)]
     c_got = send_all(c_send, far - 1, shift_far)
-    a_got = send_all(a_send, ny - 1, shift_y)
-    b_got = send_all(b_send, nx - 1, shift_x)
-    c_keep, a_keep, b_keep = sums(*keep_sums)
-
-    a_got, b_got, c_got = lax.optimization_barrier((a_got, b_got, c_got))
-    inputs = [a_keep, *a_got, b_keep, *b_got]
-    plan, a_low, b_low, at = [], 0, 0, 0
-    for k in range(nz):
-        plan.append((at, len(a_rows[k]), [(i, a_low) for i in range(1 + len(a_got))]))
-        a_low, at = a_low + len(a_rows[k]), at + len(a_rows[k])
-        plan.append((at, len(b_rows[k]), [(1 + len(a_got) + i, b_low) for i in range(1 + len(b_got))]))
-        b_low, at = b_low + len(b_rows[k]), at + len(b_rows[k])
-    (joined,) = add_rows(inputs, [plan])
+    main_got = send_all(main_send, ny - 1, shift_second)
+    c_keep, main_keep = sums(*kept)
+
+    def split_sums(keep, got, n):
+        rows = keep.shape[0]
+        cut = rows // n * (n - 1)
+        sources = range(1 + len(got))
+        return add_rows(
+            [keep, *got],
+            [[(0, cut, [(i, 0) for i in sources])], [(0, rows - cut, [(i, cut) for i in sources])]],
+        )
+
+    main_got, c_got = lax.optimization_barrier((main_got, c_got))
+    rows = main_keep.shape[0]
+    (joined,) = add_rows([main_keep, *main_got], [[(0, rows, [(i, 0) for i in range(1 + len(main_got))])]])
     across = lax.all_to_all(
         joined.reshape(nz, height - rc, joined.shape[1]), "member", split_axis=0, concat_axis=0, tiled=True
     )
-    c_rows = c_keep.shape[0]
-    cut = c_rows // nx * (nx - 1)
-    (c_send, c_keep) = add_rows(
-        [c_keep, *c_got],
-        [
-            [(0, cut, [(i, 0) for i in range(1 + len(c_got))])],
-            [(0, c_rows - cut, [(i, cut) for i in range(1 + len(c_got))])],
-        ],
-    )
-    c_got = send_all(c_send, nx - 1, shift_x)
-    c_rows = c_keep.shape[0]
-    cut = c_rows // ny * (ny - 1)
-    (c_send, c_keep) = add_rows(
-        [c_keep, *c_got],
-        [
-            [(0, cut, [(i, 0) for i in range(1 + len(c_got))])],
-            [(0, c_rows - cut, [(i, cut) for i in range(1 + len(c_got))])],
-        ],
-    )
-    c_got = send_all(c_send, ny - 1, shift_y)
+    c_send, c_keep = split_sums(c_keep, c_got, nx)
+    c_got = send_all(c_send, nx - 1, shift_first)
+    c_send, c_keep = split_sums(c_keep, c_got, ny)
+    c_got = send_all(c_send, ny - 1, shift_second)
     return tuple(finish(across, [c_keep, *c_got], width, channels))
 
 

time: 98.1 us -> 93 us (0.948)
  waiting for transfers between devices: 29.7 us -> 36.1 us
  local copies, waits for them, and re-layouts: 4.67 us -> 0.3 us
  starting transfers between devices: 23.1 us -> 19.5 us
  Pallas kernels: 38.5 us -> 35.1 us
    ppermute x12 -> x8, waiting for transfers between devices: 17.3 us -> 23 us  [shift(): lax.ppermute(value, ('member', 'tile', 'batch'), [(number(*place), number...]
    unnamed x30 -> x24, local copies, waits for them, and re-layouts: 4.43 us -> 0.06 us
    ppermute x12 -> x8, starting transfers between devices: 9.71 us -> 6.05 us  [shift(): lax.ppermute(value, ('member', 'tile', 'batch'), [(number(*place), number...]
    pallas_call x3, Pallas kernels: 12.7 us -> 9.44 us  [the longest x2 5.15 us: more_products(): pl.pallas_call(functools.partial(more_body, tuple(cuts)), in_specs=[WHOLE...]
  transfers between devices with their start and end apart: 15 -> 11, of which waited for: 9 -> 8; matrix products, arithmetic and copies ran while one was open for 1% -> 1% of each run, Pallas kernels for 24% -> 23%
where the time goes in v5:
time: 93 us; the launch traced here: 92.5 us
  waiting for transfers between devices  36.1 us (39%)
  Pallas kernels  35.1 us (38%)
  starting transfers between devices  19.5 us (21%)
    ppermute x8, waiting for transfers between devices, shift(): lax.ppermute(value, ('member', 'tile', 'batch'), [(number(*place), number...  23 us
    pallas_call x1, Pallas kernels, ordered_transposes(): pl.pallas_call(order_body, grid=(nrows // block,), in_specs=[pl.BlockSpec...  8.33 us
    pallas_call x1, Pallas kernels, slopes(): pl.pallas_call(slope_body, grid=(nrows // block,), in_specs=[pl.BlockSpec...  7.59 us
    pallas_call x1, Pallas kernels, decode(): pl.pallas_call(decode_body, in_specs=[ANY] * 3, out_specs=ANY, out_shape=...  6.47 us
    all_to_all x1, starting transfers between devices, shards(): lax.all_to_all(packed, 'member', split_axis=0, concat_axis=0, tiled=True)  6.33 us
    ppermute x8, starting transfers between devices, shift(): lax.ppermute(value, ('member', 'tile', 'batch'), [(number(*place), number...  6.05 us
    pallas_call x2, Pallas kernels, more_products(): pl.pallas_call(functools.partial(more_body, tuple(cuts)), in_specs=[WHOLE...  5.15 us
    all_to_all x1, waiting for transfers between devices, shards(): lax.all_to_all(packed, 'member', split_axis=0, concat_axis=0, tiled=True)  4.56 us
  transfers between devices with their start and end apart: 11, of which 8 were waited for; matrix products, arithmetic and copies ran while one was open for 1% of the time, Pallas kernels for 23%

profile of v5, /device:TPU:0, one launch (start us, length us, event | category | flops | bytes accessed | tf_op | source)
XLA Modules:
  0.0 92.5 jit_solution(9438596721263722274)
XLA Ops:
  0.6 6.5 %decode.1 = f32[4,14,16,128]{3,2,1,0:T(8,128)} custom-call(bf16[1024,1024]{1,0:T(8,128)(2,1)} %bitcast.9, bf16[1024,1024]{1,0:T(8,128)(2,1)} %w_in_ref.3, bf16[112,1024]{1,0:T(8,128)(2,1)} %bitcast.12), custom_call_target="tpu_custom_call" | custom-call | flops 2382364672 | bytes 5242880 | tf_op jit(solution)/shard_map/decode/pallas_call | solution.py:114
  7.1 6.3 %all-to-all-start = ((f32[4,14,16,128]{3,2,1,0:T(8,128)}), f32[4,14,16,128]{3,2,1,0:T(8,128)S(1)}, u32[]{:S(2)}, u32[]{:S(2)}) async-start(f32[4,14,16,128]{3,2,1,0:T(8,128)} %decode.1), calls=%async_computation | async-start | bytes 917504 | tf_op jit(solution)/shard_map/all_to_all | solution.py:455
  13.5 0.1 dynamic-slice_bitcast_fusion
  13.6 7.6 %slopes.1 = (f32[1024,1024]{1,0:T(8,128)}, bf16[1024,1024]{1,0:T(8,128)(2,1)}) custom-call(bf16[1024,1024]{1,0:T(8,128)(2,1)} %bitcast.10, bf16[1024,1024]{1,0:T(8,128)(2,1)} %w_in_ref.3), custom_call_target="tpu_custom_call" | custom-call | flops 2147483648 | bytes 4194304 | tf_op jit(solution)/shard_map/slopes/pallas_call | solution.py:158
  21.3 0.7 multiply_add_fusion.source_ref
  22.0 4.6 %all-to-all-done.x_ref = f32[4,14,16,128]{3,2,1,0:T(8,128)S(1)} async-done(((f32[4,14,16,128]{3,2,1,0:T(8,128)}), f32[4,14,16,128]{3,2,1,0:T(8,128)S(1)}, u32[]{:S(2)}, u32[]{:S(2)}) %all-to-all-start) | async-done | bytes 458784 | tf_op jit(solution)/shard_map/all_to_all | solution.py:455
  26.5 0.1 copy.15.index_ref
  26.6 0.1 copy.16.count_ref
  26.7 1.4 %score.1 = f32[4,14,16,128]{3,2,1,0:T(8,128)} custom-call(f32[4,14,16,128]{3,2,1,0:T(8,128)S(1)} %all-to-all-done.x_ref, bf16[128,1792]{1,0:T(8,128)(2,1)S(1)} %bitcast.8, s32[16,1]{1,0:T(8,128)S(1)} %copy.15.index_ref, s32[16,1]{1,0:T(8,128)S(1)} %copy.16.count_ref), custom_call_target="tpu_custom_call" | custom-call | flops 3440640 | bytes 917504 | tf_op jit(solution)/shard_map/score/pallas_call | solution.py:241
  28.1 3.5 %all-to-all-start.1 = ((f32[4,14,16,128]{3,2,1,0:T(8,128)}), f32[4,14,16,128]{3,2,1,0:T(8,128)S(1)}, u32[]{:S(2)}, u32[]{:S(2)}) async-start(f32[4,14,16,128]{3,2,1,0:T(8,128)} %score.1), calls=%async_computation.1 | async-start | bytes 917504 | tf_op jit(solution)/shard_map/all_to_all | solution.py:472
  31.6 8.3 %ordered_transposes.1.ordered_ref = bf16[2,1024,1024]{2,1,0:T(8,128)(2,1)} custom-call(s32[1,1024]{1,0:T(1,128)} %multiply_add_fusion.source_ref, bf16[1024,1024]{1,0:T(8,128)(2,1)} %bitcast.11, bf16[1024,1024]{1,0:T(8,128)(2,1)} %get-tuple-element.38.hidden_ref), custom_call_target="tpu_custom_call" | custom-call | flops 1073741824 | bytes 4194304 | tf_op jit(solution)/shard_map/ordered_transposes/pallas_call | solution.py:187
  39.9 4.2 %all-to-all-done.1.scored = f32[4,14,16,128]{3,2,1,0:T(8,128)S(1)} async-done(((f32[4,14,16,128]{3,2,1,0:T(8,128)}), f32[4,14,16,128]{3,2,1,0:T(8,128)S(1)}, u32[]{:S(2)}, u32[]{:S(2)}) %all-to-all-start.1) | async-done | bytes 458784 | tf_op jit(solution)/shard_map/all_to_all | solution.py:472
  44.2 4.3 %first_products.1 = (f32[256,1152]{1,0:T(8,128)S(1)}, bf16[1024,1024]{1,0:T(8,128)(2,1)S(1)}, bf16[1024,128]{1,0:T(8,128)(2,1)S(1)}) custom-call(f32[4,14,16,128]{3,2,1,0:T(8,128)S(1)} %all-to-all-done.1.scored, f32[1024,1024]{1,0:T(8,128)} %get-tuple-element.40.slope_ref, bf16[112,1024]{1,0:T(8,128)(2,1)} %bitcast.13, ...), custom_call_target="tpu_custom_call" | custom-call | flops 771751936 | bytes 10485760 | tf_op jit(solution)/shard_map/first_products/pallas_call | solution.py:298
  48.5 3.1 %more_products.2 = (f32[256,1152]{1,0:T(8,128)S(1)}, f32[256,1152]{1,0:T(8,128)S(1)}) custom-call(bf16[1024,1024]{1,0:T(8,128)(2,1)S(1)} %get-tuple-element.48.gp, bf16[1024,128]{1,0:T(8,128)(2,1)S(1)} %get-tuple-element.43.g, bf16[2,1024,1024]{2,1,0:T(8,128)(2,1)} %ordered_transposes.1.ordered_ref), custom_call_target="tpu_custom_call" | custom-call | flops 1073741824 | bytes 6291456 | tf_op jit(solution)/shard_map/more_products/pallas_call | solution.py:347
  51.6 0.6 collective-permute-start.1
  52.2 0.1 add_rows.6
  52.3 1.6 %collective-permute-start.3 = (f32[192,1152]{1,0:T(8,128)S(1)}, f32[192,1152]{1,0:T(8,128)S(1)}, u32[]{:S(2)}, u32[]{:S(2)}) collective-permute-start(f32[192,1152]{1,0:T(8,128)S(1)} %get-tuple-element.51), channel_id=1, source_target_pairs={{0,4},{1,5},{2,3},{3,2},{4,0},{5,1},{6,7},{7,6},{8,12},{9,13},{10,... | collective-permute-start | bytes 2654216 | tf_op jit(solution)/shard_map/ppermute | solution.py:482
  53.9 2.1 %more_products.3.refs_0_.refs_3_ = f32[256,1152]{1,0:T(8,128)S(1)} custom-call(bf16[1024,1024]{1,0:T(8,128)(2,1)S(1)} %get-tuple-element.48.gp, bf16[1024,128]{1,0:T(8,128)(2,1)S(1)} %get-tuple-element.43.g, bf16[2,1024,1024]{2,1,0:T(8,128)(2,1)} %ordered_transposes.1.ordered_ref), custom_call_target="tpu_custom_call" | custom-call | flops 536870912 | bytes 6291456 | tf_op jit(solution)/shard_map/more_products/pallas_call | solution.py:347
  56.0 6.6 %collective-permute-done.2.refs_2_ = f32[64,1152]{1,0:T(8,128)S(1)} collective-permute-done((f32[64,1152]{1,0:T(8,128)S(1)}, f32[64,1152]{1,0:T(8,128)S(1)}, u32[]{:S(2)}, u32[]{:S(2)}) %collective-permute-start.2) | collective-permute-done | bytes 294944 | tf_op jit(solution)/shard_map/ppermute | solution.py:482
  62.6 2.9 %collective-permute-done.3.refs_5_ = f32[192,1152]{1,0:T(8,128)S(1)} collective-permute-done((f32[192,1152]{1,0:T(8,128)S(1)}, f32[192,1152]{1,0:T(8,128)S(1)}, u32[]{:S(2)}, u32[]{:S(2)}) %collective-permute-start.3) | collective-permute-done | bytes 884768 | tf_op jit(solution)/shard_map/ppermute | solution.py:482
  65.4 0.1 add_rows.8
  65.5 1.6 %collective-permute-start.4 = (f32[96,1152]{1,0:T(8,128)S(1)}, f32[96,1152]{1,0:T(8,128)S(1)}, u32[]{:S(2)}, u32[]{:S(2)}) collective-permute-start(f32[96,1152]{1,0:T(8,128)S(1)} %get-tuple-element.53), channel_id=1, source_target_pairs={{0,1},{1,0},{2,6},{3,7},{4,5},{5,4},{6,2},{7,3},{8,9},{9,8},{10,14... | collective-permute-start | bytes 1327112 | tf_op jit(solution)/shard_map/ppermute | solution.py:482
  67.1 0.1 add_rows.7
  67.2 7.4 %collective-permute-done.5.refs_1_ = f32[32,1152]{1,0:T(8,128)S(1)} collective-permute-done((f32[32,1152]{1,0:T(8,128)S(1)}, f32[32,1152]{1,0:T(8,128)S(1)}, u32[]{:S(2)}, u32[]{:S(2)}) %collective-permute-start.5) | collective-permute-done | bytes 147488 | tf_op jit(solution)/shard_map/ppermute | solution.py:482
  74.6 0.8 add_rows.9
  75.4 3.6 %all-to-all-start.2 = ((f32[4,24,1152]{2,1,0:T(8,128)}), f32[4,24,1152]{2,1,0:T(8,128)S(1)}, u32[]{:S(2)}, u32[]{:S(2)}) async-start(f32[4,24,1152]{2,1,0:T(8,128)} %bitcast.5), calls=%async_computation.2 | async-start | bytes 884736 | tf_op jit(solution)/shard_map/all_to_all | solution.py:560
  79.1 0.7 collective-permute-start.6
  79.8 3.7 %collective-permute-done.6.refs_1_ = f32[16,1152]{1,0:T(8,128)S(1)} collective-permute-done((f32[16,1152]{1,0:T(8,128)S(1)}, f32[16,1152]{1,0:T(8,128)S(1)}, u32[]{:S(2)}, u32[]{:S(2)}) %collective-permute-start.6) | collective-permute-done | bytes 73760 | tf_op jit(solution)/shard_map/ppermute | solution.py:482
  83.5 1.6 %collective-permute-start.7 = (f32[8,1152]{1,0:T(8,128)S(1)}, f32[8,1152]{1,0:T(8,128)S(1)}, u32[]{:S(2)}, u32[]{:S(2)}) collective-permute-start(f32[8,1152]{1,0:T(8,128)S(1)} %get-tuple-element.61), channel_id=1, source_target_pairs={{0,1},{1,0},{2,6},{3,7},{4,5},{5,4},{6,2},{7,3},{8,9},{9,8},{10,14... | collective-permute-start | bytes 110600 | tf_op jit(solution)/shard_map/ppermute | solution.py:482
  85.1 2.4 %collective-permute-done.7.refs_1_ = f32[8,1152]{1,0:T(8,128)S(1)} collective-permute-done((f32[8,1152]{1,0:T(8,128)S(1)}, f32[8,1152]{1,0:T(8,128)S(1)}, u32[]{:S(2)}, u32[]{:S(2)}) %collective-permute-start.7) | collective-permute-done | bytes 36896 | tf_op jit(solution)/shard_map/ppermute | solution.py:482
  87.5 4.3 %all-to-all-done.2.across_ref = f32[4,24,1152]{2,1,0:T(8,128)S(1)} async-done(((f32[4,24,1152]{2,1,0:T(8,128)}), f32[4,24,1152]{2,1,0:T(8,128)S(1)}, u32[]{:S(2)}, u32[]{:S(2)}) %all-to-all-start.2) | async-done | bytes 442400 | tf_op jit(solution)/shard_map/all_to_all | solution.py:560
  91.8 0.7 finish.1
  (32 shorter events, 0.2 us)
Async XLA Ops:
  0.6 12.8 %copy-start.10 = (s32[1,64]{1,0:T(1,128)S(1)}, s32[1,64]{1,0:T(1,128)}, u32[]{:S(2)}) copy-start(s32[1,64]{1,0:T(1,128)} %param.18) | copy-start | bytes 772
  0.6 12.8 %copy-start.11 = (s32[1,64]{1,0:T(1,128)S(1)}, s32[1,64]{1,0:T(1,128)}, u32[]{:S(2)}) copy-start(s32[1,64]{1,0:T(1,128)} %param.17) | copy-start | bytes 772
  7.1 19.4 %all-to-all-start = ((f32[4,14,16,128]{3,2,1,0:T(8,128)}), f32[4,14,16,128]{3,2,1,0:T(8,128)S(1)}, u32[]{:S(2)}, u32[]{:S(2)}) async-start(f32[4,14,16,128]{3,2,1,0:T(8,128)} %decode.1), calls=%async_computation | async-start | bytes 917504 | tf_op jit(solution)/shard_map/all_to_all | solution.py:455
  13.5 7.7 %copy-start.1 = (s32[1,1024]{1,0:T(1,128)S(1)}, s32[1,1024]{1,0:T(1,128)}, u32[]{:S(2)}) copy-start(s32[1,1024]{1,0:T(1,128)} %constant.112) | copy-start | bytes 12292
  13.5 7.7 %copy-start.2 = (s32[1,1024]{1,0:T(1,128)S(1)}, s32[1,1024]{1,0:T(1,128)}, u32[]{:S(2)}) copy-start(s32[1,1024]{1,0:T(1,128)} %constant.111) | copy-start | bytes 12292
  13.5 7.7 %copy-start.3 = (s32[1,1024]{1,0:T(1,128)S(1)}, s32[1,1024]{1,0:T(1,128)}, u32[]{:S(2)}) copy-start(s32[1,1024]{1,0:T(1,128)} %constant.106.clone) | copy-start | bytes 12292
  13.5 7.7 %copy-start.4 = (s32[1,1024]{1,0:T(1,128)S(1)}, s32[1,1024]{1,0:T(1,128)}, u32[]{:S(2)}) copy-start(s32[1,1024]{1,0:T(1,128)} %constant.105.clone) | copy-start | bytes 12292
  13.5 7.7 %copy-start.5 = (s32[1,1024]{1,0:T(1,128)S(1)}, s32[1,1024]{1,0:T(1,128)}, u32[]{:S(2)}) copy-start(s32[1,1024]{1,0:T(1,128)} %constant.104.clone) | copy-start | bytes 12292
  13.6 7.7 %copy-start.6 = (s32[1,1024]{1,0:T(1,128)S(1)}, s32[1,1024]{1,0:T(1,128)}, u32[]{:S(2)}) copy-start(s32[1,1024]{1,0:T(1,128)} %constant.103.clone) | copy-start | bytes 12292
  13.6 7.7 %copy-start.7 = (s32[1,1024]{1,0:T(1,128)S(1)}, s32[1,1024]{1,0:T(1,128)}, u32[]{:S(2)}) copy-start(s32[1,1024]{1,0:T(1,128)} %constant.102.clone) | copy-start | bytes 12292
  13.6 7.7 %copy-start.8 = (s32[1,1024]{1,0:T(1,128)S(1)}, s32[1,1024]{1,0:T(1,128)}, u32[]{:S(2)}) copy-start(s32[1,1024]{1,0:T(1,128)} %constant.101.clone) | copy-start | bytes 12292
  13.6 7.7 %copy-start.9 = (s32[1,1024]{1,0:T(1,128)S(1)}, s32[1,1024]{1,0:T(1,128)}, u32[]{:S(2)}) copy-start(s32[1,1024]{1,0:T(1,128)} %constant.100.clone) | copy-start | bytes 12292
  13.6 13.1 %copy-start = (bf16[1,128,1792]{2,1,0:T(8,128)(2,1)S(1)}, bf16[1,128,1792]{2,1,0:T(8,128)(2,1)}, u32[]{:S(2)}) copy-start(bf16[1,128,1792]{2,1,0:T(8,128)(2,1)} %param.16) | copy-start | bytes 1376260
  28.1 16.0 %all-to-all-start.1 = ((f32[4,14,16,128]{3,2,1,0:T(8,128)}), f32[4,14,16,128]{3,2,1,0:T(8,128)S(1)}, u32[]{:S(2)}, u32[]{:S(2)}) async-start(f32[4,14,16,128]{3,2,1,0:T(8,128)} %score.1), calls=%async_computation.1 | async-start | bytes 917504 | tf_op jit(solution)/shard_map/all_to_all | solution.py:472
  48.5 3.7 %collective-permute-start = (f32[256,1152]{1,0:T(8,128)S(1)}, f32[256,1152]{1,0:T(8,128)S(1)}, u32[]{:S(2)}, u32[]{:S(2)}) collective-permute-start(f32[256,1152]{1,0:T(8,128)S(1)} %get-tuple-element.45), channel_id=1, source_target_pairs={{0,2},{1,3},{2,0},{3,1},{4,6},{5,7},{6,4},{7,5},{8,10},{9,11},{10,... | collective-permute-start | bytes 3538952 | tf_op jit(solution)/shard_map/ppermute | solution.py:482
  51.6 4.3 %collective-permute-start.1 = (f32[256,1152]{1,0:T(8,128)S(1)}, f32[256,1152]{1,0:T(8,128)S(1)}, u32[]{:S(2)}, u32[]{:S(2)}) collective-permute-start(f32[256,1152]{1,0:T(8,128)S(1)} %get-tuple-element.49), channel_id=1, source_target_pairs={{0,2},{1,3},{2,0},{3,1},{4,6},{5,7},{6,4},{7,5},{8,10},{9,11},{10,... | collective-permute-start | bytes 3538952 | tf_op jit(solution)/shard_map/ppermute | solution.py:482
  52.3 13.1 %collective-permute-start.3 = (f32[192,1152]{1,0:T(8,128)S(1)}, f32[192,1152]{1,0:T(8,128)S(1)}, u32[]{:S(2)}, u32[]{:S(2)}) collective-permute-start(f32[192,1152]{1,0:T(8,128)S(1)} %get-tuple-element.51), channel_id=1, source_target_pairs={{0,4},{1,5},{2,3},{3,2},{4,0},{5,1},{6,7},{7,6},{8,12},{9,13},{10,... | collective-permute-start | bytes 2654216 | tf_op jit(solution)/shard_map/ppermute | solution.py:482
  53.9 8.7 %collective-permute-start.2 = (f32[64,1152]{1,0:T(8,128)S(1)}, f32[64,1152]{1,0:T(8,128)S(1)}, u32[]{:S(2)}, u32[]{:S(2)}) collective-permute-start(f32[64,1152]{1,0:T(8,128)S(1)} %get-tuple-element.50), channel_id=1, source_target_pairs={{0,8},{1,9},{2,10},{3,11},{4,12},{5,13},{6,14},{7,15},{8,0},{9,1},... | collective-permute-start | bytes 884744 | tf_op jit(solution)/shard_map/ppermute | solution.py:482
  65.5 9.1 %collective-permute-start.4 = (f32[96,1152]{1,0:T(8,128)S(1)}, f32[96,1152]{1,0:T(8,128)S(1)}, u32[]{:S(2)}, u32[]{:S(2)}) collective-permute-start(f32[96,1152]{1,0:T(8,128)S(1)} %get-tuple-element.53), channel_id=1, source_target_pairs={{0,1},{1,0},{2,6},{3,7},{4,5},{5,4},{6,2},{7,3},{8,9},{9,8},{10,14... | collective-permute-start | bytes 1327112 | tf_op jit(solution)/shard_map/ppermute | solution.py:482
  67.1 7.5 %collective-permute-start.5 = (f32[32,1152]{1,0:T(8,128)S(1)}, f32[32,1152]{1,0:T(8,128)S(1)}, u32[]{:S(2)}, u32[]{:S(2)}) collective-permute-start(f32[32,1152]{1,0:T(8,128)S(1)} %get-tuple-element.54), channel_id=1, source_target_pairs={{0,16},{1,17},{2,18},{3,19},{4,20},{5,21},{6,22},{7,23},{8,24},{9,... | collective-permute-start | bytes 442376 | tf_op jit(solution)/shard_map/ppermute | solution.py:482
  75.4 16.4 %all-to-all-start.2 = ((f32[4,24,1152]{2,1,0:T(8,128)}), f32[4,24,1152]{2,1,0:T(8,128)S(1)}, u32[]{:S(2)}, u32[]{:S(2)}) async-start(f32[4,24,1152]{2,1,0:T(8,128)} %bitcast.5), calls=%async_computation.2 | async-start | bytes 884736 | tf_op jit(solution)/shard_map/all_to_all | solution.py:560
  79.1 4.4 %collective-permute-start.6 = (f32[16,1152]{1,0:T(8,128)S(1)}, f32[16,1152]{1,0:T(8,128)S(1)}, u32[]{:S(2)}, u32[]{:S(2)}) collective-permute-start(f32[16,1152]{1,0:T(8,128)S(1)} %get-tuple-element.59), channel_id=1, source_target_pairs={{0,4},{1,5},{2,3},{3,2},{4,0},{5,1},{6,7},{7,6},{8,12},{9,13},{10,... | collective-permute-start | bytes 221192 | tf_op jit(solution)/shard_map/ppermute | solution.py:482
  83.5 4.0 %collective-permute-start.7 = (f32[8,1152]{1,0:T(8,128)S(1)}, f32[8,1152]{1,0:T(8,128)S(1)}, u32[]{:S(2)}, u32[]{:S(2)}) collective-permute-start(f32[8,1152]{1,0:T(8,128)S(1)} %get-tuple-element.61), channel_id=1, source_target_pairs={{0,1},{1,0},{2,6},{3,7},{4,5},{5,4},{6,2},{7,3},{8,9},{9,8},{10,14... | collective-permute-start | bytes 110600 | tf_op jit(solution)/shard_map/ppermute | solution.py:482

commit v6 on v5

--- a/solution.py
+++ b/solution.py
@@ -17,6 +17,10 @@
 ANY = pl.BlockSpec(memory_space=pl.ANY)
 FEW = 24
 MOST = 56
+
+
+def partner(z, k, nz):
+    return z ^ k if nz & (nz - 1) == 0 else (z + k) % nz
 
 
 def params(mib=24):
@@ -69,62 +73,53 @@
     return [slice(low, low + step) for low in range(0, width, step)]
 
 
-def decode_body(latent_ref, w_in_ref, w_out_t_ref, packed_ref, rows, w_in, w_out_t, cells, packed, row_sems, w_sems, sems):
-    parts, block, _ = rows.shape
-    channels, width = w_out_t.shape
-    share = packed.shape[2]
-    column = column_steps(width)
-    row_copies = [
-        pltpu.make_async_copy(latent_ref.at[pl.ds(q * block, block)], rows.at[q], row_sems.at[q]) for q in range(parts)
-    ]
-    w_copies = [
-        pltpu.make_async_copy(w_in_ref.at[:, pl.ds(c.start, c.stop - c.start)], w_in.at[:, c], w_sems.at[k])
-        for k, c in enumerate(column)
-    ]
-    last_copy = pltpu.make_async_copy(w_out_t_ref, w_out_t, sems.at[parts])
-    for copy in [*w_copies, *row_copies[:parts // 2], last_copy, *row_copies[parts // 2:]]:
+def decode_body(pieces, latent_ref, w_in_ref, w_out_t_ref, *refs):
+    out_refs, (rows, w_in, w_out_t, cells, row_sems, sems) = refs[:len(pieces)], refs[len(pieces):]
+    count, block, _ = rows.shape
+    channels = w_out_t.shape[0]
+    share = out_refs[0].shape[1]
+    half = max(count // 2, 1)
+    me_z, nz = lax.axis_index("member"), lax.axis_size("member")
+    row_copies = []
+    for i, k in enumerate(pieces):
+        start = pl.multiple_of(partner(me_z, k, nz) * block, block)
+        row_copies.append(pltpu.make_async_copy(latent_ref.at[pl.ds(start, block)], rows.at[i], row_sems.at[i]))
+    w_copies = [pltpu.make_async_copy(w_in_ref, w_in, sems.at[0]), pltpu.make_async_copy(w_out_t_ref, w_out_t, sems.at[1])]
+    for copy in [*w_copies, *row_copies]:
         copy.start()
-
-    results = []
-    for copy in [*w_copies, *row_copies[:parts // 2], last_copy]:
+    for copy in [*w_copies, *row_copies[:half]]:
         copy.wait()
-    for q in range(parts):
-        if q == parts // 2:
-            for copy in row_copies[q:]:
+    for i in range(count):
+        if i == half:
+            for copy in row_copies[half:]:
                 copy.wait()
-        preact = jnp.dot(rows[q], w_in[...], preferred_element_type=jnp.float32)
+        preact = jnp.dot(rows[i], w_in[...], preferred_element_type=jnp.float32)
         hidden = (preact / (1.0 + jnp.exp(-preact))).astype(jnp.bfloat16)
-        cells[q, :, :channels] = lax.dot_general(hidden, w_out_t[...], NT, preferred_element_type=jnp.float32)
-        for j, row in enumerate(pack(lambda j: cells[q, pl.ds(j, share, stride=PATCH), :], channels)):
-            packed[q, j] = row
-        results.append(pltpu.make_async_copy(packed.at[q], packed_ref.at[q], sems.at[q]))
-        results[-1].start()
-    for copy in results:
-        copy.wait()
-
-
-def decode(rows_in, w_in, w_out_t, parts):
+        cells[i, :, :channels] = lax.dot_general(hidden, w_out_t[...], NT, preferred_element_type=jnp.float32)
+        for j, row in enumerate(pack(lambda j: cells[i, pl.ds(j, share, stride=PATCH), :], channels)):
+            out_refs[i][j] = row
+
+
+def decode(rows_in, w_in, w_out_t, parts, pieces):
     nrows, depth = rows_in.shape
     width = w_in.shape[1]
     channels = w_out_t.shape[0]
     block = nrows // parts
     share = block // PATCH
     carriers = packing(channels)[1]
-    out = (parts, carriers, share, LANES)
-    return pl.pallas_call(
-        decode_body,
+    count = len(pieces)
+    return pl.pallas_call(
+        functools.partial(decode_body, tuple(pieces)),
         in_specs=[ANY] * 3,
-        out_specs=ANY,
-        out_shape=jax.ShapeDtypeStruct(out, jnp.float32),
+        out_specs=[WHOLE] * count,
+        out_shape=[jax.ShapeDtypeStruct((carriers, share, LANES), jnp.float32)] * count,
         scratch_shapes=[
-            pltpu.VMEM((parts, block, depth), jnp.bfloat16),
+            pltpu.VMEM((count, block, depth), jnp.bfloat16),
             pltpu.VMEM((depth, width), jnp.bfloat16),
             pltpu.VMEM((channels, width), jnp.bfloat16),
-            pltpu.VMEM((parts, block, LANES), jnp.float32),
-            pltpu.VMEM(out, jnp.float32),
-            pltpu.SemaphoreType.DMA((parts,)),
-            pltpu.SemaphoreType.DMA((len(column_steps(width)),)),
-            pltpu.SemaphoreType.DMA((parts + 1,)),
+            pltpu.VMEM((count, block, LANES), jnp.float32),
+            pltpu.SemaphoreType.DMA((count,)),
+            pltpu.SemaphoreType.DMA((2,)),
         ],
         compiler_params=params(MOST),
         cost_estimate=cost(2 * nrows * width * (depth + channels), 5 * MIB),
@@ -201,14 +196,13 @@
     )(source, latent, hidden)
 
 
-def score_body(channels, x_ref, pool_ref, index_ref, count_ref, out_ref):
-    members, carriers, share, _ = x_ref.shape
+def target_body(channels, pool_ref, index_ref, target_ref):
+    carriers, share, _ = target_ref.shape
     npool, total = pool_ref.shape
     choose = index_ref[...] == lax.broadcasted_iota(jnp.int32, (share, npool), 1)
     flat = jnp.dot(
         jnp.where(choose, 1.0, 0.0).astype(jnp.bfloat16), pool_ref[...], preferred_element_type=jnp.float32
     )
-    weight = count_ref[...].astype(jnp.float32)
 
     def cell(j):
         start = j * channels
@@ -216,14 +210,36 @@
         part = flat[:, low:min(low + 2 * LANES, total)]
         return pltpu.roll(part, (low - start) % part.shape[1], 1)[:, :LANES]
 
-    target = pack(cell, channels)
+    for j, row in enumerate(pack(cell, channels)):
+        target_ref[j] = row
+
+
+def targets(pool, index, channels):
+    share = index.shape[0]
+    carriers = packing(channels)[1]
+    return pl.pallas_call(
+        functools.partial(target_body, channels),
+        in_specs=[WHOLE] * 2,
+        out_specs=WHOLE,
+        out_shape=jax.ShapeDtypeStruct((carriers, share, LANES), jnp.float32),
+        compiler_params=params(),
+        cost_estimate=cost(2 * share * pool.size, 2 * pool.size),
+        name="targets",
+    )(pool, index)
+
+
+def score_body(members, *refs):
+    x_refs, (target_ref, count_ref), out_refs = refs[:members], refs[members:members + 2], refs[members + 2:]
+    carriers = target_ref.shape[0]
+    weight = count_ref[...].astype(jnp.float32)
 
     def inverse_norm(delta):
         squares = sum(d * d for d in delta)
         return 1.0 / jnp.sqrt(jnp.sum(squares, axis=-1, keepdims=True) + 1.0)
 
-    xs = [[x_ref[m, j] for j in range(carriers)] for m in range(members)]
-    pair = [[jnp.zeros_like(xs[0][0])] * carriers for _ in range(members)]
+    target = [target_ref[j] for j in range(carriers)]
+    xs = [[ref[j] for j in range(carriers)] for ref in x_refs]
+    pair = [[jnp.zeros_like(target[0])] * carriers for _ in range(members)]
     for m in range(members):
         for k in range(m + 1, members):
             delta = [p - q for p, q in zip(xs[m], xs[k])]
@@ -234,26 +250,27 @@
         delta = [p - q for p, q in zip(xs[m], target)]
         inverse = inverse_norm(delta)
         for j in range(carriers):
-            out_ref[m, j] = weight * (delta[j] * inverse / members - pair[m][j] / (members * members))
-
-
-def score(grouped, pool, index, count, channels):
-    return pl.pallas_call(
-        functools.partial(score_body, channels),
-        in_specs=[WHOLE] * 4,
-        out_specs=WHOLE,
-        out_shape=jax.ShapeDtypeStruct(grouped.shape, jnp.float32),
+            out_refs[m][j] = weight * (delta[j] * inverse / members - pair[m][j] / (members * members))
+
+
+def score(pieces, target, count):
+    members = len(pieces)
+    size = members * target.size
+    return pl.pallas_call(
+        functools.partial(score_body, members),
+        in_specs=[WHOLE] * (members + 2),
+        out_specs=[WHOLE] * members,
+        out_shape=[jax.ShapeDtypeStruct(target.shape, jnp.float32)] * members,
         compiler_params=params(),
-        cost_estimate=cost(30 * grouped.size, 8 * grouped.size),
+        cost_estimate=cost(30 * size, 8 * size),
         name="score",
-    )(grouped, pool, index, count)
-
-
-def first_body(
-    scored, slope_ref, w_out_t_ref, ordered_ref, result, gp, g,
-    slope, w_out_t, latent_t, hidden_t, cells, in_sems, slope_sems,
-):
-    parts, carriers, share, _ = scored.shape
+    )(*pieces, target, count)
+
+
+def first_body(parts, *refs):
+    scored_refs, refs = refs[:parts], refs[parts:]
+    slope_ref, w_out_t_ref, ordered_ref, result, gp, g, slope, w_out_t, latent_t, hidden_t, cells, in_sems, slope_sems = refs
+    carriers, share, _ = scored_refs[0].shape
     channels, width = w_out_t.shape
     picked = result.shape[0]
     column = column_steps(width)
@@ -272,10 +289,11 @@
     for copy in [*copies, *slope_copies]:
         copy.start()
 
-    for q in range(parts):
-        rows = [scored[q, j] for j in range(carriers)]
-        for j, value in enumerate(unpack(rows, channels)):
-            cells[pl.ds(q * share * PATCH + j, share, stride=PATCH), :] = value
+    me_z = lax.axis_index("member")
+    for k, scored_ref in enumerate(scored_refs):
+        base = partner(me_z, k, parts) * (share * PATCH)
+        for j, value in enumerate(unpack([scored_ref[j] for j in range(carriers)], channels)):
+            cells[pl.ds(base + j, share, stride=PATCH), :] = value
     lane = lax.broadcasted_iota(jnp.int32, cells.shape, 1)
     g[...] = jnp.where(lane < channels, cells[...], 0.0).astype(jnp.bfloat16)
     w_copy.wait()
@@ -296,8 +314,8 @@
     channels = w_out_t.shape[0]
     steps = len(column_steps(width))
     return pl.pallas_call(
-        first_body,
-        in_specs=[WHOLE, ANY, ANY, ANY],
+        functools.partial(first_body, len(scored)),
+        in_specs=[*[WHOLE] * len(scored), ANY, ANY, ANY],
         out_specs=[WHOLE] * 3,
         out_shape=[
             jax.ShapeDtypeStruct((picked, width + LANES), jnp.float32),
@@ -316,7 +334,7 @@
         compiler_params=params(FEW),
         cost_estimate=cost(2 * nrows * width * (channels + picked), 10 * MIB),
         name="first_products",
-    )(scored, in_hbm(slope), in_hbm(w_out_t), in_hbm(ordered))
+    )(*scored, in_hbm(slope), in_hbm(w_out_t), in_hbm(ordered))
 
 
 def more_body(cuts, gp, g, ordered_ref, *refs):
@@ -385,35 +403,32 @@
     )(*inputs)
 
 
-def finish_body(across_ref, *refs):
-    *rest_refs, first_ref, second_ref = refs
-    width = first_ref.shape[1]
-    rows = across_ref.shape[1]
-    total = across_ref[0]
-    for z in range(1, across_ref.shape[0]):
-        total = total + across_ref[z]
-    last = rest_refs[0][...]
-    for ref in rest_refs[1:]:
-        last = last + ref[...]
-    for low, high, value in ((0, rows, total), (rows, first_ref.shape[0], last)):
-        first_ref[low:high] = value[:, :width]
-        second_ref[low:high] = value[:, width:width + second_ref.shape[1]]
-
-
-def finish(across, rest, width, channels):
-    height = across.shape[1] + rest[0].shape[0]
-    return pl.pallas_call(
-        finish_body,
-        in_specs=[WHOLE] * (1 + len(rest)),
+def finish_body(count, *refs):
+    main_refs, rest_refs, (first_ref, second_ref) = refs[:count], refs[count:-2], refs[-2:]
+    width, channels = first_ref.shape[1], second_ref.shape[1]
+    rows = main_refs[0].shape[0]
+    for low, high, refs in ((0, rows, main_refs), (rows, first_ref.shape[0], rest_refs)):
+        total = refs[0][...]
+        for ref in refs[1:]:
+            total = total + ref[...]
+        first_ref[low:high] = total[:, :width]
+        second_ref[low:high] = total[:, width:width + channels]
+
+
+def finish(main, rest, width, channels):
+    height = main[0].shape[0] + rest[0].shape[0]
+    return pl.pallas_call(
+        functools.partial(finish_body, len(main)),
+        in_specs=[WHOLE] * (len(main) + len(rest)),
         out_specs=[WHOLE] * 2,
         out_shape=[
             jax.ShapeDtypeStruct((height, width), jnp.float32),
             jax.ShapeDtypeStruct((height, channels), jnp.float32),
         ],
         compiler_params=params(),
-        cost_estimate=cost(across.size, 4 * across.size),
+        cost_estimate=cost(4 * height * width, 20 * height * width),
         name="finish",
-    )(across, *rest)
+    )(*main, *rest)
 
 
 def row_order(nz, nx, nc, ny, height):
@@ -424,7 +439,7 @@
     first_last, second_last, far_last = [[*range(1, n), 0] for n in (nx, ny, far)]
 
     def main(firsts):
-        return [(f, s, 0, z // near, z % near, r) for f in firsts for s in second_last for z in range(nz) for r in main_rows]
+        return [(f, s, 0, 0, k, r) for f in firsts for s in second_last for k in reversed(range(nz)) for r in main_rows]
 
     def part_c(nears):
         return [(f, s, 1, o, n, r) for n in nears for o in far_last for f in first_last for s in second_last for r in c_rows]
@@ -450,12 +465,29 @@
     table, sizes, near, far, rc = row_order(nz, nx, nc, ny, height)
     turned = 1 if nx == ny else 0
 
+    everywhere = [(z, x, c, y) for z in range(nz) for x in range(nx) for c in range(nc) for y in range(ny)]
+
+    def shift(value, target):
+        def number(z, x, c, y):
+            return (z * nt + x * nc + c) * ny + y
+
+        return lax.ppermute(
+            value, ("member", "tile", "batch"), [(number(*place), number(*target(*place))) for place in everywhere]
+        )
+
+    def exchange(values):
+        got = {k: shift(values[k], lambda z, x, c, y: (partner(z, k, nz), x, c, y)) for k in reversed(range(1, nz))}
+        return [values[0], *[got[k] for k in range(1, nz)]]
+
     share = nrows // PATCH // nz
-    packed = decode(rows_in, w_in, w_out_t, nz)
-    grouped = lax.all_to_all(packed, "member", split_axis=0, concat_axis=0, tiled=True)
+    far_first = [*reversed(range(nz))]
+    packed = dict(zip(far_first, decode(rows_in, w_in, w_out_t, nz, far_first)))
+    grouped = exchange(packed)
 
     core, first, second, relative, f, n, row = (jnp.asarray(table[k:k + 1]) for k in range(7))
-    z = (f + relative * (me_z // near)) % far * near + (n + relative * (me_z % near)) % near
+    z_main = partner(me_z, n, nz)
+    z_far = (f + me_z // near) % far * near + (n + me_z % near) % near
+    z = z_main + relative * (z_far - z_main)
     core = (core + me_c) % nc
     turn = core * turned
     x, y = first + turn * (second - first), second + turn * (first - second)
@@ -464,24 +496,15 @@
     slope, hidden = slopes(rows_in, w_in)
     index = lax.dynamic_slice_in_dim(patch_index[0], me_z * share, share, 0)[:, None]
     count = lax.dynamic_slice_in_dim(counts[0], me_z * share, share, 0)[:, None]
-    grouped, slope, hidden, source, index, count = lax.optimization_barrier(
-        (grouped, slope, hidden, source, index, count)
+    target = targets(observed[0], index, channels)
+    grouped, slope, hidden, source, target, count = lax.optimization_barrier(
+        (grouped, slope, hidden, source, target, count)
     )
 
-    scored = score(grouped, observed[0], index, count, channels)
-    returned = lax.all_to_all(scored, "member", split_axis=0, concat_axis=0, tiled=True)
+    scored = score(grouped, target, count)
+    returned = exchange(scored)
     ordered = ordered_transposes(source, rows_in, hidden)
     returned, ordered = lax.optimization_barrier((returned, ordered))
-
-    everywhere = [(z, x, c, y) for z in range(nz) for x in range(nx) for c in range(nc) for y in range(ny)]
-
-    def shift(value, target):
-        def number(z, x, c, y):
-            return (z * nt + x * nc + c) * ny + y
-
-        return lax.ppermute(
-            value, ("member", "tile", "batch"), [(number(*place), number(*target(*place))) for place in everywhere]
-        )
 
     def shift_core(value, j):
         return shift(value, lambda z, x, c, y: (z, x, (c + j) % nc, y))
@@ -555,16 +578,17 @@
         )
 
     main_got, c_got = lax.optimization_barrier((main_got, c_got))
-    rows = main_keep.shape[0]
-    (joined,) = add_rows([main_keep, *main_got], [[(0, rows, [(i, 0) for i in range(1 + len(main_got))])]])
-    across = lax.all_to_all(
-        joined.reshape(nz, height - rc, joined.shape[1]), "member", split_axis=0, concat_axis=0, tiled=True
+    rows = main_keep.shape[0] // nz
+    sources = range(1 + len(main_got))
+    joined = add_rows(
+        [main_keep, *main_got], [[(0, rows, [(i, k * rows) for i in sources])] for k in range(nz)]
     )
+    main = exchange(joined[::-1])
     c_send, c_keep = split_sums(c_keep, c_got, nx)
     c_got = send_all(c_send, nx - 1, shift_first)
     c_send, c_keep = split_sums(c_keep, c_got, ny)
     c_got = send_all(c_send, ny - 1, shift_second)
-    return tuple(finish(across, [c_keep, *c_got], width, channels))
+    return tuple(finish(main, [c_keep, *c_got], width, channels))
 
 
 def solution(mesh):

time: 93 us -> 81.1 us (0.87)
  waiting for transfers between devices: 36.1 us -> 20.9 us
  starting transfers between devices: 19.5 us -> 24.5 us
  Pallas kernels: 35.1 us -> 33.4 us
    ppermute x8 -> x17, starting transfers between devices: 6.05 us -> 24.5 us  [shift(): lax.ppermute(value, ('member', 'tile', 'batch'), [(number(*place), number...]
    all_to_all x3 -> x0, starting transfers between devices: 13.4 us -> none  [the longest x1 6.33 us: shards(): lax.all_to_all(packed, 'member', split_axis=0, concat_axis=0, tiled=True)]
    all_to_all x3 -> x0, waiting for transfers between devices: 13.1 us -> none  [the longest x1 4.56 us: shards(): lax.all_to_all(packed, 'member', split_axis=0, concat_axis=0, tiled=True)]
    ppermute x8 -> x17, waiting for transfers between devices: 23 us -> 20.9 us  [shift(): lax.ppermute(value, ('member', 'tile', 'batch'), [(number(*place), number...]
    pallas_call x4 -> x5, Pallas kernels: 12.9 us -> 12 us  [the longest x1 6.23 us: decode(): pl.pallas_call(functools.partial(decode_body, tuple(pieces)), in_specs=[A...]
  transfers between devices with their start and end apart: 11 -> 17, of which waited for: 8 -> 6; matrix products, arithmetic and copies ran while one was open for 1% -> 1% of each run, Pallas kernels for 23% -> 27%
where the time goes in v6:
time: 81.1 us; the launch traced here: 80.8 us
  Pallas kernels  33.4 us (41%)
  starting transfers between devices  24.5 us (30%)
  waiting for transfers between devices  20.9 us (26%)
  between operations  0.9 us (1%)
    ppermute x17, starting transfers between devices, shift(): lax.ppermute(value, ('member', 'tile', 'batch'), [(number(*place), number...  24.5 us
    ppermute x17, waiting for transfers between devices, shift(): lax.ppermute(value, ('member', 'tile', 'batch'), [(number(*place), number...  20.9 us
    pallas_call x1, Pallas kernels, ordered_transposes(): pl.pallas_call(order_body, grid=(nrows // block,), in_specs=[pl.BlockSpec...  8.33 us
    pallas_call x1, Pallas kernels, slopes(): pl.pallas_call(slope_body, grid=(nrows // block,), in_specs=[pl.BlockSpec...  7.59 us
    pallas_call x1, Pallas kernels, decode(): pl.pallas_call(functools.partial(decode_body, tuple(pieces)), in_specs=[A...  6.23 us
    pallas_call x2, Pallas kernels, more_products(): pl.pallas_call(functools.partial(more_body, tuple(cuts)), in_specs=[WHOLE...  5.15 us
    pallas_call x1, Pallas kernels, first_products(): pl.pallas_call(functools.partial(first_body, len(scored)), in_specs=[*[WH...  4.3 us
  transfers between devices with their start and end apart: 17, of which 6 were waited for; matrix products, arithmetic and copies ran while one was open for 1% of the time, Pallas kernels for 27%

profile of v6, /device:TPU:0, one launch (start us, length us, event | category | flops | bytes accessed | tf_op | source)
XLA Modules:
  0.0 80.8 jit_solution(5431056312553299022)
XLA Ops:
  0.6 6.2 %decode.1 = (f32[14,16,128]{2,1,0:T(8,128)}, f32[14,16,128]{2,1,0:T(8,128)}, f32[14,16,128]{2,1,0:T(8,128)}, f32[14,16,128]{2,1,0:T(8,128)}) custom-call(bf16[1024,1024]{1,0:T(8,128)(2,1)} %bitcast.8, bf16[1024,1024]{1,0:T(8,128)(2,1)} %w_in_ref.3, bf16[112,1024]{1,0:T(8,128)(2,1)} %bitcast.11), custom_call_target="tpu_custom_call" | custom-call | flops 2382364672 | bytes 5242880 | tf_op jit(solution)/shard_map/decode/pallas_call | solution.py:111
  6.9 3.1 %collective-permute-start = (f32[14,16,128]{2,1,0:T(8,128)}, f32[14,16,128]{2,1,0:T(8,128)S(1)}, u32[]{:S(2)}, u32[]{:S(2)}) collective-permute-start(f32[14,16,128]{2,1,0:T(8,128)} %get-tuple-element.51), channel_id=1, source_target_pairs={{0,8},{1,9},{2,10},{3,11},{4,12},{5,13},{6,14},{7,15},{8,0},{9,1},... | collective-permute-start | bytes 344072 | tf_op jit(solution)/shard_map/ppermute | solution.py:474
  10.0 2.6 %collective-permute-start.1 = (f32[14,16,128]{2,1,0:T(8,128)}, f32[14,16,128]{2,1,0:T(8,128)S(1)}, u32[]{:S(2)}, u32[]{:S(2)}) collective-permute-start(f32[14,16,128]{2,1,0:T(8,128)} %get-tuple-element.52), channel_id=1, source_target_pairs={{0,16},{1,17},{2,18},{3,19},{4,20},{5,21},{6,22},{7,23},{8,24},{9,... | collective-permute-start | bytes 344072 | tf_op jit(solution)/shard_map/ppermute | solution.py:474
  12.7 7.6 %slopes.1 = (f32[1024,1024]{1,0:T(8,128)}, bf16[1024,1024]{1,0:T(8,128)(2,1)}) custom-call(bf16[1024,1024]{1,0:T(8,128)(2,1)} %bitcast.9, bf16[1024,1024]{1,0:T(8,128)(2,1)} %w_in_ref.3), custom_call_target="tpu_custom_call" | custom-call | flops 2147483648 | bytes 4194304 | tf_op jit(solution)/shard_map/slopes/pallas_call | solution.py:153
  20.4 0.7 multiply_add_fusion.source_ref
  21.2 0.4 targets.1.refs_4_
  21.7 0.2 collective-permute-done.1.refs_2_
  22.0 0.4 score.1
  22.3 1.9 %collective-permute-start.3 = (f32[14,16,128]{2,1,0:T(8,128)S(1)}, f32[14,16,128]{2,1,0:T(8,128)S(1)}, u32[]{:S(2)}, u32[]{:S(2)}) collective-permute-start(f32[14,16,128]{2,1,0:T(8,128)S(1)} %get-tuple-element.63), channel_id=1, source_target_pairs={{0,8},{1,9},{2,10},{3,11},{4,12},{5,13},{6,14},{7,15},{8,0},{9,1},... | collective-permute-start | bytes 344072 | tf_op jit(solution)/shard_map/ppermute | solution.py:474
  24.2 2.4 %collective-permute-start.4 = (f32[14,16,128]{2,1,0:T(8,128)S(1)}, f32[14,16,128]{2,1,0:T(8,128)S(1)}, u32[]{:S(2)}, u32[]{:S(2)}) collective-permute-start(f32[14,16,128]{2,1,0:T(8,128)S(1)} %get-tuple-element.64), channel_id=1, source_target_pairs={{0,16},{1,17},{2,18},{3,19},{4,20},{5,21},{6,22},{7,23},{8,24},{9,... | collective-permute-start | bytes 344072 | tf_op jit(solution)/shard_map/ppermute | solution.py:474
  26.6 0.2 collective-permute-start.5
  26.8 8.3 %ordered_transposes.1.refs_6_.ordered_ref = bf16[2,1024,1024]{2,1,0:T(8,128)(2,1)} custom-call(s32[1,1024]{1,0:T(1,128)} %multiply_add_fusion.source_ref, bf16[1024,1024]{1,0:T(8,128)(2,1)} %bitcast.10, bf16[1024,1024]{1,0:T(8,128)(2,1)} %get-tuple-element.67.hidden_ref), custom_call_target="tpu_custom_call" | custom-call | flops 1073741824 | bytes 4194304 | tf_op jit(solution)/shard_map/ordered_transposes/pallas_call | solution.py:182
  35.1 4.3 %first_products.1 = (f32[256,1152]{1,0:T(8,128)S(1)}, bf16[1024,1024]{1,0:T(8,128)(2,1)S(1)}, bf16[1024,128]{1,0:T(8,128)(2,1)S(1)}) custom-call(f32[14,16,128]{2,1,0:T(8,128)S(1)} %get-tuple-element.68.refs_0_, f32[14,16,128]{2,1,0:T(8,128)S(1)} %collective-permute-done.3.refs_1_, f32[14,16,128]{2,1,0:T(8,128)S(1)} %collective-permute-done.4.refs_2_, ...), custom_call_target="tpu_custom_call" | custom-call | flops 771751936 | bytes 10485760 | tf_op jit(solution)/shard_map/first_products/pallas_call | solution.py:316
  39.5 3.1 %more_products.2 = (f32[256,1152]{1,0:T(8,128)S(1)}, f32[256,1152]{1,0:T(8,128)S(1)}) custom-call(bf16[1024,1024]{1,0:T(8,128)(2,1)S(1)} %get-tuple-element.80.gp, bf16[1024,128]{1,0:T(8,128)(2,1)S(1)} %get-tuple-element.75.g, bf16[2,1024,1024]{2,1,0:T(8,128)(2,1)} %ordered_transposes.1.refs_6_.ordered_ref), custom_call_target="tpu_custom_call" | custom-call | flops 1073741824 | bytes 6291456 | tf_op jit(solution)/shard_map/more_products/pallas_call | solution.py:365
  42.6 0.6 collective-permute-start.7
  43.2 0.1 add_rows.6
  43.3 1.6 %collective-permute-start.9 = (f32[192,1152]{1,0:T(8,128)S(1)}, f32[192,1152]{1,0:T(8,128)S(1)}, u32[]{:S(2)}, u32[]{:S(2)}) collective-permute-start(f32[192,1152]{1,0:T(8,128)S(1)} %get-tuple-element.83), channel_id=1, source_target_pairs={{0,4},{1,5},{2,3},{3,2},{4,0},{5,1},{6,7},{7,6},{8,12},{9,13},{10,... | collective-permute-start | bytes 2654216 | tf_op jit(solution)/shard_map/ppermute | solution.py:474
  44.9 1.4 %collective-permute-start.8 = (f32[64,1152]{1,0:T(8,128)S(1)}, f32[64,1152]{1,0:T(8,128)S(1)}, u32[]{:S(2)}, u32[]{:S(2)}) collective-permute-start(f32[64,1152]{1,0:T(8,128)S(1)} %get-tuple-element.82), channel_id=1, source_target_pairs={{0,8},{1,9},{2,10},{3,11},{4,12},{5,13},{6,14},{7,15},{8,0},{9,1},... | collective-permute-start | bytes 884744 | tf_op jit(solution)/shard_map/ppermute | solution.py:474
  46.3 2.1 %more_products.3.refs_0_.refs_3_ = f32[256,1152]{1,0:T(8,128)S(1)} custom-call(bf16[1024,1024]{1,0:T(8,128)(2,1)S(1)} %get-tuple-element.80.gp, bf16[1024,128]{1,0:T(8,128)(2,1)S(1)} %get-tuple-element.75.g, bf16[2,1024,1024]{2,1,0:T(8,128)(2,1)} %ordered_transposes.1.refs_6_.ordered_ref), custom_call_target="tpu_custom_call" | custom-call | flops 536870912 | bytes 6291456 | tf_op jit(solution)/shard_map/more_products/pallas_call | solution.py:365
  48.4 5.2 %collective-permute-done.8.refs_2_ = f32[64,1152]{1,0:T(8,128)S(1)} collective-permute-done((f32[64,1152]{1,0:T(8,128)S(1)}, f32[64,1152]{1,0:T(8,128)S(1)}, u32[]{:S(2)}, u32[]{:S(2)}) %collective-permute-start.8) | collective-permute-done | bytes 294944 | tf_op jit(solution)/shard_map/ppermute | solution.py:474
  53.6 2.8 %collective-permute-done.9.refs_5_ = f32[192,1152]{1,0:T(8,128)S(1)} collective-permute-done((f32[192,1152]{1,0:T(8,128)S(1)}, f32[192,1152]{1,0:T(8,128)S(1)}, u32[]{:S(2)}, u32[]{:S(2)}) %collective-permute-start.9) | collective-permute-done | bytes 884768 | tf_op jit(solution)/shard_map/ppermute | solution.py:474
  56.5 1.6 %collective-permute-start.10 = (f32[96,1152]{1,0:T(8,128)S(1)}, f32[96,1152]{1,0:T(8,128)S(1)}, u32[]{:S(2)}, u32[]{:S(2)}) collective-permute-start(f32[96,1152]{1,0:T(8,128)S(1)} %get-tuple-element.85), channel_id=1, source_target_pairs={{0,1},{1,0},{2,6},{3,7},{4,5},{5,4},{6,2},{7,3},{8,9},{9,8},{10,14... | collective-permute-start | bytes 1327112 | tf_op jit(solution)/shard_map/ppermute | solution.py:474
  58.1 2.4 %collective-permute-start.11 = (f32[32,1152]{1,0:T(8,128)S(1)}, f32[32,1152]{1,0:T(8,128)S(1)}, u32[]{:S(2)}, u32[]{:S(2)}) collective-permute-start(f32[32,1152]{1,0:T(8,128)S(1)} %get-tuple-element.86), channel_id=1, source_target_pairs={{0,16},{1,17},{2,18},{3,19},{4,20},{5,21},{6,22},{7,23},{8,24},{9,... | collective-permute-start | bytes 442376 | tf_op jit(solution)/shard_map/ppermute | solution.py:474
  60.6 6.2 %collective-permute-done.11.refs_1_ = f32[32,1152]{1,0:T(8,128)S(1)} collective-permute-done((f32[32,1152]{1,0:T(8,128)S(1)}, f32[32,1152]{1,0:T(8,128)S(1)}, u32[]{:S(2)}, u32[]{:S(2)}) %collective-permute-start.11) | collective-permute-done | bytes 147488 | tf_op jit(solution)/shard_map/ppermute | solution.py:474
  66.8 0.5 collective-permute-start.15
  67.4 0.6 collective-permute-start.12
  68.0 3.4 %collective-permute-start.13 = (f32[24,1152]{1,0:T(8,128)S(1)}, f32[24,1152]{1,0:T(8,128)S(1)}, u32[]{:S(2)}, u32[]{:S(2)}) collective-permute-start(f32[24,1152]{1,0:T(8,128)S(1)} %get-tuple-element.90), channel_id=1, source_target_pairs={{0,16},{1,17},{2,18},{3,19},{4,20},{5,21},{6,22},{7,23},{8,24},{9,... | collective-permute-start | bytes 331784 | tf_op jit(solution)/shard_map/ppermute | solution.py:474
  71.4 0.5 collective-permute-start.14
  71.9 1.6 %collective-permute-start.16 = (f32[8,1152]{1,0:T(8,128)S(1)}, f32[8,1152]{1,0:T(8,128)S(1)}, u32[]{:S(2)}, u32[]{:S(2)}) collective-permute-start(f32[8,1152]{1,0:T(8,128)S(1)} %get-tuple-element.97), channel_id=1, source_target_pairs={{0,1},{1,0},{2,6},{3,7},{4,5},{5,4},{6,2},{7,3},{8,9},{9,8},{10,14... | collective-permute-start | bytes 110600 | tf_op jit(solution)/shard_map/ppermute | solution.py:474
  73.5 2.4 %collective-permute-done.16.refs_5_ = f32[8,1152]{1,0:T(8,128)S(1)} collective-permute-done((f32[8,1152]{1,0:T(8,128)S(1)}, f32[8,1152]{1,0:T(8,128)S(1)}, u32[]{:S(2)}, u32[]{:S(2)}) %collective-permute-start.16) | collective-permute-done | bytes 36896 | tf_op jit(solution)/shard_map/ppermute | solution.py:474
  75.9 4.1 %collective-permute-done.13.refs_2_ = f32[24,1152]{1,0:T(8,128)S(1)} collective-permute-done((f32[24,1152]{1,0:T(8,128)S(1)}, f32[24,1152]{1,0:T(8,128)S(1)}, u32[]{:S(2)}, u32[]{:S(2)}) %collective-permute-start.13) | collective-permute-done | bytes 110624 | tf_op jit(solution)/shard_map/ppermute | solution.py:474
  80.1 0.7 finish.1
  (48 shorter events, 0.7 us)
Async XLA Ops:
  0.6 20.4 %copy-start = (s32[1,64]{1,0:T(1,128)S(1)}, s32[1,64]{1,0:T(1,128)}, u32[]{:S(2)}) copy-start(s32[1,64]{1,0:T(1,128)} %param.17) | copy-start | bytes 772
  6.9 14.8 %collective-permute-start = (f32[14,16,128]{2,1,0:T(8,128)}, f32[14,16,128]{2,1,0:T(8,128)S(1)}, u32[]{:S(2)}, u32[]{:S(2)}) collective-permute-start(f32[14,16,128]{2,1,0:T(8,128)} %get-tuple-element.51), channel_id=1, source_target_pairs={{0,8},{1,9},{2,10},{3,11},{4,12},{5,13},{6,14},{7,15},{8,0},{9,1},... | collective-permute-start | bytes 344072 | tf_op jit(solution)/shard_map/ppermute | solution.py:474
  10.0 11.9 %collective-permute-start.1 = (f32[14,16,128]{2,1,0:T(8,128)}, f32[14,16,128]{2,1,0:T(8,128)S(1)}, u32[]{:S(2)}, u32[]{:S(2)}) collective-permute-start(f32[14,16,128]{2,1,0:T(8,128)} %get-tuple-element.52), channel_id=1, source_target_pairs={{0,16},{1,17},{2,18},{3,19},{4,20},{5,21},{6,22},{7,23},{8,24},{9,... | collective-permute-start | bytes 344072 | tf_op jit(solution)/shard_map/ppermute | solution.py:474
  12.6 9.3 %collective-permute-start.2 = (f32[14,16,128]{2,1,0:T(8,128)}, f32[14,16,128]{2,1,0:T(8,128)S(1)}, u32[]{:S(2)}, u32[]{:S(2)}) collective-permute-start(f32[14,16,128]{2,1,0:T(8,128)} %get-tuple-element.53), channel_id=1, source_target_pairs={{0,24},{1,25},{2,26},{3,27},{4,28},{5,29},{6,30},{7,31},{8,16},{9,... | collective-permute-start | bytes 344072 | tf_op jit(solution)/shard_map/ppermute | solution.py:474
  12.6 7.7 %copy-start.3 = (s32[1,1024]{1,0:T(1,128)S(1)}, s32[1,1024]{1,0:T(1,128)}, u32[]{:S(2)}) copy-start(s32[1,1024]{1,0:T(1,128)} %constant.112) | copy-start | bytes 12292
  12.6 7.7 %copy-start.4 = (s32[1,1024]{1,0:T(1,128)S(1)}, s32[1,1024]{1,0:T(1,128)}, u32[]{:S(2)}) copy-start(s32[1,1024]{1,0:T(1,128)} %constant.111) | copy-start | bytes 12292
  12.6 7.7 %copy-start.5 = (s32[1,1024]{1,0:T(1,128)S(1)}, s32[1,1024]{1,0:T(1,128)}, u32[]{:S(2)}) copy-start(s32[1,1024]{1,0:T(1,128)} %constant.106.clone) | copy-start | bytes 12292
  12.6 7.7 %copy-start.6 = (s32[1,1024]{1,0:T(1,128)S(1)}, s32[1,1024]{1,0:T(1,128)}, u32[]{:S(2)}) copy-start(s32[1,1024]{1,0:T(1,128)} %constant.105.clone) | copy-start | bytes 12292
  12.6 7.7 %copy-start.7 = (s32[1,1024]{1,0:T(1,128)S(1)}, s32[1,1024]{1,0:T(1,128)}, u32[]{:S(2)}) copy-start(s32[1,1024]{1,0:T(1,128)} %constant.104.clone) | copy-start | bytes 12292
  12.6 7.7 %copy-start.8 = (s32[1,1024]{1,0:T(1,128)S(1)}, s32[1,1024]{1,0:T(1,128)}, u32[]{:S(2)}) copy-start(s32[1,1024]{1,0:T(1,128)} %constant.103.clone) | copy-start | bytes 12292
  12.6 7.7 %copy-start.9 = (s32[1,1024]{1,0:T(1,128)S(1)}, s32[1,1024]{1,0:T(1,128)}, u32[]{:S(2)}) copy-start(s32[1,1024]{1,0:T(1,128)} %constant.102.clone) | copy-start | bytes 12292
  12.6 7.7 %copy-start.10 = (s32[1,1024]{1,0:T(1,128)S(1)}, s32[1,1024]{1,0:T(1,128)}, u32[]{:S(2)}) copy-start(s32[1,1024]{1,0:T(1,128)} %constant.101.clone) | copy-start | bytes 12292
  12.6 7.7 %copy-start.11 = (s32[1,1024]{1,0:T(1,128)S(1)}, s32[1,1024]{1,0:T(1,128)}, u32[]{:S(2)}) copy-start(s32[1,1024]{1,0:T(1,128)} %constant.100.clone) | copy-start | bytes 12292
  12.6 8.6 %copy-start.1 = (bf16[1,128,1792]{2,1,0:T(8,128)(2,1)S(1)}, bf16[1,128,1792]{2,1,0:T(8,128)(2,1)}, u32[]{:S(2)}) copy-start(bf16[1,128,1792]{2,1,0:T(8,128)(2,1)} %param.16) | copy-start | bytes 1376260
  12.7 9.0 %copy-start.12 = (s32[1,64]{1,0:T(1,128)S(1)}, s32[1,64]{1,0:T(1,128)}, u32[]{:S(2)}) copy-start(s32[1,64]{1,0:T(1,128)} %param.18) | copy-start | bytes 772
  12.7 9.3 %copy-start.2 = (f32[14,16,128]{2,1,0:T(8,128)S(1)}, f32[14,16,128]{2,1,0:T(8,128)}, u32[]{:S(2)}) copy-start(f32[14,16,128]{2,1,0:T(8,128)} %get-tuple-element.56.refs_0_) | copy-start | bytes 344068
  22.3 12.8 %collective-permute-start.3 = (f32[14,16,128]{2,1,0:T(8,128)S(1)}, f32[14,16,128]{2,1,0:T(8,128)S(1)}, u32[]{:S(2)}, u32[]{:S(2)}) collective-permute-start(f32[14,16,128]{2,1,0:T(8,128)S(1)} %get-tuple-element.63), channel_id=1, source_target_pairs={{0,8},{1,9},{2,10},{3,11},{4,12},{5,13},{6,14},{7,15},{8,0},{9,1},... | collective-permute-start | bytes 344072 | tf_op jit(solution)/shard_map/ppermute | solution.py:474
  24.2 10.9 %collective-permute-start.4 = (f32[14,16,128]{2,1,0:T(8,128)S(1)}, f32[14,16,128]{2,1,0:T(8,128)S(1)}, u32[]{:S(2)}, u32[]{:S(2)}) collective-permute-start(f32[14,16,128]{2,1,0:T(8,128)S(1)} %get-tuple-element.64), channel_id=1, source_target_pairs={{0,16},{1,17},{2,18},{3,19},{4,20},{5,21},{6,22},{7,23},{8,24},{9,... | collective-permute-start | bytes 344072 | tf_op jit(solution)/shard_map/ppermute | solution.py:474
  26.6 8.5 %collective-permute-start.5 = (f32[14,16,128]{2,1,0:T(8,128)S(1)}, f32[14,16,128]{2,1,0:T(8,128)S(1)}, u32[]{:S(2)}, u32[]{:S(2)}) collective-permute-start(f32[14,16,128]{2,1,0:T(8,128)S(1)} %get-tuple-element.65), channel_id=1, source_target_pairs={{0,24},{1,25},{2,26},{3,27},{4,28},{5,29},{6,30},{7,31},{8,16},{9,... | collective-permute-start | bytes 344072 | tf_op jit(solution)/shard_map/ppermute | solution.py:474
  39.4 3.7 %collective-permute-start.6 = (f32[256,1152]{1,0:T(8,128)S(1)}, f32[256,1152]{1,0:T(8,128)S(1)}, u32[]{:S(2)}, u32[]{:S(2)}) collective-permute-start(f32[256,1152]{1,0:T(8,128)S(1)} %get-tuple-element.77), channel_id=1, source_target_pairs={{0,2},{1,3},{2,0},{3,1},{4,6},{5,7},{6,4},{7,5},{8,10},{9,11},{10,... | collective-permute-start | bytes 3538952 | tf_op jit(solution)/shard_map/ppermute | solution.py:474
  42.6 5.8 %collective-permute-start.7 = (f32[256,1152]{1,0:T(8,128)S(1)}, f32[256,1152]{1,0:T(8,128)S(1)}, u32[]{:S(2)}, u32[]{:S(2)}) collective-permute-start(f32[256,1152]{1,0:T(8,128)S(1)} %get-tuple-element.81), channel_id=1, source_target_pairs={{0,2},{1,3},{2,0},{3,1},{4,6},{5,7},{6,4},{7,5},{8,10},{9,11},{10,... | collective-permute-start | bytes 3538952 | tf_op jit(solution)/shard_map/ppermute | solution.py:474
  43.3 13.1 %collective-permute-start.9 = (f32[192,1152]{1,0:T(8,128)S(1)}, f32[192,1152]{1,0:T(8,128)S(1)}, u32[]{:S(2)}, u32[]{:S(2)}) collective-permute-start(f32[192,1152]{1,0:T(8,128)S(1)} %get-tuple-element.83), channel_id=1, source_target_pairs={{0,4},{1,5},{2,3},{3,2},{4,0},{5,1},{6,7},{7,6},{8,12},{9,13},{10,... | collective-permute-start | bytes 2654216 | tf_op jit(solution)/shard_map/ppermute | solution.py:474
  44.9 8.7 %collective-permute-start.8 = (f32[64,1152]{1,0:T(8,128)S(1)}, f32[64,1152]{1,0:T(8,128)S(1)}, u32[]{:S(2)}, u32[]{:S(2)}) collective-permute-start(f32[64,1152]{1,0:T(8,128)S(1)} %get-tuple-element.82), channel_id=1, source_target_pairs={{0,8},{1,9},{2,10},{3,11},{4,12},{5,13},{6,14},{7,15},{8,0},{9,1},... | collective-permute-start | bytes 884744 | tf_op jit(solution)/shard_map/ppermute | solution.py:474
  56.5 10.3 %collective-permute-start.10 = (f32[96,1152]{1,0:T(8,128)S(1)}, f32[96,1152]{1,0:T(8,128)S(1)}, u32[]{:S(2)}, u32[]{:S(2)}) collective-permute-start(f32[96,1152]{1,0:T(8,128)S(1)} %get-tuple-element.85), channel_id=1, source_target_pairs={{0,1},{1,0},{2,6},{3,7},{4,5},{5,4},{6,2},{7,3},{8,9},{9,8},{10,14... | collective-permute-start | bytes 1327112 | tf_op jit(solution)/shard_map/ppermute | solution.py:474
  58.1 8.7 %collective-permute-start.11 = (f32[32,1152]{1,0:T(8,128)S(1)}, f32[32,1152]{1,0:T(8,128)S(1)}, u32[]{:S(2)}, u32[]{:S(2)}) collective-permute-start(f32[32,1152]{1,0:T(8,128)S(1)} %get-tuple-element.86), channel_id=1, source_target_pairs={{0,16},{1,17},{2,18},{3,19},{4,20},{5,21},{6,22},{7,23},{8,24},{9,... | collective-permute-start | bytes 442376 | tf_op jit(solution)/shard_map/ppermute | solution.py:474
  66.8 5.0 %collective-permute-start.15 = (f32[16,1152]{1,0:T(8,128)S(1)}, f32[16,1152]{1,0:T(8,128)S(1)}, u32[]{:S(2)}, u32[]{:S(2)}) collective-permute-start(f32[16,1152]{1,0:T(8,128)S(1)} %get-tuple-element.95), channel_id=1, source_target_pairs={{0,4},{1,5},{2,3},{3,2},{4,0},{5,1},{6,7},{7,6},{8,12},{9,13},{10,... | collective-permute-start | bytes 221192 | tf_op jit(solution)/shard_map/ppermute | solution.py:474
  67.4 8.5 %collective-permute-start.12 = (f32[24,1152]{1,0:T(8,128)S(1)}, f32[24,1152]{1,0:T(8,128)S(1)}, u32[]{:S(2)}, u32[]{:S(2)}) collective-permute-start(f32[24,1152]{1,0:T(8,128)S(1)} %get-tuple-element.89), channel_id=1, source_target_pairs={{0,8},{1,9},{2,10},{3,11},{4,12},{5,13},{6,14},{7,15},{8,0},{9,1},... | collective-permute-start | bytes 331784 | tf_op jit(solution)/shard_map/ppermute | solution.py:474
  68.0 12.0 %collective-permute-start.13 = (f32[24,1152]{1,0:T(8,128)S(1)}, f32[24,1152]{1,0:T(8,128)S(1)}, u32[]{:S(2)}, u32[]{:S(2)}) collective-permute-start(f32[24,1152]{1,0:T(8,128)S(1)} %get-tuple-element.90), channel_id=1, source_target_pairs={{0,16},{1,17},{2,18},{3,19},{4,20},{5,21},{6,22},{7,23},{8,24},{9,... | collective-permute-start | bytes 331784 | tf_op jit(solution)/shard_map/ppermute | solution.py:474
  71.4 8.6 %collective-permute-start.14 = (f32[24,1152]{1,0:T(8,128)S(1)}, f32[24,1152]{1,0:T(8,128)S(1)}, u32[]{:S(2)}, u32[]{:S(2)}) collective-permute-start(f32[24,1152]{1,0:T(8,128)S(1)} %get-tuple-element.91), channel_id=1, source_target_pairs={{0,24},{1,25},{2,26},{3,27},{4,28},{5,29},{6,30},{7,31},{8,16},{9,... | collective-permute-start | bytes 331784 | tf_op jit(solution)/shard_map/ppermute | solution.py:474
  71.9 4.0 %collective-permute-start.16 = (f32[8,1152]{1,0:T(8,128)S(1)}, f32[8,1152]{1,0:T(8,128)S(1)}, u32[]{:S(2)}, u32[]{:S(2)}) collective-permute-start(f32[8,1152]{1,0:T(8,128)S(1)} %get-tuple-element.97), channel_id=1, source_target_pairs={{0,1},{1,0},{2,6},{3,7},{4,5},{5,4},{6,2},{7,3},{8,9},{9,8},{10,14... | collective-permute-start | bytes 110600 | tf_op jit(solution)/shard_map/ppermute | solution.py:474

commit v7 on v6

--- a/solution.py
+++ b/solution.py
@@ -127,11 +127,11 @@
     )(rows_in, w_in, w_out_t)
 
 
-def fill_choice(source_ref, choice):
+def fill_choice(source, choice):
     picked, extent = choice.shape
     for low in range(0, picked, LANES):
         high = min(low + LANES, picked)
-        across = jnp.broadcast_to(source_ref[:, low:high], (LANES, high - low))
+        across = jnp.broadcast_to(source[:, low:high], (LANES, high - low))
         down = jnp.transpose(across)
         for left in range(0, extent, LANES):
             here = lax.broadcasted_iota(jnp.int32, down.shape, 1) + left
@@ -165,25 +165,25 @@
     )(rows_in, w_in)
 
 
-def order_body(source_ref, latent_ref, hidden_ref, out_ref, choice):
+def order_body(source_of, table_ref, latent_ref, hidden_ref, out_ref, choice):
     @pl.when(pl.program_id(0) == 0)
     def _():
-        fill_choice(source_ref, choice)
+        fill_choice(source_of([table_ref[k:k + 1] for k in range(table_ref.shape[0])]), choice)
 
     for k, matrix_ref in enumerate((latent_ref, hidden_ref)):
         ordered = lax.dot_general(choice[...], matrix_ref[...], NT, preferred_element_type=jnp.float32)
         out_ref[k] = ordered.astype(jnp.bfloat16)
 
 
-def ordered_transposes(source, latent, hidden):
+def ordered_transposes(table, source_of, latent, hidden):
     nrows, extent = latent.shape
-    picked = source.shape[1]
+    picked = table.shape[1]
     block = 256 if nrows % 256 == 0 else nrows
     return pl.pallas_call(
-        order_body,
+        functools.partial(order_body, source_of),
         grid=(nrows // block,),
         in_specs=[
-            pl.BlockSpec((1, picked), lambda i: (0, 0)),
+            pl.BlockSpec(table.shape, lambda i: (0, 0)),
             pl.BlockSpec((block, extent), lambda i: (i, 0)),
             pl.BlockSpec((block, extent), lambda i: (i, 0)),
         ],
@@ -193,13 +193,19 @@
         compiler_params=params(MOST),
         cost_estimate=cost(nrows * extent * picked, 4 * MIB),
         name="ordered_transposes",
-    )(source, latent, hidden)
-
-
-def target_body(channels, pool_ref, index_ref, target_ref):
+    )(table, latent, hidden)
+
+
+def target_body(channels, pool_ref, index_ref, count_ref, target_ref, weight_ref):
     carriers, share, _ = target_ref.shape
     npool, total = pool_ref.shape
-    choose = index_ref[...] == lax.broadcasted_iota(jnp.int32, (share, npool), 1)
+    npatch = index_ref.shape[1]
+    own = lax.broadcasted_iota(jnp.int32, (share, npatch), 0) + lax.axis_index("member") * share
+    own = own == lax.broadcasted_iota(jnp.int32, (share, npatch), 1)
+    index = jnp.sum(jnp.where(own, index_ref[...], 0), axis=1, keepdims=True)
+    count = jnp.sum(jnp.where(own, count_ref[...], 0), axis=1, keepdims=True)
+    weight_ref[...] = jnp.broadcast_to(count.astype(jnp.float32), weight_ref.shape)
+    choose = index == lax.broadcasted_iota(jnp.int32, (share, npool), 1)
     flat = jnp.dot(
         jnp.where(choose, 1.0, 0.0).astype(jnp.bfloat16), pool_ref[...], preferred_element_type=jnp.float32
     )
@@ -214,24 +220,26 @@
         target_ref[j] = row
 
 
-def targets(pool, index, channels):
-    share = index.shape[0]
+def targets(pool, index, count, share, channels):
     carriers = packing(channels)[1]
     return pl.pallas_call(
         functools.partial(target_body, channels),
-        in_specs=[WHOLE] * 2,
-        out_specs=WHOLE,
-        out_shape=jax.ShapeDtypeStruct((carriers, share, LANES), jnp.float32),
+        in_specs=[WHOLE] * 3,
+        out_specs=[WHOLE] * 2,
+        out_shape=[
+            jax.ShapeDtypeStruct((carriers, share, LANES), jnp.float32),
+            jax.ShapeDtypeStruct((share, LANES), jnp.float32),
+        ],
         compiler_params=params(),
         cost_estimate=cost(2 * share * pool.size, 2 * pool.size),
         name="targets",
-    )(pool, index)
+    )(pool, index, count)
 
 
 def score_body(members, *refs):
-    x_refs, (target_ref, count_ref), out_refs = refs[:members], refs[members:members + 2], refs[members + 2:]
+    x_refs, (target_ref, weight_ref), out_refs = refs[:members], refs[members:members + 2], refs[members + 2:]
     carriers = target_ref.shape[0]
-    weight = count_ref[...].astype(jnp.float32)
+    weight = weight_ref[...]
 
     def inverse_norm(delta):
         squares = sum(d * d for d in delta)
@@ -253,7 +261,7 @@
             out_refs[m][j] = weight * (delta[j] * inverse / members - pair[m][j] / (members * members))
 
 
-def score(pieces, target, count):
+def score(pieces, target, weight):
     members = len(pieces)
     size = members * target.size
     return pl.pallas_call(
@@ -264,7 +272,7 @@
         compiler_params=params(),
         cost_estimate=cost(30 * size, 8 * size),
         name="score",
-    )(*pieces, target, count)
+    )(*pieces, target, weight)
 
 
 def first_body(parts, *refs):
@@ -290,7 +298,7 @@
         copy.start()
 
     me_z = lax.axis_index("member")
-    for k, scored_ref in enumerate(scored_refs):
+    for k, scored_ref in zip(reversed(range(parts)), scored_refs):
         base = partner(me_z, k, parts) * (share * PATCH)
         for j, value in enumerate(unpack([scored_ref[j] for j in range(carriers)], channels)):
             cells[pl.ds(base + j, share, stride=PATCH), :] = value
@@ -403,23 +411,21 @@
     )(*inputs)
 
 
-def finish_body(count, *refs):
-    main_refs, rest_refs, (first_ref, second_ref) = refs[:count], refs[count:-2], refs[-2:]
+def finish_body(*refs):
+    *parts, first_ref, second_ref = refs
     width, channels = first_ref.shape[1], second_ref.shape[1]
-    rows = main_refs[0].shape[0]
-    for low, high, refs in ((0, rows, main_refs), (rows, first_ref.shape[0], rest_refs)):
-        total = refs[0][...]
-        for ref in refs[1:]:
-            total = total + ref[...]
-        first_ref[low:high] = total[:, :width]
-        second_ref[low:high] = total[:, width:width + channels]
-
-
-def finish(main, rest, width, channels):
-    height = main[0].shape[0] + rest[0].shape[0]
-    return pl.pallas_call(
-        functools.partial(finish_body, len(main)),
-        in_specs=[WHOLE] * (len(main) + len(rest)),
+    total = parts[0][...]
+    for ref in parts[1:]:
+        total = total + ref[...]
+    first_ref[...] = total[:, :width]
+    second_ref[...] = total[:, width:width + channels]
+
+
+def finish(parts, width, channels):
+    height = parts[0].shape[0]
+    return pl.pallas_call(
+        finish_body,
+        in_specs=[WHOLE] * len(parts),
         out_specs=[WHOLE] * 2,
         out_shape=[
             jax.ShapeDtypeStruct((height, width), jnp.float32),
@@ -428,28 +434,24 @@
         compiler_params=params(),
         cost_estimate=cost(4 * height * width, 20 * height * width),
         name="finish",
-    )(*main, *rest)
+    )(*parts)
 
 
 def row_order(nz, nx, nc, ny, height):
-    near = 2 if nz % 2 == 0 else 1
-    far = nz // near
-    rc = max(height // 4, 1)
-    main_rows, c_rows = range(height - rc), range(height - rc, height)
-    first_last, second_last, far_last = [[*range(1, n), 0] for n in (nx, ny, far)]
-
-    def main(firsts):
-        return [(f, s, 0, 0, k, r) for f in firsts for s in second_last for k in reversed(range(nz)) for r in main_rows]
-
-    def part_c(nears):
-        return [(f, s, 1, o, n, r) for n in nears for o in far_last for f in first_last for s in second_last for r in c_rows]
-
-    pieces = [main(range(1, nx)), part_c(range(1, near)), part_c([0]), main([0])]
-    sizes = [len(piece) for piece in pieces]
-    cores = [*range(1, nc), 0]
-    halves = [[row for piece in part for row in piece] for part in (pieces[:2], pieces[2:])]
-    table = np.array([(core, *row) for half in halves for core in cores for row in half], np.int32).T
-    return table, sizes, near, far, rc
+    first_last, second_last = [[*range(1, n), 0] for n in (nx, ny)]
+    z_last = [*reversed(range(nz))]
+    step = max(nz // 4, 1)
+    chunks = [z_last[low:low + step] for low in range(0, nz, step)]
+
+    def part(firsts, ks):
+        return [(f, s, k, r) for f in firsts for s in second_last for k in ks for r in range(height)]
+
+    halves = [[part(firsts, ks) for ks in chunks] for firsts in (first_last[:-1], [0])]
+    table = np.array(
+        [(core, *row) for half in halves for core in [*range(1, nc), 0] for piece in half for row in piece], np.int32
+    ).T
+    sent, kept = [[len(piece) for piece in half] for half in halves]
+    return table, chunks, sent, kept
 
 
 def shards(latent, w_in, w_out, observed, patch_index, counts):
@@ -458,13 +460,12 @@
     width, channels = w_out.shape
     nz, nt, ny = (lax.axis_size(name) for name in ("member", "tile", "batch"))
     nc, nx = CORES, nt // CORES
-    me_z, me_t, me_y = (lax.axis_index(name) for name in ("member", "tile", "batch"))
-    me_x, me_c = me_t // nc, me_t % nc
     w_out_t = w_out.T
     height = depth // (nz * nt * ny)
-    table, sizes, near, far, rc = row_order(nz, nx, nc, ny, height)
+    table, chunks, sent, kept = row_order(nz, nx, nc, ny, height)
     turned = 1 if nx == ny else 0
 
+    far_first = [*reversed(range(nz))]
     everywhere = [(z, x, c, y) for z in range(nz) for x in range(nx) for c in range(nc) for y in range(ny)]
 
     def shift(value, target):
@@ -475,36 +476,11 @@
             value, ("member", "tile", "batch"), [(number(*place), number(*target(*place))) for place in everywhere]
         )
 
+    def send_to(value, k):
+        return shift(value, lambda z, x, c, y: (partner(z, k, nz), x, c, y))
+
     def exchange(values):
-        got = {k: shift(values[k], lambda z, x, c, y: (partner(z, k, nz), x, c, y)) for k in reversed(range(1, nz))}
-        return [values[0], *[got[k] for k in range(1, nz)]]
-
-    share = nrows // PATCH // nz
-    far_first = [*reversed(range(nz))]
-    packed = dict(zip(far_first, decode(rows_in, w_in, w_out_t, nz, far_first)))
-    grouped = exchange(packed)
-
-    core, first, second, relative, f, n, row = (jnp.asarray(table[k:k + 1]) for k in range(7))
-    z_main = partner(me_z, n, nz)
-    z_far = (f + me_z // near) % far * near + (n + me_z % near) % near
-    z = z_main + relative * (z_far - z_main)
-    core = (core + me_c) % nc
-    turn = core * turned
-    x, y = first + turn * (second - first), second + turn * (first - second)
-    tile = (x + me_x) % nx * nc + core
-    source = ((z * nt + tile) * ny + (y + me_y) % ny) * height + row
-    slope, hidden = slopes(rows_in, w_in)
-    index = lax.dynamic_slice_in_dim(patch_index[0], me_z * share, share, 0)[:, None]
-    count = lax.dynamic_slice_in_dim(counts[0], me_z * share, share, 0)[:, None]
-    target = targets(observed[0], index, channels)
-    grouped, slope, hidden, source, target, count = lax.optimization_barrier(
-        (grouped, slope, hidden, source, target, count)
-    )
-
-    scored = score(grouped, target, count)
-    returned = exchange(scored)
-    ordered = ordered_transposes(source, rows_in, hidden)
-    returned, ordered = lax.optimization_barrier((returned, ordered))
+        return [send_to(values[k], k) if k else values[0] for k in far_first]
 
     def shift_core(value, j):
         return shift(value, lambda z, x, c, y: (z, x, (c + j) % nc, y))
@@ -520,75 +496,69 @@
 
     shift_first, shift_second = along(lambda c: c * turned), along(lambda c: 1 - c * turned)
 
-    def shift_near(value, j):
-        return shift(value, lambda z, x, c, y: (z // near * near + (z + j) % near, x, c, y))
-
-    def shift_far(value, j):
-        return shift(value, lambda z, x, c, y: ((z // near + j) % far * near + z % near, x, c, y))
-
     def send_all(value, others, shift_one):
         if others == 1:
             return [shift_one(value, 1)]
         return [shift_one(v, j + 1) for j, v in enumerate(jnp.split(value, others, axis=0))] if others else []
 
-    n_main, nc_send, nc_keep, main_keep = sizes
-    n_send, n_keep = n_main + nc_send, nc_keep + main_keep
+    share = nrows // PATCH // nz
+    packed = dict(zip(far_first, decode(rows_in, w_in, w_out_t, nz, far_first)))
+    grouped = exchange(packed)
+
+    def source_of(columns):
+        me_z, me_t, me_y = (lax.axis_index(name) for name in ("member", "tile", "batch"))
+        core, first, second, k, row = columns[:5]
+        z = partner(me_z, k, nz)
+        core = lax.rem(core + lax.rem(me_t, nc), nc)
+        turn = core * turned
+        x, y = first + turn * (second - first), second + turn * (first - second)
+        tile = lax.rem(x + me_t // nc, nx) * nc + core
+        return ((z * nt + tile) * ny + lax.rem(y + me_y, ny)) * height + row
+
+    table = np.concatenate([table, np.zeros((-len(table) % 8, table.shape[1]), np.int32)])
+    n_send, n_keep = sum(sent), sum(kept)
     middle = 2 * n_send
+
+    slope, hidden = slopes(rows_in, w_in)
+    target, weight = targets(observed[0], patch_index, counts, share, channels)
+    grouped, slope, hidden, target, weight = lax.optimization_barrier((grouped, slope, hidden, target, weight))
+
+    scored = score(grouped, target, weight)
+    returned = exchange(dict(zip(far_first, scored)))
+    ordered = ordered_transposes(table, source_of, rows_in, hidden)
+    returned, ordered = lax.optimization_barrier((returned, ordered))
 
     other_send, gp, g = first_products(returned, slope, w_out_t, ordered, n_send)
     core_send = shift_core(other_send, 1)
     own_send, other_keep = more_products(gp, g, ordered, [(n_send, middle), (middle, middle + n_keep)])
     core_keep = shift_core(other_keep, 1)
-    main_send, c_send = add_rows(
-        [own_send, core_send],
-        [[(0, n_main, [(0, 0), (1, 0)])], [(0, nc_send, [(0, n_main), (1, n_main)])]],
-    )
-    main_send, c_send, gp = lax.optimization_barrier((main_send, c_send, gp))
-    main_got = send_all(main_send, nx - 1, shift_first)
-    c_got = send_all(c_send, near - 1, shift_near)
-    c_cut, main_cut = nc_keep // far * (far - 1), main_keep // ny * (ny - 1)
-    keeps = [c_cut, nc_keep - c_cut, main_cut, main_keep - main_cut]
-    offsets = [int(low) for low in np.cumsum([0, *keeps])]
+
+    def added(inputs, pieces):
+        return list(add_rows(inputs, [[(0, rows, [(i, low) for i in range(len(inputs))])] for low, rows in pieces]))
+
+    def pieces_of(sizes, low=0):
+        return [(low + int(at), size) for at, size in zip(np.cumsum([0, *sizes[:-1]]), sizes)]
+
+    first_sends = added([own_send, core_send], pieces_of(sent))
+    first_sends, gp = lax.optimization_barrier((first_sends, gp))
+    first_got = [send_all(value, nx - 1, shift_first) for value in first_sends]
     (own_keep,) = more_products(gp, g, ordered, [(middle + n_keep, middle + 2 * n_keep)])
 
-    def summed(k, got, low):
-        terms = [(0, offsets[k]), (1, offsets[k]), *[(2 + i, low) for i in range(len(got))]]
-        return [own_keep, core_keep, *got], [(0, keeps[k], terms)]
-
-    def sums(*wanted):
-        inputs, plans = [], []
-        for sources, plan in wanted:
-            plans.append([(at, rows, [(len(inputs) + i, low) for i, low in terms]) for at, rows, terms in plan])
-            inputs.extend(sources)
-        return add_rows(inputs, plans)
-
-    c_send, main_send = sums(summed(0, c_got, 0), summed(2, main_got, 0))
-    kept = [summed(1, c_got, c_cut), summed(3, main_got, main_cut)]
-    c_got = send_all(c_send, far - 1, shift_far)
-    main_got = send_all(main_send, ny - 1, shift_second)
-    c_keep, main_keep = sums(*kept)
-
-    def split_sums(keep, got, n):
-        rows = keep.shape[0]
-        cut = rows // n * (n - 1)
-        sources = range(1 + len(got))
-        return add_rows(
-            [keep, *got],
-            [[(0, cut, [(i, 0) for i in sources])], [(0, rows - cut, [(i, cut) for i in sources])]],
+    joined, early = {}, {}
+    for ks, (low, size), got in zip(chunks, pieces_of(kept), first_got):
+        if ks == chunks[-1] and len(chunks) > 1:
+            early[far_first[0]] = send_to(joined[far_first[0]], far_first[0])
+            got, early[far_first[0]] = lax.optimization_barrier((got, early[far_first[0]]))
+        cut = size // ny * (ny - 1)
+        terms = [(0, low), (1, low), *[(2 + i, 0) for i in range(len(got))]]
+        second_send, second_keep = add_rows(
+            [own_keep, core_keep, *got],
+            [[(0, rows, [(i, start + at) for i, start in terms])] for at, rows in ((0, cut), (cut, size - cut))],
         )
-
-    main_got, c_got = lax.optimization_barrier((main_got, c_got))
-    rows = main_keep.shape[0] // nz
-    sources = range(1 + len(main_got))
-    joined = add_rows(
-        [main_keep, *main_got], [[(0, rows, [(i, k * rows) for i in sources])] for k in range(nz)]
-    )
-    main = exchange(joined[::-1])
-    c_send, c_keep = split_sums(c_keep, c_got, nx)
-    c_got = send_all(c_send, nx - 1, shift_first)
-    c_send, c_keep = split_sums(c_keep, c_got, ny)
-    c_got = send_all(c_send, ny - 1, shift_second)
-    return tuple(finish(main, [c_keep, *c_got], width, channels))
+        got = send_all(second_send, ny - 1, shift_second)
+        joined.update(zip(ks, added([second_keep, *got], pieces_of([height] * len(ks)))))
+    parts = [early[k] if k in early else send_to(joined[k], k) if k else joined[k] for k in far_first]
+    return tuple(finish(parts, width, channels))
 
 
 def solution(mesh):

time: 81.1 us -> 74.9 us (0.924)
  waiting for transfers between devices: 20.9 us -> 10.4 us
  starting transfers between devices: 24.5 us -> 29.9 us
    ppermute x17 -> x19, waiting for transfers between devices: 20.9 us -> 10.4 us  [shift(): lax.ppermute(value, ('member', 'tile', 'batch'), [(number(*place), number...]
    ppermute x17 -> x19, starting transfers between devices: 24.5 us -> 29.9 us  [shift(): lax.ppermute(value, ('member', 'tile', 'batch'), [(number(*place), number...]
  transfers between devices with their start and end apart: 17 -> 19, of which waited for: 6 -> 9; matrix products, arithmetic and copies ran while one was open for 1% -> 0% of each run, Pallas kernels for 27% -> 29%
where the time goes in v7:
time: 74.9 us; the launch traced here: 74.6 us
  Pallas kernels  33.4 us (45%)
  starting transfers between devices  29.9 us (40%)
  waiting for transfers between devices  10.4 us (14%)
  between operations  0.79 us (1%)
    ppermute x19, starting transfers between devices, shift(): lax.ppermute(value, ('member', 'tile', 'batch'), [(number(*place), number...  29.9 us
    ppermute x19, waiting for transfers between devices, shift(): lax.ppermute(value, ('member', 'tile', 'batch'), [(number(*place), number...  10.4 us
    pallas_call x1, Pallas kernels, ordered_transposes(): pl.pallas_call(functools.partial(order_body, source_of), grid=(nrows // b...  8.34 us
    pallas_call x1, Pallas kernels, slopes(): pl.pallas_call(slope_body, grid=(nrows // block,), in_specs=[pl.BlockSpec...  7.56 us
    pallas_call x1, Pallas kernels, decode(): pl.pallas_call(functools.partial(decode_body, tuple(pieces)), in_specs=[A...  6.28 us
    pallas_call x2, Pallas kernels, more_products(): pl.pallas_call(functools.partial(more_body, tuple(cuts)), in_specs=[WHOLE...  5.15 us
    pallas_call x1, Pallas kernels, first_products(): pl.pallas_call(functools.partial(first_body, len(scored)), in_specs=[*[WH...  4.3 us
  transfers between devices with their start and end apart: 19, of which 9 were waited for; matrix products, arithmetic and copies ran while one was open for 0% of the time, Pallas kernels for 29%

profile of v7, /device:TPU:0, one launch (start us, length us, event | category | flops | bytes accessed | tf_op | source)
XLA Modules:
  0.0 74.6 jit_solution(9359279696132550338)
XLA Ops:
  0.7 6.3 %decode.1 = (f32[14,16,128]{2,1,0:T(8,128)}, f32[14,16,128]{2,1,0:T(8,128)}, f32[14,16,128]{2,1,0:T(8,128)}, f32[14,16,128]{2,1,0:T(8,128)}) custom-call(bf16[1024,1024]{1,0:T(8,128)(2,1)} %bitcast.4, bf16[1024,1024]{1,0:T(8,128)(2,1)} %w_in_ref.3, bf16[112,1024]{1,0:T(8,128)(2,1)} %bitcast.7), custom_call_target="tpu_custom_call" | custom-call | flops 2382364672 | bytes 5242880 | tf_op jit(solution)/shard_map/decode/pallas_call | solution.py:111
  6.9 5.1 %collective-permute-start = (f32[14,16,128]{2,1,0:T(8,128)}, f32[14,16,128]{2,1,0:T(8,128)S(1)}, u32[]{:S(2)}, u32[]{:S(2)}) collective-permute-start(f32[14,16,128]{2,1,0:T(8,128)} %get-tuple-element.51), channel_id=1, source_target_pairs={{0,24},{1,25},{2,26},{3,27},{4,28},{5,29},{6,30},{7,31},{8,16},{9,... | collective-permute-start | bytes 344072 | tf_op jit(solution)/shard_map/ppermute | solution.py:475
  12.1 0.6 collective-permute-start.2
  12.7 0.4 targets.1
  13.2 7.6 %slopes.1 = (f32[1024,1024]{1,0:T(8,128)}, bf16[1024,1024]{1,0:T(8,128)(2,1)}) custom-call(bf16[1024,1024]{1,0:T(8,128)(2,1)} %bitcast.5, bf16[1024,1024]{1,0:T(8,128)(2,1)} %w_in_ref.3), custom_call_target="tpu_custom_call" | custom-call | flops 2147483648 | bytes 4194304 | tf_op jit(solution)/shard_map/slopes/pallas_call | solution.py:153
  20.7 1.2 %collective-permute-done.1.refs_1_ = f32[14,16,128]{2,1,0:T(8,128)S(1)} collective-permute-done((f32[14,16,128]{2,1,0:T(8,128)}, f32[14,16,128]{2,1,0:T(8,128)S(1)}, u32[]{:S(2)}, u32[]{:S(2)}) %collective-permute-start.1) | collective-permute-done | bytes 114720 | tf_op jit(solution)/shard_map/ppermute | solution.py:475
  21.9 0.3 score.1
  22.3 2.6 %collective-permute-start.3 = (f32[14,16,128]{2,1,0:T(8,128)S(1)}, f32[14,16,128]{2,1,0:T(8,128)S(1)}, u32[]{:S(2)}, u32[]{:S(2)}) collective-permute-start(f32[14,16,128]{2,1,0:T(8,128)S(1)} %get-tuple-element.65), channel_id=1, source_target_pairs={{0,24},{1,25},{2,26},{3,27},{4,28},{5,29},{6,30},{7,31},{8,16},{9,... | collective-permute-start | bytes 344072 | tf_op jit(solution)/shard_map/ppermute | solution.py:475
  24.9 1.8 %collective-permute-start.5 = (f32[14,16,128]{2,1,0:T(8,128)S(1)}, f32[14,16,128]{2,1,0:T(8,128)S(1)}, u32[]{:S(2)}, u32[]{:S(2)}) collective-permute-start(f32[14,16,128]{2,1,0:T(8,128)S(1)} %get-tuple-element.67), channel_id=1, source_target_pairs={{0,8},{1,9},{2,10},{3,11},{4,12},{5,13},{6,14},{7,15},{8,0},{9,1},... | collective-permute-start | bytes 344072 | tf_op jit(solution)/shard_map/ppermute | solution.py:475
  26.7 8.3 %ordered_transposes.1.refs_6_.ordered_ref = bf16[2,1024,1024]{2,1,0:T(8,128)(2,1)} custom-call(s32[8,1024]{1,0:T(8,128)} %constant.2.clone.table_ref, bf16[1024,1024]{1,0:T(8,128)(2,1)} %bitcast.6, bf16[1024,1024]{1,0:T(8,128)(2,1)} %get-tuple-element.69.hidden_ref), custom_call_target="tpu_custom_call" | custom-call | flops 1073741824 | bytes 4194304 | tf_op jit(solution)/shard_map/ordered_transposes/pallas_call | solution.py:182
  35.1 4.3 %first_products.1 = (f32[256,1152]{1,0:T(8,128)S(1)}, bf16[1024,1024]{1,0:T(8,128)(2,1)S(1)}, bf16[1024,128]{1,0:T(8,128)(2,1)S(1)}) custom-call(f32[14,16,128]{2,1,0:T(8,128)S(1)} %collective-permute-done.3.refs_0_, f32[14,16,128]{2,1,0:T(8,128)S(1)} %collective-permute-done.4.refs_1_, f32[14,16,128]{2,1,0:T(8,128)S(1)} %collective-permute-done.5.refs_2_, ...), custom_call_target="tpu_custom_call" | custom-call | flops 771751936 | bytes 10485760 | tf_op jit(solution)/shard_map/first_products/pallas_call | solution.py:324
  39.5 3.1 %more_products.2 = (f32[256,1152]{1,0:T(8,128)S(1)}, f32[256,1152]{1,0:T(8,128)S(1)}) custom-call(bf16[1024,1024]{1,0:T(8,128)(2,1)S(1)} %get-tuple-element.85.gp, bf16[1024,128]{1,0:T(8,128)(2,1)S(1)} %get-tuple-element.77.g, bf16[2,1024,1024]{2,1,0:T(8,128)(2,1)} %ordered_transposes.1.refs_6_.ordered_ref), custom_call_target="tpu_custom_call" | custom-call | flops 1073741824 | bytes 6291456 | tf_op jit(solution)/shard_map/more_products/pallas_call | solution.py:373
  42.6 0.6 collective-permute-start.8
  43.3 1.6 %collective-permute-start.9 = (f32[64,1152]{1,0:T(8,128)S(1)}, f32[64,1152]{1,0:T(8,128)S(1)}, u32[]{:S(2)}, u32[]{:S(2)}) collective-permute-start(f32[64,1152]{1,0:T(8,128)S(1)} %get-tuple-element.87), channel_id=1, source_target_pairs={{0,4},{1,5},{2,3},{3,2},{4,0},{5,1},{6,7},{7,6},{8,12},{9,13},{10,... | collective-permute-start | bytes 884744 | tf_op jit(solution)/shard_map/ppermute | solution.py:475
  44.8 0.5 collective-permute-start.12
  45.4 1.5 %collective-permute-start.15 = (f32[64,1152]{1,0:T(8,128)S(1)}, f32[64,1152]{1,0:T(8,128)S(1)}, u32[]{:S(2)}, u32[]{:S(2)}) collective-permute-start(f32[64,1152]{1,0:T(8,128)S(1)} %get-tuple-element.94), channel_id=1, source_target_pairs={{0,4},{1,5},{2,3},{3,2},{4,0},{5,1},{6,7},{7,6},{8,12},{9,13},{10,... | collective-permute-start | bytes 884744 | tf_op jit(solution)/shard_map/ppermute | solution.py:475
  46.8 2.1 %more_products.3.refs_0_ = f32[256,1152]{1,0:T(8,128)S(1)} custom-call(bf16[1024,1024]{1,0:T(8,128)(2,1)S(1)} %get-tuple-element.85.gp, bf16[1024,128]{1,0:T(8,128)(2,1)S(1)} %get-tuple-element.77.g, bf16[2,1024,1024]{2,1,0:T(8,128)(2,1)} %ordered_transposes.1.refs_6_.ordered_ref), custom_call_target="tpu_custom_call" | custom-call | flops 536870912 | bytes 6291456 | tf_op jit(solution)/shard_map/more_products/pallas_call | solution.py:373
  48.9 1.1 %collective-permute-done.9.refs_2_ = f32[64,1152]{1,0:T(8,128)S(1)} collective-permute-done((f32[64,1152]{1,0:T(8,128)S(1)}, f32[64,1152]{1,0:T(8,128)S(1)}, u32[]{:S(2)}, u32[]{:S(2)}) %collective-permute-start.9) | collective-permute-done | bytes 294944 | tf_op jit(solution)/shard_map/ppermute | solution.py:475
  50.1 1.6 %collective-permute-start.10 = (f32[32,1152]{1,0:T(8,128)S(1)}, f32[32,1152]{1,0:T(8,128)S(1)}, u32[]{:S(2)}, u32[]{:S(2)}) collective-permute-start(f32[32,1152]{1,0:T(8,128)S(1)} %get-tuple-element.89), channel_id=1, source_target_pairs={{0,1},{1,0},{2,6},{3,7},{4,5},{5,4},{6,2},{7,3},{8,9},{9,8},{10,14... | collective-permute-start | bytes 442376 | tf_op jit(solution)/shard_map/ppermute | solution.py:475
  51.7 1.5 %collective-permute-start.7 = (f32[64,1152]{1,0:T(8,128)S(1)}, f32[64,1152]{1,0:T(8,128)S(1)}, u32[]{:S(2)}, u32[]{:S(2)}) collective-permute-start(f32[64,1152]{1,0:T(8,128)S(1)} %get-tuple-element.84), channel_id=1, source_target_pairs={{0,4},{1,5},{2,3},{3,2},{4,0},{5,1},{6,7},{7,6},{8,12},{9,13},{10,... | collective-permute-start | bytes 884744 | tf_op jit(solution)/shard_map/ppermute | solution.py:475
  53.2 1.3 %collective-permute-done.12.refs_2_ = f32[64,1152]{1,0:T(8,128)S(1)} collective-permute-done((f32[64,1152]{1,0:T(8,128)S(1)}, f32[64,1152]{1,0:T(8,128)S(1)}, u32[]{:S(2)}, u32[]{:S(2)}) %collective-permute-start.12) | collective-permute-done | bytes 294944 | tf_op jit(solution)/shard_map/ppermute | solution.py:475
  54.5 1.6 %collective-permute-start.13 = (f32[32,1152]{1,0:T(8,128)S(1)}, f32[32,1152]{1,0:T(8,128)S(1)}, u32[]{:S(2)}, u32[]{:S(2)}) collective-permute-start(f32[32,1152]{1,0:T(8,128)S(1)} %get-tuple-element.93), channel_id=1, source_target_pairs={{0,1},{1,0},{2,6},{3,7},{4,5},{5,4},{6,2},{7,3},{8,9},{9,8},{10,14... | collective-permute-start | bytes 442376 | tf_op jit(solution)/shard_map/ppermute | solution.py:475
  56.1 0.9 %collective-permute-done.10.refs_1_ = f32[32,1152]{1,0:T(8,128)S(1)} collective-permute-done((f32[32,1152]{1,0:T(8,128)S(1)}, f32[32,1152]{1,0:T(8,128)S(1)}, u32[]{:S(2)}, u32[]{:S(2)}) %collective-permute-start.10) | collective-permute-done | bytes 147488 | tf_op jit(solution)/shard_map/ppermute | solution.py:475
  57.0 2.6 %collective-permute-start.11 = (f32[32,1152]{1,0:T(8,128)S(1)}, f32[32,1152]{1,0:T(8,128)S(1)}, u32[]{:S(2)}, u32[]{:S(2)}) collective-permute-start(f32[32,1152]{1,0:T(8,128)S(1)} %add_rows.11), channel_id=1, source_target_pairs={{0,24},{1,25},{2,26},{3,27},{4,28},{5,29},{6,30},{7,31},{8,16},{9,... | collective-permute-start | bytes 442376 | tf_op jit(solution)/shard_map/ppermute | solution.py:475
  59.7 1.6 %collective-permute-start.16 = (f32[32,1152]{1,0:T(8,128)S(1)}, f32[32,1152]{1,0:T(8,128)S(1)}, u32[]{:S(2)}, u32[]{:S(2)}) collective-permute-start(f32[32,1152]{1,0:T(8,128)S(1)} %get-tuple-element.96), channel_id=1, source_target_pairs={{0,1},{1,0},{2,6},{3,7},{4,5},{5,4},{6,2},{7,3},{8,9},{9,8},{10,14... | collective-permute-start | bytes 442376 | tf_op jit(solution)/shard_map/ppermute | solution.py:475
  61.4 1.2 %collective-permute-start.14 = (f32[32,1152]{1,0:T(8,128)S(1)}, f32[32,1152]{1,0:T(8,128)S(1)}, u32[]{:S(2)}, u32[]{:S(2)}) collective-permute-start(f32[32,1152]{1,0:T(8,128)S(1)} %add_rows.13), channel_id=1, source_target_pairs={{0,16},{1,17},{2,18},{3,19},{4,20},{5,21},{6,22},{7,23},{8,24},{9,... | collective-permute-start | bytes 442376 | tf_op jit(solution)/shard_map/ppermute | solution.py:475
  62.5 1.8 %collective-permute-done.7.refs_2_ = f32[64,1152]{1,0:T(8,128)S(1)} collective-permute-done((f32[64,1152]{1,0:T(8,128)S(1)}, f32[64,1152]{1,0:T(8,128)S(1)}, u32[]{:S(2)}, u32[]{:S(2)}) %collective-permute-start.7) | collective-permute-done | bytes 294944 | tf_op jit(solution)/shard_map/ppermute | solution.py:475
  64.3 0.9 %collective-permute-done.11.refs_0_ = f32[32,1152]{1,0:T(8,128)S(1)} collective-permute-done((f32[32,1152]{1,0:T(8,128)S(1)}, f32[32,1152]{1,0:T(8,128)S(1)}, u32[]{:S(2)}, u32[]{:S(2)}) %collective-permute-start.11) | collective-permute-done | bytes 147488 | tf_op jit(solution)/shard_map/ppermute | solution.py:475
  65.3 1.6 %collective-permute-start.18 = (f32[32,1152]{1,0:T(8,128)S(1)}, f32[32,1152]{1,0:T(8,128)S(1)}, u32[]{:S(2)}, u32[]{:S(2)}) collective-permute-start(f32[32,1152]{1,0:T(8,128)S(1)} %get-tuple-element.99), channel_id=1, source_target_pairs={{0,1},{1,0},{2,6},{3,7},{4,5},{5,4},{6,2},{7,3},{8,9},{9,8},{10,14... | collective-permute-start | bytes 442376 | tf_op jit(solution)/shard_map/ppermute | solution.py:475
  66.9 3.9 %collective-permute-start.17 = (f32[32,1152]{1,0:T(8,128)S(1)}, f32[32,1152]{1,0:T(8,128)S(1)}, u32[]{:S(2)}, u32[]{:S(2)}) collective-permute-start(f32[32,1152]{1,0:T(8,128)S(1)} %add_rows.15), channel_id=1, source_target_pairs={{0,8},{1,9},{2,10},{3,11},{4,12},{5,13},{6,14},{7,15},{8,0},{9,1},... | collective-permute-start | bytes 442376 | tf_op jit(solution)/shard_map/ppermute | solution.py:475
  70.9 3.0 %collective-permute-done.17.refs_2_ = f32[32,1152]{1,0:T(8,128)S(1)} collective-permute-done((f32[32,1152]{1,0:T(8,128)S(1)}, f32[32,1152]{1,0:T(8,128)S(1)}, u32[]{:S(2)}, u32[]{:S(2)}) %collective-permute-start.17) | collective-permute-done | bytes 147488 | tf_op jit(solution)/shard_map/ppermute | solution.py:475
  73.9 0.7 finish.1
  (32 shorter events, 0.7 us)
Async XLA Ops:
  0.6 12.1 %copy-start = (bf16[1,128,1792]{2,1,0:T(8,128)(2,1)S(1)}, bf16[1,128,1792]{2,1,0:T(8,128)(2,1)}, u32[]{:S(2)}) copy-start(bf16[1,128,1792]{2,1,0:T(8,128)(2,1)} %param.10) | copy-start | bytes 1376260
  0.6 12.1 %copy-start.2 = (s32[1,64]{1,0:T(1,128)S(1)}, s32[1,64]{1,0:T(1,128)}, u32[]{:S(2)}) copy-start(s32[1,64]{1,0:T(1,128)} %index_ref.1) | copy-start | bytes 772
  0.7 12.1 %copy-start.3 = (s32[1,64]{1,0:T(1,128)S(1)}, s32[1,64]{1,0:T(1,128)}, u32[]{:S(2)}) copy-start(s32[1,64]{1,0:T(1,128)} %count_ref.1) | copy-start | bytes 772
  6.9 13.8 %collective-permute-start = (f32[14,16,128]{2,1,0:T(8,128)}, f32[14,16,128]{2,1,0:T(8,128)S(1)}, u32[]{:S(2)}, u32[]{:S(2)}) collective-permute-start(f32[14,16,128]{2,1,0:T(8,128)} %get-tuple-element.51), channel_id=1, source_target_pairs={{0,24},{1,25},{2,26},{3,27},{4,28},{5,29},{6,30},{7,31},{8,16},{9,... | collective-permute-start | bytes 344072 | tf_op jit(solution)/shard_map/ppermute | solution.py:475
  12.1 9.9 %collective-permute-start.1 = (f32[14,16,128]{2,1,0:T(8,128)}, f32[14,16,128]{2,1,0:T(8,128)S(1)}, u32[]{:S(2)}, u32[]{:S(2)}) collective-permute-start(f32[14,16,128]{2,1,0:T(8,128)} %get-tuple-element.52), channel_id=1, source_target_pairs={{0,16},{1,17},{2,18},{3,19},{4,20},{5,21},{6,22},{7,23},{8,24},{9,... | collective-permute-start | bytes 344072 | tf_op jit(solution)/shard_map/ppermute | solution.py:475
  12.1 9.9 %collective-permute-start.2 = (f32[14,16,128]{2,1,0:T(8,128)}, f32[14,16,128]{2,1,0:T(8,128)S(1)}, u32[]{:S(2)}, u32[]{:S(2)}) collective-permute-start(f32[14,16,128]{2,1,0:T(8,128)} %get-tuple-element.53), channel_id=1, source_target_pairs={{0,8},{1,9},{2,10},{3,11},{4,12},{5,13},{6,14},{7,15},{8,0},{9,1},... | collective-permute-start | bytes 344072 | tf_op jit(solution)/shard_map/ppermute | solution.py:475
  13.1 8.8 %copy-start.1 = (f32[14,16,128]{2,1,0:T(8,128)S(1)}, f32[14,16,128]{2,1,0:T(8,128)}, u32[]{:S(2)}) copy-start(f32[14,16,128]{2,1,0:T(8,128)} %get-tuple-element.62.refs_3_) | copy-start | bytes 344068
  22.3 12.8 %collective-permute-start.3 = (f32[14,16,128]{2,1,0:T(8,128)S(1)}, f32[14,16,128]{2,1,0:T(8,128)S(1)}, u32[]{:S(2)}, u32[]{:S(2)}) collective-permute-start(f32[14,16,128]{2,1,0:T(8,128)S(1)} %get-tuple-element.65), channel_id=1, source_target_pairs={{0,24},{1,25},{2,26},{3,27},{4,28},{5,29},{6,30},{7,31},{8,16},{9,... | collective-permute-start | bytes 344072 | tf_op jit(solution)/shard_map/ppermute | solution.py:475
  24.9 10.2 %collective-permute-start.4 = (f32[14,16,128]{2,1,0:T(8,128)S(1)}, f32[14,16,128]{2,1,0:T(8,128)S(1)}, u32[]{:S(2)}, u32[]{:S(2)}) collective-permute-start(f32[14,16,128]{2,1,0:T(8,128)S(1)} %get-tuple-element.66), channel_id=1, source_target_pairs={{0,16},{1,17},{2,18},{3,19},{4,20},{5,21},{6,22},{7,23},{8,24},{9,... | collective-permute-start | bytes 344072 | tf_op jit(solution)/shard_map/ppermute | solution.py:475
  24.9 10.2 %collective-permute-start.5 = (f32[14,16,128]{2,1,0:T(8,128)S(1)}, f32[14,16,128]{2,1,0:T(8,128)S(1)}, u32[]{:S(2)}, u32[]{:S(2)}) collective-permute-start(f32[14,16,128]{2,1,0:T(8,128)S(1)} %get-tuple-element.67), channel_id=1, source_target_pairs={{0,8},{1,9},{2,10},{3,11},{4,12},{5,13},{6,14},{7,15},{8,0},{9,1},... | collective-permute-start | bytes 344072 | tf_op jit(solution)/shard_map/ppermute | solution.py:475
  39.4 3.7 %collective-permute-start.6 = (f32[256,1152]{1,0:T(8,128)S(1)}, f32[256,1152]{1,0:T(8,128)S(1)}, u32[]{:S(2)}, u32[]{:S(2)}) collective-permute-start(f32[256,1152]{1,0:T(8,128)S(1)} %get-tuple-element.79), channel_id=1, source_target_pairs={{0,2},{1,3},{2,0},{3,1},{4,6},{5,7},{6,4},{7,5},{8,10},{9,11},{10,... | collective-permute-start | bytes 3538952 | tf_op jit(solution)/shard_map/ppermute | solution.py:475
  42.6 6.3 %collective-permute-start.8 = (f32[256,1152]{1,0:T(8,128)S(1)}, f32[256,1152]{1,0:T(8,128)S(1)}, u32[]{:S(2)}, u32[]{:S(2)}) collective-permute-start(f32[256,1152]{1,0:T(8,128)S(1)} %get-tuple-element.86), channel_id=1, source_target_pairs={{0,2},{1,3},{2,0},{3,1},{4,6},{5,7},{6,4},{7,5},{8,10},{9,11},{10,... | collective-permute-start | bytes 3538952 | tf_op jit(solution)/shard_map/ppermute | solution.py:475
  43.3 6.8 %collective-permute-start.9 = (f32[64,1152]{1,0:T(8,128)S(1)}, f32[64,1152]{1,0:T(8,128)S(1)}, u32[]{:S(2)}, u32[]{:S(2)}) collective-permute-start(f32[64,1152]{1,0:T(8,128)S(1)} %get-tuple-element.87), channel_id=1, source_target_pairs={{0,4},{1,5},{2,3},{3,2},{4,0},{5,1},{6,7},{7,6},{8,12},{9,13},{10,... | collective-permute-start | bytes 884744 | tf_op jit(solution)/shard_map/ppermute | solution.py:475
  44.8 9.6 %collective-permute-start.12 = (f32[64,1152]{1,0:T(8,128)S(1)}, f32[64,1152]{1,0:T(8,128)S(1)}, u32[]{:S(2)}, u32[]{:S(2)}) collective-permute-start(f32[64,1152]{1,0:T(8,128)S(1)} %get-tuple-element.91), channel_id=1, source_target_pairs={{0,4},{1,5},{2,3},{3,2},{4,0},{5,1},{6,7},{7,6},{8,12},{9,13},{10,... | collective-permute-start | bytes 884744 | tf_op jit(solution)/shard_map/ppermute | solution.py:475
  45.4 14.3 %collective-permute-start.15 = (f32[64,1152]{1,0:T(8,128)S(1)}, f32[64,1152]{1,0:T(8,128)S(1)}, u32[]{:S(2)}, u32[]{:S(2)}) collective-permute-start(f32[64,1152]{1,0:T(8,128)S(1)} %get-tuple-element.94), channel_id=1, source_target_pairs={{0,4},{1,5},{2,3},{3,2},{4,0},{5,1},{6,7},{7,6},{8,12},{9,13},{10,... | collective-permute-start | bytes 884744 | tf_op jit(solution)/shard_map/ppermute | solution.py:475
  50.1 6.9 %collective-permute-start.10 = (f32[32,1152]{1,0:T(8,128)S(1)}, f32[32,1152]{1,0:T(8,128)S(1)}, u32[]{:S(2)}, u32[]{:S(2)}) collective-permute-start(f32[32,1152]{1,0:T(8,128)S(1)} %get-tuple-element.89), channel_id=1, source_target_pairs={{0,1},{1,0},{2,6},{3,7},{4,5},{5,4},{6,2},{7,3},{8,9},{9,8},{10,14... | collective-permute-start | bytes 442376 | tf_op jit(solution)/shard_map/ppermute | solution.py:475
  51.7 12.6 %collective-permute-start.7 = (f32[64,1152]{1,0:T(8,128)S(1)}, f32[64,1152]{1,0:T(8,128)S(1)}, u32[]{:S(2)}, u32[]{:S(2)}) collective-permute-start(f32[64,1152]{1,0:T(8,128)S(1)} %get-tuple-element.84), channel_id=1, source_target_pairs={{0,4},{1,5},{2,3},{3,2},{4,0},{5,1},{6,7},{7,6},{8,12},{9,13},{10,... | collective-permute-start | bytes 884744 | tf_op jit(solution)/shard_map/ppermute | solution.py:475
  54.5 6.9 %collective-permute-start.13 = (f32[32,1152]{1,0:T(8,128)S(1)}, f32[32,1152]{1,0:T(8,128)S(1)}, u32[]{:S(2)}, u32[]{:S(2)}) collective-permute-start(f32[32,1152]{1,0:T(8,128)S(1)} %get-tuple-element.93), channel_id=1, source_target_pairs={{0,1},{1,0},{2,6},{3,7},{4,5},{5,4},{6,2},{7,3},{8,9},{9,8},{10,14... | collective-permute-start | bytes 442376 | tf_op jit(solution)/shard_map/ppermute | solution.py:475
  57.0 8.2 %collective-permute-start.11 = (f32[32,1152]{1,0:T(8,128)S(1)}, f32[32,1152]{1,0:T(8,128)S(1)}, u32[]{:S(2)}, u32[]{:S(2)}) collective-permute-start(f32[32,1152]{1,0:T(8,128)S(1)} %add_rows.11), channel_id=1, source_target_pairs={{0,24},{1,25},{2,26},{3,27},{4,28},{5,29},{6,30},{7,31},{8,16},{9,... | collective-permute-start | bytes 442376 | tf_op jit(solution)/shard_map/ppermute | solution.py:475
  59.7 7.2 %collective-permute-start.16 = (f32[32,1152]{1,0:T(8,128)S(1)}, f32[32,1152]{1,0:T(8,128)S(1)}, u32[]{:S(2)}, u32[]{:S(2)}) collective-permute-start(f32[32,1152]{1,0:T(8,128)S(1)} %get-tuple-element.96), channel_id=1, source_target_pairs={{0,1},{1,0},{2,6},{3,7},{4,5},{5,4},{6,2},{7,3},{8,9},{9,8},{10,14... | collective-permute-start | bytes 442376 | tf_op jit(solution)/shard_map/ppermute | solution.py:475
  61.4 9.6 %collective-permute-start.14 = (f32[32,1152]{1,0:T(8,128)S(1)}, f32[32,1152]{1,0:T(8,128)S(1)}, u32[]{:S(2)}, u32[]{:S(2)}) collective-permute-start(f32[32,1152]{1,0:T(8,128)S(1)} %add_rows.13), channel_id=1, source_target_pairs={{0,16},{1,17},{2,18},{3,19},{4,20},{5,21},{6,22},{7,23},{8,24},{9,... | collective-permute-start | bytes 442376 | tf_op jit(solution)/shard_map/ppermute | solution.py:475
  65.3 5.5 %collective-permute-start.18 = (f32[32,1152]{1,0:T(8,128)S(1)}, f32[32,1152]{1,0:T(8,128)S(1)}, u32[]{:S(2)}, u32[]{:S(2)}) collective-permute-start(f32[32,1152]{1,0:T(8,128)S(1)} %get-tuple-element.99), channel_id=1, source_target_pairs={{0,1},{1,0},{2,6},{3,7},{4,5},{5,4},{6,2},{7,3},{8,9},{9,8},{10,14... | collective-permute-start | bytes 442376 | tf_op jit(solution)/shard_map/ppermute | solution.py:475
  66.9 7.0 %collective-permute-start.17 = (f32[32,1152]{1,0:T(8,128)S(1)}, f32[32,1152]{1,0:T(8,128)S(1)}, u32[]{:S(2)}, u32[]{:S(2)}) collective-permute-start(f32[32,1152]{1,0:T(8,128)S(1)} %add_rows.15), channel_id=1, source_target_pairs={{0,8},{1,9},{2,10},{3,11},{4,12},{5,13},{6,14},{7,15},{8,0},{9,1},... | collective-permute-start | bytes 442376 | tf_op jit(solution)/shard_map/ppermute | solution.py:475

commit v8 on v7

--- a/solution.py
+++ b/solution.py
@@ -159,10 +159,10 @@
             jax.ShapeDtypeStruct((nrows, width), jnp.float32),
             jax.ShapeDtypeStruct((nrows, width), jnp.bfloat16),
         ],
-        compiler_params=params(MOST),
+        compiler_params=params(FEW),
         cost_estimate=cost(2 * nrows * width * depth, 4 * MIB),
         name="slopes",
-    )(rows_in, w_in)
+    )(in_hbm(rows_in), in_hbm(w_in))
 
 
 def order_body(source_of, table_ref, latent_ref, hidden_ref, out_ref, choice):
@@ -190,10 +190,10 @@
         out_specs=pl.BlockSpec((2, picked, block), lambda i: (0, 0, i)),
         out_shape=jax.ShapeDtypeStruct((2, picked, nrows), jnp.bfloat16),
         scratch_shapes=[pltpu.VMEM((picked, extent), jnp.bfloat16)],
-        compiler_params=params(MOST),
+        compiler_params=params(FEW),
         cost_estimate=cost(nrows * extent * picked, 4 * MIB),
         name="ordered_transposes",
-    )(table, latent, hidden)
+    )(table, in_hbm(latent), hidden)
 
 
 def target_body(channels, pool_ref, index_ref, count_ref, target_ref, weight_ref):
@@ -276,27 +276,10 @@
 
 
 def first_body(parts, *refs):
-    scored_refs, refs = refs[:parts], refs[parts:]
-    slope_ref, w_out_t_ref, ordered_ref, result, gp, g, slope, w_out_t, latent_t, hidden_t, cells, in_sems, slope_sems = refs
+    scored_refs, (slope, w_out_t, ordered, result, gp, g, cells) = refs[:parts], refs[parts:]
     carriers, share, _ = scored_refs[0].shape
     channels, width = w_out_t.shape
     picked = result.shape[0]
-    column = column_steps(width)
-    w_copy, hidden_copy, latent_copy = copies = [
-        pltpu.make_async_copy(source, target, in_sems.at[k])
-        for k, (source, target) in enumerate([
-            (w_out_t_ref, w_out_t),
-            (ordered_ref.at[1, pl.ds(0, picked)], hidden_t),
-            (ordered_ref.at[0, pl.ds(0, picked)], latent_t),
-        ])
-    ]
-    slope_copies = [
-        pltpu.make_async_copy(slope_ref.at[:, pl.ds(c.start, c.stop - c.start)], slope.at[:, c], slope_sems.at[k])
-        for k, c in enumerate(column)
-    ]
-    for copy in [*copies, *slope_copies]:
-        copy.start()
-
     me_z = lax.axis_index("member")
     for k, scored_ref in zip(reversed(range(parts)), scored_refs):
         base = partner(me_z, k, parts) * (share * PATCH)
@@ -304,67 +287,43 @@
             cells[pl.ds(base + j, share, stride=PATCH), :] = value
     lane = lax.broadcasted_iota(jnp.int32, cells.shape, 1)
     g[...] = jnp.where(lane < channels, cells[...], 0.0).astype(jnp.bfloat16)
-    w_copy.wait()
-    backward = [
-        jnp.dot(g[:, :channels], w_out_t[:, c], preferred_element_type=jnp.float32) for c in column
-    ]
-    hidden_copy.wait()
-    result[:, width:] = jnp.dot(hidden_t[...], g[...], preferred_element_type=jnp.float32)
-    latent_copy.wait()
-    for k, c in enumerate(column):
-        slope_copies[k].wait()
-        gp[:, c] = (backward[k] * slope[:, c]).astype(jnp.bfloat16)
-        result[:, c] = jnp.dot(latent_t[...], gp[:, c], preferred_element_type=jnp.float32)
+    result[:, width:] = jnp.dot(ordered[1, :picked], g[...], preferred_element_type=jnp.float32)
+    for c in column_steps(width):
+        backward = jnp.dot(g[:, :channels], w_out_t[:, c], preferred_element_type=jnp.float32)
+        gp[:, c] = (backward * slope[:, c]).astype(jnp.bfloat16)
+        result[:, c] = jnp.dot(ordered[0, :picked], gp[:, c], preferred_element_type=jnp.float32)
 
 
 def first_products(scored, slope, w_out_t, ordered, picked):
     nrows, width = slope.shape
     channels = w_out_t.shape[0]
-    steps = len(column_steps(width))
     return pl.pallas_call(
         functools.partial(first_body, len(scored)),
-        in_specs=[*[WHOLE] * len(scored), ANY, ANY, ANY],
+        in_specs=[WHOLE] * (len(scored) + 3),
         out_specs=[WHOLE] * 3,
         out_shape=[
             jax.ShapeDtypeStruct((picked, width + LANES), jnp.float32),
             jax.ShapeDtypeStruct((nrows, width), jnp.bfloat16),
             jax.ShapeDtypeStruct((nrows, LANES), jnp.bfloat16),
         ],
-        scratch_shapes=[
-            pltpu.VMEM(slope.shape, jnp.float32),
-            pltpu.VMEM(w_out_t.shape, jnp.bfloat16),
-            pltpu.VMEM((picked, nrows), jnp.bfloat16),
-            pltpu.VMEM((picked, nrows), jnp.bfloat16),
-            pltpu.VMEM((nrows, LANES), jnp.float32),
-            pltpu.SemaphoreType.DMA((3,)),
-            pltpu.SemaphoreType.DMA((steps,)),
-        ],
+        scratch_shapes=[pltpu.VMEM((nrows, LANES), jnp.float32)],
         compiler_params=params(FEW),
         cost_estimate=cost(2 * nrows * width * (channels + picked), 10 * MIB),
         name="first_products",
-    )(*scored, in_hbm(slope), in_hbm(w_out_t), in_hbm(ordered))
-
-
-def more_body(cuts, gp, g, ordered_ref, *refs):
-    out_refs, (latent_t, hidden_t, in_sems) = refs[:len(cuts)], refs[len(cuts):]
-    low, (picked, _) = cuts[0][0], latent_t.shape
+    )(*scored, slope, w_out_t, ordered)
+
+
+def more_body(cuts, gp, g, ordered, *out_refs):
+    low, high = cuts[0][0], cuts[-1][1]
     width = gp.shape[1]
-    copies = [
-        pltpu.make_async_copy(ordered_ref.at[k, pl.ds(low, picked)], target, in_sems.at[k])
-        for k, target in enumerate((latent_t, hidden_t))
-    ]
-    for copy in copies:
-        copy.start()
 
     def put(columns, product):
         for out_ref, (start, end) in zip(out_refs, cuts):
             out_ref[:, columns] = product[start - low:end - low]
 
-    for copy in copies:
-        copy.wait()
     for columns in column_steps(width):
-        put(columns, jnp.dot(latent_t[...], gp[:, columns], preferred_element_type=jnp.float32))
-    put(slice(width, None), jnp.dot(hidden_t[...], g[...], preferred_element_type=jnp.float32))
+        put(columns, jnp.dot(ordered[0, low:high], gp[:, columns], preferred_element_type=jnp.float32))
+    put(slice(width, None), jnp.dot(ordered[1, low:high], g[...], preferred_element_type=jnp.float32))
 
 
 def more_products(gp, g, ordered, cuts):
@@ -372,18 +331,13 @@
     picked = cuts[-1][1] - cuts[0][0]
     return pl.pallas_call(
         functools.partial(more_body, tuple(cuts)),
-        in_specs=[WHOLE, WHOLE, ANY],
+        in_specs=[WHOLE] * 3,
         out_specs=[WHOLE] * len(cuts),
         out_shape=[jax.ShapeDtypeStruct((end - start, width + LANES), jnp.float32) for start, end in cuts],
-        scratch_shapes=[
-            pltpu.VMEM((picked, nrows), jnp.bfloat16),
-            pltpu.VMEM((picked, nrows), jnp.bfloat16),
-            pltpu.SemaphoreType.DMA((2,)),
-        ],
         compiler_params=params(FEW),
         cost_estimate=cost(2 * nrows * picked * width, 6 * MIB),
         name="more_products",
-    )(gp, g, in_hbm(ordered))
+    )(gp, g, ordered)
 
 
 def add_body(plans, count, *refs):
@@ -397,7 +351,7 @@
             out_ref[at:at + rows] = total
 
 
-def add_rows(inputs, plans):
+def add_rows(inputs, plans, flops=0):
     columns = inputs[0].shape[1]
     sizes = [sum(rows for _, rows, _ in plan) for plan in plans]
     return pl.pallas_call(
@@ -406,7 +360,7 @@
         out_specs=[WHOLE] * len(plans),
         out_shape=[jax.ShapeDtypeStruct((size, columns), jnp.float32) for size in sizes],
         compiler_params=params(),
-        cost_estimate=cost(3 * sum(sizes) * columns, 12 * sum(sizes) * columns),
+        cost_estimate=cost(flops or 3 * sum(sizes) * columns, 12 * sum(sizes) * columns),
         name="add_rows",
     )(*inputs)
 
@@ -440,18 +394,23 @@
 def row_order(nz, nx, nc, ny, height):
     first_last, second_last = [[*range(1, n), 0] for n in (nx, ny)]
     z_last = [*reversed(range(nz))]
-    step = max(nz // 4, 1)
-    chunks = [z_last[low:low + step] for low in range(0, nz, step)]
+    by_neighbour = nz > 1 and nz & (nz - 1) == 0
+    far = [k for k in z_last if k > 1] if by_neighbour else z_last
+    chunks = [ks for ks in ([k for k in far if k % 2], [k for k in far if k % 2 == 0]) if ks]
 
     def part(firsts, ks):
         return [(f, s, k, r) for f in firsts for s in second_last for k in ks for r in range(height)]
 
-    halves = [[part(firsts, ks) for ks in chunks] for firsts in (first_last[:-1], [0])]
+    sent, kept = [[part(firsts, ks) for ks in chunks] for firsts in (first_last[:-1], [0])]
+    if by_neighbour:
+        sent.append(part(first_last, [1]))
+        kept.append(part(first_last, [0]))
     table = np.array(
-        [(core, *row) for half in halves for core in [*range(1, nc), 0] for piece in half for row in piece], np.int32
+        [(core, *row) for half in (sent, kept) for core in [*range(1, nc), 0] for piece in half for row in piece],
+        np.int32,
     ).T
-    sent, kept = [[len(piece) for piece in half] for half in halves]
-    return table, chunks, sent, kept
+    sent, kept = [[len(piece) for piece in half] for half in (sent, kept)]
+    return table, chunks, by_neighbour, sent, kept
 
 
 def shards(latent, w_in, w_out, observed, patch_index, counts):
@@ -462,7 +421,7 @@
     nc, nx = CORES, nt // CORES
     w_out_t = w_out.T
     height = depth // (nz * nt * ny)
-    table, chunks, sent, kept = row_order(nz, nx, nc, ny, height)
+    table, chunks, by_neighbour, sent, kept = row_order(nz, nx, nc, ny, height)
     turned = 1 if nx == ny else 0
 
     far_first = [*reversed(range(nz))]
@@ -533,31 +492,40 @@
     own_send, other_keep = more_products(gp, g, ordered, [(n_send, middle), (middle, middle + n_keep)])
     core_keep = shift_core(other_keep, 1)
 
-    def added(inputs, pieces):
-        return list(add_rows(inputs, [[(0, rows, [(i, low) for i in range(len(inputs))])] for low, rows in pieces]))
+    def added(inputs, pieces, flops=0):
+        return list(add_rows(inputs, [[(0, rows, [(i, low) for i in range(len(inputs))])] for low, rows in pieces], flops))
 
     def pieces_of(sizes, low=0):
         return [(low + int(at), size) for at, size in zip(np.cumsum([0, *sizes[:-1]]), sizes)]
 
     first_sends = added([own_send, core_send], pieces_of(sent))
     first_sends, gp = lax.optimization_barrier((first_sends, gp))
-    first_got = [send_all(value, nx - 1, shift_first) for value in first_sends]
+    first_got = [send_all(value, nx - 1, shift_first) for value in first_sends[:len(chunks)]]
+    neighbour = [send_to(value, 1) for value in first_sends[len(chunks):]]
     (own_keep,) = more_products(gp, g, ordered, [(middle + n_keep, middle + 2 * n_keep)])
 
-    joined, early = {}, {}
+    def split_sums(inputs, lows, rows, n):
+        cut = rows // n * (n - 1)
+        plans = [[(0, size, [(i, low + at) for i, low in enumerate(lows)])] for at, size in ((0, cut), (cut, rows - cut))]
+        return add_rows(inputs, plans)
+
+    joined = {}
     for ks, (low, size), got in zip(chunks, pieces_of(kept), first_got):
-        if ks == chunks[-1] and len(chunks) > 1:
-            early[far_first[0]] = send_to(joined[far_first[0]], far_first[0])
-            got, early[far_first[0]] = lax.optimization_barrier((got, early[far_first[0]]))
-        cut = size // ny * (ny - 1)
-        terms = [(0, low), (1, low), *[(2 + i, 0) for i in range(len(got))]]
-        second_send, second_keep = add_rows(
-            [own_keep, core_keep, *got],
-            [[(0, rows, [(i, start + at) for i, start in terms])] for at, rows in ((0, cut), (cut, size - cut))],
-        )
-        got = send_all(second_send, ny - 1, shift_second)
-        joined.update(zip(ks, added([second_keep, *got], pieces_of([height] * len(ks)))))
-    parts = [early[k] if k in early else send_to(joined[k], k) if k else joined[k] for k in far_first]
+        value, keep = split_sums([own_keep, core_keep, *got], [low, low, *[0] * len(got)], size, ny)
+        got = send_all(value, ny - 1, shift_second)
+        joined.update(zip(ks, added([keep, *got], pieces_of([height] * len(ks)))))
+    if not by_neighbour:
+        return tuple(finish(exchange(joined), width, channels))
+
+    near = {k: send_to(joined[k], 1) for k in range(nz - 1, 1, -2)}
+    far = [send_to(added([joined[k], near[k + 1]], [(0, height)])[0], k) for k in range(2, nz, 2)]
+    low, size = pieces_of(kept)[-1]
+    value, keep = split_sums([own_keep, core_keep, *neighbour], [low, low, 0], size, nx)
+    got = send_all(value, nx - 1, shift_first)
+    value, keep = split_sums([keep, *got], [0] * (1 + len(got)), keep.shape[0], ny)
+    parts = [keep, *send_all(value, ny - 1, shift_second)]
+    if far:
+        parts += added(far, [(0, height)], 4e9)
     return tuple(finish(parts, width, channels))
 
 

time: 74.9 us -> 70.3 us (0.939)
  waiting for transfers between devices: 10.4 us -> 23 us
  starting transfers between devices: 29.9 us -> 20.9 us
  Pallas kernels: 33.4 us -> 25.4 us
    ppermute x19 -> x17, waiting for transfers between devices: 10.4 us -> 23 us  [shift(): lax.ppermute(value, ('member', 'tile', 'batch'), [(number(*place), number...]
    ppermute x19 -> x17, starting transfers between devices: 29.9 us -> 20.9 us  [shift(): lax.ppermute(value, ('member', 'tile', 'batch'), [(number(*place), number...]
    pallas_call x2, Pallas kernels: 5.15 us -> 2.37 us  [more_products(): pl.pallas_call(functools.partial(more_body, tuple(cuts)), in_specs=[WHOLE...]
    pallas_call x1, Pallas kernels: 4.3 us -> 1.84 us  [first_products(): pl.pallas_call(functools.partial(first_body, len(scored)), in_specs=[WHOL...]
    pallas_call x1, Pallas kernels: 7.56 us -> 5.82 us  [slopes(): pl.pallas_call(slope_body, grid=(nrows // block,), in_specs=[pl.BlockSpec...]
    pallas_call x1, Pallas kernels: 8.34 us -> 7.24 us  [ordered_transposes(): pl.pallas_call(functools.partial(order_body, source_of), grid=(nrows // b...]
  transfers between devices with their start and end apart: 19 -> 17, of which waited for: 9 -> 8; matrix products, arithmetic and copies ran while one was open for 0% -> 0% of each run, Pallas kernels for 29% -> 23%
where the time goes in v8:
time: 70.3 us; the launch traced here: 70.1 us
  Pallas kernels  25.4 us (36%)
  waiting for transfers between devices  23 us (33%)
  starting transfers between devices  20.9 us (30%)
  between operations  0.82 us (1%)
    ppermute x17, waiting for transfers between devices, shift(): lax.ppermute(value, ('member', 'tile', 'batch'), [(number(*place), number...  23 us
    ppermute x17, starting transfers between devices, shift(): lax.ppermute(value, ('member', 'tile', 'batch'), [(number(*place), number...  20.9 us
    pallas_call x1, Pallas kernels, ordered_transposes(): pl.pallas_call(functools.partial(order_body, source_of), grid=(nrows // b...  7.24 us
    pallas_call x1, Pallas kernels, decode(): pl.pallas_call(functools.partial(decode_body, tuple(pieces)), in_specs=[A...  6.27 us
    pallas_call x1, Pallas kernels, slopes(): pl.pallas_call(slope_body, grid=(nrows // block,), in_specs=[pl.BlockSpec...  5.82 us
    pallas_call x2, Pallas kernels, more_products(): pl.pallas_call(functools.partial(more_body, tuple(cuts)), in_specs=[WHOLE...  2.37 us
    pallas_call x1, Pallas kernels, first_products(): pl.pallas_call(functools.partial(first_body, len(scored)), in_specs=[WHOL...  1.84 us
  transfers between devices with their start and end apart: 17, of which 8 were waited for; matrix products, arithmetic and copies ran while one was open for 0% of the time, Pallas kernels for 23%

profile of v8, /device:TPU:0, one launch (start us, length us, event | category | flops | bytes accessed | tf_op | source)
XLA Modules:
  0.0 70.1 jit_solution(4918216293847627735)
XLA Ops:
  0.7 6.3 %decode.1 = (f32[14,16,128]{2,1,0:T(8,128)}, f32[14,16,128]{2,1,0:T(8,128)}, f32[14,16,128]{2,1,0:T(8,128)}, f32[14,16,128]{2,1,0:T(8,128)}) custom-call(bf16[1024,1024]{1,0:T(8,128)(2,1)} %bitcast.6, bf16[1024,1024]{1,0:T(8,128)(2,1)} %w_in_ref.3, bf16[112,1024]{1,0:T(8,128)(2,1)} %bitcast.4), custom_call_target="tpu_custom_call" | custom-call | flops 2382364672 | bytes 5242880 | tf_op jit(solution)/shard_map/decode/pallas_call | solution.py:111
  6.9 5.1 %collective-permute-start = (f32[14,16,128]{2,1,0:T(8,128)}, f32[14,16,128]{2,1,0:T(8,128)S(1)}, u32[]{:S(2)}, u32[]{:S(2)}) collective-permute-start(f32[14,16,128]{2,1,0:T(8,128)} %get-tuple-element.47), channel_id=1, source_target_pairs={{0,24},{1,25},{2,26},{3,27},{4,28},{5,29},{6,30},{7,31},{8,16},{9,... | collective-permute-start | bytes 344072 | tf_op jit(solution)/shard_map/ppermute | solution.py:434
  12.1 0.6 collective-permute-start.2
  12.7 0.4 targets.1
  13.2 5.8 %slopes.1 = (f32[1024,1024]{1,0:T(8,128)S(1)}, bf16[1024,1024]{1,0:T(8,128)(2,1)S(1)}) custom-call(bf16[1024,1024]{1,0:T(8,128)(2,1)} %bitcast.7, bf16[1024,1024]{1,0:T(8,128)(2,1)} %w_in_ref.3), custom_call_target="tpu_custom_call" | custom-call | flops 2147483648 | bytes 4194304 | tf_op jit(solution)/shard_map/slopes/pallas_call | solution.py:153
  19.0 2.9 %collective-permute-done.1.refs_1_ = f32[14,16,128]{2,1,0:T(8,128)S(1)} collective-permute-done((f32[14,16,128]{2,1,0:T(8,128)}, f32[14,16,128]{2,1,0:T(8,128)S(1)}, u32[]{:S(2)}, u32[]{:S(2)}) %collective-permute-start.1) | collective-permute-done | bytes 114720 | tf_op jit(solution)/shard_map/ppermute | solution.py:434
  21.9 0.3 score.1
  22.3 2.5 %collective-permute-start.3 = (f32[14,16,128]{2,1,0:T(8,128)S(1)}, f32[14,16,128]{2,1,0:T(8,128)S(1)}, u32[]{:S(2)}, u32[]{:S(2)}) collective-permute-start(f32[14,16,128]{2,1,0:T(8,128)S(1)} %get-tuple-element.61), channel_id=1, source_target_pairs={{0,24},{1,25},{2,26},{3,27},{4,28},{5,29},{6,30},{7,31},{8,16},{9,... | collective-permute-start | bytes 344072 | tf_op jit(solution)/shard_map/ppermute | solution.py:434
  24.8 1.9 %collective-permute-start.5 = (f32[14,16,128]{2,1,0:T(8,128)S(1)}, f32[14,16,128]{2,1,0:T(8,128)S(1)}, u32[]{:S(2)}, u32[]{:S(2)}) collective-permute-start(f32[14,16,128]{2,1,0:T(8,128)S(1)} %get-tuple-element.63), channel_id=1, source_target_pairs={{0,8},{1,9},{2,10},{3,11},{4,12},{5,13},{6,14},{7,15},{8,0},{9,1},... | collective-permute-start | bytes 344072 | tf_op jit(solution)/shard_map/ppermute | solution.py:434
  26.7 7.2 %ordered_transposes.1.refs_6_.ordered = bf16[2,1024,1024]{2,1,0:T(8,128)(2,1)S(1)} custom-call(s32[8,1024]{1,0:T(8,128)S(1)} %copy-done.3, bf16[1024,1024]{1,0:T(8,128)(2,1)} %bitcast.8, bf16[1024,1024]{1,0:T(8,128)(2,1)S(1)} %get-tuple-element.65.hidden_ref), custom_call_target="tpu_custom_call" | custom-call | flops 1073741824 | bytes 4194304 | tf_op jit(solution)/shard_map/ordered_transposes/pallas_call | solution.py:182
  34.0 0.1 collective-permute-done.4.refs_1_
  34.1 1.8 %first_products.1 = (f32[256,1152]{1,0:T(8,128)S(1)}, bf16[1024,1024]{1,0:T(8,128)(2,1)S(1)}, bf16[1024,128]{1,0:T(8,128)(2,1)S(1)}) custom-call(f32[14,16,128]{2,1,0:T(8,128)S(1)} %collective-permute-done.3.refs_0_, f32[14,16,128]{2,1,0:T(8,128)S(1)} %collective-permute-done.4.refs_1_, f32[14,16,128]{2,1,0:T(8,128)S(1)} %collective-permute-done.5.refs_2_, ...), custom_call_target="tpu_custom_call" | custom-call | flops 771751936 | bytes 10485760 | tf_op jit(solution)/shard_map/first_products/pallas_call | solution.py:300
  36.1 1.5 %more_products.2 = (f32[256,1152]{1,0:T(8,128)S(1)}, f32[256,1152]{1,0:T(8,128)S(1)}) custom-call(bf16[1024,1024]{1,0:T(8,128)(2,1)S(1)} %get-tuple-element.79.gp, bf16[1024,128]{1,0:T(8,128)(2,1)S(1)} %get-tuple-element.73.g, bf16[2,1024,1024]{2,1,0:T(8,128)(2,1)S(1)} %ordered_transposes.1.refs_6_.ordered), custom_call_target="tpu_custom_call" | custom-call | flops 1073741824 | bytes 6291456 | tf_op jit(solution)/shard_map/more_products/pallas_call | solution.py:332
  37.6 0.6 collective-permute-start.7
  38.2 0.7 %collective-permute-done.6.refs_1_ = f32[256,1152]{1,0:T(8,128)S(1)} collective-permute-done((f32[256,1152]{1,0:T(8,128)S(1)}, f32[256,1152]{1,0:T(8,128)S(1)}, u32[]{:S(2)}, u32[]{:S(2)}) %collective-permute-start.6) | collective-permute-done | bytes 1179680 | tf_op jit(solution)/shard_map/ppermute | solution.py:434
  38.9 0.1 add_rows.9
  39.0 0.1 collective-permute-start.8
  39.1 1.5 %collective-permute-start.13 = (f32[64,1152]{1,0:T(8,128)S(1)}, f32[64,1152]{1,0:T(8,128)S(1)}, u32[]{:S(2)}, u32[]{:S(2)}) collective-permute-start(f32[64,1152]{1,0:T(8,128)S(1)} %get-tuple-element.89), channel_id=1, source_target_pairs={{0,4},{1,5},{2,3},{3,2},{4,0},{5,1},{6,7},{7,6},{8,12},{9,13},{10,... | collective-permute-start | bytes 884744 | tf_op jit(solution)/shard_map/ppermute | solution.py:434
  40.7 0.5 collective-permute-start.11
  41.2 0.8 %more_products.3.refs_0_ = f32[256,1152]{1,0:T(8,128)S(1)} custom-call(bf16[1024,1024]{1,0:T(8,128)(2,1)S(1)} %get-tuple-element.79.gp, bf16[1024,128]{1,0:T(8,128)(2,1)S(1)} %get-tuple-element.73.g, bf16[2,1024,1024]{2,1,0:T(8,128)(2,1)S(1)} %ordered_transposes.1.refs_6_.ordered), custom_call_target="tpu_custom_call" | custom-call | flops 536870912 | bytes 6291456 | tf_op jit(solution)/shard_map/more_products/pallas_call | solution.py:332
  42.0 3.8 %collective-permute-done.13.refs_2_ = f32[64,1152]{1,0:T(8,128)S(1)} collective-permute-done((f32[64,1152]{1,0:T(8,128)S(1)}, f32[64,1152]{1,0:T(8,128)S(1)}, u32[]{:S(2)}, u32[]{:S(2)}) %collective-permute-start.13) | collective-permute-done | bytes 294944 | tf_op jit(solution)/shard_map/ppermute | solution.py:434
  45.9 1.6 %collective-permute-start.14 = (f32[32,1152]{1,0:T(8,128)S(1)}, f32[32,1152]{1,0:T(8,128)S(1)}, u32[]{:S(2)}, u32[]{:S(2)}) collective-permute-start(f32[32,1152]{1,0:T(8,128)S(1)} %get-tuple-element.91), channel_id=1, source_target_pairs={{0,1},{1,0},{2,6},{3,7},{4,5},{5,4},{6,2},{7,3},{8,9},{9,8},{10,14... | collective-permute-start | bytes 442376 | tf_op jit(solution)/shard_map/ppermute | solution.py:434
  47.5 2.6 %collective-permute-done.11.refs_2_ = f32[64,1152]{1,0:T(8,128)S(1)} collective-permute-done((f32[64,1152]{1,0:T(8,128)S(1)}, f32[64,1152]{1,0:T(8,128)S(1)}, u32[]{:S(2)}, u32[]{:S(2)}) %collective-permute-start.11) | collective-permute-done | bytes 294944 | tf_op jit(solution)/shard_map/ppermute | solution.py:434
  50.2 1.6 %collective-permute-start.12 = (f32[32,1152]{1,0:T(8,128)S(1)}, f32[32,1152]{1,0:T(8,128)S(1)}, u32[]{:S(2)}, u32[]{:S(2)}) collective-permute-start(f32[32,1152]{1,0:T(8,128)S(1)} %get-tuple-element.88), channel_id=1, source_target_pairs={{0,1},{1,0},{2,6},{3,7},{4,5},{5,4},{6,2},{7,3},{8,9},{9,8},{10,14... | collective-permute-start | bytes 442376 | tf_op jit(solution)/shard_map/ppermute | solution.py:434
  51.8 2.7 %collective-permute-done.8.refs_2_ = f32[128,1152]{1,0:T(8,128)S(1)} collective-permute-done((f32[128,1152]{1,0:T(8,128)S(1)}, f32[128,1152]{1,0:T(8,128)S(1)}, u32[]{:S(2)}, u32[]{:S(2)}) %collective-permute-start.8) | collective-permute-done | bytes 589856 | tf_op jit(solution)/shard_map/ppermute | solution.py:434
  54.5 1.6 %collective-permute-start.9 = (f32[64,1152]{1,0:T(8,128)S(1)}, f32[64,1152]{1,0:T(8,128)S(1)}, u32[]{:S(2)}, u32[]{:S(2)}) collective-permute-start(f32[64,1152]{1,0:T(8,128)S(1)} %get-tuple-element.83), channel_id=1, source_target_pairs={{0,4},{1,5},{2,3},{3,2},{4,0},{5,1},{6,7},{7,6},{8,12},{9,13},{10,... | collective-permute-start | bytes 884744 | tf_op jit(solution)/shard_map/ppermute | solution.py:434
  56.1 0.4 collective-permute-start.15
  56.5 4.8 %collective-permute-done.15.refs_1_ = f32[32,1152]{1,0:T(8,128)S(1)} collective-permute-done((f32[32,1152]{1,0:T(8,128)S(1)}, f32[32,1152]{1,0:T(8,128)S(1)}, u32[]{:S(2)}, u32[]{:S(2)}) %collective-permute-start.15) | collective-permute-done | bytes 147488 | tf_op jit(solution)/shard_map/ppermute | solution.py:434
  61.4 1.3 %collective-permute-start.16 = (f32[32,1152]{1,0:T(8,128)S(1)}, f32[32,1152]{1,0:T(8,128)S(1)}, u32[]{:S(2)}, u32[]{:S(2)}) collective-permute-start(f32[32,1152]{1,0:T(8,128)S(1)} %add_rows.16), channel_id=1, source_target_pairs={{0,16},{1,17},{2,18},{3,19},{4,20},{5,21},{6,22},{7,23},{8,24},{9,... | collective-permute-start | bytes 442376 | tf_op jit(solution)/shard_map/ppermute | solution.py:434
  62.7 1.6 %collective-permute-start.10 = (f32[32,1152]{1,0:T(8,128)S(1)}, f32[32,1152]{1,0:T(8,128)S(1)}, u32[]{:S(2)}, u32[]{:S(2)}) collective-permute-start(f32[32,1152]{1,0:T(8,128)S(1)} %get-tuple-element.85), channel_id=1, source_target_pairs={{0,1},{1,0},{2,6},{3,7},{4,5},{5,4},{6,2},{7,3},{8,9},{9,8},{10,14... | collective-permute-start | bytes 442376 | tf_op jit(solution)/shard_map/ppermute | solution.py:434
  64.2 5.2 %collective-permute-done.16.refs_0_ = f32[32,1152]{1,0:T(8,128)S(1)} collective-permute-done((f32[32,1152]{1,0:T(8,128)S(1)}, f32[32,1152]{1,0:T(8,128)S(1)}, u32[]{:S(2)}, u32[]{:S(2)}) %collective-permute-start.16) | collective-permute-done | bytes 147488 | tf_op jit(solution)/shard_map/ppermute | solution.py:434
  69.5 0.7 finish.1
  (32 shorter events, 0.4 us)
Async XLA Ops:
  0.6 12.1 %copy-start = (bf16[1,128,1792]{2,1,0:T(8,128)(2,1)S(1)}, bf16[1,128,1792]{2,1,0:T(8,128)(2,1)}, u32[]{:S(2)}) copy-start(bf16[1,128,1792]{2,1,0:T(8,128)(2,1)} %param.10) | copy-start | bytes 1376260
  0.6 12.1 %copy-start.4 = (s32[1,64]{1,0:T(1,128)S(1)}, s32[1,64]{1,0:T(1,128)}, u32[]{:S(2)}) copy-start(s32[1,64]{1,0:T(1,128)} %index_ref.1) | copy-start | bytes 772
  0.7 12.1 %copy-start.5 = (s32[1,64]{1,0:T(1,128)S(1)}, s32[1,64]{1,0:T(1,128)}, u32[]{:S(2)}) copy-start(s32[1,64]{1,0:T(1,128)} %count_ref.1) | copy-start | bytes 772
  6.9 12.1 %collective-permute-start = (f32[14,16,128]{2,1,0:T(8,128)}, f32[14,16,128]{2,1,0:T(8,128)S(1)}, u32[]{:S(2)}, u32[]{:S(2)}) collective-permute-start(f32[14,16,128]{2,1,0:T(8,128)} %get-tuple-element.47), channel_id=1, source_target_pairs={{0,24},{1,25},{2,26},{3,27},{4,28},{5,29},{6,30},{7,31},{8,16},{9,... | collective-permute-start | bytes 344072 | tf_op jit(solution)/shard_map/ppermute | solution.py:434
  12.1 9.9 %collective-permute-start.1 = (f32[14,16,128]{2,1,0:T(8,128)}, f32[14,16,128]{2,1,0:T(8,128)S(1)}, u32[]{:S(2)}, u32[]{:S(2)}) collective-permute-start(f32[14,16,128]{2,1,0:T(8,128)} %get-tuple-element.48), channel_id=1, source_target_pairs={{0,16},{1,17},{2,18},{3,19},{4,20},{5,21},{6,22},{7,23},{8,24},{9,... | collective-permute-start | bytes 344072 | tf_op jit(solution)/shard_map/ppermute | solution.py:434
  12.1 9.9 %collective-permute-start.2 = (f32[14,16,128]{2,1,0:T(8,128)}, f32[14,16,128]{2,1,0:T(8,128)S(1)}, u32[]{:S(2)}, u32[]{:S(2)}) collective-permute-start(f32[14,16,128]{2,1,0:T(8,128)} %get-tuple-element.49), channel_id=1, source_target_pairs={{0,8},{1,9},{2,10},{3,11},{4,12},{5,13},{6,14},{7,15},{8,0},{9,1},... | collective-permute-start | bytes 344072 | tf_op jit(solution)/shard_map/ppermute | solution.py:434
  13.1 8.8 %copy-start.2 = (f32[14,16,128]{2,1,0:T(8,128)S(1)}, f32[14,16,128]{2,1,0:T(8,128)}, u32[]{:S(2)}) copy-start(f32[14,16,128]{2,1,0:T(8,128)} %get-tuple-element.58.refs_3_) | copy-start | bytes 344068
  13.2 13.6 %copy-start.3 = (s32[8,1024]{1,0:T(8,128)S(1)}, s32[8,1024]{1,0:T(8,128)}, u32[]{:S(2)}) copy-start(s32[8,1024]{1,0:T(8,128)} %constant.2.clone.table_ref) | copy-start | bytes 98308
  22.3 11.7 %collective-permute-start.3 = (f32[14,16,128]{2,1,0:T(8,128)S(1)}, f32[14,16,128]{2,1,0:T(8,128)S(1)}, u32[]{:S(2)}, u32[]{:S(2)}) collective-permute-start(f32[14,16,128]{2,1,0:T(8,128)S(1)} %get-tuple-element.61), channel_id=1, source_target_pairs={{0,24},{1,25},{2,26},{3,27},{4,28},{5,29},{6,30},{7,31},{8,16},{9,... | collective-permute-start | bytes 344072 | tf_op jit(solution)/shard_map/ppermute | solution.py:434
  24.8 9.3 %collective-permute-start.4 = (f32[14,16,128]{2,1,0:T(8,128)S(1)}, f32[14,16,128]{2,1,0:T(8,128)S(1)}, u32[]{:S(2)}, u32[]{:S(2)}) collective-permute-start(f32[14,16,128]{2,1,0:T(8,128)S(1)} %get-tuple-element.62), channel_id=1, source_target_pairs={{0,16},{1,17},{2,18},{3,19},{4,20},{5,21},{6,22},{7,23},{8,24},{9,... | collective-permute-start | bytes 344072 | tf_op jit(solution)/shard_map/ppermute | solution.py:434
  24.8 9.3 %copy-start.1 = (bf16[1024,112]{0,1:T(8,128)(2,1)S(1)}, bf16[1024,112]{0,1:T(8,128)(2,1)}, u32[]{:S(2)}) copy-start(bf16[1024,112]{0,1:T(8,128)(2,1)} %param.9) | copy-start | bytes 688132
  24.8 9.3 %collective-permute-start.5 = (f32[14,16,128]{2,1,0:T(8,128)S(1)}, f32[14,16,128]{2,1,0:T(8,128)S(1)}, u32[]{:S(2)}, u32[]{:S(2)}) collective-permute-start(f32[14,16,128]{2,1,0:T(8,128)S(1)} %get-tuple-element.63), channel_id=1, source_target_pairs={{0,8},{1,9},{2,10},{3,11},{4,12},{5,13},{6,14},{7,15},{8,0},{9,1},... | collective-permute-start | bytes 344072 | tf_op jit(solution)/shard_map/ppermute | solution.py:434
  36.0 2.9 %collective-permute-start.6 = (f32[256,1152]{1,0:T(8,128)S(1)}, f32[256,1152]{1,0:T(8,128)S(1)}, u32[]{:S(2)}, u32[]{:S(2)}) collective-permute-start(f32[256,1152]{1,0:T(8,128)S(1)} %get-tuple-element.75), channel_id=1, source_target_pairs={{0,2},{1,3},{2,0},{3,1},{4,6},{5,7},{6,4},{7,5},{8,10},{9,11},{10,... | collective-permute-start | bytes 3538952 | tf_op jit(solution)/shard_map/ppermute | solution.py:434
  37.6 4.4 %collective-permute-start.7 = (f32[256,1152]{1,0:T(8,128)S(1)}, f32[256,1152]{1,0:T(8,128)S(1)}, u32[]{:S(2)}, u32[]{:S(2)}) collective-permute-start(f32[256,1152]{1,0:T(8,128)S(1)} %get-tuple-element.80), channel_id=1, source_target_pairs={{0,2},{1,3},{2,0},{3,1},{4,6},{5,7},{6,4},{7,5},{8,10},{9,11},{10,... | collective-permute-start | bytes 3538952 | tf_op jit(solution)/shard_map/ppermute | solution.py:434
  39.0 15.4 %collective-permute-start.8 = (f32[128,1152]{1,0:T(8,128)S(1)}, f32[128,1152]{1,0:T(8,128)S(1)}, u32[]{:S(2)}, u32[]{:S(2)}) collective-permute-start(f32[128,1152]{1,0:T(8,128)S(1)} %get-tuple-element.81), channel_id=1, source_target_pairs={{0,8},{1,9},{2,10},{3,11},{4,12},{5,13},{6,14},{7,15},{8,0},{9,1},... | collective-permute-start | bytes 1769480 | tf_op jit(solution)/shard_map/ppermute | solution.py:434
  39.1 6.8 %collective-permute-start.13 = (f32[64,1152]{1,0:T(8,128)S(1)}, f32[64,1152]{1,0:T(8,128)S(1)}, u32[]{:S(2)}, u32[]{:S(2)}) collective-permute-start(f32[64,1152]{1,0:T(8,128)S(1)} %get-tuple-element.89), channel_id=1, source_target_pairs={{0,4},{1,5},{2,3},{3,2},{4,0},{5,1},{6,7},{7,6},{8,12},{9,13},{10,... | collective-permute-start | bytes 884744 | tf_op jit(solution)/shard_map/ppermute | solution.py:434
  40.7 9.5 %collective-permute-start.11 = (f32[64,1152]{1,0:T(8,128)S(1)}, f32[64,1152]{1,0:T(8,128)S(1)}, u32[]{:S(2)}, u32[]{:S(2)}) collective-permute-start(f32[64,1152]{1,0:T(8,128)S(1)} %get-tuple-element.86), channel_id=1, source_target_pairs={{0,4},{1,5},{2,3},{3,2},{4,0},{5,1},{6,7},{7,6},{8,12},{9,13},{10,... | collective-permute-start | bytes 884744 | tf_op jit(solution)/shard_map/ppermute | solution.py:434
  45.9 10.2 %collective-permute-start.14 = (f32[32,1152]{1,0:T(8,128)S(1)}, f32[32,1152]{1,0:T(8,128)S(1)}, u32[]{:S(2)}, u32[]{:S(2)}) collective-permute-start(f32[32,1152]{1,0:T(8,128)S(1)} %get-tuple-element.91), channel_id=1, source_target_pairs={{0,1},{1,0},{2,6},{3,7},{4,5},{5,4},{6,2},{7,3},{8,9},{9,8},{10,14... | collective-permute-start | bytes 442376 | tf_op jit(solution)/shard_map/ppermute | solution.py:434
  50.2 6.3 %collective-permute-start.12 = (f32[32,1152]{1,0:T(8,128)S(1)}, f32[32,1152]{1,0:T(8,128)S(1)}, u32[]{:S(2)}, u32[]{:S(2)}) collective-permute-start(f32[32,1152]{1,0:T(8,128)S(1)} %get-tuple-element.88), channel_id=1, source_target_pairs={{0,1},{1,0},{2,6},{3,7},{4,5},{5,4},{6,2},{7,3},{8,9},{9,8},{10,14... | collective-permute-start | bytes 442376 | tf_op jit(solution)/shard_map/ppermute | solution.py:434
  54.5 8.1 %collective-permute-start.9 = (f32[64,1152]{1,0:T(8,128)S(1)}, f32[64,1152]{1,0:T(8,128)S(1)}, u32[]{:S(2)}, u32[]{:S(2)}) collective-permute-start(f32[64,1152]{1,0:T(8,128)S(1)} %get-tuple-element.83), channel_id=1, source_target_pairs={{0,4},{1,5},{2,3},{3,2},{4,0},{5,1},{6,7},{7,6},{8,12},{9,13},{10,... | collective-permute-start | bytes 884744 | tf_op jit(solution)/shard_map/ppermute | solution.py:434
  56.1 5.2 %collective-permute-start.15 = (f32[32,1152]{1,0:T(8,128)S(1)}, f32[32,1152]{1,0:T(8,128)S(1)}, u32[]{:S(2)}, u32[]{:S(2)}) collective-permute-start(f32[32,1152]{1,0:T(8,128)S(1)} %add_rows.15), channel_id=1, source_target_pairs={{0,8},{1,9},{2,10},{3,11},{4,12},{5,13},{6,14},{7,15},{8,0},{9,1},... | collective-permute-start | bytes 442376 | tf_op jit(solution)/shard_map/ppermute | solution.py:434
  61.4 8.1 %collective-permute-start.16 = (f32[32,1152]{1,0:T(8,128)S(1)}, f32[32,1152]{1,0:T(8,128)S(1)}, u32[]{:S(2)}, u32[]{:S(2)}) collective-permute-start(f32[32,1152]{1,0:T(8,128)S(1)} %add_rows.16), channel_id=1, source_target_pairs={{0,16},{1,17},{2,18},{3,19},{4,20},{5,21},{6,22},{7,23},{8,24},{9,... | collective-permute-start | bytes 442376 | tf_op jit(solution)/shard_map/ppermute | solution.py:434
  62.7 6.8 %collective-permute-start.10 = (f32[32,1152]{1,0:T(8,128)S(1)}, f32[32,1152]{1,0:T(8,128)S(1)}, u32[]{:S(2)}, u32[]{:S(2)}) collective-permute-start(f32[32,1152]{1,0:T(8,128)S(1)} %get-tuple-element.85), channel_id=1, source_target_pairs={{0,1},{1,0},{2,6},{3,7},{4,5},{5,4},{6,2},{7,3},{8,9},{9,8},{10,14... | collective-permute-start | bytes 442376 | tf_op jit(solution)/shard_map/ppermute | solution.py:434

commit v9 on v8

--- a/solution.py
+++ b/solution.py
@@ -394,23 +394,19 @@
 def row_order(nz, nx, nc, ny, height):
     first_last, second_last = [[*range(1, n), 0] for n in (nx, ny)]
     z_last = [*reversed(range(nz))]
-    by_neighbour = nz > 1 and nz & (nz - 1) == 0
-    far = [k for k in z_last if k > 1] if by_neighbour else z_last
-    chunks = [ks for ks in ([k for k in far if k % 2], [k for k in far if k % 2 == 0]) if ks]
+    far = [k for k in z_last if k > 1]
+    chunks = [[k for k in far if k % 2], [k for k in far if k % 2 == 0], *[[k] for k in z_last if k < 2]]
+    chunks = [ks for ks in chunks if ks]
 
     def part(firsts, ks):
         return [(f, s, k, r) for f in firsts for s in second_last for k in ks for r in range(height)]
 
-    sent, kept = [[part(firsts, ks) for ks in chunks] for firsts in (first_last[:-1], [0])]
-    if by_neighbour:
-        sent.append(part(first_last, [1]))
-        kept.append(part(first_last, [0]))
+    halves = [[part(firsts, ks) for ks in chunks] for firsts in (first_last[:-1], [0])]
     table = np.array(
-        [(core, *row) for half in (sent, kept) for core in [*range(1, nc), 0] for piece in half for row in piece],
-        np.int32,
+        [(core, *row) for half in halves for core in [*range(1, nc), 0] for piece in half for row in piece], np.int32
     ).T
-    sent, kept = [[len(piece) for piece in half] for half in (sent, kept)]
-    return table, chunks, by_neighbour, sent, kept
+    sent, kept = [[len(piece) for piece in half] for half in halves]
+    return table, chunks, sent, kept
 
 
 def shards(latent, w_in, w_out, observed, patch_index, counts):
@@ -421,7 +417,7 @@
     nc, nx = CORES, nt // CORES
     w_out_t = w_out.T
     height = depth // (nz * nt * ny)
-    table, chunks, by_neighbour, sent, kept = row_order(nz, nx, nc, ny, height)
+    table, chunks, sent, kept = row_order(nz, nx, nc, ny, height)
     turned = 1 if nx == ny else 0
 
     far_first = [*reversed(range(nz))]
@@ -500,33 +496,31 @@
 
     first_sends = added([own_send, core_send], pieces_of(sent))
     first_sends, gp = lax.optimization_barrier((first_sends, gp))
-    first_got = [send_all(value, nx - 1, shift_first) for value in first_sends[:len(chunks)]]
-    neighbour = [send_to(value, 1) for value in first_sends[len(chunks):]]
+    first_got = [send_all(value, nx - 1, shift_first) for value in first_sends]
     (own_keep,) = more_products(gp, g, ordered, [(middle + n_keep, middle + 2 * n_keep)])
 
-    def split_sums(inputs, lows, rows, n):
-        cut = rows // n * (n - 1)
-        plans = [[(0, size, [(i, low + at) for i, low in enumerate(lows)])] for at, size in ((0, cut), (cut, rows - cut))]
-        return add_rows(inputs, plans)
-
-    joined = {}
+    joined, near = {}, {}
     for ks, (low, size), got in zip(chunks, pieces_of(kept), first_got):
-        value, keep = split_sums([own_keep, core_keep, *got], [low, low, *[0] * len(got)], size, ny)
-        got = send_all(value, ny - 1, shift_second)
-        joined.update(zip(ks, added([keep, *got], pieces_of([height] * len(ks)))))
-    if not by_neighbour:
+        if ks == chunks[-1] and len(chunks) > 3 and nz & (nz - 1) == 0:
+            near = {k: send_to(joined[k], 1) for k in chunks[0]}
+            got, near = lax.optimization_barrier((got, near))
+        cut = size // ny * (ny - 1)
+        terms = [(0, low), (1, low), *[(2 + i, 0) for i in range(len(got))]]
+        second_send, second_keep = add_rows(
+            [own_keep, core_keep, *got],
+            [[(0, rows, [(i, start + at) for i, start in terms])] for at, rows in ((0, cut), (cut, size - cut))],
+        )
+        got = send_all(second_send, ny - 1, shift_second)
+        joined.update(zip(ks, added([second_keep, *got], pieces_of([height] * len(ks)))))
+
+    if nz & (nz - 1):
         return tuple(finish(exchange(joined), width, channels))
-
-    near = {k: send_to(joined[k], 1) for k in range(nz - 1, 1, -2)}
+    near.update({k: send_to(joined[k], 1) for k in range(1, nz, 2) if k not in near})
+    parts = [joined[0], *([near[1]] if near else [])]
     far = [send_to(added([joined[k], near[k + 1]], [(0, height)])[0], k) for k in range(2, nz, 2)]
-    low, size = pieces_of(kept)[-1]
-    value, keep = split_sums([own_keep, core_keep, *neighbour], [low, low, 0], size, nx)
-    got = send_all(value, nx - 1, shift_first)
-    value, keep = split_sums([keep, *got], [0] * (1 + len(got)), keep.shape[0], ny)
-    parts = [keep, *send_all(value, ny - 1, shift_second)]
     if far:
-        parts += added(far, [(0, height)], 4e9)
-    return tuple(finish(parts, width, channels))
+        parts += added(far, [(0, height)], 1.2e10)
+    return tuple(finish(parts[::-1], width, channels))
 
 
 def solution(mesh):

time: 70.3 us -> 69.3 us (0.986)
  waiting for transfers between devices: 23 us -> 17.4 us
  starting transfers between devices: 20.9 us -> 25.5 us
    ppermute x17 -> x19, waiting for transfers between devices: 23 us -> 17.4 us  [shift(): lax.ppermute(value, ('member', 'tile', 'batch'), [(number(*place), number...]
    ppermute x17 -> x19, starting transfers between devices: 20.9 us -> 25.5 us  [shift(): lax.ppermute(value, ('member', 'tile', 'batch'), [(number(*place), number...]
  transfers between devices with their start and end apart: 17 -> 19, of which waited for: 8 -> 10; matrix products, arithmetic and copies ran while one was open for 0% -> 0% of each run, Pallas kernels for 23% -> 24%
where the time goes in v9:
time: 69.3 us; the launch traced here: 69.1 us
  starting transfers between devices  25.5 us (37%)
  Pallas kernels  25.4 us (37%)
  waiting for transfers between devices  17.4 us (25%)
  between operations  0.82 us (1%)
    ppermute x19, starting transfers between devices, shift(): lax.ppermute(value, ('member', 'tile', 'batch'), [(number(*place), number...  25.5 us
    ppermute x19, waiting for transfers between devices, shift(): lax.ppermute(value, ('member', 'tile', 'batch'), [(number(*place), number...  17.4 us
    pallas_call x1, Pallas kernels, ordered_transposes(): pl.pallas_call(functools.partial(order_body, source_of), grid=(nrows // b...  7.25 us
    pallas_call x1, Pallas kernels, decode(): pl.pallas_call(functools.partial(decode_body, tuple(pieces)), in_specs=[A...  6.28 us
    pallas_call x1, Pallas kernels, slopes(): pl.pallas_call(slope_body, grid=(nrows // block,), in_specs=[pl.BlockSpec...  5.82 us
    pallas_call x2, Pallas kernels, more_products(): pl.pallas_call(functools.partial(more_body, tuple(cuts)), in_specs=[WHOLE...  2.37 us
    pallas_call x1, Pallas kernels, first_products(): pl.pallas_call(functools.partial(first_body, len(scored)), in_specs=[WHOL...  1.84 us
  transfers between devices with their start and end apart: 19, of which 10 were waited for; matrix products, arithmetic and copies ran while one was open for 0% of the time, Pallas kernels for 24%

profile of v9, /device:TPU:0, one launch (start us, length us, event | category | flops | bytes accessed | tf_op | source)
XLA Modules:
  0.0 69.1 jit_solution(7524858991010239935)
XLA Ops:
  0.7 6.3 %decode.1 = (f32[14,16,128]{2,1,0:T(8,128)}, f32[14,16,128]{2,1,0:T(8,128)}, f32[14,16,128]{2,1,0:T(8,128)}, f32[14,16,128]{2,1,0:T(8,128)}) custom-call(bf16[1024,1024]{1,0:T(8,128)(2,1)} %bitcast.6, bf16[1024,1024]{1,0:T(8,128)(2,1)} %w_in_ref.3, bf16[112,1024]{1,0:T(8,128)(2,1)} %bitcast.4), custom_call_target="tpu_custom_call" | custom-call | flops 2382364672 | bytes 5242880 | tf_op jit(solution)/shard_map/decode/pallas_call | solution.py:111
  6.9 5.1 %collective-permute-start = (f32[14,16,128]{2,1,0:T(8,128)}, f32[14,16,128]{2,1,0:T(8,128)S(1)}, u32[]{:S(2)}, u32[]{:S(2)}) collective-permute-start(f32[14,16,128]{2,1,0:T(8,128)} %get-tuple-element.51), channel_id=1, source_target_pairs={{0,24},{1,25},{2,26},{3,27},{4,28},{5,29},{6,30},{7,31},{8,16},{9,... | collective-permute-start | bytes 344072 | tf_op jit(solution)/shard_map/ppermute | solution.py:430
  12.1 0.6 collective-permute-start.2
  12.7 0.4 targets.1
  13.2 5.8 %slopes.1 = (f32[1024,1024]{1,0:T(8,128)S(1)}, bf16[1024,1024]{1,0:T(8,128)(2,1)S(1)}) custom-call(bf16[1024,1024]{1,0:T(8,128)(2,1)} %bitcast.7, bf16[1024,1024]{1,0:T(8,128)(2,1)} %w_in_ref.3), custom_call_target="tpu_custom_call" | custom-call | flops 2147483648 | bytes 4194304 | tf_op jit(solution)/shard_map/slopes/pallas_call | solution.py:153
  19.0 2.9 %collective-permute-done.1.refs_1_ = f32[14,16,128]{2,1,0:T(8,128)S(1)} collective-permute-done((f32[14,16,128]{2,1,0:T(8,128)}, f32[14,16,128]{2,1,0:T(8,128)S(1)}, u32[]{:S(2)}, u32[]{:S(2)}) %collective-permute-start.1) | collective-permute-done | bytes 114720 | tf_op jit(solution)/shard_map/ppermute | solution.py:430
  22.3 2.5 %collective-permute-start.3 = (f32[14,16,128]{2,1,0:T(8,128)S(1)}, f32[14,16,128]{2,1,0:T(8,128)S(1)}, u32[]{:S(2)}, u32[]{:S(2)}) collective-permute-start(f32[14,16,128]{2,1,0:T(8,128)S(1)} %get-tuple-element.65), channel_id=1, source_target_pairs={{0,24},{1,25},{2,26},{3,27},{4,28},{5,29},{6,30},{7,31},{8,16},{9,... | collective-permute-start | bytes 344072 | tf_op jit(solution)/shard_map/ppermute | solution.py:430
  24.8 1.9 %collective-permute-start.5 = (f32[14,16,128]{2,1,0:T(8,128)S(1)}, f32[14,16,128]{2,1,0:T(8,128)S(1)}, u32[]{:S(2)}, u32[]{:S(2)}) collective-permute-start(f32[14,16,128]{2,1,0:T(8,128)S(1)} %get-tuple-element.67), channel_id=1, source_target_pairs={{0,8},{1,9},{2,10},{3,11},{4,12},{5,13},{6,14},{7,15},{8,0},{9,1},... | collective-permute-start | bytes 344072 | tf_op jit(solution)/shard_map/ppermute | solution.py:430
  26.7 7.2 %ordered_transposes.1.refs_6_.ordered = bf16[2,1024,1024]{2,1,0:T(8,128)(2,1)S(1)} custom-call(s32[8,1024]{1,0:T(8,128)S(1)} %copy-done.3, bf16[1024,1024]{1,0:T(8,128)(2,1)} %bitcast.8, bf16[1024,1024]{1,0:T(8,128)(2,1)S(1)} %get-tuple-element.69.hidden_ref), custom_call_target="tpu_custom_call" | custom-call | flops 1073741824 | bytes 4194304 | tf_op jit(solution)/shard_map/ordered_transposes/pallas_call | solution.py:182
  34.1 1.8 %first_products.1 = (f32[256,1152]{1,0:T(8,128)S(1)}, bf16[1024,1024]{1,0:T(8,128)(2,1)S(1)}, bf16[1024,128]{1,0:T(8,128)(2,1)S(1)}) custom-call(f32[14,16,128]{2,1,0:T(8,128)S(1)} %collective-permute-done.3.refs_0_, f32[14,16,128]{2,1,0:T(8,128)S(1)} %collective-permute-done.4.refs_1_, f32[14,16,128]{2,1,0:T(8,128)S(1)} %collective-permute-done.5.refs_2_, ...), custom_call_target="tpu_custom_call" | custom-call | flops 771751936 | bytes 10485760 | tf_op jit(solution)/shard_map/first_products/pallas_call | solution.py:300
  36.1 1.5 %more_products.2 = (f32[256,1152]{1,0:T(8,128)S(1)}, f32[256,1152]{1,0:T(8,128)S(1)}) custom-call(bf16[1024,1024]{1,0:T(8,128)(2,1)S(1)} %get-tuple-element.84.gp, bf16[1024,128]{1,0:T(8,128)(2,1)S(1)} %get-tuple-element.77.g, bf16[2,1024,1024]{2,1,0:T(8,128)(2,1)S(1)} %ordered_transposes.1.refs_6_.ordered), custom_call_target="tpu_custom_call" | custom-call | flops 1073741824 | bytes 6291456 | tf_op jit(solution)/shard_map/more_products/pallas_call | solution.py:332
  37.6 0.6 collective-permute-start.7
  38.2 0.7 %collective-permute-done.6.refs_1_ = f32[256,1152]{1,0:T(8,128)S(1)} collective-permute-done((f32[256,1152]{1,0:T(8,128)S(1)}, f32[256,1152]{1,0:T(8,128)S(1)}, u32[]{:S(2)}, u32[]{:S(2)}) %collective-permute-start.6) | collective-permute-done | bytes 1179680 | tf_op jit(solution)/shard_map/ppermute | solution.py:430
  39.0 1.6 %collective-permute-start.11 = (f32[64,1152]{1,0:T(8,128)S(1)}, f32[64,1152]{1,0:T(8,128)S(1)}, u32[]{:S(2)}, u32[]{:S(2)}) collective-permute-start(f32[64,1152]{1,0:T(8,128)S(1)} %get-tuple-element.90), channel_id=1, source_target_pairs={{0,4},{1,5},{2,3},{3,2},{4,0},{5,1},{6,7},{7,6},{8,12},{9,13},{10,... | collective-permute-start | bytes 884744 | tf_op jit(solution)/shard_map/ppermute | solution.py:430
  40.6 0.5 collective-permute-start.8
  41.1 0.8 %more_products.3.refs_0_ = f32[256,1152]{1,0:T(8,128)S(1)} custom-call(bf16[1024,1024]{1,0:T(8,128)(2,1)S(1)} %get-tuple-element.84.gp, bf16[1024,128]{1,0:T(8,128)(2,1)S(1)} %get-tuple-element.77.g, bf16[2,1024,1024]{2,1,0:T(8,128)(2,1)S(1)} %ordered_transposes.1.refs_6_.ordered), custom_call_target="tpu_custom_call" | custom-call | flops 536870912 | bytes 6291456 | tf_op jit(solution)/shard_map/more_products/pallas_call | solution.py:332
  42.0 1.6 %collective-permute-start.15 = (f32[64,1152]{1,0:T(8,128)S(1)}, f32[64,1152]{1,0:T(8,128)S(1)}, u32[]{:S(2)}, u32[]{:S(2)}) collective-permute-start(f32[64,1152]{1,0:T(8,128)S(1)} %get-tuple-element.94), channel_id=1, source_target_pairs={{0,4},{1,5},{2,3},{3,2},{4,0},{5,1},{6,7},{7,6},{8,12},{9,13},{10,... | collective-permute-start | bytes 884744 | tf_op jit(solution)/shard_map/ppermute | solution.py:430
  43.5 2.3 %collective-permute-done.11.refs_2_ = f32[64,1152]{1,0:T(8,128)S(1)} collective-permute-done((f32[64,1152]{1,0:T(8,128)S(1)}, f32[64,1152]{1,0:T(8,128)S(1)}, u32[]{:S(2)}, u32[]{:S(2)}) %collective-permute-start.11) | collective-permute-done | bytes 294944 | tf_op jit(solution)/shard_map/ppermute | solution.py:430
  45.9 1.6 %collective-permute-start.12 = (f32[32,1152]{1,0:T(8,128)S(1)}, f32[32,1152]{1,0:T(8,128)S(1)}, u32[]{:S(2)}, u32[]{:S(2)}) collective-permute-start(f32[32,1152]{1,0:T(8,128)S(1)} %get-tuple-element.92), channel_id=1, source_target_pairs={{0,1},{1,0},{2,6},{3,7},{4,5},{5,4},{6,2},{7,3},{8,9},{9,8},{10,14... | collective-permute-start | bytes 442376 | tf_op jit(solution)/shard_map/ppermute | solution.py:430
  47.4 1.5 %collective-permute-start.10 = (f32[64,1152]{1,0:T(8,128)S(1)}, f32[64,1152]{1,0:T(8,128)S(1)}, u32[]{:S(2)}, u32[]{:S(2)}) collective-permute-start(f32[64,1152]{1,0:T(8,128)S(1)} %get-tuple-element.89), channel_id=1, source_target_pairs={{0,4},{1,5},{2,3},{3,2},{4,0},{5,1},{6,7},{7,6},{8,12},{9,13},{10,... | collective-permute-start | bytes 884744 | tf_op jit(solution)/shard_map/ppermute | solution.py:430
  48.9 1.1 %collective-permute-done.8.refs_2_ = f32[64,1152]{1,0:T(8,128)S(1)} collective-permute-done((f32[64,1152]{1,0:T(8,128)S(1)}, f32[64,1152]{1,0:T(8,128)S(1)}, u32[]{:S(2)}, u32[]{:S(2)}) %collective-permute-start.8) | collective-permute-done | bytes 294944 | tf_op jit(solution)/shard_map/ppermute | solution.py:430
  50.1 1.6 %collective-permute-start.9 = (f32[32,1152]{1,0:T(8,128)S(1)}, f32[32,1152]{1,0:T(8,128)S(1)}, u32[]{:S(2)}, u32[]{:S(2)}) collective-permute-start(f32[32,1152]{1,0:T(8,128)S(1)} %get-tuple-element.88), channel_id=1, source_target_pairs={{0,1},{1,0},{2,6},{3,7},{4,5},{5,4},{6,2},{7,3},{8,9},{9,8},{10,14... | collective-permute-start | bytes 442376 | tf_op jit(solution)/shard_map/ppermute | solution.py:430
  51.7 1.0 %collective-permute-done.12.refs_1_ = f32[32,1152]{1,0:T(8,128)S(1)} collective-permute-done((f32[32,1152]{1,0:T(8,128)S(1)}, f32[32,1152]{1,0:T(8,128)S(1)}, u32[]{:S(2)}, u32[]{:S(2)}) %collective-permute-start.12) | collective-permute-done | bytes 147488 | tf_op jit(solution)/shard_map/ppermute | solution.py:430
  52.8 2.5 %collective-permute-done.15.refs_2_ = f32[64,1152]{1,0:T(8,128)S(1)} collective-permute-done((f32[64,1152]{1,0:T(8,128)S(1)}, f32[64,1152]{1,0:T(8,128)S(1)}, u32[]{:S(2)}, u32[]{:S(2)}) %collective-permute-start.15) | collective-permute-done | bytes 294944 | tf_op jit(solution)/shard_map/ppermute | solution.py:430
  55.3 1.6 %collective-permute-start.16 = (f32[32,1152]{1,0:T(8,128)S(1)}, f32[32,1152]{1,0:T(8,128)S(1)}, u32[]{:S(2)}, u32[]{:S(2)}) collective-permute-start(f32[32,1152]{1,0:T(8,128)S(1)} %get-tuple-element.96), channel_id=1, source_target_pairs={{0,1},{1,0},{2,6},{3,7},{4,5},{5,4},{6,2},{7,3},{8,9},{9,8},{10,14... | collective-permute-start | bytes 442376 | tf_op jit(solution)/shard_map/ppermute | solution.py:430
  57.0 3.0 %collective-permute-done.10.refs_2_ = f32[64,1152]{1,0:T(8,128)S(1)} collective-permute-done((f32[64,1152]{1,0:T(8,128)S(1)}, f32[64,1152]{1,0:T(8,128)S(1)}, u32[]{:S(2)}, u32[]{:S(2)}) %collective-permute-start.10) | collective-permute-done | bytes 294944 | tf_op jit(solution)/shard_map/ppermute | solution.py:430
  60.1 1.0 %collective-permute-start.14 = (f32[32,1152]{1,0:T(8,128)S(1)}, f32[32,1152]{1,0:T(8,128)S(1)}, u32[]{:S(2)}, u32[]{:S(2)}) collective-permute-start(f32[32,1152]{1,0:T(8,128)S(1)} %add_rows.16), channel_id=1, source_target_pairs={{0,16},{1,17},{2,18},{3,19},{4,20},{5,21},{6,22},{7,23},{8,24},{9,... | collective-permute-start | bytes 442376 | tf_op jit(solution)/shard_map/ppermute | solution.py:430
  61.1 2.0 %collective-permute-start.17 = (f32[32,1152]{1,0:T(8,128)S(1)}, f32[32,1152]{1,0:T(8,128)S(1)}, u32[]{:S(2)}, u32[]{:S(2)}) collective-permute-start(f32[32,1152]{1,0:T(8,128)S(1)} %add_rows.19), channel_id=1, source_target_pairs={{0,8},{1,9},{2,10},{3,11},{4,12},{5,13},{6,14},{7,15},{8,0},{9,1},... | collective-permute-start | bytes 442376 | tf_op jit(solution)/shard_map/ppermute | solution.py:430
  63.2 1.6 %collective-permute-start.18 = (f32[32,1152]{1,0:T(8,128)S(1)}, f32[32,1152]{1,0:T(8,128)S(1)}, u32[]{:S(2)}, u32[]{:S(2)}) collective-permute-start(f32[32,1152]{1,0:T(8,128)S(1)} %get-tuple-element.99), channel_id=1, source_target_pairs={{0,1},{1,0},{2,6},{3,7},{4,5},{5,4},{6,2},{7,3},{8,9},{9,8},{10,14... | collective-permute-start | bytes 442376 | tf_op jit(solution)/shard_map/ppermute | solution.py:430
  64.8 2.7 %collective-permute-done.14.refs_0_ = f32[32,1152]{1,0:T(8,128)S(1)} collective-permute-done((f32[32,1152]{1,0:T(8,128)S(1)}, f32[32,1152]{1,0:T(8,128)S(1)}, u32[]{:S(2)}, u32[]{:S(2)}) %collective-permute-start.14) | collective-permute-done | bytes 147488 | tf_op jit(solution)/shard_map/ppermute | solution.py:430
  67.5 0.9 %collective-permute-done.18.refs_1_ = f32[32,1152]{1,0:T(8,128)S(1)} collective-permute-done((f32[32,1152]{1,0:T(8,128)S(1)}, f32[32,1152]{1,0:T(8,128)S(1)}, u32[]{:S(2)}, u32[]{:S(2)}) %collective-permute-start.18) | collective-permute-done | bytes 147488 | tf_op jit(solution)/shard_map/ppermute | solution.py:430
  68.4 0.7 finish.1
  (38 shorter events, 1.1 us)
Async XLA Ops:
  0.6 12.1 %copy-start = (bf16[1,128,1792]{2,1,0:T(8,128)(2,1)S(1)}, bf16[1,128,1792]{2,1,0:T(8,128)(2,1)}, u32[]{:S(2)}) copy-start(bf16[1,128,1792]{2,1,0:T(8,128)(2,1)} %param.10) | copy-start | bytes 1376260
  0.6 12.1 %copy-start.4 = (s32[1,64]{1,0:T(1,128)S(1)}, s32[1,64]{1,0:T(1,128)}, u32[]{:S(2)}) copy-start(s32[1,64]{1,0:T(1,128)} %index_ref.1) | copy-start | bytes 772
  0.7 12.1 %copy-start.5 = (s32[1,64]{1,0:T(1,128)S(1)}, s32[1,64]{1,0:T(1,128)}, u32[]{:S(2)}) copy-start(s32[1,64]{1,0:T(1,128)} %count_ref.1) | copy-start | bytes 772
  6.9 12.1 %collective-permute-start = (f32[14,16,128]{2,1,0:T(8,128)}, f32[14,16,128]{2,1,0:T(8,128)S(1)}, u32[]{:S(2)}, u32[]{:S(2)}) collective-permute-start(f32[14,16,128]{2,1,0:T(8,128)} %get-tuple-element.51), channel_id=1, source_target_pairs={{0,24},{1,25},{2,26},{3,27},{4,28},{5,29},{6,30},{7,31},{8,16},{9,... | collective-permute-start | bytes 344072 | tf_op jit(solution)/shard_map/ppermute | solution.py:430
  12.1 9.9 %collective-permute-start.1 = (f32[14,16,128]{2,1,0:T(8,128)}, f32[14,16,128]{2,1,0:T(8,128)S(1)}, u32[]{:S(2)}, u32[]{:S(2)}) collective-permute-start(f32[14,16,128]{2,1,0:T(8,128)} %get-tuple-element.52), channel_id=1, source_target_pairs={{0,16},{1,17},{2,18},{3,19},{4,20},{5,21},{6,22},{7,23},{8,24},{9,... | collective-permute-start | bytes 344072 | tf_op jit(solution)/shard_map/ppermute | solution.py:430
  12.1 9.9 %collective-permute-start.2 = (f32[14,16,128]{2,1,0:T(8,128)}, f32[14,16,128]{2,1,0:T(8,128)S(1)}, u32[]{:S(2)}, u32[]{:S(2)}) collective-permute-start(f32[14,16,128]{2,1,0:T(8,128)} %get-tuple-element.53), channel_id=1, source_target_pairs={{0,8},{1,9},{2,10},{3,11},{4,12},{5,13},{6,14},{7,15},{8,0},{9,1},... | collective-permute-start | bytes 344072 | tf_op jit(solution)/shard_map/ppermute | solution.py:430
  13.1 8.8 %copy-start.2 = (f32[14,16,128]{2,1,0:T(8,128)S(1)}, f32[14,16,128]{2,1,0:T(8,128)}, u32[]{:S(2)}) copy-start(f32[14,16,128]{2,1,0:T(8,128)} %get-tuple-element.62.refs_3_) | copy-start | bytes 344068
  13.2 13.6 %copy-start.3 = (s32[8,1024]{1,0:T(8,128)S(1)}, s32[8,1024]{1,0:T(8,128)}, u32[]{:S(2)}) copy-start(s32[8,1024]{1,0:T(8,128)} %constant.2.clone.table_ref) | copy-start | bytes 98308
  22.3 11.7 %collective-permute-start.3 = (f32[14,16,128]{2,1,0:T(8,128)S(1)}, f32[14,16,128]{2,1,0:T(8,128)S(1)}, u32[]{:S(2)}, u32[]{:S(2)}) collective-permute-start(f32[14,16,128]{2,1,0:T(8,128)S(1)} %get-tuple-element.65), channel_id=1, source_target_pairs={{0,24},{1,25},{2,26},{3,27},{4,28},{5,29},{6,30},{7,31},{8,16},{9,... | collective-permute-start | bytes 344072 | tf_op jit(solution)/shard_map/ppermute | solution.py:430
  24.8 9.3 %collective-permute-start.4 = (f32[14,16,128]{2,1,0:T(8,128)S(1)}, f32[14,16,128]{2,1,0:T(8,128)S(1)}, u32[]{:S(2)}, u32[]{:S(2)}) collective-permute-start(f32[14,16,128]{2,1,0:T(8,128)S(1)} %get-tuple-element.66), channel_id=1, source_target_pairs={{0,16},{1,17},{2,18},{3,19},{4,20},{5,21},{6,22},{7,23},{8,24},{9,... | collective-permute-start | bytes 344072 | tf_op jit(solution)/shard_map/ppermute | solution.py:430
  24.8 9.3 %copy-start.1 = (bf16[1024,112]{0,1:T(8,128)(2,1)S(1)}, bf16[1024,112]{0,1:T(8,128)(2,1)}, u32[]{:S(2)}) copy-start(bf16[1024,112]{0,1:T(8,128)(2,1)} %param.9) | copy-start | bytes 688132
  24.8 9.3 %collective-permute-start.5 = (f32[14,16,128]{2,1,0:T(8,128)S(1)}, f32[14,16,128]{2,1,0:T(8,128)S(1)}, u32[]{:S(2)}, u32[]{:S(2)}) collective-permute-start(f32[14,16,128]{2,1,0:T(8,128)S(1)} %get-tuple-element.67), channel_id=1, source_target_pairs={{0,8},{1,9},{2,10},{3,11},{4,12},{5,13},{6,14},{7,15},{8,0},{9,1},... | collective-permute-start | bytes 344072 | tf_op jit(solution)/shard_map/ppermute | solution.py:430
  36.0 2.9 %collective-permute-start.6 = (f32[256,1152]{1,0:T(8,128)S(1)}, f32[256,1152]{1,0:T(8,128)S(1)}, u32[]{:S(2)}, u32[]{:S(2)}) collective-permute-start(f32[256,1152]{1,0:T(8,128)S(1)} %get-tuple-element.79), channel_id=1, source_target_pairs={{0,2},{1,3},{2,0},{3,1},{4,6},{5,7},{6,4},{7,5},{8,10},{9,11},{10,... | collective-permute-start | bytes 3538952 | tf_op jit(solution)/shard_map/ppermute | solution.py:430
  37.6 5.9 %collective-permute-start.7 = (f32[256,1152]{1,0:T(8,128)S(1)}, f32[256,1152]{1,0:T(8,128)S(1)}, u32[]{:S(2)}, u32[]{:S(2)}) collective-permute-start(f32[256,1152]{1,0:T(8,128)S(1)} %get-tuple-element.85), channel_id=1, source_target_pairs={{0,2},{1,3},{2,0},{3,1},{4,6},{5,7},{6,4},{7,5},{8,10},{9,11},{10,... | collective-permute-start | bytes 3538952 | tf_op jit(solution)/shard_map/ppermute | solution.py:430
  39.0 6.8 %collective-permute-start.11 = (f32[64,1152]{1,0:T(8,128)S(1)}, f32[64,1152]{1,0:T(8,128)S(1)}, u32[]{:S(2)}, u32[]{:S(2)}) collective-permute-start(f32[64,1152]{1,0:T(8,128)S(1)} %get-tuple-element.90), channel_id=1, source_target_pairs={{0,4},{1,5},{2,3},{3,2},{4,0},{5,1},{6,7},{7,6},{8,12},{9,13},{10,... | collective-permute-start | bytes 884744 | tf_op jit(solution)/shard_map/ppermute | solution.py:430
  40.6 9.5 %collective-permute-start.8 = (f32[64,1152]{1,0:T(8,128)S(1)}, f32[64,1152]{1,0:T(8,128)S(1)}, u32[]{:S(2)}, u32[]{:S(2)}) collective-permute-start(f32[64,1152]{1,0:T(8,128)S(1)} %get-tuple-element.86), channel_id=1, source_target_pairs={{0,4},{1,5},{2,3},{3,2},{4,0},{5,1},{6,7},{7,6},{8,12},{9,13},{10,... | collective-permute-start | bytes 884744 | tf_op jit(solution)/shard_map/ppermute | solution.py:430
  42.0 13.3 %collective-permute-start.15 = (f32[64,1152]{1,0:T(8,128)S(1)}, f32[64,1152]{1,0:T(8,128)S(1)}, u32[]{:S(2)}, u32[]{:S(2)}) collective-permute-start(f32[64,1152]{1,0:T(8,128)S(1)} %get-tuple-element.94), channel_id=1, source_target_pairs={{0,4},{1,5},{2,3},{3,2},{4,0},{5,1},{6,7},{7,6},{8,12},{9,13},{10,... | collective-permute-start | bytes 884744 | tf_op jit(solution)/shard_map/ppermute | solution.py:430
  45.9 6.9 %collective-permute-start.12 = (f32[32,1152]{1,0:T(8,128)S(1)}, f32[32,1152]{1,0:T(8,128)S(1)}, u32[]{:S(2)}, u32[]{:S(2)}) collective-permute-start(f32[32,1152]{1,0:T(8,128)S(1)} %get-tuple-element.92), channel_id=1, source_target_pairs={{0,1},{1,0},{2,6},{3,7},{4,5},{5,4},{6,2},{7,3},{8,9},{9,8},{10,14... | collective-permute-start | bytes 442376 | tf_op jit(solution)/shard_map/ppermute | solution.py:430
  47.4 12.6 %collective-permute-start.10 = (f32[64,1152]{1,0:T(8,128)S(1)}, f32[64,1152]{1,0:T(8,128)S(1)}, u32[]{:S(2)}, u32[]{:S(2)}) collective-permute-start(f32[64,1152]{1,0:T(8,128)S(1)} %get-tuple-element.89), channel_id=1, source_target_pairs={{0,4},{1,5},{2,3},{3,2},{4,0},{5,1},{6,7},{7,6},{8,12},{9,13},{10,... | collective-permute-start | bytes 884744 | tf_op jit(solution)/shard_map/ppermute | solution.py:430
  50.1 6.9 %collective-permute-start.9 = (f32[32,1152]{1,0:T(8,128)S(1)}, f32[32,1152]{1,0:T(8,128)S(1)}, u32[]{:S(2)}, u32[]{:S(2)}) collective-permute-start(f32[32,1152]{1,0:T(8,128)S(1)} %get-tuple-element.88), channel_id=1, source_target_pairs={{0,1},{1,0},{2,6},{3,7},{4,5},{5,4},{6,2},{7,3},{8,9},{9,8},{10,14... | collective-permute-start | bytes 442376 | tf_op jit(solution)/shard_map/ppermute | solution.py:430
  52.7 7.3 %collective-permute-start.13 = (f32[32,1152]{1,0:T(8,128)S(1)}, f32[32,1152]{1,0:T(8,128)S(1)}, u32[]{:S(2)}, u32[]{:S(2)}) collective-permute-start(f32[32,1152]{1,0:T(8,128)S(1)} %add_rows.15), channel_id=1, source_target_pairs={{0,8},{1,9},{2,10},{3,11},{4,12},{5,13},{6,14},{7,15},{8,0},{9,1},... | collective-permute-start | bytes 442376 | tf_op jit(solution)/shard_map/ppermute | solution.py:430
  55.3 5.8 %collective-permute-start.16 = (f32[32,1152]{1,0:T(8,128)S(1)}, f32[32,1152]{1,0:T(8,128)S(1)}, u32[]{:S(2)}, u32[]{:S(2)}) collective-permute-start(f32[32,1152]{1,0:T(8,128)S(1)} %get-tuple-element.96), channel_id=1, source_target_pairs={{0,1},{1,0},{2,6},{3,7},{4,5},{5,4},{6,2},{7,3},{8,9},{9,8},{10,14... | collective-permute-start | bytes 442376 | tf_op jit(solution)/shard_map/ppermute | solution.py:430
  60.1 7.5 %collective-permute-start.14 = (f32[32,1152]{1,0:T(8,128)S(1)}, f32[32,1152]{1,0:T(8,128)S(1)}, u32[]{:S(2)}, u32[]{:S(2)}) collective-permute-start(f32[32,1152]{1,0:T(8,128)S(1)} %add_rows.16), channel_id=1, source_target_pairs={{0,16},{1,17},{2,18},{3,19},{4,20},{5,21},{6,22},{7,23},{8,24},{9,... | collective-permute-start | bytes 442376 | tf_op jit(solution)/shard_map/ppermute | solution.py:430
  61.1 7.3 %collective-permute-start.17 = (f32[32,1152]{1,0:T(8,128)S(1)}, f32[32,1152]{1,0:T(8,128)S(1)}, u32[]{:S(2)}, u32[]{:S(2)}) collective-permute-start(f32[32,1152]{1,0:T(8,128)S(1)} %add_rows.19), channel_id=1, source_target_pairs={{0,8},{1,9},{2,10},{3,11},{4,12},{5,13},{6,14},{7,15},{8,0},{9,1},... | collective-permute-start | bytes 442376 | tf_op jit(solution)/shard_map/ppermute | solution.py:430
  63.2 5.2 %collective-permute-start.18 = (f32[32,1152]{1,0:T(8,128)S(1)}, f32[32,1152]{1,0:T(8,128)S(1)}, u32[]{:S(2)}, u32[]{:S(2)}) collective-permute-start(f32[32,1152]{1,0:T(8,128)S(1)} %get-tuple-element.99), channel_id=1, source_target_pairs={{0,1},{1,0},{2,6},{3,7},{4,5},{5,4},{6,2},{7,3},{8,9},{9,8},{10,14... | collective-permute-start | bytes 442376 | tf_op jit(solution)/shard_map/ppermute | solution.py:430

commit v10 on v9

--- a/solution.py
+++ b/solution.py
@@ -275,11 +275,16 @@
     )(*pieces, target, weight)
 
 
-def first_body(parts, *refs):
-    scored_refs, (slope, w_out_t, ordered, result, gp, g, cells) = refs[:parts], refs[parts:]
+def first_body(parts, cuts, *refs):
+    scored_refs, (slope, w_out_t, ordered, *results, gp, g, cells) = refs[:parts], refs[parts:]
     carriers, share, _ = scored_refs[0].shape
     channels, width = w_out_t.shape
-    picked = result.shape[0]
+    picked = cuts[-1]
+
+    def put(columns, product):
+        for result, low, high in zip(results, cuts[:-1], cuts[1:]):
+            result[:, columns] = product[low:high]
+
     me_z = lax.axis_index("member")
     for k, scored_ref in zip(reversed(range(parts)), scored_refs):
         base = partner(me_z, k, parts) * (share * PATCH)
@@ -287,28 +292,28 @@
             cells[pl.ds(base + j, share, stride=PATCH), :] = value
     lane = lax.broadcasted_iota(jnp.int32, cells.shape, 1)
     g[...] = jnp.where(lane < channels, cells[...], 0.0).astype(jnp.bfloat16)
-    result[:, width:] = jnp.dot(ordered[1, :picked], g[...], preferred_element_type=jnp.float32)
+    put(slice(width, None), jnp.dot(ordered[1, :picked], g[...], preferred_element_type=jnp.float32))
     for c in column_steps(width):
         backward = jnp.dot(g[:, :channels], w_out_t[:, c], preferred_element_type=jnp.float32)
         gp[:, c] = (backward * slope[:, c]).astype(jnp.bfloat16)
-        result[:, c] = jnp.dot(ordered[0, :picked], gp[:, c], preferred_element_type=jnp.float32)
-
-
-def first_products(scored, slope, w_out_t, ordered, picked):
+        put(c, jnp.dot(ordered[0, :picked], gp[:, c], preferred_element_type=jnp.float32))
+
+
+def first_products(scored, slope, w_out_t, ordered, cuts):
     nrows, width = slope.shape
     channels = w_out_t.shape[0]
     return pl.pallas_call(
-        functools.partial(first_body, len(scored)),
+        functools.partial(first_body, len(scored), tuple(cuts)),
         in_specs=[WHOLE] * (len(scored) + 3),
-        out_specs=[WHOLE] * 3,
+        out_specs=[WHOLE] * (len(cuts) + 1),
         out_shape=[
-            jax.ShapeDtypeStruct((picked, width + LANES), jnp.float32),
+            *[jax.ShapeDtypeStruct((high - low, width + LANES), jnp.float32) for low, high in zip(cuts[:-1], cuts[1:])],
             jax.ShapeDtypeStruct((nrows, width), jnp.bfloat16),
             jax.ShapeDtypeStruct((nrows, LANES), jnp.bfloat16),
         ],
         scratch_shapes=[pltpu.VMEM((nrows, LANES), jnp.float32)],
         compiler_params=params(FEW),
-        cost_estimate=cost(2 * nrows * width * (channels + picked), 10 * MIB),
+        cost_estimate=cost(2 * nrows * width * (channels + cuts[-1]), 10 * MIB),
         name="first_products",
     )(*scored, slope, w_out_t, ordered)
 
@@ -483,10 +488,10 @@
     ordered = ordered_transposes(table, source_of, rows_in, hidden)
     returned, ordered = lax.optimization_barrier((returned, ordered))
 
-    other_send, gp, g = first_products(returned, slope, w_out_t, ordered, n_send)
-    core_send = shift_core(other_send, 1)
+    cuts = [0, sum(sent[:2]), n_send] if len(sent) > 2 else [0, n_send]
+    *other_sends, gp, g = first_products(returned, slope, w_out_t, ordered, cuts)
+    core_send = shift_core(other_sends[0], 1)
     own_send, other_keep = more_products(gp, g, ordered, [(n_send, middle), (middle, middle + n_keep)])
-    core_keep = shift_core(other_keep, 1)
 
     def added(inputs, pieces, flops=0):
         return list(add_rows(inputs, [[(0, rows, [(i, low) for i in range(len(inputs))])] for low, rows in pieces], flops))
@@ -494,8 +499,18 @@
     def pieces_of(sizes, low=0):
         return [(low + int(at), size) for at, size in zip(np.cumsum([0, *sizes[:-1]]), sizes)]
 
-    first_sends = added([own_send, core_send], pieces_of(sent))
-    first_sends, gp = lax.optimization_barrier((first_sends, gp))
+
+    def summed_sends(value, start, end):
+        plans = [
+            [(0, rows, [(0, low), (1, low - start)])] for low, rows in pieces_of(sent) if start <= low < end
+        ]
+        return list(add_rows([own_send, value], plans))
+
+    first_sends = summed_sends(core_send, 0, cuts[1])
+    first_sends, gp, other_keep, later = lax.optimization_barrier((first_sends, gp, other_keep, other_sends[1:]))
+    for value, start, end in zip(later, cuts[1:-1], cuts[2:]):
+        first_sends += summed_sends(shift_core(value, 1), start, end)
+    core_keep = shift_core(other_keep, 1)
     first_got = [send_all(value, nx - 1, shift_first) for value in first_sends]
     (own_keep,) = more_products(gp, g, ordered, [(middle + n_keep, middle + 2 * n_keep)])
 

time: 69.3 us -> 68.9 us (level)
    ppermute x19 -> x20, waiting for transfers between devices: 17.4 us -> 17 us  [shift(): lax.ppermute(value, ('member', 'tile', 'batch'), [(number(*place), number...]
    ppermute x19 -> x20, starting transfers between devices: 25.5 us -> 25.4 us  [shift(): lax.ppermute(value, ('member', 'tile', 'batch'), [(number(*place), number...]
  transfers between devices with their start and end apart: 19 -> 20, of which waited for: 10 -> 11; matrix products, arithmetic and copies ran while one was open for 0% -> 0% of each run, Pallas kernels for 24% -> 24%
where the time goes in v10:
time: 68.9 us; the launch traced here: 68.7 us
  Pallas kernels  25.4 us (37%)
  starting transfers between devices  25.4 us (37%)
  waiting for transfers between devices  17 us (25%)
  between operations  0.83 us (1%)
    ppermute x20, starting transfers between devices, shift(): lax.ppermute(value, ('member', 'tile', 'batch'), [(number(*place), number...  25.4 us
    ppermute x20, waiting for transfers between devices, shift(): lax.ppermute(value, ('member', 'tile', 'batch'), [(number(*place), number...  17 us
    pallas_call x1, Pallas kernels, ordered_transposes(): pl.pallas_call(functools.partial(order_body, source_of), grid=(nrows // b...  7.24 us
    pallas_call x1, Pallas kernels, decode(): pl.pallas_call(functools.partial(decode_body, tuple(pieces)), in_specs=[A...  6.26 us
    pallas_call x1, Pallas kernels, slopes(): pl.pallas_call(slope_body, grid=(nrows // block,), in_specs=[pl.BlockSpec...  5.82 us
    pallas_call x2, Pallas kernels, more_products(): pl.pallas_call(functools.partial(more_body, tuple(cuts)), in_specs=[WHOLE...  2.37 us
    pallas_call x1, Pallas kernels, first_products(): pl.pallas_call(functools.partial(first_body, len(scored), tuple(cuts)), i...  1.84 us
  transfers between devices with their start and end apart: 20, of which 11 were waited for; matrix products, arithmetic and copies ran while one was open for 0% of the time, Pallas kernels for 24%

profile of v10, /device:TPU:0, one launch (start us, length us, event | category | flops | bytes accessed | tf_op | source)
XLA Modules:
  0.0 68.7 jit_solution(15114568214800269114)
XLA Ops:
  0.7 6.3 %decode.1 = (f32[14,16,128]{2,1,0:T(8,128)}, f32[14,16,128]{2,1,0:T(8,128)}, f32[14,16,128]{2,1,0:T(8,128)}, f32[14,16,128]{2,1,0:T(8,128)}) custom-call(bf16[1024,1024]{1,0:T(8,128)(2,1)} %bitcast.6, bf16[1024,1024]{1,0:T(8,128)(2,1)} %w_in_ref.3, bf16[112,1024]{1,0:T(8,128)(2,1)} %bitcast.4), custom_call_target="tpu_custom_call" | custom-call | flops 2382364672 | bytes 5242880 | tf_op jit(solution)/shard_map/decode/pallas_call | solution.py:111
  6.9 5.1 %collective-permute-start = (f32[14,16,128]{2,1,0:T(8,128)}, f32[14,16,128]{2,1,0:T(8,128)S(1)}, u32[]{:S(2)}, u32[]{:S(2)}) collective-permute-start(f32[14,16,128]{2,1,0:T(8,128)} %get-tuple-element.52), channel_id=1, source_target_pairs={{0,24},{1,25},{2,26},{3,27},{4,28},{5,29},{6,30},{7,31},{8,16},{9,... | collective-permute-start | bytes 344072 | tf_op jit(solution)/shard_map/ppermute | solution.py:435
  12.1 0.6 collective-permute-start.2
  12.7 0.4 targets.1
  13.2 5.8 %slopes.1 = (f32[1024,1024]{1,0:T(8,128)S(1)}, bf16[1024,1024]{1,0:T(8,128)(2,1)S(1)}) custom-call(bf16[1024,1024]{1,0:T(8,128)(2,1)} %bitcast.7, bf16[1024,1024]{1,0:T(8,128)(2,1)} %w_in_ref.3), custom_call_target="tpu_custom_call" | custom-call | flops 2147483648 | bytes 4194304 | tf_op jit(solution)/shard_map/slopes/pallas_call | solution.py:153
  19.0 2.9 %collective-permute-done.1.refs_1_ = f32[14,16,128]{2,1,0:T(8,128)S(1)} collective-permute-done((f32[14,16,128]{2,1,0:T(8,128)}, f32[14,16,128]{2,1,0:T(8,128)S(1)}, u32[]{:S(2)}, u32[]{:S(2)}) %collective-permute-start.1) | collective-permute-done | bytes 114720 | tf_op jit(solution)/shard_map/ppermute | solution.py:435
  22.3 2.5 %collective-permute-start.3 = (f32[14,16,128]{2,1,0:T(8,128)S(1)}, f32[14,16,128]{2,1,0:T(8,128)S(1)}, u32[]{:S(2)}, u32[]{:S(2)}) collective-permute-start(f32[14,16,128]{2,1,0:T(8,128)S(1)} %get-tuple-element.66), channel_id=1, source_target_pairs={{0,24},{1,25},{2,26},{3,27},{4,28},{5,29},{6,30},{7,31},{8,16},{9,... | collective-permute-start | bytes 344072 | tf_op jit(solution)/shard_map/ppermute | solution.py:435
  24.8 1.9 %collective-permute-start.5 = (f32[14,16,128]{2,1,0:T(8,128)S(1)}, f32[14,16,128]{2,1,0:T(8,128)S(1)}, u32[]{:S(2)}, u32[]{:S(2)}) collective-permute-start(f32[14,16,128]{2,1,0:T(8,128)S(1)} %get-tuple-element.68), channel_id=1, source_target_pairs={{0,8},{1,9},{2,10},{3,11},{4,12},{5,13},{6,14},{7,15},{8,0},{9,1},... | collective-permute-start | bytes 344072 | tf_op jit(solution)/shard_map/ppermute | solution.py:435
  26.7 7.2 %ordered_transposes.1.refs_6_.ordered = bf16[2,1024,1024]{2,1,0:T(8,128)(2,1)S(1)} custom-call(s32[8,1024]{1,0:T(8,128)S(1)} %copy-done.3, bf16[1024,1024]{1,0:T(8,128)(2,1)} %bitcast.8, bf16[1024,1024]{1,0:T(8,128)(2,1)S(1)} %get-tuple-element.70.hidden_ref), custom_call_target="tpu_custom_call" | custom-call | flops 1073741824 | bytes 4194304 | tf_op jit(solution)/shard_map/ordered_transposes/pallas_call | solution.py:182
  34.1 1.8 %first_products.1 = (f32[128,1152]{1,0:T(8,128)S(1)}, f32[128,1152]{1,0:T(8,128)S(1)}, bf16[1024,1024]{1,0:T(8,128)(2,1)S(1)}, bf16[1024,128]{1,0:T(8,128)(2,1)S(1)}) custom-call(f32[14,16,128]{2,1,0:T(8,128)S(1)} %collective-permute-done.3.refs_0_, f32[14,16,128]{2,1,0:T(8,128)S(1)} %collective-permute-done.4.refs_1_, ...), custom_call_target="tpu_custom_call" | custom-call | flops 771751936 | bytes 10485760 | tf_op jit(solution)/shard_map/first_products/pallas_call | solution.py:305
  36.0 1.5 %more_products.2 = (f32[256,1152]{1,0:T(8,128)S(1)}, f32[256,1152]{1,0:T(8,128)S(1)}) custom-call(bf16[1024,1024]{1,0:T(8,128)(2,1)S(1)} %get-tuple-element.85.gp, bf16[1024,128]{1,0:T(8,128)(2,1)S(1)} %get-tuple-element.78.g, bf16[2,1024,1024]{2,1,0:T(8,128)(2,1)S(1)} %ordered_transposes.1.refs_6_.ordered), custom_call_target="tpu_custom_call" | custom-call | flops 1073741824 | bytes 6291456 | tf_op jit(solution)/shard_map/more_products/pallas_call | solution.py:337
  37.6 0.5 collective-permute-done.6.refs_1_
  38.3 0.4 collective-permute-start.10
  38.7 1.5 %collective-permute-start.12 = (f32[64,1152]{1,0:T(8,128)S(1)}, f32[64,1152]{1,0:T(8,128)S(1)}, u32[]{:S(2)}, u32[]{:S(2)}) collective-permute-start(f32[64,1152]{1,0:T(8,128)S(1)} %get-tuple-element.92), channel_id=1, source_target_pairs={{0,4},{1,5},{2,3},{3,2},{4,0},{5,1},{6,7},{7,6},{8,12},{9,13},{10,... | collective-permute-start | bytes 884744 | tf_op jit(solution)/shard_map/ppermute | solution.py:435
  40.2 0.5 collective-permute-start.8
  40.7 0.8 %more_products.3.refs_0_ = f32[256,1152]{1,0:T(8,128)S(1)} custom-call(bf16[1024,1024]{1,0:T(8,128)(2,1)S(1)} %get-tuple-element.85.gp, bf16[1024,128]{1,0:T(8,128)(2,1)S(1)} %get-tuple-element.78.g, bf16[2,1024,1024]{2,1,0:T(8,128)(2,1)S(1)} %ordered_transposes.1.refs_6_.ordered), custom_call_target="tpu_custom_call" | custom-call | flops 536870912 | bytes 6291456 | tf_op jit(solution)/shard_map/more_products/pallas_call | solution.py:337
  41.9 1.6 %collective-permute-start.16 = (f32[64,1152]{1,0:T(8,128)S(1)}, f32[64,1152]{1,0:T(8,128)S(1)}, u32[]{:S(2)}, u32[]{:S(2)}) collective-permute-start(f32[64,1152]{1,0:T(8,128)S(1)} %get-tuple-element.96), channel_id=1, source_target_pairs={{0,4},{1,5},{2,3},{3,2},{4,0},{5,1},{6,7},{7,6},{8,12},{9,13},{10,... | collective-permute-start | bytes 884744 | tf_op jit(solution)/shard_map/ppermute | solution.py:435
  43.5 1.9 %collective-permute-done.12.refs_2_ = f32[64,1152]{1,0:T(8,128)S(1)} collective-permute-done((f32[64,1152]{1,0:T(8,128)S(1)}, f32[64,1152]{1,0:T(8,128)S(1)}, u32[]{:S(2)}, u32[]{:S(2)}) %collective-permute-start.12) | collective-permute-done | bytes 294944 | tf_op jit(solution)/shard_map/ppermute | solution.py:435
  45.5 1.6 %collective-permute-start.13 = (f32[32,1152]{1,0:T(8,128)S(1)}, f32[32,1152]{1,0:T(8,128)S(1)}, u32[]{:S(2)}, u32[]{:S(2)}) collective-permute-start(f32[32,1152]{1,0:T(8,128)S(1)} %get-tuple-element.94), channel_id=1, source_target_pairs={{0,1},{1,0},{2,6},{3,7},{4,5},{5,4},{6,2},{7,3},{8,9},{9,8},{10,14... | collective-permute-start | bytes 442376 | tf_op jit(solution)/shard_map/ppermute | solution.py:435
  47.0 1.5 %collective-permute-start.11 = (f32[64,1152]{1,0:T(8,128)S(1)}, f32[64,1152]{1,0:T(8,128)S(1)}, u32[]{:S(2)}, u32[]{:S(2)}) collective-permute-start(f32[64,1152]{1,0:T(8,128)S(1)} %get-tuple-element.91), channel_id=1, source_target_pairs={{0,4},{1,5},{2,3},{3,2},{4,0},{5,1},{6,7},{7,6},{8,12},{9,13},{10,... | collective-permute-start | bytes 884744 | tf_op jit(solution)/shard_map/ppermute | solution.py:435
  48.5 1.1 %collective-permute-done.8.refs_2_ = f32[64,1152]{1,0:T(8,128)S(1)} collective-permute-done((f32[64,1152]{1,0:T(8,128)S(1)}, f32[64,1152]{1,0:T(8,128)S(1)}, u32[]{:S(2)}, u32[]{:S(2)}) %collective-permute-start.8) | collective-permute-done | bytes 294944 | tf_op jit(solution)/shard_map/ppermute | solution.py:435
  49.7 1.6 %collective-permute-start.9 = (f32[32,1152]{1,0:T(8,128)S(1)}, f32[32,1152]{1,0:T(8,128)S(1)}, u32[]{:S(2)}, u32[]{:S(2)}) collective-permute-start(f32[32,1152]{1,0:T(8,128)S(1)} %get-tuple-element.89), channel_id=1, source_target_pairs={{0,1},{1,0},{2,6},{3,7},{4,5},{5,4},{6,2},{7,3},{8,9},{9,8},{10,14... | collective-permute-start | bytes 442376 | tf_op jit(solution)/shard_map/ppermute | solution.py:435
  51.3 1.0 %collective-permute-done.13.refs_1_ = f32[32,1152]{1,0:T(8,128)S(1)} collective-permute-done((f32[32,1152]{1,0:T(8,128)S(1)}, f32[32,1152]{1,0:T(8,128)S(1)}, u32[]{:S(2)}, u32[]{:S(2)}) %collective-permute-start.13) | collective-permute-done | bytes 147488 | tf_op jit(solution)/shard_map/ppermute | solution.py:435
  52.4 2.5 %collective-permute-done.16.refs_2_ = f32[64,1152]{1,0:T(8,128)S(1)} collective-permute-done((f32[64,1152]{1,0:T(8,128)S(1)}, f32[64,1152]{1,0:T(8,128)S(1)}, u32[]{:S(2)}, u32[]{:S(2)}) %collective-permute-start.16) | collective-permute-done | bytes 294944 | tf_op jit(solution)/shard_map/ppermute | solution.py:435
  54.9 1.6 %collective-permute-start.17 = (f32[32,1152]{1,0:T(8,128)S(1)}, f32[32,1152]{1,0:T(8,128)S(1)}, u32[]{:S(2)}, u32[]{:S(2)}) collective-permute-start(f32[32,1152]{1,0:T(8,128)S(1)} %get-tuple-element.98), channel_id=1, source_target_pairs={{0,1},{1,0},{2,6},{3,7},{4,5},{5,4},{6,2},{7,3},{8,9},{9,8},{10,14... | collective-permute-start | bytes 442376 | tf_op jit(solution)/shard_map/ppermute | solution.py:435
  56.6 3.0 %collective-permute-done.11.refs_2_ = f32[64,1152]{1,0:T(8,128)S(1)} collective-permute-done((f32[64,1152]{1,0:T(8,128)S(1)}, f32[64,1152]{1,0:T(8,128)S(1)}, u32[]{:S(2)}, u32[]{:S(2)}) %collective-permute-start.11) | collective-permute-done | bytes 294944 | tf_op jit(solution)/shard_map/ppermute | solution.py:435
  59.6 1.0 %collective-permute-start.15 = (f32[32,1152]{1,0:T(8,128)S(1)}, f32[32,1152]{1,0:T(8,128)S(1)}, u32[]{:S(2)}, u32[]{:S(2)}) collective-permute-start(f32[32,1152]{1,0:T(8,128)S(1)} %add_rows.18), channel_id=1, source_target_pairs={{0,16},{1,17},{2,18},{3,19},{4,20},{5,21},{6,22},{7,23},{8,24},{9,... | collective-permute-start | bytes 442376 | tf_op jit(solution)/shard_map/ppermute | solution.py:435
  60.7 2.0 %collective-permute-start.18 = (f32[32,1152]{1,0:T(8,128)S(1)}, f32[32,1152]{1,0:T(8,128)S(1)}, u32[]{:S(2)}, u32[]{:S(2)}) collective-permute-start(f32[32,1152]{1,0:T(8,128)S(1)} %add_rows.21), channel_id=1, source_target_pairs={{0,8},{1,9},{2,10},{3,11},{4,12},{5,13},{6,14},{7,15},{8,0},{9,1},... | collective-permute-start | bytes 442376 | tf_op jit(solution)/shard_map/ppermute | solution.py:435
  62.8 1.6 %collective-permute-start.19 = (f32[32,1152]{1,0:T(8,128)S(1)}, f32[32,1152]{1,0:T(8,128)S(1)}, u32[]{:S(2)}, u32[]{:S(2)}) collective-permute-start(f32[32,1152]{1,0:T(8,128)S(1)} %get-tuple-element.101), channel_id=1, source_target_pairs={{0,1},{1,0},{2,6},{3,7},{4,5},{5,4},{6,2},{7,3},{8,9},{9,8},{10,14... | collective-permute-start | bytes 442376 | tf_op jit(solution)/shard_map/ppermute | solution.py:435
  64.4 2.7 %collective-permute-done.15.refs_0_ = f32[32,1152]{1,0:T(8,128)S(1)} collective-permute-done((f32[32,1152]{1,0:T(8,128)S(1)}, f32[32,1152]{1,0:T(8,128)S(1)}, u32[]{:S(2)}, u32[]{:S(2)}) %collective-permute-start.15) | collective-permute-done | bytes 147488 | tf_op jit(solution)/shard_map/ppermute | solution.py:435
  67.1 0.9 %collective-permute-done.19.refs_1_ = f32[32,1152]{1,0:T(8,128)S(1)} collective-permute-done((f32[32,1152]{1,0:T(8,128)S(1)}, f32[32,1152]{1,0:T(8,128)S(1)}, u32[]{:S(2)}, u32[]{:S(2)}) %collective-permute-start.19) | collective-permute-done | bytes 147488 | tf_op jit(solution)/shard_map/ppermute | solution.py:435
  68.0 0.7 finish.1
  (41 shorter events, 1.6 us)
Async XLA Ops:
  0.6 12.1 %copy-start = (bf16[1,128,1792]{2,1,0:T(8,128)(2,1)S(1)}, bf16[1,128,1792]{2,1,0:T(8,128)(2,1)}, u32[]{:S(2)}) copy-start(bf16[1,128,1792]{2,1,0:T(8,128)(2,1)} %param.10) | copy-start | bytes 1376260
  0.6 12.1 %copy-start.4 = (s32[1,64]{1,0:T(1,128)S(1)}, s32[1,64]{1,0:T(1,128)}, u32[]{:S(2)}) copy-start(s32[1,64]{1,0:T(1,128)} %index_ref.1) | copy-start | bytes 772
  0.7 12.0 %copy-start.5 = (s32[1,64]{1,0:T(1,128)S(1)}, s32[1,64]{1,0:T(1,128)}, u32[]{:S(2)}) copy-start(s32[1,64]{1,0:T(1,128)} %count_ref.1) | copy-start | bytes 772
  6.9 12.1 %collective-permute-start = (f32[14,16,128]{2,1,0:T(8,128)}, f32[14,16,128]{2,1,0:T(8,128)S(1)}, u32[]{:S(2)}, u32[]{:S(2)}) collective-permute-start(f32[14,16,128]{2,1,0:T(8,128)} %get-tuple-element.52), channel_id=1, source_target_pairs={{0,24},{1,25},{2,26},{3,27},{4,28},{5,29},{6,30},{7,31},{8,16},{9,... | collective-permute-start | bytes 344072 | tf_op jit(solution)/shard_map/ppermute | solution.py:435
  12.0 9.9 %collective-permute-start.1 = (f32[14,16,128]{2,1,0:T(8,128)}, f32[14,16,128]{2,1,0:T(8,128)S(1)}, u32[]{:S(2)}, u32[]{:S(2)}) collective-permute-start(f32[14,16,128]{2,1,0:T(8,128)} %get-tuple-element.53), channel_id=1, source_target_pairs={{0,16},{1,17},{2,18},{3,19},{4,20},{5,21},{6,22},{7,23},{8,24},{9,... | collective-permute-start | bytes 344072 | tf_op jit(solution)/shard_map/ppermute | solution.py:435
  12.1 9.9 %collective-permute-start.2 = (f32[14,16,128]{2,1,0:T(8,128)}, f32[14,16,128]{2,1,0:T(8,128)S(1)}, u32[]{:S(2)}, u32[]{:S(2)}) collective-permute-start(f32[14,16,128]{2,1,0:T(8,128)} %get-tuple-element.54), channel_id=1, source_target_pairs={{0,8},{1,9},{2,10},{3,11},{4,12},{5,13},{6,14},{7,15},{8,0},{9,1},... | collective-permute-start | bytes 344072 | tf_op jit(solution)/shard_map/ppermute | solution.py:435
  13.1 8.8 %copy-start.2 = (f32[14,16,128]{2,1,0:T(8,128)S(1)}, f32[14,16,128]{2,1,0:T(8,128)}, u32[]{:S(2)}) copy-start(f32[14,16,128]{2,1,0:T(8,128)} %get-tuple-element.63.refs_3_) | copy-start | bytes 344068
  13.1 13.6 %copy-start.3 = (s32[8,1024]{1,0:T(8,128)S(1)}, s32[8,1024]{1,0:T(8,128)}, u32[]{:S(2)}) copy-start(s32[8,1024]{1,0:T(8,128)} %constant.2.clone.table_ref) | copy-start | bytes 98308
  22.3 11.7 %collective-permute-start.3 = (f32[14,16,128]{2,1,0:T(8,128)S(1)}, f32[14,16,128]{2,1,0:T(8,128)S(1)}, u32[]{:S(2)}, u32[]{:S(2)}) collective-permute-start(f32[14,16,128]{2,1,0:T(8,128)S(1)} %get-tuple-element.66), channel_id=1, source_target_pairs={{0,24},{1,25},{2,26},{3,27},{4,28},{5,29},{6,30},{7,31},{8,16},{9,... | collective-permute-start | bytes 344072 | tf_op jit(solution)/shard_map/ppermute | solution.py:435
  24.8 9.3 %collective-permute-start.4 = (f32[14,16,128]{2,1,0:T(8,128)S(1)}, f32[14,16,128]{2,1,0:T(8,128)S(1)}, u32[]{:S(2)}, u32[]{:S(2)}) collective-permute-start(f32[14,16,128]{2,1,0:T(8,128)S(1)} %get-tuple-element.67), channel_id=1, source_target_pairs={{0,16},{1,17},{2,18},{3,19},{4,20},{5,21},{6,22},{7,23},{8,24},{9,... | collective-permute-start | bytes 344072 | tf_op jit(solution)/shard_map/ppermute | solution.py:435
  24.8 9.3 %copy-start.1 = (bf16[1024,112]{0,1:T(8,128)(2,1)S(1)}, bf16[1024,112]{0,1:T(8,128)(2,1)}, u32[]{:S(2)}) copy-start(bf16[1024,112]{0,1:T(8,128)(2,1)} %param.9) | copy-start | bytes 688132
  24.8 9.3 %collective-permute-start.5 = (f32[14,16,128]{2,1,0:T(8,128)S(1)}, f32[14,16,128]{2,1,0:T(8,128)S(1)}, u32[]{:S(2)}, u32[]{:S(2)}) collective-permute-start(f32[14,16,128]{2,1,0:T(8,128)S(1)} %get-tuple-element.68), channel_id=1, source_target_pairs={{0,8},{1,9},{2,10},{3,11},{4,12},{5,13},{6,14},{7,15},{8,0},{9,1},... | collective-permute-start | bytes 344072 | tf_op jit(solution)/shard_map/ppermute | solution.py:435
  36.0 2.1 %collective-permute-start.6 = (f32[128,1152]{1,0:T(8,128)S(1)}, f32[128,1152]{1,0:T(8,128)S(1)}, u32[]{:S(2)}, u32[]{:S(2)}) collective-permute-start(f32[128,1152]{1,0:T(8,128)S(1)} %get-tuple-element.80), channel_id=1, source_target_pairs={{0,2},{1,3},{2,0},{3,1},{4,6},{5,7},{6,4},{7,5},{8,10},{9,11},{10,... | collective-permute-start | bytes 1769480 | tf_op jit(solution)/shard_map/ppermute | solution.py:435
  38.1 7.3 %collective-permute-start.7 = (f32[256,1152]{1,0:T(8,128)S(1)}, f32[256,1152]{1,0:T(8,128)S(1)}, u32[]{:S(2)}, u32[]{:S(2)}) collective-permute-start(f32[256,1152]{1,0:T(8,128)S(1)} %get-tuple-element.86), channel_id=1, source_target_pairs={{0,2},{1,3},{2,0},{3,1},{4,6},{5,7},{6,4},{7,5},{8,10},{9,11},{10,... | collective-permute-start | bytes 3538952 | tf_op jit(solution)/shard_map/ppermute | solution.py:435
  38.3 3.6 %collective-permute-start.10 = (f32[128,1152]{1,0:T(8,128)S(1)}, f32[128,1152]{1,0:T(8,128)S(1)}, u32[]{:S(2)}, u32[]{:S(2)}) collective-permute-start(f32[128,1152]{1,0:T(8,128)S(1)} %get-tuple-element.90), channel_id=1, source_target_pairs={{0,2},{1,3},{2,0},{3,1},{4,6},{5,7},{6,4},{7,5},{8,10},{9,11},{10,... | collective-permute-start | bytes 1769480 | tf_op jit(solution)/shard_map/ppermute | solution.py:435
  38.7 6.7 %collective-permute-start.12 = (f32[64,1152]{1,0:T(8,128)S(1)}, f32[64,1152]{1,0:T(8,128)S(1)}, u32[]{:S(2)}, u32[]{:S(2)}) collective-permute-start(f32[64,1152]{1,0:T(8,128)S(1)} %get-tuple-element.92), channel_id=1, source_target_pairs={{0,4},{1,5},{2,3},{3,2},{4,0},{5,1},{6,7},{7,6},{8,12},{9,13},{10,... | collective-permute-start | bytes 884744 | tf_op jit(solution)/shard_map/ppermute | solution.py:435
  40.2 9.5 %collective-permute-start.8 = (f32[64,1152]{1,0:T(8,128)S(1)}, f32[64,1152]{1,0:T(8,128)S(1)}, u32[]{:S(2)}, u32[]{:S(2)}) collective-permute-start(f32[64,1152]{1,0:T(8,128)S(1)} %get-tuple-element.87), channel_id=1, source_target_pairs={{0,4},{1,5},{2,3},{3,2},{4,0},{5,1},{6,7},{7,6},{8,12},{9,13},{10,... | collective-permute-start | bytes 884744 | tf_op jit(solution)/shard_map/ppermute | solution.py:435
  41.9 13.0 %collective-permute-start.16 = (f32[64,1152]{1,0:T(8,128)S(1)}, f32[64,1152]{1,0:T(8,128)S(1)}, u32[]{:S(2)}, u32[]{:S(2)}) collective-permute-start(f32[64,1152]{1,0:T(8,128)S(1)} %get-tuple-element.96), channel_id=1, source_target_pairs={{0,4},{1,5},{2,3},{3,2},{4,0},{5,1},{6,7},{7,6},{8,12},{9,13},{10,... | collective-permute-start | bytes 884744 | tf_op jit(solution)/shard_map/ppermute | solution.py:435
  45.5 6.9 %collective-permute-start.13 = (f32[32,1152]{1,0:T(8,128)S(1)}, f32[32,1152]{1,0:T(8,128)S(1)}, u32[]{:S(2)}, u32[]{:S(2)}) collective-permute-start(f32[32,1152]{1,0:T(8,128)S(1)} %get-tuple-element.94), channel_id=1, source_target_pairs={{0,1},{1,0},{2,6},{3,7},{4,5},{5,4},{6,2},{7,3},{8,9},{9,8},{10,14... | collective-permute-start | bytes 442376 | tf_op jit(solution)/shard_map/ppermute | solution.py:435
  47.0 12.6 %collective-permute-start.11 = (f32[64,1152]{1,0:T(8,128)S(1)}, f32[64,1152]{1,0:T(8,128)S(1)}, u32[]{:S(2)}, u32[]{:S(2)}) collective-permute-start(f32[64,1152]{1,0:T(8,128)S(1)} %get-tuple-element.91), channel_id=1, source_target_pairs={{0,4},{1,5},{2,3},{3,2},{4,0},{5,1},{6,7},{7,6},{8,12},{9,13},{10,... | collective-permute-start | bytes 884744 | tf_op jit(solution)/shard_map/ppermute | solution.py:435
  49.7 6.9 %collective-permute-start.9 = (f32[32,1152]{1,0:T(8,128)S(1)}, f32[32,1152]{1,0:T(8,128)S(1)}, u32[]{:S(2)}, u32[]{:S(2)}) collective-permute-start(f32[32,1152]{1,0:T(8,128)S(1)} %get-tuple-element.89), channel_id=1, source_target_pairs={{0,1},{1,0},{2,6},{3,7},{4,5},{5,4},{6,2},{7,3},{8,9},{9,8},{10,14... | collective-permute-start | bytes 442376 | tf_op jit(solution)/shard_map/ppermute | solution.py:435
  52.3 7.3 %collective-permute-start.14 = (f32[32,1152]{1,0:T(8,128)S(1)}, f32[32,1152]{1,0:T(8,128)S(1)}, u32[]{:S(2)}, u32[]{:S(2)}) collective-permute-start(f32[32,1152]{1,0:T(8,128)S(1)} %add_rows.17), channel_id=1, source_target_pairs={{0,8},{1,9},{2,10},{3,11},{4,12},{5,13},{6,14},{7,15},{8,0},{9,1},... | collective-permute-start | bytes 442376 | tf_op jit(solution)/shard_map/ppermute | solution.py:435
  54.9 5.7 %collective-permute-start.17 = (f32[32,1152]{1,0:T(8,128)S(1)}, f32[32,1152]{1,0:T(8,128)S(1)}, u32[]{:S(2)}, u32[]{:S(2)}) collective-permute-start(f32[32,1152]{1,0:T(8,128)S(1)} %get-tuple-element.98), channel_id=1, source_target_pairs={{0,1},{1,0},{2,6},{3,7},{4,5},{5,4},{6,2},{7,3},{8,9},{9,8},{10,14... | collective-permute-start | bytes 442376 | tf_op jit(solution)/shard_map/ppermute | solution.py:435
  59.6 7.5 %collective-permute-start.15 = (f32[32,1152]{1,0:T(8,128)S(1)}, f32[32,1152]{1,0:T(8,128)S(1)}, u32[]{:S(2)}, u32[]{:S(2)}) collective-permute-start(f32[32,1152]{1,0:T(8,128)S(1)} %add_rows.18), channel_id=1, source_target_pairs={{0,16},{1,17},{2,18},{3,19},{4,20},{5,21},{6,22},{7,23},{8,24},{9,... | collective-permute-start | bytes 442376 | tf_op jit(solution)/shard_map/ppermute | solution.py:435
  60.7 7.3 %collective-permute-start.18 = (f32[32,1152]{1,0:T(8,128)S(1)}, f32[32,1152]{1,0:T(8,128)S(1)}, u32[]{:S(2)}, u32[]{:S(2)}) collective-permute-start(f32[32,1152]{1,0:T(8,128)S(1)} %add_rows.21), channel_id=1, source_target_pairs={{0,8},{1,9},{2,10},{3,11},{4,12},{5,13},{6,14},{7,15},{8,0},{9,1},... | collective-permute-start | bytes 442376 | tf_op jit(solution)/shard_map/ppermute | solution.py:435
  62.8 5.2 %collective-permute-start.19 = (f32[32,1152]{1,0:T(8,128)S(1)}, f32[32,1152]{1,0:T(8,128)S(1)}, u32[]{:S(2)}, u32[]{:S(2)}) collective-permute-start(f32[32,1152]{1,0:T(8,128)S(1)} %get-tuple-element.101), channel_id=1, source_target_pairs={{0,1},{1,0},{2,6},{3,7},{4,5},{5,4},{6,2},{7,3},{8,9},{9,8},{10,14... | collective-permute-start | bytes 442376 | tf_op jit(solution)/shard_map/ppermute | solution.py:435

commit v11 on v10

--- a/solution.py
+++ b/solution.py
@@ -95,7 +95,7 @@
                 copy.wait()
         preact = jnp.dot(rows[i], w_in[...], preferred_element_type=jnp.float32)
         hidden = (preact / (1.0 + jnp.exp(-preact))).astype(jnp.bfloat16)
-        cells[i, :, :channels] = lax.dot_general(hidden, w_out_t[...], NT, preferred_element_type=jnp.float32)
+        cells[i, :block, :channels] = lax.dot_general(hidden, w_out_t[...], NT, preferred_element_type=jnp.float32)
         for j, row in enumerate(pack(lambda j: cells[i, pl.ds(j, share, stride=PATCH), :], channels)):
             out_refs[i][j] = row
 
@@ -117,7 +117,7 @@
             pltpu.VMEM((count, block, depth), jnp.bfloat16),
             pltpu.VMEM((depth, width), jnp.bfloat16),
             pltpu.VMEM((channels, width), jnp.bfloat16),
-            pltpu.VMEM((count, block, LANES), jnp.float32),
+            pltpu.VMEM((count, block + PATCH, LANES), jnp.float32),
             pltpu.SemaphoreType.DMA((count,)),
             pltpu.SemaphoreType.DMA((2,)),
         ],
@@ -290,8 +290,8 @@
         base = partner(me_z, k, parts) * (share * PATCH)
         for j, value in enumerate(unpack([scored_ref[j] for j in range(carriers)], channels)):
             cells[pl.ds(base + j, share, stride=PATCH), :] = value
-    lane = lax.broadcasted_iota(jnp.int32, cells.shape, 1)
-    g[...] = jnp.where(lane < channels, cells[...], 0.0).astype(jnp.bfloat16)
+    lane = lax.broadcasted_iota(jnp.int32, g.shape, 1)
+    g[...] = jnp.where(lane < channels, cells[:g.shape[0]], 0.0).astype(jnp.bfloat16)
     put(slice(width, None), jnp.dot(ordered[1, :picked], g[...], preferred_element_type=jnp.float32))
     for c in column_steps(width):
         backward = jnp.dot(g[:, :channels], w_out_t[:, c], preferred_element_type=jnp.float32)
@@ -311,7 +311,7 @@
             jax.ShapeDtypeStruct((nrows, width), jnp.bfloat16),
             jax.ShapeDtypeStruct((nrows, LANES), jnp.bfloat16),
         ],
-        scratch_shapes=[pltpu.VMEM((nrows, LANES), jnp.float32)],
+        scratch_shapes=[pltpu.VMEM((nrows + PATCH, LANES), jnp.float32)],
         compiler_params=params(FEW),
         cost_estimate=cost(2 * nrows * width * (channels + cuts[-1]), 10 * MIB),
         name="first_products",

time: 68.9 us -> 68.9 us (level)
  no operation moved by 1% of the time
where the time goes in v11:
time: 68.9 us; the launch traced here: 68.7 us
  Pallas kernels  25.4 us (37%)
  starting transfers between devices  25.4 us (37%)
  waiting for transfers between devices  17 us (25%)
  between operations  0.83 us (1%)
    ppermute x20, starting transfers between devices, shift(): lax.ppermute(value, ('member', 'tile', 'batch'), [(number(*place), number...  25.4 us
    ppermute x20, waiting for transfers between devices, shift(): lax.ppermute(value, ('member', 'tile', 'batch'), [(number(*place), number...  17 us
    pallas_call x1, Pallas kernels, ordered_transposes(): pl.pallas_call(functools.partial(order_body, source_of), grid=(nrows // b...  7.24 us
    pallas_call x1, Pallas kernels, decode(): pl.pallas_call(functools.partial(decode_body, tuple(pieces)), in_specs=[A...  6.26 us
    pallas_call x1, Pallas kernels, slopes(): pl.pallas_call(slope_body, grid=(nrows // block,), in_specs=[pl.BlockSpec...  5.82 us
    pallas_call x2, Pallas kernels, more_products(): pl.pallas_call(functools.partial(more_body, tuple(cuts)), in_specs=[WHOLE...  2.37 us
    pallas_call x1, Pallas kernels, first_products(): pl.pallas_call(functools.partial(first_body, len(scored), tuple(cuts)), i...  1.84 us
  transfers between devices with their start and end apart: 20, of which 11 were waited for; matrix products, arithmetic and copies ran while one was open for 0% of the time, Pallas kernels for 24%

profile of v11, /device:TPU:0, one launch (start us, length us, event | category | flops | bytes accessed | tf_op | source)
XLA Modules:
  0.0 68.7 jit_solution(7568301291329375179)
XLA Ops:
  0.7 6.3 %decode.1 = (f32[14,16,128]{2,1,0:T(8,128)}, f32[14,16,128]{2,1,0:T(8,128)}, f32[14,16,128]{2,1,0:T(8,128)}, f32[14,16,128]{2,1,0:T(8,128)}) custom-call(bf16[1024,1024]{1,0:T(8,128)(2,1)} %bitcast.6, bf16[1024,1024]{1,0:T(8,128)(2,1)} %w_in_ref.3, bf16[112,1024]{1,0:T(8,128)(2,1)} %bitcast.4), custom_call_target="tpu_custom_call" | custom-call | flops 2382364672 | bytes 5242880 | tf_op jit(solution)/shard_map/decode/pallas_call | solution.py:111
  6.9 5.1 %collective-permute-start = (f32[14,16,128]{2,1,0:T(8,128)}, f32[14,16,128]{2,1,0:T(8,128)S(1)}, u32[]{:S(2)}, u32[]{:S(2)}) collective-permute-start(f32[14,16,128]{2,1,0:T(8,128)} %get-tuple-element.52), channel_id=1, source_target_pairs={{0,24},{1,25},{2,26},{3,27},{4,28},{5,29},{6,30},{7,31},{8,16},{9,... | collective-permute-start | bytes 344072 | tf_op jit(solution)/shard_map/ppermute | solution.py:435
  12.1 0.6 collective-permute-start.2
  12.7 0.4 targets.1
  13.2 5.8 %slopes.1 = (f32[1024,1024]{1,0:T(8,128)S(1)}, bf16[1024,1024]{1,0:T(8,128)(2,1)S(1)}) custom-call(bf16[1024,1024]{1,0:T(8,128)(2,1)} %bitcast.7, bf16[1024,1024]{1,0:T(8,128)(2,1)} %w_in_ref.3), custom_call_target="tpu_custom_call" | custom-call | flops 2147483648 | bytes 4194304 | tf_op jit(solution)/shard_map/slopes/pallas_call | solution.py:153
  19.0 2.9 %collective-permute-done.1.refs_1_ = f32[14,16,128]{2,1,0:T(8,128)S(1)} collective-permute-done((f32[14,16,128]{2,1,0:T(8,128)}, f32[14,16,128]{2,1,0:T(8,128)S(1)}, u32[]{:S(2)}, u32[]{:S(2)}) %collective-permute-start.1) | collective-permute-done | bytes 114720 | tf_op jit(solution)/shard_map/ppermute | solution.py:435
  22.3 2.5 %collective-permute-start.3 = (f32[14,16,128]{2,1,0:T(8,128)S(1)}, f32[14,16,128]{2,1,0:T(8,128)S(1)}, u32[]{:S(2)}, u32[]{:S(2)}) collective-permute-start(f32[14,16,128]{2,1,0:T(8,128)S(1)} %get-tuple-element.66), channel_id=1, source_target_pairs={{0,24},{1,25},{2,26},{3,27},{4,28},{5,29},{6,30},{7,31},{8,16},{9,... | collective-permute-start | bytes 344072 | tf_op jit(solution)/shard_map/ppermute | solution.py:435
  24.8 1.9 %collective-permute-start.5 = (f32[14,16,128]{2,1,0:T(8,128)S(1)}, f32[14,16,128]{2,1,0:T(8,128)S(1)}, u32[]{:S(2)}, u32[]{:S(2)}) collective-permute-start(f32[14,16,128]{2,1,0:T(8,128)S(1)} %get-tuple-element.68), channel_id=1, source_target_pairs={{0,8},{1,9},{2,10},{3,11},{4,12},{5,13},{6,14},{7,15},{8,0},{9,1},... | collective-permute-start | bytes 344072 | tf_op jit(solution)/shard_map/ppermute | solution.py:435
  26.7 7.2 %ordered_transposes.1.refs_6_.ordered = bf16[2,1024,1024]{2,1,0:T(8,128)(2,1)S(1)} custom-call(s32[8,1024]{1,0:T(8,128)S(1)} %copy-done.3, bf16[1024,1024]{1,0:T(8,128)(2,1)} %bitcast.8, bf16[1024,1024]{1,0:T(8,128)(2,1)S(1)} %get-tuple-element.70.hidden_ref), custom_call_target="tpu_custom_call" | custom-call | flops 1073741824 | bytes 4194304 | tf_op jit(solution)/shard_map/ordered_transposes/pallas_call | solution.py:182
  34.1 1.8 %first_products.1 = (f32[128,1152]{1,0:T(8,128)S(1)}, f32[128,1152]{1,0:T(8,128)S(1)}, bf16[1024,1024]{1,0:T(8,128)(2,1)S(1)}, bf16[1024,128]{1,0:T(8,128)(2,1)S(1)}) custom-call(f32[14,16,128]{2,1,0:T(8,128)S(1)} %collective-permute-done.3.refs_0_, f32[14,16,128]{2,1,0:T(8,128)S(1)} %collective-permute-done.4.refs_1_, ...), custom_call_target="tpu_custom_call" | custom-call | flops 771751936 | bytes 10485760 | tf_op jit(solution)/shard_map/first_products/pallas_call | solution.py:305
  36.0 1.5 %more_products.2 = (f32[256,1152]{1,0:T(8,128)S(1)}, f32[256,1152]{1,0:T(8,128)S(1)}) custom-call(bf16[1024,1024]{1,0:T(8,128)(2,1)S(1)} %get-tuple-element.85.gp, bf16[1024,128]{1,0:T(8,128)(2,1)S(1)} %get-tuple-element.78.g, bf16[2,1024,1024]{2,1,0:T(8,128)(2,1)S(1)} %ordered_transposes.1.refs_6_.ordered), custom_call_target="tpu_custom_call" | custom-call | flops 1073741824 | bytes 6291456 | tf_op jit(solution)/shard_map/more_products/pallas_call | solution.py:337
  37.6 0.5 collective-permute-done.6.refs_1_
  38.3 0.4 collective-permute-start.10
  38.7 1.5 %collective-permute-start.12 = (f32[64,1152]{1,0:T(8,128)S(1)}, f32[64,1152]{1,0:T(8,128)S(1)}, u32[]{:S(2)}, u32[]{:S(2)}) collective-permute-start(f32[64,1152]{1,0:T(8,128)S(1)} %get-tuple-element.92), channel_id=1, source_target_pairs={{0,4},{1,5},{2,3},{3,2},{4,0},{5,1},{6,7},{7,6},{8,12},{9,13},{10,... | collective-permute-start | bytes 884744 | tf_op jit(solution)/shard_map/ppermute | solution.py:435
  40.2 0.5 collective-permute-start.8
  40.7 0.8 %more_products.3.refs_0_ = f32[256,1152]{1,0:T(8,128)S(1)} custom-call(bf16[1024,1024]{1,0:T(8,128)(2,1)S(1)} %get-tuple-element.85.gp, bf16[1024,128]{1,0:T(8,128)(2,1)S(1)} %get-tuple-element.78.g, bf16[2,1024,1024]{2,1,0:T(8,128)(2,1)S(1)} %ordered_transposes.1.refs_6_.ordered), custom_call_target="tpu_custom_call" | custom-call | flops 536870912 | bytes 6291456 | tf_op jit(solution)/shard_map/more_products/pallas_call | solution.py:337
  41.9 1.6 %collective-permute-start.16 = (f32[64,1152]{1,0:T(8,128)S(1)}, f32[64,1152]{1,0:T(8,128)S(1)}, u32[]{:S(2)}, u32[]{:S(2)}) collective-permute-start(f32[64,1152]{1,0:T(8,128)S(1)} %get-tuple-element.96), channel_id=1, source_target_pairs={{0,4},{1,5},{2,3},{3,2},{4,0},{5,1},{6,7},{7,6},{8,12},{9,13},{10,... | collective-permute-start | bytes 884744 | tf_op jit(solution)/shard_map/ppermute | solution.py:435
  43.5 1.9 %collective-permute-done.12.refs_2_ = f32[64,1152]{1,0:T(8,128)S(1)} collective-permute-done((f32[64,1152]{1,0:T(8,128)S(1)}, f32[64,1152]{1,0:T(8,128)S(1)}, u32[]{:S(2)}, u32[]{:S(2)}) %collective-permute-start.12) | collective-permute-done | bytes 294944 | tf_op jit(solution)/shard_map/ppermute | solution.py:435
  45.5 1.6 %collective-permute-start.13 = (f32[32,1152]{1,0:T(8,128)S(1)}, f32[32,1152]{1,0:T(8,128)S(1)}, u32[]{:S(2)}, u32[]{:S(2)}) collective-permute-start(f32[32,1152]{1,0:T(8,128)S(1)} %get-tuple-element.94), channel_id=1, source_target_pairs={{0,1},{1,0},{2,6},{3,7},{4,5},{5,4},{6,2},{7,3},{8,9},{9,8},{10,14... | collective-permute-start | bytes 442376 | tf_op jit(solution)/shard_map/ppermute | solution.py:435
  47.0 1.5 %collective-permute-start.11 = (f32[64,1152]{1,0:T(8,128)S(1)}, f32[64,1152]{1,0:T(8,128)S(1)}, u32[]{:S(2)}, u32[]{:S(2)}) collective-permute-start(f32[64,1152]{1,0:T(8,128)S(1)} %get-tuple-element.91), channel_id=1, source_target_pairs={{0,4},{1,5},{2,3},{3,2},{4,0},{5,1},{6,7},{7,6},{8,12},{9,13},{10,... | collective-permute-start | bytes 884744 | tf_op jit(solution)/shard_map/ppermute | solution.py:435
  48.5 1.1 %collective-permute-done.8.refs_2_ = f32[64,1152]{1,0:T(8,128)S(1)} collective-permute-done((f32[64,1152]{1,0:T(8,128)S(1)}, f32[64,1152]{1,0:T(8,128)S(1)}, u32[]{:S(2)}, u32[]{:S(2)}) %collective-permute-start.8) | collective-permute-done | bytes 294944 | tf_op jit(solution)/shard_map/ppermute | solution.py:435
  49.7 1.6 %collective-permute-start.9 = (f32[32,1152]{1,0:T(8,128)S(1)}, f32[32,1152]{1,0:T(8,128)S(1)}, u32[]{:S(2)}, u32[]{:S(2)}) collective-permute-start(f32[32,1152]{1,0:T(8,128)S(1)} %get-tuple-element.89), channel_id=1, source_target_pairs={{0,1},{1,0},{2,6},{3,7},{4,5},{5,4},{6,2},{7,3},{8,9},{9,8},{10,14... | collective-permute-start | bytes 442376 | tf_op jit(solution)/shard_map/ppermute | solution.py:435
  51.3 1.0 %collective-permute-done.13.refs_1_ = f32[32,1152]{1,0:T(8,128)S(1)} collective-permute-done((f32[32,1152]{1,0:T(8,128)S(1)}, f32[32,1152]{1,0:T(8,128)S(1)}, u32[]{:S(2)}, u32[]{:S(2)}) %collective-permute-start.13) | collective-permute-done | bytes 147488 | tf_op jit(solution)/shard_map/ppermute | solution.py:435
  52.4 2.5 %collective-permute-done.16.refs_2_ = f32[64,1152]{1,0:T(8,128)S(1)} collective-permute-done((f32[64,1152]{1,0:T(8,128)S(1)}, f32[64,1152]{1,0:T(8,128)S(1)}, u32[]{:S(2)}, u32[]{:S(2)}) %collective-permute-start.16) | collective-permute-done | bytes 294944 | tf_op jit(solution)/shard_map/ppermute | solution.py:435
  54.9 1.6 %collective-permute-start.17 = (f32[32,1152]{1,0:T(8,128)S(1)}, f32[32,1152]{1,0:T(8,128)S(1)}, u32[]{:S(2)}, u32[]{:S(2)}) collective-permute-start(f32[32,1152]{1,0:T(8,128)S(1)} %get-tuple-element.98), channel_id=1, source_target_pairs={{0,1},{1,0},{2,6},{3,7},{4,5},{5,4},{6,2},{7,3},{8,9},{9,8},{10,14... | collective-permute-start | bytes 442376 | tf_op jit(solution)/shard_map/ppermute | solution.py:435
  56.6 3.0 %collective-permute-done.11.refs_2_ = f32[64,1152]{1,0:T(8,128)S(1)} collective-permute-done((f32[64,1152]{1,0:T(8,128)S(1)}, f32[64,1152]{1,0:T(8,128)S(1)}, u32[]{:S(2)}, u32[]{:S(2)}) %collective-permute-start.11) | collective-permute-done | bytes 294944 | tf_op jit(solution)/shard_map/ppermute | solution.py:435
  59.6 1.0 %collective-permute-start.15 = (f32[32,1152]{1,0:T(8,128)S(1)}, f32[32,1152]{1,0:T(8,128)S(1)}, u32[]{:S(2)}, u32[]{:S(2)}) collective-permute-start(f32[32,1152]{1,0:T(8,128)S(1)} %add_rows.18), channel_id=1, source_target_pairs={{0,16},{1,17},{2,18},{3,19},{4,20},{5,21},{6,22},{7,23},{8,24},{9,... | collective-permute-start | bytes 442376 | tf_op jit(solution)/shard_map/ppermute | solution.py:435
  60.7 2.0 %collective-permute-start.18 = (f32[32,1152]{1,0:T(8,128)S(1)}, f32[32,1152]{1,0:T(8,128)S(1)}, u32[]{:S(2)}, u32[]{:S(2)}) collective-permute-start(f32[32,1152]{1,0:T(8,128)S(1)} %add_rows.21), channel_id=1, source_target_pairs={{0,8},{1,9},{2,10},{3,11},{4,12},{5,13},{6,14},{7,15},{8,0},{9,1},... | collective-permute-start | bytes 442376 | tf_op jit(solution)/shard_map/ppermute | solution.py:435
  62.8 1.6 %collective-permute-start.19 = (f32[32,1152]{1,0:T(8,128)S(1)}, f32[32,1152]{1,0:T(8,128)S(1)}, u32[]{:S(2)}, u32[]{:S(2)}) collective-permute-start(f32[32,1152]{1,0:T(8,128)S(1)} %get-tuple-element.101), channel_id=1, source_target_pairs={{0,1},{1,0},{2,6},{3,7},{4,5},{5,4},{6,2},{7,3},{8,9},{9,8},{10,14... | collective-permute-start | bytes 442376 | tf_op jit(solution)/shard_map/ppermute | solution.py:435
  64.4 2.7 %collective-permute-done.15.refs_0_ = f32[32,1152]{1,0:T(8,128)S(1)} collective-permute-done((f32[32,1152]{1,0:T(8,128)S(1)}, f32[32,1152]{1,0:T(8,128)S(1)}, u32[]{:S(2)}, u32[]{:S(2)}) %collective-permute-start.15) | collective-permute-done | bytes 147488 | tf_op jit(solution)/shard_map/ppermute | solution.py:435
  67.1 0.9 %collective-permute-done.19.refs_1_ = f32[32,1152]{1,0:T(8,128)S(1)} collective-permute-done((f32[32,1152]{1,0:T(8,128)S(1)}, f32[32,1152]{1,0:T(8,128)S(1)}, u32[]{:S(2)}, u32[]{:S(2)}) %collective-permute-start.19) | collective-permute-done | bytes 147488 | tf_op jit(solution)/shard_map/ppermute | solution.py:435
  68.0 0.7 finish.1
  (41 shorter events, 1.6 us)
Async XLA Ops:
  0.6 12.1 %copy-start = (bf16[1,128,1792]{2,1,0:T(8,128)(2,1)S(1)}, bf16[1,128,1792]{2,1,0:T(8,128)(2,1)}, u32[]{:S(2)}) copy-start(bf16[1,128,1792]{2,1,0:T(8,128)(2,1)} %param.10) | copy-start | bytes 1376260
  0.6 12.1 %copy-start.4 = (s32[1,64]{1,0:T(1,128)S(1)}, s32[1,64]{1,0:T(1,128)}, u32[]{:S(2)}) copy-start(s32[1,64]{1,0:T(1,128)} %index_ref.1) | copy-start | bytes 772
  0.7 12.0 %copy-start.5 = (s32[1,64]{1,0:T(1,128)S(1)}, s32[1,64]{1,0:T(1,128)}, u32[]{:S(2)}) copy-start(s32[1,64]{1,0:T(1,128)} %count_ref.1) | copy-start | bytes 772
  6.9 12.1 %collective-permute-start = (f32[14,16,128]{2,1,0:T(8,128)}, f32[14,16,128]{2,1,0:T(8,128)S(1)}, u32[]{:S(2)}, u32[]{:S(2)}) collective-permute-start(f32[14,16,128]{2,1,0:T(8,128)} %get-tuple-element.52), channel_id=1, source_target_pairs={{0,24},{1,25},{2,26},{3,27},{4,28},{5,29},{6,30},{7,31},{8,16},{9,... | collective-permute-start | bytes 344072 | tf_op jit(solution)/shard_map/ppermute | solution.py:435
  12.0 9.9 %collective-permute-start.1 = (f32[14,16,128]{2,1,0:T(8,128)}, f32[14,16,128]{2,1,0:T(8,128)S(1)}, u32[]{:S(2)}, u32[]{:S(2)}) collective-permute-start(f32[14,16,128]{2,1,0:T(8,128)} %get-tuple-element.53), channel_id=1, source_target_pairs={{0,16},{1,17},{2,18},{3,19},{4,20},{5,21},{6,22},{7,23},{8,24},{9,... | collective-permute-start | bytes 344072 | tf_op jit(solution)/shard_map/ppermute | solution.py:435
  12.1 9.9 %collective-permute-start.2 = (f32[14,16,128]{2,1,0:T(8,128)}, f32[14,16,128]{2,1,0:T(8,128)S(1)}, u32[]{:S(2)}, u32[]{:S(2)}) collective-permute-start(f32[14,16,128]{2,1,0:T(8,128)} %get-tuple-element.54), channel_id=1, source_target_pairs={{0,8},{1,9},{2,10},{3,11},{4,12},{5,13},{6,14},{7,15},{8,0},{9,1},... | collective-permute-start | bytes 344072 | tf_op jit(solution)/shard_map/ppermute | solution.py:435
  13.1 8.8 %copy-start.2 = (f32[14,16,128]{2,1,0:T(8,128)S(1)}, f32[14,16,128]{2,1,0:T(8,128)}, u32[]{:S(2)}) copy-start(f32[14,16,128]{2,1,0:T(8,128)} %get-tuple-element.63.refs_3_) | copy-start | bytes 344068
  13.1 13.6 %copy-start.3 = (s32[8,1024]{1,0:T(8,128)S(1)}, s32[8,1024]{1,0:T(8,128)}, u32[]{:S(2)}) copy-start(s32[8,1024]{1,0:T(8,128)} %constant.2.clone.table_ref) | copy-start | bytes 98308
  22.3 11.7 %collective-permute-start.3 = (f32[14,16,128]{2,1,0:T(8,128)S(1)}, f32[14,16,128]{2,1,0:T(8,128)S(1)}, u32[]{:S(2)}, u32[]{:S(2)}) collective-permute-start(f32[14,16,128]{2,1,0:T(8,128)S(1)} %get-tuple-element.66), channel_id=1, source_target_pairs={{0,24},{1,25},{2,26},{3,27},{4,28},{5,29},{6,30},{7,31},{8,16},{9,... | collective-permute-start | bytes 344072 | tf_op jit(solution)/shard_map/ppermute | solution.py:435
  24.8 9.3 %collective-permute-start.4 = (f32[14,16,128]{2,1,0:T(8,128)S(1)}, f32[14,16,128]{2,1,0:T(8,128)S(1)}, u32[]{:S(2)}, u32[]{:S(2)}) collective-permute-start(f32[14,16,128]{2,1,0:T(8,128)S(1)} %get-tuple-element.67), channel_id=1, source_target_pairs={{0,16},{1,17},{2,18},{3,19},{4,20},{5,21},{6,22},{7,23},{8,24},{9,... | collective-permute-start | bytes 344072 | tf_op jit(solution)/shard_map/ppermute | solution.py:435
  24.8 9.3 %copy-start.1 = (bf16[1024,112]{0,1:T(8,128)(2,1)S(1)}, bf16[1024,112]{0,1:T(8,128)(2,1)}, u32[]{:S(2)}) copy-start(bf16[1024,112]{0,1:T(8,128)(2,1)} %param.9) | copy-start | bytes 688132
  24.8 9.3 %collective-permute-start.5 = (f32[14,16,128]{2,1,0:T(8,128)S(1)}, f32[14,16,128]{2,1,0:T(8,128)S(1)}, u32[]{:S(2)}, u32[]{:S(2)}) collective-permute-start(f32[14,16,128]{2,1,0:T(8,128)S(1)} %get-tuple-element.68), channel_id=1, source_target_pairs={{0,8},{1,9},{2,10},{3,11},{4,12},{5,13},{6,14},{7,15},{8,0},{9,1},... | collective-permute-start | bytes 344072 | tf_op jit(solution)/shard_map/ppermute | solution.py:435
  36.0 2.1 %collective-permute-start.6 = (f32[128,1152]{1,0:T(8,128)S(1)}, f32[128,1152]{1,0:T(8,128)S(1)}, u32[]{:S(2)}, u32[]{:S(2)}) collective-permute-start(f32[128,1152]{1,0:T(8,128)S(1)} %get-tuple-element.80), channel_id=1, source_target_pairs={{0,2},{1,3},{2,0},{3,1},{4,6},{5,7},{6,4},{7,5},{8,10},{9,11},{10,... | collective-permute-start | bytes 1769480 | tf_op jit(solution)/shard_map/ppermute | solution.py:435
  38.1 7.3 %collective-permute-start.7 = (f32[256,1152]{1,0:T(8,128)S(1)}, f32[256,1152]{1,0:T(8,128)S(1)}, u32[]{:S(2)}, u32[]{:S(2)}) collective-permute-start(f32[256,1152]{1,0:T(8,128)S(1)} %get-tuple-element.86), channel_id=1, source_target_pairs={{0,2},{1,3},{2,0},{3,1},{4,6},{5,7},{6,4},{7,5},{8,10},{9,11},{10,... | collective-permute-start | bytes 3538952 | tf_op jit(solution)/shard_map/ppermute | solution.py:435
  38.3 3.6 %collective-permute-start.10 = (f32[128,1152]{1,0:T(8,128)S(1)}, f32[128,1152]{1,0:T(8,128)S(1)}, u32[]{:S(2)}, u32[]{:S(2)}) collective-permute-start(f32[128,1152]{1,0:T(8,128)S(1)} %get-tuple-element.90), channel_id=1, source_target_pairs={{0,2},{1,3},{2,0},{3,1},{4,6},{5,7},{6,4},{7,5},{8,10},{9,11},{10,... | collective-permute-start | bytes 1769480 | tf_op jit(solution)/shard_map/ppermute | solution.py:435
  38.7 6.7 %collective-permute-start.12 = (f32[64,1152]{1,0:T(8,128)S(1)}, f32[64,1152]{1,0:T(8,128)S(1)}, u32[]{:S(2)}, u32[]{:S(2)}) collective-permute-start(f32[64,1152]{1,0:T(8,128)S(1)} %get-tuple-element.92), channel_id=1, source_target_pairs={{0,4},{1,5},{2,3},{3,2},{4,0},{5,1},{6,7},{7,6},{8,12},{9,13},{10,... | collective-permute-start | bytes 884744 | tf_op jit(solution)/shard_map/ppermute | solution.py:435
  40.2 9.5 %collective-permute-start.8 = (f32[64,1152]{1,0:T(8,128)S(1)}, f32[64,1152]{1,0:T(8,128)S(1)}, u32[]{:S(2)}, u32[]{:S(2)}) collective-permute-start(f32[64,1152]{1,0:T(8,128)S(1)} %get-tuple-element.87), channel_id=1, source_target_pairs={{0,4},{1,5},{2,3},{3,2},{4,0},{5,1},{6,7},{7,6},{8,12},{9,13},{10,... | collective-permute-start | bytes 884744 | tf_op jit(solution)/shard_map/ppermute | solution.py:435
  41.9 13.0 %collective-permute-start.16 = (f32[64,1152]{1,0:T(8,128)S(1)}, f32[64,1152]{1,0:T(8,128)S(1)}, u32[]{:S(2)}, u32[]{:S(2)}) collective-permute-start(f32[64,1152]{1,0:T(8,128)S(1)} %get-tuple-element.96), channel_id=1, source_target_pairs={{0,4},{1,5},{2,3},{3,2},{4,0},{5,1},{6,7},{7,6},{8,12},{9,13},{10,... | collective-permute-start | bytes 884744 | tf_op jit(solution)/shard_map/ppermute | solution.py:435
  45.5 6.9 %collective-permute-start.13 = (f32[32,1152]{1,0:T(8,128)S(1)}, f32[32,1152]{1,0:T(8,128)S(1)}, u32[]{:S(2)}, u32[]{:S(2)}) collective-permute-start(f32[32,1152]{1,0:T(8,128)S(1)} %get-tuple-element.94), channel_id=1, source_target_pairs={{0,1},{1,0},{2,6},{3,7},{4,5},{5,4},{6,2},{7,3},{8,9},{9,8},{10,14... | collective-permute-start | bytes 442376 | tf_op jit(solution)/shard_map/ppermute | solution.py:435
  47.0 12.6 %collective-permute-start.11 = (f32[64,1152]{1,0:T(8,128)S(1)}, f32[64,1152]{1,0:T(8,128)S(1)}, u32[]{:S(2)}, u32[]{:S(2)}) collective-permute-start(f32[64,1152]{1,0:T(8,128)S(1)} %get-tuple-element.91), channel_id=1, source_target_pairs={{0,4},{1,5},{2,3},{3,2},{4,0},{5,1},{6,7},{7,6},{8,12},{9,13},{10,... | collective-permute-start | bytes 884744 | tf_op jit(solution)/shard_map/ppermute | solution.py:435
  49.7 6.9 %collective-permute-start.9 = (f32[32,1152]{1,0:T(8,128)S(1)}, f32[32,1152]{1,0:T(8,128)S(1)}, u32[]{:S(2)}, u32[]{:S(2)}) collective-permute-start(f32[32,1152]{1,0:T(8,128)S(1)} %get-tuple-element.89), channel_id=1, source_target_pairs={{0,1},{1,0},{2,6},{3,7},{4,5},{5,4},{6,2},{7,3},{8,9},{9,8},{10,14... | collective-permute-start | bytes 442376 | tf_op jit(solution)/shard_map/ppermute | solution.py:435
  52.3 7.3 %collective-permute-start.14 = (f32[32,1152]{1,0:T(8,128)S(1)}, f32[32,1152]{1,0:T(8,128)S(1)}, u32[]{:S(2)}, u32[]{:S(2)}) collective-permute-start(f32[32,1152]{1,0:T(8,128)S(1)} %add_rows.17), channel_id=1, source_target_pairs={{0,8},{1,9},{2,10},{3,11},{4,12},{5,13},{6,14},{7,15},{8,0},{9,1},... | collective-permute-start | bytes 442376 | tf_op jit(solution)/shard_map/ppermute | solution.py:435
  54.9 5.7 %collective-permute-start.17 = (f32[32,1152]{1,0:T(8,128)S(1)}, f32[32,1152]{1,0:T(8,128)S(1)}, u32[]{:S(2)}, u32[]{:S(2)}) collective-permute-start(f32[32,1152]{1,0:T(8,128)S(1)} %get-tuple-element.98), channel_id=1, source_target_pairs={{0,1},{1,0},{2,6},{3,7},{4,5},{5,4},{6,2},{7,3},{8,9},{9,8},{10,14... | collective-permute-start | bytes 442376 | tf_op jit(solution)/shard_map/ppermute | solution.py:435
  59.6 7.5 %collective-permute-start.15 = (f32[32,1152]{1,0:T(8,128)S(1)}, f32[32,1152]{1,0:T(8,128)S(1)}, u32[]{:S(2)}, u32[]{:S(2)}) collective-permute-start(f32[32,1152]{1,0:T(8,128)S(1)} %add_rows.18), channel_id=1, source_target_pairs={{0,16},{1,17},{2,18},{3,19},{4,20},{5,21},{6,22},{7,23},{8,24},{9,... | collective-permute-start | bytes 442376 | tf_op jit(solution)/shard_map/ppermute | solution.py:435
  60.7 7.3 %collective-permute-start.18 = (f32[32,1152]{1,0:T(8,128)S(1)}, f32[32,1152]{1,0:T(8,128)S(1)}, u32[]{:S(2)}, u32[]{:S(2)}) collective-permute-start(f32[32,1152]{1,0:T(8,128)S(1)} %add_rows.21), channel_id=1, source_target_pairs={{0,8},{1,9},{2,10},{3,11},{4,12},{5,13},{6,14},{7,15},{8,0},{9,1},... | collective-permute-start | bytes 442376 | tf_op jit(solution)/shard_map/ppermute | solution.py:435
  62.8 5.2 %collective-permute-start.19 = (f32[32,1152]{1,0:T(8,128)S(1)}, f32[32,1152]{1,0:T(8,128)S(1)}, u32[]{:S(2)}, u32[]{:S(2)}) collective-permute-start(f32[32,1152]{1,0:T(8,128)S(1)} %get-tuple-element.101), channel_id=1, source_target_pairs={{0,1},{1,0},{2,6},{3,7},{4,5},{5,4},{6,2},{7,3},{8,9},{9,8},{10,14... | collective-permute-start | bytes 442376 | tf_op jit(solution)/shard_map/ppermute | solution.py:435
